TPU v7x, 32 devices: a whole 2x2x4 slice. The times are simulated.
32 devices in a mesh: grid: 8 (over z, y), rep: 4 (over x, core).
Axes of the slice: x: 2, y: 2, z: 4, core: 2. Of those that a mesh axis runs over, the one named last changes fastest.
Arguments:
- amplitudes: bfloat16 [256, 30000], P('grid', 'rep'), may hold values from -6 to 6
- coupling: bfloat16 [30000, 28800], P('rep', 'grid'), may hold values from -0.046875 to 0.046875
- integrals: float32 [256, 60, 480], P('grid', 'rep'), may hold values from -6 to 6
- row_energy: float32 [256], P('grid'), may hold values from -4 to -0.8
- occ_energy: float32 [60], P('rep'), may hold values from -2 to -0.4
- vir_energy: float32 [480], replicated, may hold values from 0.2 to 3
- row_irrep: int32 [256], P('grid'), may hold values from 0 to 7, as said below
- occ_irrep: int32 [60], P('rep'), may hold values from 0 to 7
- vir_irrep: int32 [480], replicated, may hold values from 0 to 7
Outputs:
- updated: float32 [256, 60, 480], P('grid', 'rep')
Inputs may be any that keep to these rules, and one draw needn't show every extreme that they name: `row_irrep`: in every draw the 32 rows of some index of grid all carry irrep 0.
All inputs are finite; a program needn't handle non-finite values.
Results may differ from a plain program's by a relative error of at most 0.0003.
Values may be sent and summed in bfloat16 or wider, within the bound.
No kernel may reach another device: no remote copies, remote signals or barrier semaphores. Data moves between devices by JAX's collectives and lax.ppermute only.
A program may use at most 192 MiB of HBM per device.

v0:
```python
import jax
import jax.numpy as jnp
from jax import lax
from jax.sharding import PartitionSpec as P

NOCC = 60


def body(
    amplitudes,
    coupling,
    integrals,
    row_energy,
    occ_energy,
    vir_energy,
    row_irrep,
    occ_irrep,
    vir_irrep,
):
    cycle_terms = jnp.dot(
        lax.all_gather(amplitudes, "grid", axis=0, tiled=True),
        coupling,
        preferred_element_type=jnp.float32,
    )
    row_count = cycle_terms.shape[0]
    vir_local = coupling.shape[1] // NOCC
    cycle_terms = cycle_terms.reshape(row_count, vir_local, NOCC)
    summed_all = lax.psum(cycle_terms, "rep")
    slice_width = NOCC // lax.axis_size("rep")
    portion = lax.dynamic_slice_in_dim(
        summed_all, lax.axis_index("rep") * slice_width, slice_width, 2
    )
    arrived = lax.all_to_all(portion, "grid", split_axis=0, concat_axis=1, tiled=True)
    arrived = jnp.transpose(arrived, (0, 2, 1))
    denominator = row_energy[:, None, None] + occ_energy[None, :, None] - vir_energy[None, None, :]
    labels = jnp.bitwise_xor(
        jnp.bitwise_xor(row_irrep[:, None, None], occ_irrep[None, :, None]),
        vir_irrep[None, None, :],
    )
    allowed_mask = labels == 0
    return jnp.where(allowed_mask, (integrals + arrived) / denominator, jnp.float32(0.0))


def solution(mesh):
    return jax.shard_map(
        body,
        mesh=mesh,
        in_specs=(
            P("grid", "rep"),
            P("rep", "grid"),
            P("grid", "rep", None),
            P("grid"),
            P("rep"),
            P(),
            P("grid"),
            P("rep"),
            P(),
        ),
        out_specs=P("grid", "rep", None),
        check_vma=False,
    )
```

profile of v0, /device:TPU:0, one launch (start us, length us, event | category | flops | bytes accessed | tf_op | source)
XLA Modules:
  0.0 321.8 jit_solution(7897129799139306925)
XLA Ops:
  6.5 0.7 all-gather.2.cloned.1.call-update
  7.3 0.0 all-reduce.2.cloned.1.call-start
  7.3 74.3 %all-gather.2.cloned.1.call-done = bf16[256,7500]{1,0:T(8,128)(2,1)} async-done(((bf16[32,7500]{1,0:T(8,128)(2,1)}), bf16[256,7500]{1,0:T(8,128)(2,1)}) %all-gather.2.cloned.1.call-update) | async-done | bytes 3840016 | tf_op jit(solution)/shard_map/all_gather | solution.py:21
  81.6 24.1 %fusion.3 = f32[256,3600]{0,1:T(8,128)} fusion(bf16[256,7500]{1,0:T(8,128)(2,1)} %all-gather.2.cloned.1.call-done, bf16[7500,3600]{0,1:T(8,128)(2,1)} %param.10), kind=kOutput, calls=%fused_computation.8 | convolution fusion | flops 13824000000 | bytes 61526400 | tf_op jit(solution)/shard_map/dot_general | solution.py:20
  105.7 4.7 %reshape.69 = f32[256,60,60]{0,2,1:T(8,128)} reshape(f32[256,3600]{0,1:T(8,128)} %fusion.3) | data formatting | bytes 7372800 | tf_op jit(solution)/shard_map/reshape | solution.py:27
  110.4 9.3 %copy.14 = f32[256,60,60]{1,2,0:T(8,128)} copy(f32[256,60,60]{0,2,1:T(8,128)} %reshape.69) | data formatting | bytes 7372800 | tf_op jit(solution)/shard_map/reshape | solution.py:27
  119.8 0.0 all-reduce.2.cloned.1.call-update
  119.8 0.0 copy-start.3
  119.8 0.0 copy-start.5
  119.8 0.0 copy-start.6
  119.8 151.3 %all-reduce.2.cloned.1.call-done = f32[256,60,60]{1,2,0:T(8,128)} async-done(((f32[256,60,60]{1,2,0:T(8,128)}), f32[256,60,60]{1,2,0:T(8,128)}) %all-reduce.2.cloned.1.call-update) | async-done | bytes 3686416 | tf_op jit(solution)/shard_map/psum | solution.py:28
  271.2 2.1 fusion.2
  273.3 3.0 reshape.70
  276.3 5.5 %all-to-all-start = ((f32[8,1,28800]{2,1,0:T(1,128)}), f32[8,1,28800]{2,1,0:T(1,128)S(1)}, u32[]{:S(2)}, u32[]{:S(2)}) async-start(f32[8,1,28800]{2,1,0:T(1,128)} %reshape.70), calls=%async_computation | async-start | bytes 1843200 | tf_op jit(solution)/shard_map/all_to_all | solution.py:33
  281.9 0.1 broadcast_add_fusion
  281.9 0.1 broadcast_xor_fusion
  282.0 22.9 %all-to-all-done = f32[8,1,28800]{2,1,0:T(1,128)S(1)} async-done(((f32[8,1,28800]{2,1,0:T(1,128)}), f32[8,1,28800]{2,1,0:T(1,128)S(1)}, u32[]{:S(2)}, u32[]{:S(2)}) %all-to-all-start) | async-done | bytes 921632 | tf_op jit(solution)/shard_map/all_to_all | solution.py:33
  304.9 0.5 broadcast.48
  305.4 2.8 reduce
  308.3 0.9 reshape.71
  309.2 0.0 copy-start.2
  309.2 2.4 copy.16
  311.7 2.0 all_to_all.16
  313.7 1.2 fusion.1
  (11 shorter events, 0.0 us)
Async XLA Ops:
  6.5 75.0 %all-gather.2.cloned.1.call-start = ((), (), s32[]{:S(2)}) async-start(), calls=%async_computation.1 | async-start | bytes 4349952 | tf_op jit(solution)/shard_map/all_gather | solution.py:21
  7.3 263.9 %all-reduce.2.cloned.1.call-start = ((), (), s32[]{:S(2)}) async-start(), calls=%async_computation.2 | async-start | bytes 16777216 | tf_op jit(solution)/shard_map/psum | solution.py:28
  119.8 162.1 %copy-start.3 = (f32[15]{0:T(128)S(1)}, f32[15]{0:T(128)}, u32[]{:S(2)}) copy-start(f32[15]{0:T(128)} %param.13) | copy-start | bytes 184
  119.8 162.0 %copy-start.4 = (f32[32]{0:T(128)S(1)}, f32[32]{0:T(128)}, u32[]{:S(2)}) copy-start(f32[32]{0:T(128)} %param.12) | copy-start | bytes 388
  119.8 162.1 %copy-start.5 = (s32[15]{0:T(128)S(1)}, s32[15]{0:T(128)}, u32[]{:S(2)}) copy-start(s32[15]{0:T(128)} %param.16) | copy-start | bytes 184
  119.8 162.1 %copy-start.6 = (s32[32]{0:T(128)S(1)}, s32[32]{0:T(128)}, u32[]{:S(2)}) copy-start(s32[32]{0:T(128)} %param.15) | copy-start | bytes 388
  276.3 28.6 %all-to-all-start = ((f32[8,1,28800]{2,1,0:T(1,128)}), f32[8,1,28800]{2,1,0:T(1,128)S(1)}, u32[]{:S(2)}, u32[]{:S(2)}) async-start(f32[8,1,28800]{2,1,0:T(1,128)} %reshape.70), calls=%async_computation | async-start | bytes 1843200 | tf_op jit(solution)/shard_map/all_to_all | solution.py:33
  309.2 4.5 %copy-start = (f32[32,15,480]{2,0,1:T(8,128)S(1)}, f32[32,15,480]{2,0,1:T(8,128)}, u32[]{:S(2)}) copy-start(f32[32,15,480]{2,0,1:T(8,128)} %param.11) | copy-start | bytes 2764804
  309.2 4.5 %copy-start.1 = (f32[480]{0:T(512)S(1)}, f32[480]{0:T(512)}, u32[]{:S(2)}) copy-start(f32[480]{0:T(512)} %param.14) | copy-start | bytes 5764
  309.2 4.5 %copy-start.2 = (s32[480]{0:T(512)S(1)}, s32[480]{0:T(512)}, u32[]{:S(2)}) copy-start(s32[480]{0:T(512)} %param.17) | copy-start | bytes 5764
Sparse Core Ops, SparseCore 0:
  9.5 71.9 all-gather.1
  119.9 151.2 all-reduce.1
where the time goes:
time: 322 us
  waiting for transfers between devices  249 us (77%)
  local copies, waits for them, and re-layouts  25.1 us (8%)
  matrix products  24.1 us (7%)
  between operations  13.5 us (4%)
  starting transfers between devices  5.56 us (2%)
  other arithmetic  4.21 us (1%)
    psum x1, waiting for transfers between devices, body(): summed_all = lax.psum(cycle_terms, 'rep')  151 us
    all_gather x1, waiting for transfers between devices, body(): lax.all_gather(amplitudes, 'grid', axis=0, tiled=True)  74.3 us
    dot_general x1, matrix products, body(): jnp.dot(lax.all_gather(amplitudes, 'grid', axis=0, tiled=True), coupling,...  24.1 us
    all_to_all x1, waiting for transfers between devices, body(): lax.all_to_all(portion, 'grid', split_axis=0, concat_axis=1, tiled=True)  22.9 us
    reshape x2, local copies, waits for them, and re-layouts, body(): cycle_terms = cycle_terms.reshape(row_count, vir_local, NOCC)  14.1 us
  transfers between devices with their start and end apart: 3, of which 3 were waited for; matrix products, arithmetic and copies ran while one was open for 0% of the time, Pallas kernels for 0%

commit v1 on v0

v1 whole, which is shorter than its diff:
```python
import functools

import jax
import jax.numpy as jnp
import numpy as np
from jax import lax
from jax.experimental import pallas as pl
from jax.experimental.pallas import tpu as pltpu
from jax.sharding import PartitionSpec as P

NOCC = 60
LANES = 128
K_BLOCK = 2048
C_BLOCK = 240
STEPS = 8.0
TOP = 32767.0
VMEM_LIMIT = 48 * 1024 * 1024


def ceil_to(value, unit):
    return -(-value // unit) * unit


def encode(rows, count):
    index = lax.broadcasted_iota(jnp.int32, rows.shape, 0)
    rows = jnp.where(index < count, rows, 0.0)
    largest = jnp.max(jnp.abs(rows), axis=0, keepdims=True)
    level = jnp.ceil(jnp.log2(jnp.maximum(largest, 1e-30)) * STEPS) + 1.0
    coded = jnp.floor(rows * (jnp.exp2(level * (-1.0 / STEPS)) * TOP) + 0.5)
    return jnp.where(index == count, level, coded)


def decode(block, count):
    index = lax.broadcasted_iota(jnp.int32, block.shape, 0)
    scale = jnp.exp2(block[count : count + 1] * (1.0 / STEPS)) * (1.0 / TOP)
    return jnp.where(index < count, block * scale, 0.0)


def to_code(block):
    return block.astype(jnp.int32).astype(jnp.int16)


def from_code(block):
    return block.astype(jnp.int32).astype(jnp.float32)


def matrix_kernel(first, blocks, valid, *refs):
    place_ref = refs[0]
    pieces = refs[1 : 1 + blocks]
    coupling_ref = refs[1 + blocks]
    total_in = None if first else refs[2 + blocks]
    total_out, gathered = refs[-2:]
    rows = pieces[0].shape[0]
    depth = gathered.shape[1]

    @pl.when(pl.program_id(0) == 0)
    def _():
        for piece in range(blocks):
            at = pl.multiple_of(place_ref[piece] * rows, rows)
            gathered[pl.ds(at, rows), :] = pieces[piece][...]

    whole = valid // LANES * LANES
    contract = (((1,), (1,)), ((), ()))
    total = lax.dot_general(
        coupling_ref[:, :whole], gathered[:, :whole], contract, preferred_element_type=jnp.float32
    )
    if whole < valid:
        tail = slice(whole, whole + LANES)
        keep = lambda x: jnp.where(
            lax.broadcasted_iota(jnp.int32, x.shape, 1) < valid - whole, x, jnp.zeros_like(x)
        )
        total += lax.dot_general(
            keep(coupling_ref[:, tail]),
            keep(gathered[:, tail]),
            contract,
            preferred_element_type=jnp.float32,
        )
    for part in range(total_out.shape[0]):
        own = total[:, part * LANES : (part + 1) * LANES]
        total_out[part] = own if first else total_in[part] + own


def multiply(place, pieces, coupling, at, total, padded_columns):
    blocks = len(pieces)
    rows, width = pieces[0].shape
    slab = rows * blocks
    columns = coupling.shape[0]
    depth = min(K_BLOCK, ceil_to(width, LANES))
    pieces = [jnp.pad(p, ((0, 0), (0, depth - width))) if depth > width else p for p in pieces]
    first = total is None
    column_block = min(C_BLOCK, ceil_to(columns, 16))
    block_spec = pl.BlockSpec((slab // LANES, column_block, LANES), lambda i, p: (0, i, 0))
    in_specs = [pl.BlockSpec((rows, depth), lambda i, p: (0, 0))] * blocks
    in_specs += [pl.BlockSpec((column_block, K_BLOCK), lambda i, p: (i, at // K_BLOCK))]
    args = [*pieces, coupling]
    if not first:
        in_specs += [block_spec]
        args += [total]
    return pl.pallas_call(
        functools.partial(matrix_kernel, first, blocks, width),
        out_shape=jax.ShapeDtypeStruct((slab // LANES, padded_columns, LANES), jnp.float32),
        grid_spec=pltpu.PrefetchScalarGridSpec(
            num_scalar_prefetch=1,
            grid=(pl.cdiv(columns, column_block),),
            in_specs=in_specs,
            out_specs=block_spec,
            scratch_shapes=[pltpu.VMEM((slab, depth), jnp.bfloat16)],
        ),
        input_output_aliases={} if first else {len(args): 0},
        compiler_params=pltpu.CompilerParams(
            vmem_limit_bytes=VMEM_LIMIT, dimension_semantics=("arbitrary",)
        ),
        cost_estimate=pl.CostEstimate(
            flops=2 * columns * width * slab,
            bytes_accessed=2 * columns * width + 8 * columns * slab,
            transcendentals=0,
        ),
        name="matrix",
    )(place, *args)


def column_rows(total_ref, part, j, bp, width):
    rows = pl.ds(part * width + j, bp, stride=NOCC)
    return jnp.concatenate([total_ref[h, rows, :] for h in range(total_ref.shape[0])], axis=1)


def first_send_kernel(count, width, rep_ref, total_ref, out_ref):
    low = rep_ref[0] % 2

    def step(j, carry):
        for high in range(2):
            rows = column_rows(total_ref, 2 * high + 1 - low, j, out_ref.shape[2], width)
            out_ref[high, j] = to_code(encode(rows, count))
        return carry

    lax.fori_loop(0, width, step, 0)


def second_send_kernel(count, width, rep_ref, total_ref, got_ref, out_ref):
    low, high = rep_ref[0] % 2, 1 - rep_ref[0] // 2

    def step(j, carry):
        rows = column_rows(total_ref, 2 * high + low, j, out_ref.shape[1], width)
        rows = rows + decode(from_code(got_ref[high, j]), count)
        out_ref[j] = to_code(encode(rows, count))
        return carry

    lax.fori_loop(0, width, step, 0)


def keep_kernel(count, width, rep_ref, total_ref, got_ref, out_ref):
    low, high = rep_ref[0] % 2, rep_ref[0] // 2

    def step(j, carry):
        rows = column_rows(total_ref, 2 * high + low, j, out_ref.shape[1], width)
        out_ref[j] = rows + decode(from_code(got_ref[high, j]), count)
        return carry

    lax.fori_loop(0, width, step, 0)


def third_send_kernel(count, width, rows_dev, kept_ref, got_ref, out_ref):
    pack = LANES // rows_dev
    groups = out_ref.shape[1]
    bp, slab = kept_ref.shape[1:]

    def step(jj, carry):
        coded = []
        for jq in range(pack):
            j = jnp.minimum(jq * groups + jj, width - 1)
            coded.append(encode(kept_ref[j] + decode(from_code(got_ref[j]), count), count))
        for g in range(slab // rows_dev):
            own = [block[:, g * rows_dev : (g + 1) * rows_dev] for block in coded]
            out_ref[g, jj] = to_code(jnp.concatenate(own, axis=1))
        return carry

    lax.fori_loop(0, groups, step, 0)


def update_kernel(
    count,
    width,
    rows_dev,
    occ_energy_ref,
    occ_irrep_ref,
    got_ref,
    integrals_ref,
    row_energy_ref,
    vir_energy_ref,
    row_irrep_ref,
    vir_irrep_ref,
    out_ref,
    stage,
):
    pack = LANES // rows_dev
    groups = got_ref.shape[1]
    for jj in range(groups):
        for g in range(got_ref.shape[0]):
            block = from_code(got_ref[g, jj])
            stage[g * count : (g + 1) * count, :] = decode(block, count)[:count]
        turned = stage[...].T
        for jq in range(pack):
            j = jq * groups + jj
            if j >= width:
                continue
            cycle = turned[jq * rows_dev : (jq + 1) * rows_dev]
            denominator = row_energy_ref[...] + occ_energy_ref[j] - vir_energy_ref[...]
            labels = row_irrep_ref[...] ^ occ_irrep_ref[j] ^ vir_irrep_ref[...]
            out_ref[j] = jnp.where(
                labels == 0, (integrals_ref[j] + cycle) / denominator, jnp.float32(0.0)
            )


def local_call(kernel, out_shape, args, scalars=0, scratch=(), name=None):
    in_specs = [pl.BlockSpec(memory_space=pltpu.SMEM)] * scalars
    in_specs += [pl.BlockSpec(memory_space=pltpu.VMEM)] * (len(args) - scalars)
    return pl.pallas_call(
        kernel,
        out_shape=out_shape,
        in_specs=in_specs,
        out_specs=pl.BlockSpec(memory_space=pltpu.VMEM),
        scratch_shapes=list(scratch),
        compiler_params=pltpu.CompilerParams(vmem_limit_bytes=VMEM_LIMIT),
        cost_estimate=pl.CostEstimate(flops=10**7, bytes_accessed=4 * 10**6, transcendentals=0),
        name=name,
    )(*args)


def body(
    amplitudes,
    coupling,
    integrals,
    row_energy,
    occ_energy,
    vir_energy,
    row_irrep,
    occ_irrep,
    vir_irrep,
):
    grid_size = lax.axis_size("grid")
    me = lax.axis_index("grid")
    rep = lax.axis_index("rep").astype(jnp.int32).reshape(1)
    rows_dev, depth = amplitudes.shape
    coupling = coupling.T
    count = coupling.shape[0] // NOCC
    bp = ceil_to(count + 1, 16)
    slab = rows_dev * grid_size
    width = NOCC // lax.axis_size("rep")

    walk = [*range(0, grid_size, 2), *range(1, grid_size, 2)[::-1]]
    step_of = np.argsort(walk)
    onward = [(walk[i], walk[(i + 1) % grid_size]) for i in range(grid_size)]
    back = [(b, a) for a, b in onward]
    position = jnp.asarray(step_of, jnp.int32)[me]

    total = None
    for number, at in enumerate(range(0, depth, K_BLOCK)):
        own = amplitudes[:, at : at + K_BLOCK]
        pieces, offsets = [own], [0]
        longer = grid_size // 2
        hops = (longer, grid_size - 1 - longer)
        if number % 2:
            hops = hops[::-1]
        ahead = behind = own
        for hop in range(1, longer + 1):
            if hop <= hops[0]:
                ahead = lax.ppermute(ahead, "grid", onward)
                pieces.append(ahead)
                offsets.append(-hop)
            if hop <= hops[1]:
                behind = lax.ppermute(behind, "grid", back)
                pieces.append(behind)
                offsets.append(hop)
        place = jnp.asarray(walk, jnp.int32)[
            (position + jnp.asarray(offsets, jnp.int32) + grid_size) % grid_size
        ]
        total = multiply(place, pieces, coupling, at, total, bp * NOCC)

    low_pairs = [(i, i ^ 1) for i in range(lax.axis_size("rep"))]
    high_pairs = [(i, i ^ 2) for i in range(lax.axis_size("rep"))]
    shape = (width, bp, slab)
    send = local_call(
        functools.partial(first_send_kernel, count, width),
        jax.ShapeDtypeStruct((2, *shape), jnp.int16),
        (rep, total),
        1,
        name="first_send",
    )
    got = lax.ppermute(send, "rep", low_pairs)
    send = local_call(
        functools.partial(second_send_kernel, count, width),
        jax.ShapeDtypeStruct(shape, jnp.int16),
        (rep, total, got),
        1,
        name="second_send",
    )
    kept = local_call(
        functools.partial(keep_kernel, count, width),
        jax.ShapeDtypeStruct(shape, jnp.float32),
        (rep, total, got),
        1,
        name="keep",
    )
    got = lax.ppermute(send, "rep", high_pairs)

    groups = -(-width // (LANES // rows_dev))
    send = local_call(
        functools.partial(third_send_kernel, count, width, rows_dev),
        jax.ShapeDtypeStruct((grid_size, groups, bp, LANES), jnp.int16),
        (kept, got),
        name="third_send",
    )
    got = lax.all_to_all(send, "grid", split_axis=0, concat_axis=0, tiled=True)

    updated = local_call(
        functools.partial(update_kernel, count, width, rows_dev),
        jax.ShapeDtypeStruct((width, rows_dev, count * grid_size), jnp.float32),
        (
            occ_energy,
            occ_irrep,
            got,
            jnp.transpose(integrals, (1, 0, 2)),
            row_energy[:, None],
            vir_energy[None, :],
            row_irrep[:, None],
            vir_irrep[None, :],
        ),
        2,
        scratch=[pltpu.VMEM((count * grid_size, LANES), jnp.float32)],
        name="update",
    )
    return jnp.transpose(updated, (1, 0, 2))


def solution(mesh):
    return jax.shard_map(
        body,
        mesh=mesh,
        in_specs=(
            P("grid", "rep"),
            P("rep", "grid"),
            P("grid", "rep", None),
            P("grid"),
            P("rep"),
            P(),
            P("grid"),
            P("rep"),
            P(),
        ),
        out_specs=P("grid", "rep", None),
        check_vma=False,
    )
```

time: 322 us -> 143 us (0.44)
  waiting for transfers between devices: 249 us -> 31.5 us
  Pallas kernels: 0 us -> 62.8 us
  starting transfers between devices: 5.56 us -> 39.8 us
  matrix products: 24.1 us -> 0 us
  local copies, waits for them, and re-layouts: 25.1 us -> 6.09 us
  between operations: 13.5 us -> 0.29 us
    psum x1 -> x0, waiting for transfers between devices: 151 us -> none  [body(): summed_all = lax.psum(cycle_terms, 'rep')]
    all_gather x1 -> x0, waiting for transfers between devices: 74.3 us -> none  [body(): lax.all_gather(amplitudes, 'grid', axis=0, tiled=True)]
    pallas_call x0 -> x9, Pallas kernels: none -> 62.8 us  [the longest x4 56.3 us: multiply(): pl.pallas_call(functools.partial(matrix_kernel, first, blocks, width), ou...]
    ppermute x0 -> x30, starting transfers between devices: none -> 34.8 us  [the longest x14 16.8 us: body(): ahead = lax.ppermute(ahead, 'grid', onward)]
    dot_general x1 -> x0, matrix products: 24.1 us -> none  [body(): jnp.dot(lax.all_gather(amplitudes, 'grid', axis=0, tiled=True), coupling,...]
    ppermute x0 -> x30, waiting for transfers between devices: none -> 17.7 us  [the longest x1 11.5 us: body(): got = lax.ppermute(send, 'rep', high_pairs)]
    reshape x2 -> x0, local copies, waits for them, and re-layouts: 14.1 us -> none  [body(): cycle_terms = cycle_terms.reshape(row_count, vir_local, NOCC)]
    all_to_all x1, waiting for transfers between devices: 22.9 us -> 13.8 us  [body(): got = lax.all_to_all(send, 'grid', split_axis=0, concat_axis=0, tiled=True)]
  transfers between devices with their start and end apart: 3 -> 31, of which waited for: 3 -> 10; matrix products, arithmetic and copies ran while one was open for 0% -> 5% of each run, Pallas kernels for 0% -> 21%
where the time goes in v1:
time: 143 us; the launch traced here: 142 us
  Pallas kernels  62.8 us (44%)
  starting transfers between devices  39.8 us (28%)
  waiting for transfers between devices  31.5 us (22%)
  local copies, waits for them, and re-layouts  6.09 us (4%)
    pallas_call x4, Pallas kernels, multiply(): pl.pallas_call(functools.partial(matrix_kernel, first, blocks, width), ou...  56.3 us
    ppermute x14, starting transfers between devices, body(): ahead = lax.ppermute(ahead, 'grid', onward)  16.8 us
    ppermute x14, starting transfers between devices, body(): behind = lax.ppermute(behind, 'grid', back)  16.4 us
    all_to_all x1, waiting for transfers between devices, body(): got = lax.all_to_all(send, 'grid', split_axis=0, concat_axis=0, tiled=True)  13.8 us
    ppermute x1, waiting for transfers between devices, body(): got = lax.ppermute(send, 'rep', high_pairs)  11.5 us
    pallas_call x5, Pallas kernels, local_call(): pl.pallas_call(kernel, out_shape=out_shape, in_specs=in_specs, out_specs=...  6.45 us
    all_to_all x1, starting transfers between devices, body(): got = lax.all_to_all(send, 'grid', split_axis=0, concat_axis=0, tiled=True)  4.97 us
  transfers between devices with their start and end apart: 31, of which 10 were waited for; matrix products, arithmetic and copies ran while one was open for 5% of the time, Pallas kernels for 21%

profile of v1, /device:TPU:0, one launch (start us, length us, event | category | flops | bytes accessed | tf_op | source)
XLA Modules:
  0.0 141.8 jit_solution(17284249388475083822)
XLA Ops:
  0.9 3.0 %collective-permute-start.1 = (bf16[32,1356]{1,0:T(8,128)(2,1)S(1)}, bf16[32,1356]{1,0:T(8,128)(2,1)S(1)}, u32[]{:S(2)}, u32[]{:S(2)}) collective-permute-start(bf16[32,1356]{1,0:T(8,128)(2,1)S(1)} %slice.12), channel_id=1, source_target_pairs={{8,0},{16,8},{24,16},{28,24},{20,28},{12,20},{4,12},{0,4},{9,1},{1... | collective-permute-start | bytes 260360 | tf_op jit(solution)/shard_map/ppermute | solution.py:271
  5.0 2.0 %collective-permute-start.21 = (bf16[32,2048]{1,0:T(8,128)(2,1)S(1)}, bf16[32,2048]{1,0:T(8,128)(2,1)S(1)}, u32[]{:S(2)}, u32[]{:S(2)}) collective-permute-start(bf16[32,2048]{1,0:T(8,128)(2,1)S(1)} %get-tuple-element.5.refs_1_), channel_id=1, source_target_pairs={{0,8},{8,16},{16,24},{24,28},{28,20},{20,12},{12,4},{4,0},{1,9},{9... | collective-permute-start | bytes 393224 | tf_op jit(solution)/shard_map/ppermute | solution.py:267
  7.1 1.9 %collective-permute-start.15 = (bf16[32,2048]{1,0:T(8,128)(2,1)S(1)}, bf16[32,2048]{1,0:T(8,128)(2,1)S(1)}, u32[]{:S(2)}, u32[]{:S(2)}) collective-permute-start(bf16[32,2048]{1,0:T(8,128)(2,1)S(1)} %get-tuple-element.7.refs_1_), channel_id=1, source_target_pairs={{8,0},{16,8},{24,16},{28,24},{20,28},{12,20},{4,12},{0,4},{9,1},{1... | collective-permute-start | bytes 393224 | tf_op jit(solution)/shard_map/ppermute | solution.py:271
  9.4 1.8 %collective-permute-start.7 = (bf16[32,2048]{1,0:T(8,128)(2,1)S(1)}, bf16[32,2048]{1,0:T(8,128)(2,1)S(1)}, u32[]{:S(2)}, u32[]{:S(2)}) collective-permute-start(bf16[32,2048]{1,0:T(8,128)(2,1)S(1)} %get-tuple-element.6.refs_1_), channel_id=1, source_target_pairs={{0,8},{8,16},{16,24},{24,28},{28,20},{20,12},{12,4},{4,0},{1,9},{9... | collective-permute-start | bytes 393224 | tf_op jit(solution)/shard_map/ppermute | solution.py:267
  11.9 1.7 %collective-permute-start.3 = (bf16[32,1356]{1,0:T(8,128)(2,1)S(1)}, bf16[32,1356]{1,0:T(8,128)(2,1)S(1)}, u32[]{:S(2)}, u32[]{:S(2)}) collective-permute-start(bf16[32,1356]{1,0:T(8,128)(2,1)S(1)} %collective-permute-done.1), channel_id=1, source_target_pairs={{8,0},{16,8},{24,16},{28,24},{20,28},{12,20},{4,12},{0,4},{9,1},{1... | collective-permute-start | bytes 260360 | tf_op jit(solution)/shard_map/ppermute | solution.py:271
  13.6 1.5 %collective-permute-start.2 = (bf16[32,1356]{1,0:T(8,128)(2,1)S(1)}, bf16[32,1356]{1,0:T(8,128)(2,1)S(1)}, u32[]{:S(2)}, u32[]{:S(2)}) collective-permute-start(bf16[32,1356]{1,0:T(8,128)(2,1)S(1)} %collective-permute-done), channel_id=1, source_target_pairs={{0,8},{8,16},{16,24},{24,28},{28,20},{20,12},{12,4},{4,0},{1,9},{9... | collective-permute-start | bytes 260360 | tf_op jit(solution)/shard_map/ppermute | solution.py:267
  15.6 1.9 %collective-permute-start.23 = (bf16[32,2048]{1,0:T(8,128)(2,1)S(1)}, bf16[32,2048]{1,0:T(8,128)(2,1)S(1)}, u32[]{:S(2)}, u32[]{:S(2)}) collective-permute-start(bf16[32,2048]{1,0:T(8,128)(2,1)S(1)} %collective-permute-done.21.refs_2_), channel_id=1, source_target_pairs={{0,8},{8,16},{16,24},{24,28},{28,20},{20,12},{12,4},{4,0},{1,9},{9... | collective-permute-start | bytes 393224 | tf_op jit(solution)/shard_map/ppermute | solution.py:267
  18.3 1.6 %collective-permute-start.24 = (bf16[32,2048]{1,0:T(8,128)(2,1)S(1)}, bf16[32,2048]{1,0:T(8,128)(2,1)S(1)}, u32[]{:S(2)}, u32[]{:S(2)}) collective-permute-start(bf16[32,2048]{1,0:T(8,128)(2,1)S(1)} %collective-permute-done.22.refs_3_), channel_id=1, source_target_pairs={{8,0},{16,8},{24,16},{28,24},{20,28},{12,20},{4,12},{0,4},{9,1},{1... | collective-permute-start | bytes 393224 | tf_op jit(solution)/shard_map/ppermute | solution.py:271
  19.9 1.6 %collective-permute-start.5 = (bf16[32,1356]{1,0:T(8,128)(2,1)S(1)}, bf16[32,1356]{1,0:T(8,128)(2,1)S(1)}, u32[]{:S(2)}, u32[]{:S(2)}) collective-permute-start(bf16[32,1356]{1,0:T(8,128)(2,1)S(1)} %collective-permute-done.3), channel_id=1, source_target_pairs={{8,0},{16,8},{24,16},{28,24},{20,28},{12,20},{4,12},{0,4},{9,1},{1... | collective-permute-start | bytes 260360 | tf_op jit(solution)/shard_map/ppermute | solution.py:271
  23.1 1.6 %collective-permute-start.17 = (bf16[32,2048]{1,0:T(8,128)(2,1)S(1)}, bf16[32,2048]{1,0:T(8,128)(2,1)S(1)}, u32[]{:S(2)}, u32[]{:S(2)}) collective-permute-start(bf16[32,2048]{1,0:T(8,128)(2,1)S(1)} %collective-permute-done.15.refs_3_), channel_id=1, source_target_pairs={{8,0},{16,8},{24,16},{28,24},{20,28},{12,20},{4,12},{0,4},{9,1},{1... | collective-permute-start | bytes 393224 | tf_op jit(solution)/shard_map/ppermute | solution.py:271
  29.0 1.4 collective-permute-start.25
  32.4 1.6 %collective-permute-start.26 = (bf16[32,2048]{1,0:T(8,128)(2,1)S(1)}, bf16[32,2048]{1,0:T(8,128)(2,1)S(1)}, u32[]{:S(2)}, u32[]{:S(2)}) collective-permute-start(bf16[32,2048]{1,0:T(8,128)(2,1)S(1)} %collective-permute-done.24.refs_5_), channel_id=1, source_target_pairs={{8,0},{16,8},{24,16},{28,24},{20,28},{12,20},{4,12},{0,4},{9,1},{1... | collective-permute-start | bytes 393224 | tf_op jit(solution)/shard_map/ppermute | solution.py:271
  39.7 1.8 %collective-permute-start.18 = (bf16[32,2048]{1,0:T(8,128)(2,1)S(1)}, bf16[32,2048]{1,0:T(8,128)(2,1)S(1)}, u32[]{:S(2)}, u32[]{:S(2)}) collective-permute-start(bf16[32,2048]{1,0:T(8,128)(2,1)S(1)} %collective-permute-done.16.refs_4_), channel_id=1, source_target_pairs={{0,8},{8,16},{16,24},{24,28},{28,20},{20,12},{12,4},{4,0},{1,9},{9... | collective-permute-start | bytes 393224 | tf_op jit(solution)/shard_map/ppermute | solution.py:267
  44.2 14.5 %matrix.4.refs_10_ = f32[2,3840,128]{2,1,0:T(8,128)S(1)} custom-call(s32[8]{0:T(128)S(1)} %gather_fusion.1, bf16[32,2048]{1,0:T(8,128)(2,1)S(1)} %get-tuple-element.5.refs_1_, bf16[32,2048]{1,0:T(8,128)(2,1)S(1)} %collective-permute-done.21.refs_2_, bf16[32,2048]{1,0:T(8,128)(2,1)S(1)} %collective-permute-done.22.refs_3_, ...), custom_call_target="tpu_custom_call" | custom-call | flops 3774873600 | bytes 22118400 | tf_op jit(solution)/shard_map/matrix/pallas_call | solution.py:99
  58.7 14.5 %matrix.5.refs_10_ = f32[2,3840,128]{2,1,0:T(8,128)S(1)} custom-call(s32[8]{0:T(128)S(1)} %gather_fusion, bf16[32,2048]{1,0:T(8,128)(2,1)S(1)} %get-tuple-element.7.refs_1_, bf16[32,2048]{1,0:T(8,128)(2,1)S(1)} %collective-permute-done.14.refs_2_, bf16[32,2048]{1,0:T(8,128)(2,1)S(1)} %collective-permute-done.15.refs_3_, ...), custom_call_target="tpu_custom_call", output_to_operand_aliasing={{}: (10, {})} | custom-call | flops 3774873600 | bytes 22118400 | tf_op jit(solution)/shard_map/matrix/pallas_call | solution.py:99
  73.2 14.5 %matrix.6.refs_10_ = f32[2,3840,128]{2,1,0:T(8,128)S(1)} custom-call(s32[8]{0:T(128)S(1)} %gather_fusion.1, bf16[32,2048]{1,0:T(8,128)(2,1)S(1)} %get-tuple-element.6.refs_1_, bf16[32,2048]{1,0:T(8,128)(2,1)S(1)} %collective-permute-done.7.refs_2_, bf16[32,2048]{1,0:T(8,128)(2,1)S(1)} %collective-permute-done.8.refs_3_, ...), custom_call_target="tpu_custom_call", output_to_operand_aliasing={{}: (10, {})} | custom-call | flops 3774873600 | bytes 22118400 | tf_op jit(solution)/shard_map/matrix/pallas_call | solution.py:99
  87.7 12.9 %matrix.7.total_ref = f32[2,3840,128]{2,1,0:T(8,128)S(1)} custom-call(s32[8]{0:T(128)S(1)} %gather_fusion, bf16[32,1408]{1,0:T(8,128)(2,1)S(1)} %pad.25.refs_1_, bf16[32,1408]{1,0:T(8,128)(2,1)S(1)} %pad.26.refs_2_, bf16[32,1408]{1,0:T(8,128)(2,1)S(1)} %pad.27.refs_3_, bf16[32,1408]{1,0:T(8,128)(2,1)S(1)} %pad.28.refs_4_, ...), custom_call_target="tpu_custom_call", output_to_operand_aliasing={{}: (10, {})} | custom-call | flops 2499379200 | bytes 17136000 | tf_op jit(solution)/shard_map/matrix/pallas_call | solution.py:99
  101.8 2.6 %collective-permute-done.28.got_ref = s16[2,15,64,256]{3,2,1,0:T(8,128)(2,1)S(1)} collective-permute-done((s16[2,15,64,256]{3,2,1,0:T(8,128)(2,1)S(1)}, s16[2,15,64,256]{3,2,1,0:T(8,128)(2,1)S(1)}, u32[]{:S(2)}, u32[]{:S(2)}) %collective-permute-start.28) | collective-permute-done | bytes 983072 | tf_op jit(solution)/shard_map/ppermute | solution.py:289
  105.3 1.6 %collective-permute-start.29 = (s16[15,64,256]{2,1,0:T(8,128)(2,1)S(1)}, s16[15,64,256]{2,1,0:T(8,128)(2,1)S(1)}, u32[]{:S(2)}, u32[]{:S(2)}) collective-permute-start(s16[15,64,256]{2,1,0:T(8,128)(2,1)S(1)} %second_send.1), channel_id=1, source_target_pairs={{0,2},{1,3},{2,0},{3,1},{4,6},{5,7},{6,4},{7,5},{8,10},{9,11},{10,... | collective-permute-start | bytes 1474568 | tf_op jit(solution)/shard_map/ppermute | solution.py:304
  107.2 11.5 %collective-permute-done.29.got_ref = s16[15,64,256]{2,1,0:T(8,128)(2,1)S(1)} collective-permute-done((s16[15,64,256]{2,1,0:T(8,128)(2,1)S(1)}, s16[15,64,256]{2,1,0:T(8,128)(2,1)S(1)}, u32[]{:S(2)}, u32[]{:S(2)}) %collective-permute-start.29) | collective-permute-done | bytes 491552 | tf_op jit(solution)/shard_map/ppermute | solution.py:304
  118.6 2.1 %third_send.1 = s16[8,4,64,128]{3,2,1,0:T(8,128)(2,1)} custom-call(f32[15,64,256]{2,1,0:T(8,128)S(1)} %keep.1.kept_ref, s16[15,64,256]{2,1,0:T(8,128)(2,1)S(1)} %collective-permute-done.29.got_ref), custom_call_target="tpu_custom_call" | custom-call | flops 10000000 | bytes 4000000 | tf_op jit(solution)/shard_map/third_send/pallas_call | solution.py:217
  120.7 5.0 %all-to-all-start = ((s16[8,4,64,128]{3,2,1,0:T(8,128)(2,1)}), s16[8,4,64,128]{3,2,1,0:T(8,128)(2,1)S(1)}, u32[]{:S(2)}, u32[]{:S(2)}) async-start(s16[8,4,64,128]{3,2,1,0:T(8,128)(2,1)} %third_send.1), calls=%async_computation | async-start | bytes 1048576 | tf_op jit(solution)/shard_map/all_to_all | solution.py:313
  125.9 13.8 %all-to-all-done.got_ref = s16[8,4,64,128]{3,2,1,0:T(8,128)(2,1)S(1)} async-done(((s16[8,4,64,128]{3,2,1,0:T(8,128)(2,1)}), s16[8,4,64,128]{3,2,1,0:T(8,128)(2,1)S(1)}, u32[]{:S(2)}, u32[]{:S(2)}) %all-to-all-start) | async-done | bytes 524320 | tf_op jit(solution)/shard_map/all_to_all | solution.py:313
  139.7 2.1 %update.1 = f32[15,32,480]{2,1,0:T(8,128)} custom-call(f32[15]{0:T(128)S(1)} %copy-done.3, s32[15]{0:T(128)S(1)} %copy-done.4, s16[8,4,64,128]{3,2,1,0:T(8,128)(2,1)S(1)} %all-to-all-done.got_ref, f32[15,32,480]{2,1,0:T(8,128)S(1)} %bitcast.9, f32[32,1]{1,0:T(8,128)S(1)} %copy.24.row_energy_ref, f32[1,480]{1,0:T(1,128)S(1)} %bitcast.10, ...), custom_call_target="tpu_custom_call" | custom-call | flops 10000000 | bytes 4000000 | tf_op jit(solution)/shard_map/update/pallas_call | solution.py:217
  (79 shorter events, 23.5 us)
Async XLA Ops:
  0.9 8.1 %collective-permute-start.1 = (bf16[32,1356]{1,0:T(8,128)(2,1)S(1)}, bf16[32,1356]{1,0:T(8,128)(2,1)S(1)}, u32[]{:S(2)}, u32[]{:S(2)}) collective-permute-start(bf16[32,1356]{1,0:T(8,128)(2,1)S(1)} %slice.12), channel_id=1, source_target_pairs={{8,0},{16,8},{24,16},{28,24},{20,28},{12,20},{4,12},{0,4},{9,1},{1... | collective-permute-start | bytes 260360 | tf_op jit(solution)/shard_map/ppermute | solution.py:271
  5.0 6.9 %collective-permute-start.21 = (bf16[32,2048]{1,0:T(8,128)(2,1)S(1)}, bf16[32,2048]{1,0:T(8,128)(2,1)S(1)}, u32[]{:S(2)}, u32[]{:S(2)}) collective-permute-start(bf16[32,2048]{1,0:T(8,128)(2,1)S(1)} %get-tuple-element.5.refs_1_), channel_id=1, source_target_pairs={{0,8},{8,16},{16,24},{24,28},{28,20},{20,12},{12,4},{4,0},{1,9},{9... | collective-permute-start | bytes 393224 | tf_op jit(solution)/shard_map/ppermute | solution.py:267
  7.1 8.3 %collective-permute-start.15 = (bf16[32,2048]{1,0:T(8,128)(2,1)S(1)}, bf16[32,2048]{1,0:T(8,128)(2,1)S(1)}, u32[]{:S(2)}, u32[]{:S(2)}) collective-permute-start(bf16[32,2048]{1,0:T(8,128)(2,1)S(1)} %get-tuple-element.7.refs_1_), channel_id=1, source_target_pairs={{8,0},{16,8},{24,16},{28,24},{20,28},{12,20},{4,12},{0,4},{9,1},{1... | collective-permute-start | bytes 393224 | tf_op jit(solution)/shard_map/ppermute | solution.py:271
  9.4 8.9 %collective-permute-start.7 = (bf16[32,2048]{1,0:T(8,128)(2,1)S(1)}, bf16[32,2048]{1,0:T(8,128)(2,1)S(1)}, u32[]{:S(2)}, u32[]{:S(2)}) collective-permute-start(bf16[32,2048]{1,0:T(8,128)(2,1)S(1)} %get-tuple-element.6.refs_1_), channel_id=1, source_target_pairs={{0,8},{8,16},{16,24},{24,28},{28,20},{20,12},{12,4},{4,0},{1,9},{9... | collective-permute-start | bytes 393224 | tf_op jit(solution)/shard_map/ppermute | solution.py:267
  11.9 8.0 %collective-permute-start.3 = (bf16[32,1356]{1,0:T(8,128)(2,1)S(1)}, bf16[32,1356]{1,0:T(8,128)(2,1)S(1)}, u32[]{:S(2)}, u32[]{:S(2)}) collective-permute-start(bf16[32,1356]{1,0:T(8,128)(2,1)S(1)} %collective-permute-done.1), channel_id=1, source_target_pairs={{8,0},{16,8},{24,16},{28,24},{20,28},{12,20},{4,12},{0,4},{9,1},{1... | collective-permute-start | bytes 260360 | tf_op jit(solution)/shard_map/ppermute | solution.py:271
  13.6 7.9 %collective-permute-start.2 = (bf16[32,1356]{1,0:T(8,128)(2,1)S(1)}, bf16[32,1356]{1,0:T(8,128)(2,1)S(1)}, u32[]{:S(2)}, u32[]{:S(2)}) collective-permute-start(bf16[32,1356]{1,0:T(8,128)(2,1)S(1)} %collective-permute-done), channel_id=1, source_target_pairs={{0,8},{8,16},{16,24},{24,28},{28,20},{20,12},{12,4},{4,0},{1,9},{9... | collective-permute-start | bytes 260360 | tf_op jit(solution)/shard_map/ppermute | solution.py:267
  15.5 7.7 %collective-permute-start.8 = (bf16[32,2048]{1,0:T(8,128)(2,1)S(1)}, bf16[32,2048]{1,0:T(8,128)(2,1)S(1)}, u32[]{:S(2)}, u32[]{:S(2)}) collective-permute-start(bf16[32,2048]{1,0:T(8,128)(2,1)S(1)} %get-tuple-element.6.refs_1_), channel_id=1, source_target_pairs={{8,0},{16,8},{24,16},{28,24},{20,28},{12,20},{4,12},{0,4},{9,1},{1... | collective-permute-start | bytes 393224 | tf_op jit(solution)/shard_map/ppermute | solution.py:271
  15.6 12.7 %collective-permute-start.23 = (bf16[32,2048]{1,0:T(8,128)(2,1)S(1)}, bf16[32,2048]{1,0:T(8,128)(2,1)S(1)}, u32[]{:S(2)}, u32[]{:S(2)}) collective-permute-start(bf16[32,2048]{1,0:T(8,128)(2,1)S(1)} %collective-permute-done.21.refs_2_), channel_id=1, source_target_pairs={{0,8},{8,16},{16,24},{24,28},{28,20},{20,12},{12,4},{4,0},{1,9},{9... | collective-permute-start | bytes 393224 | tf_op jit(solution)/shard_map/ppermute | solution.py:267
  18.3 10.7 %collective-permute-start.24 = (bf16[32,2048]{1,0:T(8,128)(2,1)S(1)}, bf16[32,2048]{1,0:T(8,128)(2,1)S(1)}, u32[]{:S(2)}, u32[]{:S(2)}) collective-permute-start(bf16[32,2048]{1,0:T(8,128)(2,1)S(1)} %collective-permute-done.22.refs_3_), channel_id=1, source_target_pairs={{8,0},{16,8},{24,16},{28,24},{20,28},{12,20},{4,12},{0,4},{9,1},{1... | collective-permute-start | bytes 393224 | tf_op jit(solution)/shard_map/ppermute | solution.py:271
  23.1 8.5 %collective-permute-start.17 = (bf16[32,2048]{1,0:T(8,128)(2,1)S(1)}, bf16[32,2048]{1,0:T(8,128)(2,1)S(1)}, u32[]{:S(2)}, u32[]{:S(2)}) collective-permute-start(bf16[32,2048]{1,0:T(8,128)(2,1)S(1)} %collective-permute-done.15.refs_3_), channel_id=1, source_target_pairs={{8,0},{16,8},{24,16},{28,24},{20,28},{12,20},{4,12},{0,4},{9,1},{1... | collective-permute-start | bytes 393224 | tf_op jit(solution)/shard_map/ppermute | solution.py:271
  25.6 6.8 %collective-permute-start.16 = (bf16[32,2048]{1,0:T(8,128)(2,1)S(1)}, bf16[32,2048]{1,0:T(8,128)(2,1)S(1)}, u32[]{:S(2)}, u32[]{:S(2)}) collective-permute-start(bf16[32,2048]{1,0:T(8,128)(2,1)S(1)} %collective-permute-done.14.refs_2_), channel_id=1, source_target_pairs={{0,8},{8,16},{16,24},{24,28},{28,20},{20,12},{12,4},{4,0},{1,9},{9... | collective-permute-start | bytes 393224 | tf_op jit(solution)/shard_map/ppermute | solution.py:267
  26.9 7.0 %collective-permute-start.9 = (bf16[32,2048]{1,0:T(8,128)(2,1)S(1)}, bf16[32,2048]{1,0:T(8,128)(2,1)S(1)}, u32[]{:S(2)}, u32[]{:S(2)}) collective-permute-start(bf16[32,2048]{1,0:T(8,128)(2,1)S(1)} %collective-permute-done.7.refs_2_), channel_id=1, source_target_pairs={{0,8},{8,16},{16,24},{24,28},{28,20},{20,12},{12,4},{4,0},{1,9},{9... | collective-permute-start | bytes 393224 | tf_op jit(solution)/shard_map/ppermute | solution.py:267
  29.0 7.0 %collective-permute-start.25 = (bf16[32,2048]{1,0:T(8,128)(2,1)S(1)}, bf16[32,2048]{1,0:T(8,128)(2,1)S(1)}, u32[]{:S(2)}, u32[]{:S(2)}) collective-permute-start(bf16[32,2048]{1,0:T(8,128)(2,1)S(1)} %collective-permute-done.23.refs_4_), channel_id=1, source_target_pairs={{0,8},{8,16},{16,24},{24,28},{28,20},{20,12},{12,4},{4,0},{1,9},{9... | collective-permute-start | bytes 393224 | tf_op jit(solution)/shard_map/ppermute | solution.py:267
  31.7 8.0 %collective-permute-start.10 = (bf16[32,2048]{1,0:T(8,128)(2,1)S(1)}, bf16[32,2048]{1,0:T(8,128)(2,1)S(1)}, u32[]{:S(2)}, u32[]{:S(2)}) collective-permute-start(bf16[32,2048]{1,0:T(8,128)(2,1)S(1)} %collective-permute-done.8.refs_3_), channel_id=1, source_target_pairs={{8,0},{16,8},{24,16},{28,24},{20,28},{12,20},{4,12},{0,4},{9,1},{1... | collective-permute-start | bytes 393224 | tf_op jit(solution)/shard_map/ppermute | solution.py:271
  32.4 9.1 %collective-permute-start.26 = (bf16[32,2048]{1,0:T(8,128)(2,1)S(1)}, bf16[32,2048]{1,0:T(8,128)(2,1)S(1)}, u32[]{:S(2)}, u32[]{:S(2)}) collective-permute-start(bf16[32,2048]{1,0:T(8,128)(2,1)S(1)} %collective-permute-done.24.refs_5_), channel_id=1, source_target_pairs={{8,0},{16,8},{24,16},{28,24},{20,28},{12,20},{4,12},{0,4},{9,1},{1... | collective-permute-start | bytes 393224 | tf_op jit(solution)/shard_map/ppermute | solution.py:271
  34.0 8.2 %collective-permute-start.19 = (bf16[32,2048]{1,0:T(8,128)(2,1)S(1)}, bf16[32,2048]{1,0:T(8,128)(2,1)S(1)}, u32[]{:S(2)}, u32[]{:S(2)}) collective-permute-start(bf16[32,2048]{1,0:T(8,128)(2,1)S(1)} %collective-permute-done.17.refs_5_), channel_id=1, source_target_pairs={{8,0},{16,8},{24,16},{28,24},{20,28},{12,20},{4,12},{0,4},{9,1},{1... | collective-permute-start | bytes 393224 | tf_op jit(solution)/shard_map/ppermute | solution.py:271
  35.0 7.9 %collective-permute-start.11 = (bf16[32,2048]{1,0:T(8,128)(2,1)S(1)}, bf16[32,2048]{1,0:T(8,128)(2,1)S(1)}, u32[]{:S(2)}, u32[]{:S(2)}) collective-permute-start(bf16[32,2048]{1,0:T(8,128)(2,1)S(1)} %collective-permute-done.9.refs_4_), channel_id=1, source_target_pairs={{0,8},{8,16},{16,24},{24,28},{28,20},{20,12},{12,4},{4,0},{1,9},{9... | collective-permute-start | bytes 393224 | tf_op jit(solution)/shard_map/ppermute | solution.py:267
  36.0 8.2 %collective-permute-start.27 = (bf16[32,2048]{1,0:T(8,128)(2,1)S(1)}, bf16[32,2048]{1,0:T(8,128)(2,1)S(1)}, u32[]{:S(2)}, u32[]{:S(2)}) collective-permute-start(bf16[32,2048]{1,0:T(8,128)(2,1)S(1)} %collective-permute-done.25.refs_6_), channel_id=1, source_target_pairs={{0,8},{8,16},{16,24},{24,28},{28,20},{20,12},{12,4},{4,0},{1,9},{9... | collective-permute-start | bytes 393224 | tf_op jit(solution)/shard_map/ppermute | solution.py:267
  39.7 19.0 %collective-permute-start.18 = (bf16[32,2048]{1,0:T(8,128)(2,1)S(1)}, bf16[32,2048]{1,0:T(8,128)(2,1)S(1)}, u32[]{:S(2)}, u32[]{:S(2)}) collective-permute-start(bf16[32,2048]{1,0:T(8,128)(2,1)S(1)} %collective-permute-done.16.refs_4_), channel_id=1, source_target_pairs={{0,8},{8,16},{16,24},{24,28},{28,20},{20,12},{12,4},{4,0},{1,9},{9... | collective-permute-start | bytes 393224 | tf_op jit(solution)/shard_map/ppermute | solution.py:267
  41.5 31.7 %collective-permute-start.12 = (bf16[32,2048]{1,0:T(8,128)(2,1)S(1)}, bf16[32,2048]{1,0:T(8,128)(2,1)S(1)}, u32[]{:S(2)}, u32[]{:S(2)}) collective-permute-start(bf16[32,2048]{1,0:T(8,128)(2,1)S(1)} %collective-permute-done.10.refs_5_), channel_id=1, source_target_pairs={{8,0},{16,8},{24,16},{28,24},{20,28},{12,20},{4,12},{0,4},{9,1},{1... | collective-permute-start | bytes 393224 | tf_op jit(solution)/shard_map/ppermute | solution.py:271
  42.2 16.5 %collective-permute-start.20 = (bf16[32,2048]{1,0:T(8,128)(2,1)S(1)}, bf16[32,2048]{1,0:T(8,128)(2,1)S(1)}, u32[]{:S(2)}, u32[]{:S(2)}) collective-permute-start(bf16[32,2048]{1,0:T(8,128)(2,1)S(1)} %collective-permute-done.19.refs_7_), channel_id=1, source_target_pairs={{8,0},{16,8},{24,16},{28,24},{20,28},{12,20},{4,12},{0,4},{9,1},{1... | collective-permute-start | bytes 393224 | tf_op jit(solution)/shard_map/ppermute | solution.py:271
  42.9 30.3 %collective-permute-start.13 = (bf16[32,2048]{1,0:T(8,128)(2,1)S(1)}, bf16[32,2048]{1,0:T(8,128)(2,1)S(1)}, u32[]{:S(2)}, u32[]{:S(2)}) collective-permute-start(bf16[32,2048]{1,0:T(8,128)(2,1)S(1)} %collective-permute-done.11.refs_6_), channel_id=1, source_target_pairs={{0,8},{8,16},{16,24},{24,28},{28,20},{20,12},{12,4},{4,0},{1,9},{9... | collective-permute-start | bytes 393224 | tf_op jit(solution)/shard_map/ppermute | solution.py:267
  105.3 13.3 %collective-permute-start.29 = (s16[15,64,256]{2,1,0:T(8,128)(2,1)S(1)}, s16[15,64,256]{2,1,0:T(8,128)(2,1)S(1)}, u32[]{:S(2)}, u32[]{:S(2)}) collective-permute-start(s16[15,64,256]{2,1,0:T(8,128)(2,1)S(1)} %second_send.1), channel_id=1, source_target_pairs={{0,2},{1,3},{2,0},{3,1},{4,6},{5,7},{6,4},{7,5},{8,10},{9,11},{10,... | collective-permute-start | bytes 1474568 | tf_op jit(solution)/shard_map/ppermute | solution.py:304
  120.7 19.0 %all-to-all-start = ((s16[8,4,64,128]{3,2,1,0:T(8,128)(2,1)}), s16[8,4,64,128]{3,2,1,0:T(8,128)(2,1)S(1)}, u32[]{:S(2)}, u32[]{:S(2)}) async-start(s16[8,4,64,128]{3,2,1,0:T(8,128)(2,1)} %third_send.1), calls=%async_computation | async-start | bytes 1048576 | tf_op jit(solution)/shard_map/all_to_all | solution.py:313
  (14 other events, 252.3 us)

commit v2 on v1

v2 whole, which is shorter than its diff:
```python
import functools

import jax
import jax.numpy as jnp
from jax import lax
from jax.experimental import pallas as pl
from jax.experimental.pallas import tpu as pltpu
from jax.sharding import PartitionSpec as P

NOCC = 60
LANES = 128
K_BLOCK = 2048
C_BLOCK = 720
TAIL_PARTS = 2
STEPS = 8.0
TOP = 32767.0
VMEM_LIMIT = 48 * 1024 * 1024


def ceil_to(value, unit):
    return -(-value // unit) * unit


def encode(rows, count):
    index = lax.broadcasted_iota(jnp.int32, rows.shape, 0)
    rows = jnp.where(index < count, rows, 0.0)
    largest = jnp.max(jnp.abs(rows), axis=0, keepdims=True)
    level = jnp.ceil(jnp.log2(jnp.maximum(largest, 1e-30)) * STEPS) + 1.0
    coded = jnp.floor(rows * (jnp.exp2(level * (-1.0 / STEPS)) * TOP) + 0.5)
    return jnp.where(index == count, level, coded)


def decode(block, count):
    index = lax.broadcasted_iota(jnp.int32, block.shape, 0)
    scale = jnp.exp2(block[count : count + 1] * (1.0 / STEPS)) * (1.0 / TOP)
    return jnp.where(index < count, block * scale, 0.0)


def to_code(block):
    return block.astype(jnp.int32).astype(jnp.int16)


def from_code(block):
    return block.astype(jnp.int32).astype(jnp.float32)


def walk_index(place, size):
    return jnp.where(place < size // 2, 2 * place, 2 * (size - 1 - place) + 1)


def walk_place(index, size):
    return jnp.where(index % 2 == 0, index // 2, size - 1 - index // 2)


def matrix_kernel(first, offsets, valid, *refs):
    blocks = len(offsets)
    me_ref = refs[0]
    pieces = refs[1 : 1 + blocks]
    coupling_ref = refs[1 + blocks]
    total_in = None if first else refs[2 + blocks]
    total_out, gathered, turned = refs[-3:]
    rows = pieces[0].shape[0]
    depth = gathered.shape[1]

    @pl.when(pl.program_id(0) == 0)
    def _():
        place = walk_place(me_ref[0], blocks)
        for piece in range(blocks):
            source = walk_index(lax.rem(place + offsets[piece] + blocks, blocks), blocks)
            at = pl.multiple_of(source * rows, rows)
            gathered[pl.ds(at, rows), :valid] = pieces[piece][...]
        for at in range(0, depth, LANES):
            turned[at : at + LANES, :] = gathered[:, at : at + LANES].T
        if valid < depth:
            at = valid // LANES * LANES
            tile = turned[at : at + LANES, :]
            index = lax.broadcasted_iota(jnp.int32, tile.shape, 0)
            turned[at : at + LANES, :] = jnp.where(index < valid - at, tile, jnp.zeros_like(tile))

    whole = valid // LANES * LANES
    total = jnp.dot(
        coupling_ref[:, :whole], turned[:whole, :], preferred_element_type=jnp.float32
    )
    if whole < valid:
        tile = coupling_ref[:, whole : whole + LANES]
        index = lax.broadcasted_iota(jnp.int32, tile.shape, 1)
        tile = jnp.where(index < valid - whole, tile, jnp.zeros_like(tile))
        total += jnp.dot(tile, turned[whole:depth, :], preferred_element_type=jnp.float32)
    for part in range(total_out.shape[0]):
        own = total[:, part * LANES : (part + 1) * LANES]
        total_out[part] = own if first else total_in[part] + own


def multiply(me, offsets, pieces, coupling, at, total, padded_columns):
    blocks = len(pieces)
    rows, width = pieces[0].shape
    slab = rows * blocks
    columns = coupling.shape[0]
    depth = ceil_to(width, LANES)
    first = total is None
    column_block = min(C_BLOCK, ceil_to(columns, 16))
    block_spec = pl.BlockSpec((slab // LANES, column_block, LANES), lambda i, p: (0, i, 0))
    in_specs = [pl.BlockSpec((rows, width), lambda i, p: (0, 0))] * blocks
    in_specs += [pl.BlockSpec((column_block, K_BLOCK), lambda i, p: (i, at // K_BLOCK))]
    args = [*pieces, coupling]
    if not first:
        in_specs += [block_spec]
        args += [total]
    return pl.pallas_call(
        functools.partial(matrix_kernel, first, tuple(offsets), width),
        out_shape=jax.ShapeDtypeStruct((slab // LANES, padded_columns, LANES), jnp.float32),
        grid_spec=pltpu.PrefetchScalarGridSpec(
            num_scalar_prefetch=1,
            grid=(pl.cdiv(columns, column_block),),
            in_specs=in_specs,
            out_specs=block_spec,
            scratch_shapes=[
                pltpu.VMEM((slab, depth), jnp.bfloat16),
                pltpu.VMEM((depth, slab), jnp.bfloat16),
            ],
        ),
        input_output_aliases={} if first else {len(args): 0},
        compiler_params=pltpu.CompilerParams(
            vmem_limit_bytes=VMEM_LIMIT, dimension_semantics=("arbitrary",)
        ),
        cost_estimate=pl.CostEstimate(
            flops=2 * columns * width * slab,
            bytes_accessed=2 * columns * width + 8 * columns * slab,
            transcendentals=0,
        ),
        name="matrix",
    )(me, *args)


def column_rows(total_ref, part, j, bp, width):
    rows = pl.ds(part * width + j, bp, stride=NOCC)
    return jnp.concatenate([total_ref[h, rows, :] for h in range(total_ref.shape[0])], axis=1)


def first_send_kernel(count, width, start, rep_ref, total_ref, out_ref):
    low = rep_ref[0] % 2

    def step(j, carry):
        for high in range(2):
            part = 2 * high + 1 - low
            rows = column_rows(total_ref, part, start + j, out_ref.shape[2], width)
            out_ref[high, j] = to_code(encode(rows, count))
        return carry

    lax.fori_loop(0, out_ref.shape[1], step, 0)


def second_send_kernel(count, width, start, rep_ref, total_ref, got_ref, out_ref):
    low, high = rep_ref[0] % 2, 1 - rep_ref[0] // 2

    def step(j, carry):
        rows = column_rows(total_ref, 2 * high + low, start + j, out_ref.shape[1], width)
        rows = rows + decode(from_code(got_ref[high, j]), count)
        out_ref[j] = to_code(encode(rows, count))
        return carry

    lax.fori_loop(0, out_ref.shape[0], step, 0)


def keep_kernel(count, width, start, rep_ref, total_ref, got_ref, out_ref):
    low, high = rep_ref[0] % 2, rep_ref[0] // 2

    def step(j, carry):
        rows = column_rows(total_ref, 2 * high + low, start + j, out_ref.shape[1], width)
        out_ref[j] = rows + decode(from_code(got_ref[high, j]), count)
        return carry

    lax.fori_loop(0, out_ref.shape[0], step, 0)


def third_send_kernel(count, rows_dev, kept_ref, got_ref, out_ref):
    pack = LANES // rows_dev
    groups = out_ref.shape[1]
    size, _, slab = kept_ref.shape

    def step(jj, carry):
        coded = []
        for jq in range(pack):
            j = jnp.minimum(jq * groups + jj, size - 1)
            coded.append(encode(kept_ref[j] + decode(from_code(got_ref[j]), count), count))
        for g in range(slab // rows_dev):
            own = [block[:, g * rows_dev : (g + 1) * rows_dev] for block in coded]
            out_ref[g, jj] = to_code(jnp.concatenate(own, axis=1))
        return carry

    lax.fori_loop(0, groups, step, 0)


def update_kernel(count, width, rows_dev, parts, occ_energy_ref, occ_irrep_ref, *refs):
    arrived = refs[:parts]
    (
        integrals_ref,
        row_energy_ref,
        vir_energy_ref,
        row_irrep_ref,
        vir_irrep_ref,
        out_ref,
        stage,
    ) = refs[parts:]
    pack = LANES // rows_dev
    start = 0
    for got_ref in arrived:
        groups = got_ref.shape[1]
        size = min(groups * pack, width - start)
        for jj in range(groups):
            for g in range(got_ref.shape[0]):
                block = from_code(got_ref[g, jj])
                stage[g * count : (g + 1) * count, :] = decode(block, count)[:count]
            turned = stage[...].T
            for jq in range(pack):
                if jq * groups + jj >= size:
                    continue
                j = start + jq * groups + jj
                cycle = turned[jq * rows_dev : (jq + 1) * rows_dev]
                denominator = row_energy_ref[...] + occ_energy_ref[j] - vir_energy_ref[...]
                labels = row_irrep_ref[...] ^ occ_irrep_ref[j] ^ vir_irrep_ref[...]
                out_ref[j] = jnp.where(
                    labels == 0, (integrals_ref[j] + cycle) / denominator, jnp.float32(0.0)
                )
        start += size


def local_call(kernel, out_shape, args, scalars=0, scratch=(), name=None):
    in_specs = [pl.BlockSpec(memory_space=pltpu.SMEM)] * scalars
    in_specs += [pl.BlockSpec(memory_space=pltpu.VMEM)] * (len(args) - scalars)
    return pl.pallas_call(
        kernel,
        out_shape=out_shape,
        in_specs=in_specs,
        out_specs=pl.BlockSpec(memory_space=pltpu.VMEM),
        scratch_shapes=list(scratch),
        compiler_params=pltpu.CompilerParams(vmem_limit_bytes=VMEM_LIMIT),
        cost_estimate=pl.CostEstimate(flops=10**7, bytes_accessed=4 * 10**6, transcendentals=0),
        name=name,
    )(*args)


def body(
    amplitudes,
    coupling,
    integrals,
    row_energy,
    occ_energy,
    vir_energy,
    row_irrep,
    occ_irrep,
    vir_irrep,
):
    grid_size = lax.axis_size("grid")
    me = lax.axis_index("grid").astype(jnp.int32).reshape(1)
    rep = lax.axis_index("rep").astype(jnp.int32).reshape(1)
    rows_dev, depth = amplitudes.shape
    coupling = coupling.T
    count = coupling.shape[0] // NOCC
    bp = ceil_to(count + 1, 16)
    slab = rows_dev * grid_size
    width = NOCC // lax.axis_size("rep")

    walk = [*range(0, grid_size, 2), *range(1, grid_size, 2)[::-1]]
    onward = [(walk[i], walk[(i + 1) % grid_size]) for i in range(grid_size)]
    back = [(b, a) for a, b in onward]

    longer = grid_size // 2
    ends = []
    jobs = []
    for number, at in enumerate(range(0, depth, K_BLOCK)):
        own = amplitudes[:, at : at + K_BLOCK]
        if number > 1:
            own, *_ = lax.optimization_barrier((own, *ends[number - 2]))
        pieces, offsets = [own], [0]
        hops = (longer, grid_size - 1 - longer)
        if number % 2:
            hops = hops[::-1]
        ahead = behind = own
        for hop in range(1, longer + 1):
            if hop <= hops[0]:
                ahead = lax.ppermute(ahead, "grid", onward)
                pieces.append(ahead)
                offsets.append(-hop)
            if hop <= hops[1]:
                behind = lax.ppermute(behind, "grid", back)
                pieces.append(behind)
                offsets.append(hop)
        ends.append((ahead, behind))
        jobs.append((at, offsets, pieces))
    total = None
    for number, (at, offsets, pieces) in enumerate(jobs):
        if number + 1 < len(jobs):
            late = jobs[number + 1][2][-3:-1] if number % 2 == 0 else jobs[number + 1][2][1:3]
            pieces = lax.optimization_barrier((*pieces, *late))[: len(pieces)]
        total = multiply(me, offsets, pieces, coupling, at, total, bp * NOCC)

    low_pairs = [(i, i ^ 1) for i in range(lax.axis_size("rep"))]
    high_pairs = [(i, i ^ 2) for i in range(lax.axis_size("rep"))]
    pack = LANES // rows_dev
    cut = ceil_to(-(-width // TAIL_PARTS), pack)
    arrived = []
    for start in range(0, width, cut):
        size = min(cut, width - start)
        span = (count, width, start)
        shape = (size, bp, slab)
        send = local_call(
            functools.partial(first_send_kernel, *span),
            jax.ShapeDtypeStruct((2, *shape), jnp.int16),
            (rep, total),
            1,
            name="first_send",
        )
        got = lax.ppermute(send, "rep", low_pairs)
        send = local_call(
            functools.partial(second_send_kernel, *span),
            jax.ShapeDtypeStruct(shape, jnp.int16),
            (rep, total, got),
            1,
            name="second_send",
        )
        kept = local_call(
            functools.partial(keep_kernel, *span),
            jax.ShapeDtypeStruct(shape, jnp.float32),
            (rep, total, got),
            1,
            name="keep",
        )
        got = lax.ppermute(send, "rep", high_pairs)
        send = local_call(
            functools.partial(third_send_kernel, count, rows_dev),
            jax.ShapeDtypeStruct((grid_size, -(-size // pack), bp, LANES), jnp.int16),
            (kept, got),
            name="third_send",
        )
        arrived.append(lax.all_to_all(send, "grid", split_axis=0, concat_axis=0, tiled=True))

    updated = local_call(
        functools.partial(update_kernel, count, width, rows_dev, len(arrived)),
        jax.ShapeDtypeStruct((width, rows_dev, count * grid_size), jnp.float32),
        (
            occ_energy,
            occ_irrep,
            *arrived,
            jnp.transpose(integrals, (1, 0, 2)),
            row_energy[:, None],
            vir_energy[None, :],
            row_irrep[:, None],
            vir_irrep[None, :],
        ),
        2,
        scratch=[pltpu.VMEM((count * grid_size, LANES), jnp.float32)],
        name="update",
    )
    return jnp.transpose(updated, (1, 0, 2))


def solution(mesh):
    return jax.shard_map(
        body,
        mesh=mesh,
        in_specs=(
            P("grid", "rep"),
            P("rep", "grid"),
            P("grid", "rep", None),
            P("grid"),
            P("rep"),
            P(),
            P("grid"),
            P("rep"),
            P(),
        ),
        out_specs=P("grid", "rep", None),
        check_vma=False,
    )
```

time: 143 us -> 130 us (0.909)
  Pallas kernels: 62.8 us -> 43 us
  starting transfers between devices: 39.8 us -> 48.2 us
  waiting for transfers between devices: 31.5 us -> 33.5 us
  local copies, waits for them, and re-layouts: 6.09 us -> 4.28 us
    pallas_call x4, Pallas kernels: 56.3 us -> 36 us  [multiply(): pl.pallas_call(functools.partial(matrix_kernel, first, tuple(offsets), wi...]
    ppermute x14, starting transfers between devices: 16.4 us -> 8.7 us  [body(): behind = lax.ppermute(behind, 'grid', back)]
    ppermute x14, starting transfers between devices: 16.8 us -> 24.3 us  [body(): ahead = lax.ppermute(ahead, 'grid', onward)]
    all_to_all x1 -> x2, starting transfers between devices: 4.97 us -> 11.4 us  [body(): lax.all_to_all(send, 'grid', split_axis=0, concat_axis=0, tiled=True)]
    all_to_all x1 -> x2, waiting for transfers between devices: 13.8 us -> 8.04 us  [body(): lax.all_to_all(send, 'grid', split_axis=0, concat_axis=0, tiled=True)]
    ppermute x14, waiting for transfers between devices: 2.02 us -> 7.34 us  [body(): ahead = lax.ppermute(ahead, 'grid', onward)]
    ppermute x14, waiting for transfers between devices: 1.68 us -> 6 us  [body(): behind = lax.ppermute(behind, 'grid', back)]
    gather x2 -> x0, local copies, waits for them, and re-layouts: 2.59 us -> none  [body(): jnp.asarray(walk, jnp.int32)]
  transfers between devices with their start and end apart: 31 -> 34, of which waited for: 10 -> 13; matrix products, arithmetic and copies ran while one was open for 5% -> 1% of each run, Pallas kernels for 21% -> 25%
where the time goes in v2:
time: 130 us; the launch traced here: 129 us
  starting transfers between devices  48.2 us (37%)
  Pallas kernels  43 us (33%)
  waiting for transfers between devices  33.5 us (26%)
  local copies, waits for them, and re-layouts  4.28 us (3%)
    pallas_call x4, Pallas kernels, multiply(): pl.pallas_call(functools.partial(matrix_kernel, first, tuple(offsets), wi...  36 us
    ppermute x14, starting transfers between devices, body(): ahead = lax.ppermute(ahead, 'grid', onward)  24.3 us
    ppermute x2, waiting for transfers between devices, body(): got = lax.ppermute(send, 'rep', high_pairs)  11.5 us
    all_to_all x2, starting transfers between devices, body(): lax.all_to_all(send, 'grid', split_axis=0, concat_axis=0, tiled=True)  11.4 us
    ppermute x14, starting transfers between devices, body(): behind = lax.ppermute(behind, 'grid', back)  8.7 us
    all_to_all x2, waiting for transfers between devices, body(): lax.all_to_all(send, 'grid', split_axis=0, concat_axis=0, tiled=True)  8.04 us
    ppermute x14, waiting for transfers between devices, body(): ahead = lax.ppermute(ahead, 'grid', onward)  7.34 us
    pallas_call x9, Pallas kernels, local_call(): pl.pallas_call(kernel, out_shape=out_shape, in_specs=in_specs, out_specs=...  7.05 us
  transfers between devices with their start and end apart: 34, of which 13 were waited for; matrix products, arithmetic and copies ran while one was open for 1% of the time, Pallas kernels for 25%

profile of v2, /device:TPU:0, one launch (start us, length us, event | category | flops | bytes accessed | tf_op | source)
XLA Modules:
  0.0 129.3 jit_solution(8090826016791706099)
XLA Ops:
  1.1 3.1 %collective-permute-start.14 = (bf16[32,2048]{1,0:T(8,128)(2,1)S(1)}, bf16[32,2048]{1,0:T(8,128)(2,1)S(1)}, u32[]{:S(2)}, u32[]{:S(2)}) collective-permute-start(bf16[32,2048]{1,0:T(8,128)(2,1)S(1)} %get-tuple-element.49.refs_1_), channel_id=1, source_target_pairs={{0,8},{8,16},{16,24},{24,28},{28,20},{20,12},{12,4},{4,0},{1,9},{9... | collective-permute-start | bytes 393224 | tf_op jit(solution)/shard_map/ppermute | solution.py:282
  4.1 3.4 %collective-permute-done.14.refs_2_ = bf16[32,2048]{1,0:T(8,128)(2,1)S(1)} collective-permute-done((bf16[32,2048]{1,0:T(8,128)(2,1)S(1)}, bf16[32,2048]{1,0:T(8,128)(2,1)S(1)}, u32[]{:S(2)}, u32[]{:S(2)}) %collective-permute-start.14) | collective-permute-done | bytes 131104 | tf_op jit(solution)/shard_map/ppermute | solution.py:282
  7.6 1.8 %collective-permute-start.15 = (bf16[32,2048]{1,0:T(8,128)(2,1)S(1)}, bf16[32,2048]{1,0:T(8,128)(2,1)S(1)}, u32[]{:S(2)}, u32[]{:S(2)}) collective-permute-start(bf16[32,2048]{1,0:T(8,128)(2,1)S(1)} %collective-permute-done.14.refs_2_), channel_id=1, source_target_pairs={{0,8},{8,16},{16,24},{24,28},{28,20},{20,12},{12,4},{4,0},{1,9},{9... | collective-permute-start | bytes 393224 | tf_op jit(solution)/shard_map/ppermute | solution.py:282
  9.6 1.7 %collective-permute-start.19 = (bf16[32,2048]{1,0:T(8,128)(2,1)S(1)}, bf16[32,2048]{1,0:T(8,128)(2,1)S(1)}, u32[]{:S(2)}, u32[]{:S(2)}) collective-permute-start(bf16[32,2048]{1,0:T(8,128)(2,1)S(1)} %collective-permute-done.18.refs_3_), channel_id=1, source_target_pairs={{8,0},{16,8},{24,16},{28,24},{20,28},{12,20},{4,12},{0,4},{9,1},{1... | collective-permute-start | bytes 393224 | tf_op jit(solution)/shard_map/ppermute | solution.py:286
  12.5 1.8 %collective-permute-start.16 = (bf16[32,2048]{1,0:T(8,128)(2,1)S(1)}, bf16[32,2048]{1,0:T(8,128)(2,1)S(1)}, u32[]{:S(2)}, u32[]{:S(2)}) collective-permute-start(bf16[32,2048]{1,0:T(8,128)(2,1)S(1)} %collective-permute-done.15.refs_4_), channel_id=1, source_target_pairs={{0,8},{8,16},{16,24},{24,28},{28,20},{20,12},{12,4},{4,0},{1,9},{9... | collective-permute-start | bytes 393224 | tf_op jit(solution)/shard_map/ppermute | solution.py:282
  14.3 1.6 %collective-permute-start = (bf16[32,2048]{1,0:T(8,128)(2,1)S(1)}, bf16[32,2048]{1,0:T(8,128)(2,1)S(1)}, u32[]{:S(2)}, u32[]{:S(2)}) collective-permute-start(bf16[32,2048]{1,0:T(8,128)(2,1)S(1)} %get-tuple-element.41.refs_1_), channel_id=1, source_target_pairs={{0,8},{8,16},{16,24},{24,28},{28,20},{20,12},{12,4},{4,0},{1,9},{9... | collective-permute-start | bytes 393224 | tf_op jit(solution)/shard_map/ppermute | solution.py:282
  17.6 2.2 %collective-permute-start.17 = (bf16[32,2048]{1,0:T(8,128)(2,1)S(1)}, bf16[32,2048]{1,0:T(8,128)(2,1)S(1)}, u32[]{:S(2)}, u32[]{:S(2)}) collective-permute-start(bf16[32,2048]{1,0:T(8,128)(2,1)S(1)} %collective-permute-done.16.refs_6_), channel_id=1, source_target_pairs={{0,8},{8,16},{16,24},{24,28},{28,20},{20,12},{12,4},{4,0},{1,9},{9... | collective-permute-start | bytes 393224 | tf_op jit(solution)/shard_map/ppermute | solution.py:282
  20.6 1.9 %collective-permute-start.1 = (bf16[32,2048]{1,0:T(8,128)(2,1)S(1)}, bf16[32,2048]{1,0:T(8,128)(2,1)S(1)}, u32[]{:S(2)}, u32[]{:S(2)}) collective-permute-start(bf16[32,2048]{1,0:T(8,128)(2,1)S(1)} %collective-permute-done.refs_2_), channel_id=1, source_target_pairs={{0,8},{8,16},{16,24},{24,28},{28,20},{20,12},{12,4},{4,0},{1,9},{9... | collective-permute-start | bytes 393224 | tf_op jit(solution)/shard_map/ppermute | solution.py:282
  23.7 1.8 %collective-permute-start.21 = (bf16[32,2048]{1,0:T(8,128)(2,1)S(1)}, bf16[32,2048]{1,0:T(8,128)(2,1)S(1)}, u32[]{:S(2)}, u32[]{:S(2)}) collective-permute-start(bf16[32,2048]{1,0:T(8,128)(2,1)S(1)} %get-tuple-element.33.refs_1_), channel_id=1, source_target_pairs={{0,8},{8,16},{16,24},{24,28},{28,20},{20,12},{12,4},{4,0},{1,9},{9... | collective-permute-start | bytes 393224 | tf_op jit(solution)/shard_map/ppermute | solution.py:282
  27.0 2.0 %collective-permute-start.2 = (bf16[32,2048]{1,0:T(8,128)(2,1)S(1)}, bf16[32,2048]{1,0:T(8,128)(2,1)S(1)}, u32[]{:S(2)}, u32[]{:S(2)}) collective-permute-start(bf16[32,2048]{1,0:T(8,128)(2,1)S(1)} %collective-permute-done.1.refs_4_), channel_id=1, source_target_pairs={{0,8},{8,16},{16,24},{24,28},{28,20},{20,12},{12,4},{4,0},{1,9},{9... | collective-permute-start | bytes 393224 | tf_op jit(solution)/shard_map/ppermute | solution.py:282
  29.1 1.9 %collective-permute-start.22 = (bf16[32,2048]{1,0:T(8,128)(2,1)S(1)}, bf16[32,2048]{1,0:T(8,128)(2,1)S(1)}, u32[]{:S(2)}, u32[]{:S(2)}) collective-permute-start(bf16[32,2048]{1,0:T(8,128)(2,1)S(1)} %get-tuple-element.33.refs_1_), channel_id=1, source_target_pairs={{8,0},{16,8},{24,16},{28,24},{20,28},{12,20},{4,12},{0,4},{9,1},{1... | collective-permute-start | bytes 393224 | tf_op jit(solution)/shard_map/ppermute | solution.py:286
  36.0 3.5 %collective-permute-done.8.refs_3_ = bf16[32,1356]{1,0:T(8,128)(2,1)S(1)} collective-permute-done((bf16[32,1356]{1,0:T(8,128)(2,1)S(1)}, bf16[32,1356]{1,0:T(8,128)(2,1)S(1)}, u32[]{:S(2)}, u32[]{:S(2)}) %collective-permute-start.8) | collective-permute-done | bytes 86816 | tf_op jit(solution)/shard_map/ppermute | solution.py:286
  43.5 9.3 %matrix.4.refs_10_ = f32[2,3840,128]{2,1,0:T(8,128)S(1)} custom-call(s32[1]{0:T(128)} %bitcast.1.refs_0_, bf16[32,2048]{1,0:T(8,128)(2,1)S(1)} %get-tuple-element.49.refs_1_, bf16[32,2048]{1,0:T(8,128)(2,1)S(1)} %collective-permute-done.14.refs_2_, bf16[32,2048]{1,0:T(8,128)(2,1)S(1)} %collective-permute-done.18.refs_3_, ...), custom_call_target="tpu_custom_call" | custom-call | flops 3774873600 | bytes 22118400 | tf_op jit(solution)/shard_map/matrix/pallas_call | solution.py:109
  57.0 9.4 %matrix.5.refs_10_ = f32[2,3840,128]{2,1,0:T(8,128)S(1)} custom-call(s32[1]{0:T(128)} %bitcast.1.refs_0_, bf16[32,2048]{1,0:T(8,128)(2,1)S(1)} %get-tuple-element.41.refs_1_, bf16[32,2048]{1,0:T(8,128)(2,1)S(1)} %collective-permute-done.refs_2_, bf16[32,2048]{1,0:T(8,128)(2,1)S(1)} %collective-permute-done.3.refs_3_, ...), custom_call_target="tpu_custom_call", output_to_operand_aliasing={{}: (10, {})} | custom-call | flops 3774873600 | bytes 22118400 | tf_op jit(solution)/shard_map/matrix/pallas_call | solution.py:109
  67.0 9.4 %matrix.6.refs_10_ = f32[2,3840,128]{2,1,0:T(8,128)S(1)} custom-call(s32[1]{0:T(128)} %bitcast.1.refs_0_, bf16[32,2048]{1,0:T(8,128)(2,1)S(1)} %get-tuple-element.33.refs_1_, bf16[32,2048]{1,0:T(8,128)(2,1)S(1)} %collective-permute-done.21.refs_2_, bf16[32,2048]{1,0:T(8,128)(2,1)S(1)} %collective-permute-done.22.refs_3_, ...), custom_call_target="tpu_custom_call", output_to_operand_aliasing={{}: (10, {})} | custom-call | flops 3774873600 | bytes 22118400 | tf_op jit(solution)/shard_map/matrix/pallas_call | solution.py:109
  76.4 7.9 %matrix.7.total_ref = f32[2,3840,128]{2,1,0:T(8,128)S(1)} custom-call(s32[1]{0:T(128)} %bitcast.1.refs_0_, bf16[32,1356]{1,0:T(8,128)(2,1)S(1)} %slice.12.refs_1_, bf16[32,1356]{1,0:T(8,128)(2,1)S(1)} %collective-permute-done.7.refs_2_, bf16[32,1356]{1,0:T(8,128)(2,1)S(1)} %collective-permute-done.8.refs_3_, ...), custom_call_target="tpu_custom_call", output_to_operand_aliasing={{}: (10, {})} | custom-call | flops 2499379200 | bytes 17136000 | tf_op jit(solution)/shard_map/matrix/pallas_call | solution.py:109
  87.1 1.7 %collective-permute-start.31 = (s16[7,64,256]{2,1,0:T(8,128)(2,1)S(1)}, s16[7,64,256]{2,1,0:T(8,128)(2,1)S(1)}, u32[]{:S(2)}, u32[]{:S(2)}) collective-permute-start(s16[7,64,256]{2,1,0:T(8,128)(2,1)S(1)} %second_send.3), channel_id=1, source_target_pairs={{0,2},{1,3},{2,0},{3,1},{4,6},{5,7},{6,4},{7,5},{8,10},{9,11},{10,... | collective-permute-start | bytes 688136 | tf_op jit(solution)/shard_map/ppermute | solution.py:329
  88.9 5.9 %collective-permute-done.31.got_ref = s16[7,64,256]{2,1,0:T(8,128)(2,1)S(1)} collective-permute-done((s16[7,64,256]{2,1,0:T(8,128)(2,1)S(1)}, s16[7,64,256]{2,1,0:T(8,128)(2,1)S(1)}, u32[]{:S(2)}, u32[]{:S(2)}) %collective-permute-start.31) | collective-permute-done | bytes 229408 | tf_op jit(solution)/shard_map/ppermute | solution.py:329
  96.2 5.7 %all-to-all-start.1 = ((s16[8,2,64,128]{3,2,1,0:T(8,128)(2,1)}), s16[8,2,64,128]{3,2,1,0:T(8,128)(2,1)S(1)}, u32[]{:S(2)}, u32[]{:S(2)}) async-start(s16[8,2,64,128]{3,2,1,0:T(8,128)(2,1)} %third_send.3), calls=%async_computation.1 | async-start | bytes 524288 | tf_op jit(solution)/shard_map/all_to_all | solution.py:336
  101.9 2.1 %copy-done.1 = f32[2,3840,128]{2,1,0:T(8,128)S(1)} copy-done((f32[2,3840,128]{2,1,0:T(8,128)S(1)}, f32[2,3840,128]{2,1,0:T(8,128)}, u32[]{:S(2)}) %copy-start.1) | copy-done | bytes 3932184
  106.3 5.6 %collective-permute-done.29.got_ref = s16[8,64,256]{2,1,0:T(8,128)(2,1)S(1)} collective-permute-done((s16[8,64,256]{2,1,0:T(8,128)(2,1)S(1)}, s16[8,64,256]{2,1,0:T(8,128)(2,1)S(1)}, u32[]{:S(2)}, u32[]{:S(2)}) %collective-permute-start.29) | collective-permute-done | bytes 262176 | tf_op jit(solution)/shard_map/ppermute | solution.py:329
  113.3 5.7 %all-to-all-start = ((s16[8,2,64,128]{3,2,1,0:T(8,128)(2,1)}), s16[8,2,64,128]{3,2,1,0:T(8,128)(2,1)S(1)}, u32[]{:S(2)}, u32[]{:S(2)}) async-start(s16[8,2,64,128]{3,2,1,0:T(8,128)(2,1)} %third_send.2), calls=%async_computation | async-start | bytes 524288 | tf_op jit(solution)/shard_map/all_to_all | solution.py:336
  119.2 8.0 %all-to-all-done.refs_0_ = s16[8,2,64,128]{3,2,1,0:T(8,128)(2,1)S(1)} async-done(((s16[8,2,64,128]{3,2,1,0:T(8,128)(2,1)}), s16[8,2,64,128]{3,2,1,0:T(8,128)(2,1)S(1)}, u32[]{:S(2)}, u32[]{:S(2)}) %all-to-all-start) | async-done | bytes 262176 | tf_op jit(solution)/shard_map/all_to_all | solution.py:336
  127.2 2.1 %update.1 = f32[15,32,480]{2,1,0:T(8,128)} custom-call(f32[15]{0:T(128)S(1)} %copy-done.5, s32[15]{0:T(128)S(1)} %copy-done.6, s16[8,2,64,128]{3,2,1,0:T(8,128)(2,1)S(1)} %all-to-all-done.refs_0_, s16[8,2,64,128]{3,2,1,0:T(8,128)(2,1)S(1)} %all-to-all-done.1.refs_1_, f32[15,32,480]{2,1,0:T(8,128)S(1)} %bitcast.9, f32[32,1]{1,0:T(8,128)S(1)} %copy.13.refs_3_, ...), custom_call_target="tpu_custom_call" | custom-call | flops 10000000 | bytes 4000000 | tf_op jit(solution)/shard_map/update/pallas_call | solution.py:231
  (79 shorter events, 29.6 us)
Async XLA Ops:
  1.1 6.5 %collective-permute-start.14 = (bf16[32,2048]{1,0:T(8,128)(2,1)S(1)}, bf16[32,2048]{1,0:T(8,128)(2,1)S(1)}, u32[]{:S(2)}, u32[]{:S(2)}) collective-permute-start(bf16[32,2048]{1,0:T(8,128)(2,1)S(1)} %get-tuple-element.49.refs_1_), channel_id=1, source_target_pairs={{0,8},{8,16},{16,24},{24,28},{28,20},{20,12},{12,4},{4,0},{1,9},{9... | collective-permute-start | bytes 393224 | tf_op jit(solution)/shard_map/ppermute | solution.py:282
  9.4 6.5 %collective-permute-start.3 = (bf16[32,2048]{1,0:T(8,128)(2,1)S(1)}, bf16[32,2048]{1,0:T(8,128)(2,1)S(1)}, u32[]{:S(2)}, u32[]{:S(2)}) collective-permute-start(bf16[32,2048]{1,0:T(8,128)(2,1)S(1)} %get-tuple-element.41.refs_1_), channel_id=1, source_target_pairs={{8,0},{16,8},{24,16},{28,24},{20,28},{12,20},{4,12},{0,4},{9,1},{1... | collective-permute-start | bytes 393224 | tf_op jit(solution)/shard_map/ppermute | solution.py:286
  9.6 7.1 %collective-permute-start.19 = (bf16[32,2048]{1,0:T(8,128)(2,1)S(1)}, bf16[32,2048]{1,0:T(8,128)(2,1)S(1)}, u32[]{:S(2)}, u32[]{:S(2)}) collective-permute-start(bf16[32,2048]{1,0:T(8,128)(2,1)S(1)} %collective-permute-done.18.refs_3_), channel_id=1, source_target_pairs={{8,0},{16,8},{24,16},{28,24},{20,28},{12,20},{4,12},{0,4},{9,1},{1... | collective-permute-start | bytes 393224 | tf_op jit(solution)/shard_map/ppermute | solution.py:286
  15.9 6.7 %collective-permute-start.4 = (bf16[32,2048]{1,0:T(8,128)(2,1)S(1)}, bf16[32,2048]{1,0:T(8,128)(2,1)S(1)}, u32[]{:S(2)}, u32[]{:S(2)}) collective-permute-start(bf16[32,2048]{1,0:T(8,128)(2,1)S(1)} %collective-permute-done.3.refs_3_), channel_id=1, source_target_pairs={{8,0},{16,8},{24,16},{28,24},{20,28},{12,20},{4,12},{0,4},{9,1},{1... | collective-permute-start | bytes 393224 | tf_op jit(solution)/shard_map/ppermute | solution.py:286
  16.7 7.0 %collective-permute-start.20 = (bf16[32,2048]{1,0:T(8,128)(2,1)S(1)}, bf16[32,2048]{1,0:T(8,128)(2,1)S(1)}, u32[]{:S(2)}, u32[]{:S(2)}) collective-permute-start(bf16[32,2048]{1,0:T(8,128)(2,1)S(1)} %collective-permute-done.19.refs_5_), channel_id=1, source_target_pairs={{8,0},{16,8},{24,16},{28,24},{20,28},{12,20},{4,12},{0,4},{9,1},{1... | collective-permute-start | bytes 393224 | tf_op jit(solution)/shard_map/ppermute | solution.py:286
  20.6 6.4 %collective-permute-start.1 = (bf16[32,2048]{1,0:T(8,128)(2,1)S(1)}, bf16[32,2048]{1,0:T(8,128)(2,1)S(1)}, u32[]{:S(2)}, u32[]{:S(2)}) collective-permute-start(bf16[32,2048]{1,0:T(8,128)(2,1)S(1)} %collective-permute-done.refs_2_), channel_id=1, source_target_pairs={{0,8},{8,16},{16,24},{24,28},{28,20},{20,12},{12,4},{4,0},{1,9},{9... | collective-permute-start | bytes 393224 | tf_op jit(solution)/shard_map/ppermute | solution.py:282
  22.6 6.4 %collective-permute-start.5 = (bf16[32,2048]{1,0:T(8,128)(2,1)S(1)}, bf16[32,2048]{1,0:T(8,128)(2,1)S(1)}, u32[]{:S(2)}, u32[]{:S(2)}) collective-permute-start(bf16[32,2048]{1,0:T(8,128)(2,1)S(1)} %collective-permute-done.4.refs_5_), channel_id=1, source_target_pairs={{8,0},{16,8},{24,16},{28,24},{20,28},{12,20},{4,12},{0,4},{9,1},{1... | collective-permute-start | bytes 393224 | tf_op jit(solution)/shard_map/ppermute | solution.py:286
  23.7 7.3 %collective-permute-start.21 = (bf16[32,2048]{1,0:T(8,128)(2,1)S(1)}, bf16[32,2048]{1,0:T(8,128)(2,1)S(1)}, u32[]{:S(2)}, u32[]{:S(2)}) collective-permute-start(bf16[32,2048]{1,0:T(8,128)(2,1)S(1)} %get-tuple-element.33.refs_1_), channel_id=1, source_target_pairs={{0,8},{8,16},{16,24},{24,28},{28,20},{20,12},{12,4},{4,0},{1,9},{9... | collective-permute-start | bytes 393224 | tf_op jit(solution)/shard_map/ppermute | solution.py:282
  29.1 12.4 %collective-permute-start.22 = (bf16[32,2048]{1,0:T(8,128)(2,1)S(1)}, bf16[32,2048]{1,0:T(8,128)(2,1)S(1)}, u32[]{:S(2)}, u32[]{:S(2)}) collective-permute-start(bf16[32,2048]{1,0:T(8,128)(2,1)S(1)} %get-tuple-element.33.refs_1_), channel_id=1, source_target_pairs={{8,0},{16,8},{24,16},{28,24},{20,28},{12,20},{4,12},{0,4},{9,1},{1... | collective-permute-start | bytes 393224 | tf_op jit(solution)/shard_map/ppermute | solution.py:286
  31.0 11.1 %collective-permute-start.23 = (bf16[32,2048]{1,0:T(8,128)(2,1)S(1)}, bf16[32,2048]{1,0:T(8,128)(2,1)S(1)}, u32[]{:S(2)}, u32[]{:S(2)}) collective-permute-start(bf16[32,2048]{1,0:T(8,128)(2,1)S(1)} %collective-permute-done.21.refs_2_), channel_id=1, source_target_pairs={{0,8},{8,16},{16,24},{24,28},{28,20},{20,12},{12,4},{4,0},{1,9},{9... | collective-permute-start | bytes 393224 | tf_op jit(solution)/shard_map/ppermute | solution.py:282
  39.5 13.4 %collective-permute-start.10 = (bf16[32,1356]{1,0:T(8,128)(2,1)S(1)}, bf16[32,1356]{1,0:T(8,128)(2,1)S(1)}, u32[]{:S(2)}, u32[]{:S(2)}) collective-permute-start(bf16[32,1356]{1,0:T(8,128)(2,1)S(1)} %collective-permute-done.8.refs_3_), channel_id=1, source_target_pairs={{8,0},{16,8},{24,16},{28,24},{20,28},{12,20},{4,12},{0,4},{9,1},{1... | collective-permute-start | bytes 260360 | tf_op jit(solution)/shard_map/ppermute | solution.py:286
  40.0 13.5 %collective-permute-start.9 = (bf16[32,1356]{1,0:T(8,128)(2,1)S(1)}, bf16[32,1356]{1,0:T(8,128)(2,1)S(1)}, u32[]{:S(2)}, u32[]{:S(2)}) collective-permute-start(bf16[32,1356]{1,0:T(8,128)(2,1)S(1)} %collective-permute-done.7.refs_2_), channel_id=1, source_target_pairs={{0,8},{8,16},{16,24},{24,28},{28,20},{20,12},{12,4},{4,0},{1,9},{9... | collective-permute-start | bytes 260360 | tf_op jit(solution)/shard_map/ppermute | solution.py:282
  41.5 13.5 %collective-permute-start.24 = (bf16[32,2048]{1,0:T(8,128)(2,1)S(1)}, bf16[32,2048]{1,0:T(8,128)(2,1)S(1)}, u32[]{:S(2)}, u32[]{:S(2)}) collective-permute-start(bf16[32,2048]{1,0:T(8,128)(2,1)S(1)} %collective-permute-done.22.refs_3_), channel_id=1, source_target_pairs={{8,0},{16,8},{24,16},{28,24},{20,28},{12,20},{4,12},{0,4},{9,1},{1... | collective-permute-start | bytes 393224 | tf_op jit(solution)/shard_map/ppermute | solution.py:286
  42.1 13.5 %collective-permute-start.25 = (bf16[32,2048]{1,0:T(8,128)(2,1)S(1)}, bf16[32,2048]{1,0:T(8,128)(2,1)S(1)}, u32[]{:S(2)}, u32[]{:S(2)}) collective-permute-start(bf16[32,2048]{1,0:T(8,128)(2,1)S(1)} %collective-permute-done.23.refs_4_), channel_id=1, source_target_pairs={{0,8},{8,16},{16,24},{24,28},{28,20},{20,12},{12,4},{4,0},{1,9},{9... | collective-permute-start | bytes 393224 | tf_op jit(solution)/shard_map/ppermute | solution.py:282
  52.9 13.5 %collective-permute-start.12 = (bf16[32,1356]{1,0:T(8,128)(2,1)S(1)}, bf16[32,1356]{1,0:T(8,128)(2,1)S(1)}, u32[]{:S(2)}, u32[]{:S(2)}) collective-permute-start(bf16[32,1356]{1,0:T(8,128)(2,1)S(1)} %collective-permute-done.10.refs_5_), channel_id=1, source_target_pairs={{8,0},{16,8},{24,16},{28,24},{20,28},{12,20},{4,12},{0,4},{9,1},{1... | collective-permute-start | bytes 260360 | tf_op jit(solution)/shard_map/ppermute | solution.py:286
  53.5 13.5 %collective-permute-start.11 = (bf16[32,1356]{1,0:T(8,128)(2,1)S(1)}, bf16[32,1356]{1,0:T(8,128)(2,1)S(1)}, u32[]{:S(2)}, u32[]{:S(2)}) collective-permute-start(bf16[32,1356]{1,0:T(8,128)(2,1)S(1)} %collective-permute-done.9.refs_4_), channel_id=1, source_target_pairs={{0,8},{8,16},{16,24},{24,28},{28,20},{20,12},{12,4},{4,0},{1,9},{9... | collective-permute-start | bytes 260360 | tf_op jit(solution)/shard_map/ppermute | solution.py:282
  55.0 12.0 %collective-permute-start.26 = (bf16[32,2048]{1,0:T(8,128)(2,1)S(1)}, bf16[32,2048]{1,0:T(8,128)(2,1)S(1)}, u32[]{:S(2)}, u32[]{:S(2)}) collective-permute-start(bf16[32,2048]{1,0:T(8,128)(2,1)S(1)} %collective-permute-done.24.refs_5_), channel_id=1, source_target_pairs={{8,0},{16,8},{24,16},{28,24},{20,28},{12,20},{4,12},{0,4},{9,1},{1... | collective-permute-start | bytes 393224 | tf_op jit(solution)/shard_map/ppermute | solution.py:286
  55.5 11.5 %collective-permute-start.27 = (bf16[32,2048]{1,0:T(8,128)(2,1)S(1)}, bf16[32,2048]{1,0:T(8,128)(2,1)S(1)}, u32[]{:S(2)}, u32[]{:S(2)}) collective-permute-start(bf16[32,2048]{1,0:T(8,128)(2,1)S(1)} %collective-permute-done.25.refs_6_), channel_id=1, source_target_pairs={{0,8},{8,16},{16,24},{24,28},{28,20},{20,12},{12,4},{4,0},{1,9},{9... | collective-permute-start | bytes 393224 | tf_op jit(solution)/shard_map/ppermute | solution.py:282
  66.4 10.0 %collective-permute-start.13 = (bf16[32,1356]{1,0:T(8,128)(2,1)S(1)}, bf16[32,1356]{1,0:T(8,128)(2,1)S(1)}, u32[]{:S(2)}, u32[]{:S(2)}) collective-permute-start(bf16[32,1356]{1,0:T(8,128)(2,1)S(1)} %collective-permute-done.12.refs_7_), channel_id=1, source_target_pairs={{8,0},{16,8},{24,16},{28,24},{20,28},{12,20},{4,12},{0,4},{9,1},{1... | collective-permute-start | bytes 260360 | tf_op jit(solution)/shard_map/ppermute | solution.py:286
  85.5 16.4 %collective-permute-start.28 = (s16[2,8,64,256]{3,2,1,0:T(8,128)(2,1)S(1)}, s16[2,8,64,256]{3,2,1,0:T(8,128)(2,1)S(1)}, u32[]{:S(2)}, u32[]{:S(2)}) collective-permute-start(s16[2,8,64,256]{3,2,1,0:T(8,128)(2,1)S(1)} %first_send.2), channel_id=1, source_target_pairs={{0,1},{1,0},{2,3},{3,2},{4,5},{5,4},{6,7},{7,6},{8,9},{9,8},{10,11... | collective-permute-start | bytes 1572872 | tf_op jit(solution)/shard_map/ppermute | solution.py:314
  87.1 7.7 %collective-permute-start.31 = (s16[7,64,256]{2,1,0:T(8,128)(2,1)S(1)}, s16[7,64,256]{2,1,0:T(8,128)(2,1)S(1)}, u32[]{:S(2)}, u32[]{:S(2)}) collective-permute-start(s16[7,64,256]{2,1,0:T(8,128)(2,1)S(1)} %second_send.3), channel_id=1, source_target_pairs={{0,2},{1,3},{2,0},{3,1},{4,6},{5,7},{6,4},{7,5},{8,10},{9,11},{10,... | collective-permute-start | bytes 688136 | tf_op jit(solution)/shard_map/ppermute | solution.py:329
  96.2 17.1 %all-to-all-start.1 = ((s16[8,2,64,128]{3,2,1,0:T(8,128)(2,1)}), s16[8,2,64,128]{3,2,1,0:T(8,128)(2,1)S(1)}, u32[]{:S(2)}, u32[]{:S(2)}) async-start(s16[8,2,64,128]{3,2,1,0:T(8,128)(2,1)} %third_send.3), calls=%async_computation.1 | async-start | bytes 524288 | tf_op jit(solution)/shard_map/all_to_all | solution.py:336
  104.6 7.3 %collective-permute-start.29 = (s16[8,64,256]{2,1,0:T(8,128)(2,1)S(1)}, s16[8,64,256]{2,1,0:T(8,128)(2,1)S(1)}, u32[]{:S(2)}, u32[]{:S(2)}) collective-permute-start(s16[8,64,256]{2,1,0:T(8,128)(2,1)S(1)} %second_send.2), channel_id=1, source_target_pairs={{0,2},{1,3},{2,0},{3,1},{4,6},{5,7},{6,4},{7,5},{8,10},{9,11},{10,... | collective-permute-start | bytes 786440 | tf_op jit(solution)/shard_map/ppermute | solution.py:329
  113.3 13.9 %all-to-all-start = ((s16[8,2,64,128]{3,2,1,0:T(8,128)(2,1)}), s16[8,2,64,128]{3,2,1,0:T(8,128)(2,1)S(1)}, u32[]{:S(2)}, u32[]{:S(2)}) async-start(s16[8,2,64,128]{3,2,1,0:T(8,128)(2,1)} %third_send.2), calls=%async_computation | async-start | bytes 524288 | tf_op jit(solution)/shard_map/all_to_all | solution.py:336
  (19 other events, 200.2 us)

commit v3 on v0

v3 whole, which is shorter than its diff:
```python
import functools

import jax
import jax.numpy as jnp
from jax import lax
from jax.experimental import pallas as pl
from jax.experimental.pallas import tpu as pltpu
from jax.sharding import PartitionSpec as P

NOCC = 60
LANES = 128
K_BLOCK = 3840
C_BLOCK = 480
B_ROWS = 32
STEPS = 8.0
TOP = 32767.0
MIB = 1024 * 1024


def ceil_to(value, unit):
    return -(-value // unit) * unit


def encode(rows, count):
    index = lax.broadcasted_iota(jnp.int32, rows.shape, 0)
    rows = jnp.where(index < count, rows, 0.0)
    largest = jnp.max(jnp.abs(rows), axis=0, keepdims=True)
    level = jnp.ceil(jnp.log2(jnp.maximum(largest, 1e-30)) * STEPS) + 1.0
    coded = jnp.floor(rows * (jnp.exp2(level * (-1.0 / STEPS)) * TOP) + 0.5)
    return jnp.where(index == count, level, coded)


def decode(block, count):
    index = lax.broadcasted_iota(jnp.int32, block.shape, 0)
    scale = jnp.exp2(block[count : count + 1] * (1.0 / STEPS)) * (1.0 / TOP)
    return jnp.where(index < count, block * scale, 0.0)


def to_code(block):
    return block.astype(jnp.int32).astype(jnp.int16)


def from_code(block):
    return block.astype(jnp.int32).astype(jnp.float32)


def walk_index(place, size):
    return jnp.where(place < size // 2, 2 * place, 2 * (size - 1 - place) + 1)


def walk_place(index, size):
    return jnp.where(index % 2 == 0, index // 2, size - 1 - index // 2)


def gather_pieces(me_ref, offsets, pieces, gathered, turned):
    blocks = len(offsets)
    rows, width = pieces[0].shape
    place = walk_place(me_ref[0], blocks)
    for offset, piece in zip(offsets, pieces):
        source = walk_index(lax.rem(place + offset + blocks, blocks), blocks)
        at = pl.multiple_of(source * rows, rows)
        gathered[pl.ds(at, rows), :width] = piece[...]
    for at in range(0, turned.shape[0], LANES):
        tile = gathered[:, at : at + LANES].T
        if at + LANES > width:
            index = lax.broadcasted_iota(jnp.int32, tile.shape, 0)
            tile = jnp.where(index < width - at, tile, jnp.zeros_like(tile))
        turned[at : at + LANES, :] = tile


def add_products(coupling_ref, edge_ref, at, width, turned, total_in, total_out, columns):
    all_columns = coupling_ref.shape[0]
    block = C_BLOCK if all_columns % 16 == 0 else all_columns
    low, many = columns
    whole = width // LANES * LANES

    def step(coupling_block, edge_block=None):
        total = jnp.dot(coupling_block[...], turned[:whole, :], preferred_element_type=jnp.float32)
        if whole < width:
            total += jnp.dot(
                edge_block[...], turned[whole:, :], preferred_element_type=jnp.float32
            )
        rows = pl.ds(pl.program_id(0) * block, block)
        for part in range(total_out.shape[0]):
            own = total[:, part * LANES : (part + 1) * LANES]
            total_out[part, rows, :] = own if total_in is None else total_in[part, rows, :] + own

    index_map = lambda i: (i, 0)
    specs = [pl.BlockSpec((block, whole), index_map)]
    args = [coupling_ref.at[low : low + many, at : at + whole]]
    if whole < width:
        specs.append(pl.BlockSpec((block, LANES), index_map))
        args.append(edge_ref.at[low : low + many])
    pltpu.emit_pipeline(step, grid=(pl.cdiv(many, block),), in_specs=specs)(*args)


def start_kernel(offsets, at, columns, me_ref, *refs):
    pieces, refs = refs[: len(offsets)], refs[len(offsets) :]
    coupling_ref, edge_ref = refs[:2]
    totals, (gathered, turned) = refs[2:-2], refs[-2:]
    gather_pieces(me_ref, offsets, pieces, gathered, turned)
    width = pieces[0].shape[1]
    outs = totals[-len(columns) :]
    ins = totals[: -len(columns)] or [None] * len(columns)
    for span, total_in, total_out in zip(columns, ins, outs):
        add_products(coupling_ref, edge_ref, at, width, turned, total_in, total_out, span)


def last_kernel(offsets, at, columns, span, me_ref, rep_ref, *refs):
    pieces = refs[: len(offsets)]
    coupling_ref, edge_ref, total_in, total_out, turned, send_ref, gathered = refs[len(offsets) :]
    gather_pieces(me_ref, offsets, pieces, gathered, turned)
    width = pieces[0].shape[1]
    add_products(coupling_ref, edge_ref, at, width, turned, total_in, total_out, columns)
    first_send(span, rep_ref, total_out, send_ref)


def rest_kernel(at, width, columns, span, rep_ref, turned, *refs):
    coupling_ref, edge_ref, total_in, total_out, send = refs
    add_products(coupling_ref, edge_ref, at, width, turned, total_in, total_out, columns)
    first_send(span, rep_ref, total_out, send)


def column_rows(total_ref, width, part, j, offset, bp):
    rows = pl.ds(offset + part * width + j, bp, stride=NOCC)
    return jnp.concatenate([total_ref[h, rows, :] for h in range(total_ref.shape[0])], axis=1)


def first_send(span, rep_ref, total_ref, out_ref):
    offset, count, width = span
    low = rep_ref[0] % 2

    def step(j, carry):
        for high in range(2):
            rows = column_rows(total_ref, width, 2 * high + 1 - low, j, offset, out_ref.shape[2])
            out_ref[high, j] = to_code(encode(rows, count))
        return carry

    lax.fori_loop(0, width, step, 0)


def second_send_kernel(span, rep_ref, total_ref, got_ref, out_ref):
    offset, count, width = span
    low, high = rep_ref[0] % 2, 1 - rep_ref[0] // 2

    def step(j, carry):
        rows = column_rows(total_ref, width, 2 * high + low, j, offset, out_ref.shape[1])
        rows = rows + decode(from_code(got_ref[high, j]), count)
        out_ref[j] = to_code(encode(rows, count))
        return carry

    lax.fori_loop(0, width, step, 0)


def keep_kernel(span, rep_ref, total_ref, got_ref, out_ref):
    offset, count, width = span
    low, high = rep_ref[0] % 2, rep_ref[0] // 2

    def step(j, carry):
        rows = column_rows(total_ref, width, 2 * high + low, j, offset, out_ref.shape[1])
        out_ref[j] = rows + decode(from_code(got_ref[high, j]), count)
        return carry

    lax.fori_loop(0, width, step, 0)


def third_send_kernel(count, rows_dev, kept_ref, got_ref, out_ref):
    pack = LANES // rows_dev
    groups = out_ref.shape[1]
    size, _, slab = kept_ref.shape

    def step(jj, carry):
        coded = []
        for jq in range(pack):
            j = jnp.minimum(jq * groups + jj, size - 1)
            coded.append(encode(kept_ref[j] + decode(from_code(got_ref[j]), count), count))
        for g in range(slab // rows_dev):
            own = [block[:, g * rows_dev : (g + 1) * rows_dev] for block in coded]
            out_ref[g, jj] = to_code(jnp.concatenate(own, axis=1))
        return carry

    lax.fori_loop(0, groups, step, 0)


def update_kernel(counts, width, rows_dev, occ_energy_ref, occ_irrep_ref, *refs):
    arrived = refs[: len(counts)]
    (
        integrals_ref,
        row_energy_ref,
        vir_energy_ref,
        row_irrep_ref,
        vir_irrep_ref,
        out_ref,
        stage,
    ) = refs[len(counts) :]
    pack = LANES // rows_dev
    grid_size, groups = arrived[0].shape[:2]
    for jj in range(groups):
        at = 0
        for g in range(grid_size):
            for count, got_ref in zip(counts, arrived):
                block = decode(from_code(got_ref[g, jj]), count)
                stage[at : at + count, :] = block[:count]
                at += count
        turned = stage[...].T
        for jq in range(pack):
            j = jq * groups + jj
            if j >= width:
                continue
            cycle = turned[jq * rows_dev : (jq + 1) * rows_dev]
            denominator = row_energy_ref[...] + occ_energy_ref[j] - vir_energy_ref[...]
            labels = row_irrep_ref[...] ^ occ_irrep_ref[j] ^ vir_irrep_ref[...]
            out_ref[j] = jnp.where(
                labels == 0, (integrals_ref[j] + cycle) / denominator, jnp.float32(0.0)
            )


def local_call(kernel, out_shape, specs, args, scratch=(), aliases={}, cost=(10**7, 4 * 10**6), room=0):
    spaces = {"s": pltpu.SMEM, "v": pltpu.VMEM, "a": pl.ANY}
    return pl.pallas_call(
        kernel,
        out_shape=out_shape,
        in_specs=[pl.BlockSpec(memory_space=spaces[letter]) for letter in specs],
        out_specs=jax.tree.map(lambda _: pl.BlockSpec(memory_space=pltpu.VMEM), out_shape),
        scratch_shapes=list(scratch),
        input_output_aliases=aliases,
        compiler_params=pltpu.CompilerParams(vmem_limit_bytes=8 * MIB + room),
        cost_estimate=pl.CostEstimate(
            flops=cost[0], bytes_accessed=cost[1], transcendentals=0
        ),
        name=kernel.func.__name__,
    )(*args)


def body(
    amplitudes,
    coupling,
    integrals,
    row_energy,
    occ_energy,
    vir_energy,
    row_irrep,
    occ_irrep,
    vir_irrep,
):
    grid_size = lax.axis_size("grid")
    me = lax.axis_index("grid").astype(jnp.int32).reshape(1)
    rep = lax.axis_index("rep").astype(jnp.int32).reshape(1)
    rows_dev, depth = amplitudes.shape
    coupling = coupling.T
    columns = coupling.shape[0]
    edge = depth % LANES
    edge = jnp.pad(coupling[:, depth - edge :], ((0, 0), (0, LANES - edge)))
    count = columns // NOCC
    slab = rows_dev * grid_size
    width = NOCC // lax.axis_size("rep")

    walk = [*range(0, grid_size, 2), *range(1, grid_size, 2)[::-1]]
    onward = [(walk[i], walk[(i + 1) % grid_size]) for i in range(grid_size)]
    back = [(b, a) for a, b in onward]

    longer = grid_size // 2
    jobs = []
    for number, at in enumerate(range(0, depth, K_BLOCK)):
        own = amplitudes[:, at : at + K_BLOCK]
        pieces, offsets = [own], [0]
        hops = (longer, grid_size - 1 - longer)
        if number % 2:
            hops = hops[::-1]
        ahead = behind = own
        for hop in range(1, longer + 1):
            if hop <= hops[0]:
                ahead = lax.ppermute(ahead, "grid", onward)
                pieces.append(ahead)
                offsets.append(-hop)
            if hop <= hops[1]:
                behind = lax.ppermute(behind, "grid", back)
                pieces.append(behind)
                offsets.append(hop)
        jobs.append((at, tuple(offsets), pieces))

    firsts = list(range(0, count, B_ROWS - 1))
    counts = [min(B_ROWS - 1, count - first) for first in firsts]
    bp = ceil_to(counts[0] + 1, 16)
    send_shape = jax.ShapeDtypeStruct((2, width, bp, slab), jnp.int16)
    lows = [first * NOCC // 16 * 16 for first in firsts]
    highs = [
        min(columns, ceil_to((first + number) * NOCC, 16)) for first, number in zip(firsts, counts)
    ]
    parts = [(low, high - low) for low, high in zip(lows, highs)]
    spans = [
        (first * NOCC - low, number, width) for first, low, number in zip(firsts, lows, counts)
    ]
    total_shapes = [
        jax.ShapeDtypeStruct(
            (slab // LANES, max(span[0] + bp * NOCC, ceil_to(part[1], C_BLOCK)), LANES),
            jnp.float32,
        )
        for span, part in zip(spans, parts)
    ]

    def work(many, size):
        return 2 * many * size * slab, 2 * many * size + 8 * many * slab

    room = 4 * K_BLOCK * ((C_BLOCK if columns % 16 == 0 else columns) + slab)
    sends = []
    totals = []
    for number, (at, offsets, pieces) in enumerate(jobs):
        size = pieces[0].shape[1]
        deep = ceil_to(size, LANES)
        holder = pltpu.VMEM((slab, deep), jnp.bfloat16)
        turned = jax.ShapeDtypeStruct((deep, slab), jnp.bfloat16)
        pieces_specs = "v" * len(pieces)
        if number + 1 < len(jobs):
            args = (me, *pieces, coupling, edge, *totals)
            totals = local_call(
                functools.partial(start_kernel, offsets, at, parts),
                tuple(total_shapes),
                "s" + pieces_specs + "aa" + "v" * len(totals),
                args,
                [holder, pltpu.VMEM((deep, slab), jnp.bfloat16)],
                {len(args) - len(totals) + i: i for i in range(len(totals))},
                work(columns, size),
                room,
            )
            totals = list(totals)
            continue
        totals[0], turned, send = local_call(
            functools.partial(last_kernel, offsets, at, parts[0], spans[0]),
            (total_shapes[0], turned, send_shape),
            "ss" + pieces_specs + "aav",
            (me, rep, *pieces, coupling, edge, totals[0]),
            [holder],
            {len(pieces) + 4: 0},
            work(parts[0][1], size),
            room,
        )
        sends.append(send)
        for part in range(1, len(spans)):
            totals[part], send = local_call(
                functools.partial(rest_kernel, at, size, parts[part], spans[part]),
                (total_shapes[part], send_shape),
                "svaav",
                (rep, turned, coupling, edge, totals[part]),
                aliases={4: 0},
                cost=work(parts[part][1], size),
                room=room,
            )
            sends.append(send)

    low_pairs = [(i, i ^ 1) for i in range(lax.axis_size("rep"))]
    high_pairs = [(i, i ^ 2) for i in range(lax.axis_size("rep"))]
    pack = LANES // rows_dev
    groups = -(-width // pack)
    shape = (width, bp, slab)
    got = [lax.ppermute(send, "rep", low_pairs) for send in sends]
    sends = [
        local_call(
            functools.partial(second_send_kernel, span),
            jax.ShapeDtypeStruct(shape, jnp.int16),
            "svv",
            (rep, total, mine),
        )
        for span, total, mine in zip(spans, totals, got)
    ]
    kept = [
        local_call(
            functools.partial(keep_kernel, span),
            jax.ShapeDtypeStruct(shape, jnp.float32),
            "svv",
            (rep, total, mine),
        )
        for span, total, mine in zip(spans, totals, got)
    ]
    got = [lax.ppermute(send, "rep", high_pairs) for send in sends]
    arrived = []
    for part, span in enumerate(spans):
        mine = kept[part]
        if part + 1 < len(spans):
            mine, _ = lax.optimization_barrier((mine, sends[part + 1]))
        send = local_call(
            functools.partial(third_send_kernel, span[1], rows_dev),
            jax.ShapeDtypeStruct((grid_size, groups, bp, LANES), jnp.int16),
            "vv",
            (mine, got[part]),
        )
        arrived.append(lax.all_to_all(send, "grid", split_axis=0, concat_axis=0, tiled=True))

    updated = local_call(
        functools.partial(update_kernel, counts, width, rows_dev),
        jax.ShapeDtypeStruct((width, rows_dev, count * grid_size), jnp.float32),
        "ss" + "v" * (len(arrived) + 5),
        (
            occ_energy,
            occ_irrep,
            *arrived,
            jnp.transpose(integrals, (1, 0, 2)),
            row_energy[:, None],
            vir_energy[None, :],
            row_irrep[:, None],
            vir_irrep[None, :],
        ),
        [pltpu.VMEM((count * grid_size, LANES), jnp.float32)],
    )
    return jnp.transpose(updated, (1, 0, 2))


def solution(mesh):
    return jax.shard_map(
        body,
        mesh=mesh,
        in_specs=(
            P("grid", "rep"),
            P("rep", "grid"),
            P("grid", "rep", None),
            P("grid"),
            P("rep"),
            P(),
            P("grid"),
            P("rep"),
            P(),
        ),
        out_specs=P("grid", "rep", None),
        check_vma=False,
    )
```

time: 322 us -> 125 us (0.39)
  waiting for transfers between devices: 249 us -> 40.3 us
  Pallas kernels: 0 us -> 41.7 us
  starting transfers between devices: 5.56 us -> 30.7 us
  matrix products: 24.1 us -> 0 us
  local copies, waits for them, and re-layouts: 25.1 us -> 11.1 us
  between operations: 13.5 us -> 0.24 us
  other arithmetic: 4.21 us -> 0 us
    psum x1 -> x0, waiting for transfers between devices: 151 us -> none  [body(): summed_all = lax.psum(cycle_terms, 'rep')]
    all_gather x1 -> x0, waiting for transfers between devices: 74.3 us -> none  [body(): lax.all_gather(amplitudes, 'grid', axis=0, tiled=True)]
    pallas_call x0 -> x10, Pallas kernels: none -> 41.7 us  [local_call(): pl.pallas_call(kernel, out_shape=out_shape, in_specs=[pl.BlockSpec(memory...]
    ppermute x0 -> x18, waiting for transfers between devices: none -> 32.3 us  [the longest x7 12.8 us: body(): ahead = lax.ppermute(ahead, 'grid', onward)]
    dot_general x1 -> x0, matrix products: 24.1 us -> none  [body(): jnp.dot(lax.all_gather(amplitudes, 'grid', axis=0, tiled=True), coupling,...]
    ppermute x0 -> x18, starting transfers between devices: none -> 19.5 us  [the longest x7 12.4 us: body(): ahead = lax.ppermute(ahead, 'grid', onward)]
    all_to_all x1 -> x2, waiting for transfers between devices: 22.9 us -> 8.04 us  [body(): lax.all_to_all(send, 'grid', split_axis=0, concat_axis=0, tiled=True)]
    reshape x2 -> x0, local copies, waits for them, and re-layouts: 14.1 us -> none  [body(): cycle_terms = cycle_terms.reshape(row_count, vir_local, NOCC)]
  transfers between devices with their start and end apart: 3 -> 20, of which waited for: 3 -> 10; matrix products, arithmetic and copies ran while one was open for 0% -> 4% of each run, Pallas kernels for 0% -> 17%
where the time goes in v3:
time: 125 us; the launch traced here: 124 us
  Pallas kernels  41.7 us (33%)
  waiting for transfers between devices  40.3 us (32%)
  starting transfers between devices  30.7 us (25%)
  local copies, waits for them, and re-layouts  11.1 us (9%)
    pallas_call x10, Pallas kernels, local_call(): pl.pallas_call(kernel, out_shape=out_shape, in_specs=[pl.BlockSpec(memory...  41.7 us
    ppermute x7, waiting for transfers between devices, body(): ahead = lax.ppermute(ahead, 'grid', onward)  12.8 us
    ppermute x7, starting transfers between devices, body(): ahead = lax.ppermute(ahead, 'grid', onward)  12.4 us
    ppermute x2, waiting for transfers between devices, body(): got = [lax.ppermute(send, 'rep', high_pairs) for send in sends]  11.8 us
    all_to_all x2, starting transfers between devices, body(): lax.all_to_all(send, 'grid', split_axis=0, concat_axis=0, tiled=True)  11.1 us
    all_to_all x2, waiting for transfers between devices, body(): lax.all_to_all(send, 'grid', split_axis=0, concat_axis=0, tiled=True)  8.04 us
    ppermute x7, waiting for transfers between devices, body(): behind = lax.ppermute(behind, 'grid', back)  6.38 us
    unnamed x38, local copies, waits for them, and re-layouts  5.47 us
  transfers between devices with their start and end apart: 20, of which 10 were waited for; matrix products, arithmetic and copies ran while one was open for 4% of the time, Pallas kernels for 17%

profile of v3, /device:TPU:0, one launch (start us, length us, event | category | flops | bytes accessed | tf_op | source)
XLA Modules:
  0.0 124.0 jit_solution(8364388059610161684)
XLA Ops:
  1.0 3.1 %collective-permute-start.7 = (bf16[32,3840]{1,0:T(8,128)(2,1)S(1)}, bf16[32,3840]{1,0:T(8,128)(2,1)S(1)}, u32[]{:S(2)}, u32[]{:S(2)}) collective-permute-start(bf16[32,3840]{1,0:T(8,128)(2,1)S(1)} %slice.11.refs_0_), channel_id=1, source_target_pairs={{0,8},{8,16},{16,24},{24,28},{28,20},{20,12},{12,4},{4,0},{1,9},{9... | collective-permute-start | bytes 737288 | tf_op jit(solution)/shard_map/ppermute | solution.py:273
  4.0 5.9 %collective-permute-done.7.refs_1_ = bf16[32,3840]{1,0:T(8,128)(2,1)S(1)} collective-permute-done((bf16[32,3840]{1,0:T(8,128)(2,1)S(1)}, bf16[32,3840]{1,0:T(8,128)(2,1)S(1)}, u32[]{:S(2)}, u32[]{:S(2)}) %collective-permute-start.7) | collective-permute-done | bytes 245792 | tf_op jit(solution)/shard_map/ppermute | solution.py:273
  9.9 1.8 %collective-permute-start.9 = (bf16[32,3840]{1,0:T(8,128)(2,1)S(1)}, bf16[32,3840]{1,0:T(8,128)(2,1)S(1)}, u32[]{:S(2)}, u32[]{:S(2)}) collective-permute-start(bf16[32,3840]{1,0:T(8,128)(2,1)S(1)} %collective-permute-done.7.refs_1_), channel_id=1, source_target_pairs={{0,8},{8,16},{16,24},{24,28},{28,20},{20,12},{12,4},{4,0},{1,9},{9... | collective-permute-start | bytes 737288 | tf_op jit(solution)/shard_map/ppermute | solution.py:273
  13.0 1.7 %collective-permute-start.10 = (bf16[32,3840]{1,0:T(8,128)(2,1)S(1)}, bf16[32,3840]{1,0:T(8,128)(2,1)S(1)}, u32[]{:S(2)}, u32[]{:S(2)}) collective-permute-start(bf16[32,3840]{1,0:T(8,128)(2,1)S(1)} %collective-permute-done.8.refs_2_), channel_id=1, source_target_pairs={{8,0},{16,8},{24,16},{28,24},{20,28},{12,20},{4,12},{0,4},{9,1},{1... | collective-permute-start | bytes 737288 | tf_op jit(solution)/shard_map/ppermute | solution.py:277
  14.7 2.4 %collective-permute-done.9.refs_3_ = bf16[32,3840]{1,0:T(8,128)(2,1)S(1)} collective-permute-done((bf16[32,3840]{1,0:T(8,128)(2,1)S(1)}, bf16[32,3840]{1,0:T(8,128)(2,1)S(1)}, u32[]{:S(2)}, u32[]{:S(2)}) %collective-permute-start.9) | collective-permute-done | bytes 245792 | tf_op jit(solution)/shard_map/ppermute | solution.py:273
  17.1 1.5 %collective-permute-start.11 = (bf16[32,3840]{1,0:T(8,128)(2,1)S(1)}, bf16[32,3840]{1,0:T(8,128)(2,1)S(1)}, u32[]{:S(2)}, u32[]{:S(2)}) collective-permute-start(bf16[32,3840]{1,0:T(8,128)(2,1)S(1)} %collective-permute-done.9.refs_3_), channel_id=1, source_target_pairs={{0,8},{8,16},{16,24},{24,28},{28,20},{20,12},{12,4},{4,0},{1,9},{9... | collective-permute-start | bytes 737288 | tf_op jit(solution)/shard_map/ppermute | solution.py:273
  18.6 1.6 %collective-permute-start = (bf16[32,3660]{1,0:T(8,128)(2,1)S(1)}, bf16[32,3660]{1,0:T(8,128)(2,1)S(1)}, u32[]{:S(2)}, u32[]{:S(2)}) collective-permute-start(bf16[32,3660]{1,0:T(8,128)(2,1)S(1)} %slice.9.refs_0_), channel_id=1, source_target_pairs={{0,8},{8,16},{16,24},{24,28},{28,20},{20,12},{12,4},{4,0},{1,9},{9... | collective-permute-start | bytes 702728 | tf_op jit(solution)/shard_map/ppermute | solution.py:273
  21.7 5.0 %collective-permute-done.10.refs_4_ = bf16[32,3840]{1,0:T(8,128)(2,1)S(1)} collective-permute-done((bf16[32,3840]{1,0:T(8,128)(2,1)S(1)}, bf16[32,3840]{1,0:T(8,128)(2,1)S(1)}, u32[]{:S(2)}, u32[]{:S(2)}) %collective-permute-start.10) | collective-permute-done | bytes 245792 | tf_op jit(solution)/shard_map/ppermute | solution.py:277
  27.0 1.8 %collective-permute-start.13 = (bf16[32,3840]{1,0:T(8,128)(2,1)S(1)}, bf16[32,3840]{1,0:T(8,128)(2,1)S(1)}, u32[]{:S(2)}, u32[]{:S(2)}) collective-permute-start(bf16[32,3840]{1,0:T(8,128)(2,1)S(1)} %collective-permute-done.11.refs_5_), channel_id=1, source_target_pairs={{0,8},{8,16},{16,24},{24,28},{28,20},{20,12},{12,4},{4,0},{1,9},{9... | collective-permute-start | bytes 737288 | tf_op jit(solution)/shard_map/ppermute | solution.py:273
  28.8 2.3 %collective-permute-done.refs_1_ = bf16[32,3660]{1,0:T(8,128)(2,1)S(1)} collective-permute-done((bf16[32,3660]{1,0:T(8,128)(2,1)S(1)}, bf16[32,3660]{1,0:T(8,128)(2,1)S(1)}, u32[]{:S(2)}, u32[]{:S(2)}) %collective-permute-start) | collective-permute-done | bytes 234272 | tf_op jit(solution)/shard_map/ppermute | solution.py:273
  33.1 2.2 %slice.12 = bf16[3600,76]{1,0:T(8,128)(2,1)} slice(bf16[3600,7500]{1,0:T(8,128)(2,1)} %bitcast.12), slice={[0:3600], [7424:7500]} | slice | bytes 1094400 | tf_op jit(solution)/shard_map/slice | solution.py:253
  36.6 2.2 %collective-permute-done.2.refs_3_ = bf16[32,3660]{1,0:T(8,128)(2,1)} collective-permute-done((bf16[32,3660]{1,0:T(8,128)(2,1)S(1)}, bf16[32,3660]{1,0:T(8,128)(2,1)}, u32[]{:S(2)}, u32[]{:S(2)}) %collective-permute-start.2) | collective-permute-done | bytes 234272 | tf_op jit(solution)/shard_map/ppermute | solution.py:273
  45.1 15.9 %start_kernel.1 = (f32[2,1920,128]{2,1,0:T(8,128)S(1)}, f32[2,1924,128]{2,1,0:T(8,128)S(1)}) custom-call(s32[1]{0:T(128)} %bitcast.1.me_ref, bf16[32,3840]{1,0:T(8,128)(2,1)S(1)} %slice.11.refs_0_, bf16[32,3840]{1,0:T(8,128)(2,1)S(1)} %collective-permute-done.7.refs_1_, bf16[32,3840]{1,0:T(8,128)(2,1)S(1)} %collective-permute-done.8.refs_2_, ...), custom_call_target="tpu_custom_call" | custom-call | flops 7077888000 | bytes 35020800 | tf_op jit(solution)/shard_map/start_kernel/pallas_call | solution.py:220
  61.1 10.2 %last_kernel.1 = (f32[2,1920,128]{2,1,0:T(8,128)S(1)}, bf16[3712,256]{1,0:T(8,128)(2,1)S(1)}, s16[2,15,32,256]{3,2,1,0:T(8,128)(2,1)S(1)}) custom-call(s32[1]{0:T(128)} %bitcast.1.me_ref, s32[1]{0:T(128)} %bitcast.rep_ref, bf16[32,3660]{1,0:T(8,128)(2,1)S(1)} %slice.9.refs_0_, bf16[32,3660]{1,0:T(8,128)(2,1)S(1)} %copy-done.10, ...), custom_call_target="tpu_custom_call", output_to_operand_aliasing={{0}: (12, {})} | custom-call | flops 3507978240 | bytes 17536896 | tf_op jit(solution)/shard_map/last_kernel/pallas_call | solution.py:220
  71.3 8.2 %rest_kernel.1 = (f32[2,1924,128]{2,1,0:T(8,128)S(1)}, s16[2,15,32,256]{3,2,1,0:T(8,128)(2,1)S(1)}) custom-call(s32[1]{0:T(128)} %bitcast.rep_ref, bf16[3712,256]{1,0:T(8,128)(2,1)S(1)} %get-tuple-element.16.turned, bf16[3600,7500]{1,0:T(8,128)(2,1)} %bitcast.15, bf16[3600,128]{1,0:T(8,128)(2,1)S(1)} %pad.4.refs_9_.refs_1_, ...), custom_call_target="tpu_custom_call", output_to_operand_aliasing={{0}: (4, {})} | custom-call | flops 3268116480 | bytes 16337792 | tf_op jit(solution)/shard_map/rest_kernel/pallas_call | solution.py:220
  83.7 6.6 %collective-permute-done.17.got_ref = s16[15,32,256]{2,1,0:T(8,128)(2,1)S(1)} collective-permute-done((s16[15,32,256]{2,1,0:T(8,128)(2,1)S(1)}, s16[15,32,256]{2,1,0:T(8,128)(2,1)S(1)}, u32[]{:S(2)}, u32[]{:S(2)}) %collective-permute-start.17) | collective-permute-done | bytes 245792 | tf_op jit(solution)/shard_map/ppermute | solution.py:375
  90.3 1.6 %third_send_kernel.3 = s16[8,4,32,128]{3,2,1,0:T(8,128)(2,1)} custom-call(f32[15,32,256]{2,1,0:T(8,128)S(1)} %keep_kernel.3.kept_ref, s16[15,32,256]{2,1,0:T(8,128)(2,1)S(1)} %collective-permute-done.17.got_ref), custom_call_target="tpu_custom_call" | custom-call | flops 10000000 | bytes 4000000 | tf_op jit(solution)/shard_map/third_send_kernel/pallas_call | solution.py:220
  91.9 5.4 %all-to-all-start.1 = ((s16[8,4,32,128]{3,2,1,0:T(8,128)(2,1)}), s16[8,4,32,128]{3,2,1,0:T(8,128)(2,1)S(1)}, u32[]{:S(2)}, u32[]{:S(2)}) async-start(s16[8,4,32,128]{3,2,1,0:T(8,128)(2,1)} %third_send_kernel.3), calls=%async_computation.1 | async-start | bytes 524288 | tf_op jit(solution)/shard_map/all_to_all | solution.py:387
  98.2 1.6 %collective-permute-start.16 = (s16[15,32,256]{2,1,0:T(8,128)(2,1)S(1)}, s16[15,32,256]{2,1,0:T(8,128)(2,1)S(1)}, u32[]{:S(2)}, u32[]{:S(2)}) collective-permute-start(s16[15,32,256]{2,1,0:T(8,128)(2,1)S(1)} %second_send_kernel.3), channel_id=1, source_target_pairs={{0,2},{1,3},{2,0},{3,1},{4,6},{5,7},{6,4},{7,5},{8,10},{9,11},{10,... | collective-permute-start | bytes 737288 | tf_op jit(solution)/shard_map/ppermute | solution.py:375
  100.0 5.1 %collective-permute-done.16.got_ref = s16[15,32,256]{2,1,0:T(8,128)(2,1)S(1)} collective-permute-done((s16[15,32,256]{2,1,0:T(8,128)(2,1)S(1)}, s16[15,32,256]{2,1,0:T(8,128)(2,1)S(1)}, u32[]{:S(2)}, u32[]{:S(2)}) %collective-permute-start.16) | collective-permute-done | bytes 245792 | tf_op jit(solution)/shard_map/ppermute | solution.py:375
  105.1 1.6 %third_send_kernel.2 = s16[8,4,32,128]{3,2,1,0:T(8,128)(2,1)} custom-call(f32[15,32,256]{2,1,0:T(8,128)S(1)} %keep_kernel.2.kept_ref, s16[15,32,256]{2,1,0:T(8,128)(2,1)S(1)} %collective-permute-done.16.got_ref), custom_call_target="tpu_custom_call" | custom-call | flops 10000000 | bytes 4000000 | tf_op jit(solution)/shard_map/third_send_kernel/pallas_call | solution.py:220
  106.7 5.7 %all-to-all-start = ((s16[8,4,32,128]{3,2,1,0:T(8,128)(2,1)}), s16[8,4,32,128]{3,2,1,0:T(8,128)(2,1)S(1)}, u32[]{:S(2)}, u32[]{:S(2)}) async-start(s16[8,4,32,128]{3,2,1,0:T(8,128)(2,1)} %third_send_kernel.2), calls=%async_computation | async-start | bytes 524288 | tf_op jit(solution)/shard_map/all_to_all | solution.py:387
  112.6 8.0 %all-to-all-done.refs_0_ = s16[8,4,32,128]{3,2,1,0:T(8,128)(2,1)S(1)} async-done(((s16[8,4,32,128]{3,2,1,0:T(8,128)(2,1)}), s16[8,4,32,128]{3,2,1,0:T(8,128)(2,1)S(1)}, u32[]{:S(2)}, u32[]{:S(2)}) %all-to-all-start) | async-done | bytes 262176 | tf_op jit(solution)/shard_map/all_to_all | solution.py:387
  121.8 2.1 %update_kernel.1 = f32[15,32,480]{2,1,0:T(8,128)} custom-call(f32[15]{0:T(128)S(1)} %copy-done.15, s32[15]{0:T(128)S(1)} %copy-done.16, s16[8,4,32,128]{3,2,1,0:T(8,128)(2,1)S(1)} %all-to-all-done.refs_0_, s16[8,4,32,128]{3,2,1,0:T(8,128)(2,1)S(1)} %all-to-all-done.1.refs_1_, f32[15,32,480]{2,1,0:T(8,128)S(1)} %bitcast.9, f32[32,1]{1,0:T(8,128)S(1)} %copy.12.refs_3_, ...), custom_call_target="tpu_custom_call" | custom-call | flops 10000000 | bytes 4000000 | tf_op jit(solution)/shard_map/update_kernel/pallas_call | solution.py:220
  (70 shorter events, 20.2 us)
Async XLA Ops:
  1.0 9.0 %collective-permute-start.7 = (bf16[32,3840]{1,0:T(8,128)(2,1)S(1)}, bf16[32,3840]{1,0:T(8,128)(2,1)S(1)}, u32[]{:S(2)}, u32[]{:S(2)}) collective-permute-start(bf16[32,3840]{1,0:T(8,128)(2,1)S(1)} %slice.11.refs_0_), channel_id=1, source_target_pairs={{0,8},{8,16},{16,24},{24,28},{28,20},{20,12},{12,4},{4,0},{1,9},{9... | collective-permute-start | bytes 737288 | tf_op jit(solution)/shard_map/ppermute | solution.py:273
  4.0 8.9 %collective-permute-start.8 = (bf16[32,3840]{1,0:T(8,128)(2,1)S(1)}, bf16[32,3840]{1,0:T(8,128)(2,1)S(1)}, u32[]{:S(2)}, u32[]{:S(2)}) collective-permute-start(bf16[32,3840]{1,0:T(8,128)(2,1)S(1)} %slice.11.refs_0_), channel_id=1, source_target_pairs={{8,0},{16,8},{24,16},{28,24},{20,28},{12,20},{4,12},{0,4},{9,1},{1... | collective-permute-start | bytes 737288 | tf_op jit(solution)/shard_map/ppermute | solution.py:277
  9.9 7.1 %collective-permute-start.9 = (bf16[32,3840]{1,0:T(8,128)(2,1)S(1)}, bf16[32,3840]{1,0:T(8,128)(2,1)S(1)}, u32[]{:S(2)}, u32[]{:S(2)}) collective-permute-start(bf16[32,3840]{1,0:T(8,128)(2,1)S(1)} %collective-permute-done.7.refs_1_), channel_id=1, source_target_pairs={{0,8},{8,16},{16,24},{24,28},{28,20},{20,12},{12,4},{4,0},{1,9},{9... | collective-permute-start | bytes 737288 | tf_op jit(solution)/shard_map/ppermute | solution.py:273
  12.7 8.8 %collective-permute-start.1 = (bf16[32,3660]{1,0:T(8,128)(2,1)S(1)}, bf16[32,3660]{1,0:T(8,128)(2,1)S(1)}, u32[]{:S(2)}, u32[]{:S(2)}) collective-permute-start(bf16[32,3660]{1,0:T(8,128)(2,1)S(1)} %slice.9.refs_0_), channel_id=1, source_target_pairs={{8,0},{16,8},{24,16},{28,24},{20,28},{12,20},{4,12},{0,4},{9,1},{1... | collective-permute-start | bytes 702728 | tf_op jit(solution)/shard_map/ppermute | solution.py:277
  13.0 13.7 %collective-permute-start.10 = (bf16[32,3840]{1,0:T(8,128)(2,1)S(1)}, bf16[32,3840]{1,0:T(8,128)(2,1)S(1)}, u32[]{:S(2)}, u32[]{:S(2)}) collective-permute-start(bf16[32,3840]{1,0:T(8,128)(2,1)S(1)} %collective-permute-done.8.refs_2_), channel_id=1, source_target_pairs={{8,0},{16,8},{24,16},{28,24},{20,28},{12,20},{4,12},{0,4},{9,1},{1... | collective-permute-start | bytes 737288 | tf_op jit(solution)/shard_map/ppermute | solution.py:277
  17.1 9.9 %collective-permute-start.11 = (bf16[32,3840]{1,0:T(8,128)(2,1)S(1)}, bf16[32,3840]{1,0:T(8,128)(2,1)S(1)}, u32[]{:S(2)}, u32[]{:S(2)}) collective-permute-start(bf16[32,3840]{1,0:T(8,128)(2,1)S(1)} %collective-permute-done.9.refs_3_), channel_id=1, source_target_pairs={{0,8},{8,16},{16,24},{24,28},{28,20},{20,12},{12,4},{4,0},{1,9},{9... | collective-permute-start | bytes 737288 | tf_op jit(solution)/shard_map/ppermute | solution.py:273
  18.6 12.5 %collective-permute-start = (bf16[32,3660]{1,0:T(8,128)(2,1)S(1)}, bf16[32,3660]{1,0:T(8,128)(2,1)S(1)}, u32[]{:S(2)}, u32[]{:S(2)}) collective-permute-start(bf16[32,3660]{1,0:T(8,128)(2,1)S(1)} %slice.9.refs_0_), channel_id=1, source_target_pairs={{0,8},{8,16},{16,24},{24,28},{28,20},{20,12},{12,4},{4,0},{1,9},{9... | collective-permute-start | bytes 702728 | tf_op jit(solution)/shard_map/ppermute | solution.py:273
  21.5 11.1 %collective-permute-start.3 = (bf16[32,3660]{1,0:T(8,128)(2,1)S(1)}, bf16[32,3660]{1,0:T(8,128)(2,1)S(1)}, u32[]{:S(2)}, u32[]{:S(2)}) collective-permute-start(bf16[32,3660]{1,0:T(8,128)(2,1)S(1)} %collective-permute-done.1.refs_2_), channel_id=1, source_target_pairs={{8,0},{16,8},{24,16},{28,24},{20,28},{12,20},{4,12},{0,4},{9,1},{1... | collective-permute-start | bytes 702728 | tf_op jit(solution)/shard_map/ppermute | solution.py:277
  26.7 14.2 %collective-permute-start.12 = (bf16[32,3840]{1,0:T(8,128)(2,1)S(1)}, bf16[32,3840]{1,0:T(8,128)(2,1)S(1)}, u32[]{:S(2)}, u32[]{:S(2)}) collective-permute-start(bf16[32,3840]{1,0:T(8,128)(2,1)S(1)} %collective-permute-done.10.refs_4_), channel_id=1, source_target_pairs={{8,0},{16,8},{24,16},{28,24},{20,28},{12,20},{4,12},{0,4},{9,1},{1... | collective-permute-start | bytes 737288 | tf_op jit(solution)/shard_map/ppermute | solution.py:277
  27.0 14.6 %collective-permute-start.13 = (bf16[32,3840]{1,0:T(8,128)(2,1)S(1)}, bf16[32,3840]{1,0:T(8,128)(2,1)S(1)}, u32[]{:S(2)}, u32[]{:S(2)}) collective-permute-start(bf16[32,3840]{1,0:T(8,128)(2,1)S(1)} %collective-permute-done.11.refs_5_), channel_id=1, source_target_pairs={{0,8},{8,16},{16,24},{24,28},{28,20},{20,12},{12,4},{4,0},{1,9},{9... | collective-permute-start | bytes 737288 | tf_op jit(solution)/shard_map/ppermute | solution.py:273
  31.1 7.8 %collective-permute-start.2 = (bf16[32,3660]{1,0:T(8,128)(2,1)S(1)}, bf16[32,3660]{1,0:T(8,128)(2,1)}, u32[]{:S(2)}, u32[]{:S(2)}) collective-permute-start(bf16[32,3660]{1,0:T(8,128)(2,1)S(1)} %collective-permute-done.refs_1_), channel_id=1, source_target_pairs={{0,8},{8,16},{16,24},{24,28},{28,20},{20,12},{12,4},{4,0},{1,9},{9... | collective-permute-start | bytes 702728 | tf_op jit(solution)/shard_map/ppermute | solution.py:273
  32.5 7.5 %collective-permute-start.5 = (bf16[32,3660]{1,0:T(8,128)(2,1)S(1)}, bf16[32,3660]{1,0:T(8,128)(2,1)}, u32[]{:S(2)}, u32[]{:S(2)}) collective-permute-start(bf16[32,3660]{1,0:T(8,128)(2,1)S(1)} %collective-permute-done.3.refs_4_), channel_id=1, source_target_pairs={{8,0},{16,8},{24,16},{28,24},{20,28},{12,20},{4,12},{0,4},{9,1},{1... | collective-permute-start | bytes 702728 | tf_op jit(solution)/shard_map/ppermute | solution.py:277
  38.9 22.2 %collective-permute-start.4 = (bf16[32,3660]{1,0:T(8,128)(2,1)}, bf16[32,3660]{1,0:T(8,128)(2,1)S(1)}, u32[]{:S(2)}, u32[]{:S(2)}) collective-permute-start(bf16[32,3660]{1,0:T(8,128)(2,1)} %collective-permute-done.2.refs_3_), channel_id=1, source_target_pairs={{0,8},{8,16},{16,24},{24,28},{28,20},{20,12},{12,4},{4,0},{1,9},{9... | collective-permute-start | bytes 702728 | tf_op jit(solution)/shard_map/ppermute | solution.py:273
  40.0 21.0 %collective-permute-start.6 = (bf16[32,3660]{1,0:T(8,128)(2,1)}, bf16[32,3660]{1,0:T(8,128)(2,1)S(1)}, u32[]{:S(2)}, u32[]{:S(2)}) collective-permute-start(bf16[32,3660]{1,0:T(8,128)(2,1)} %collective-permute-done.5.refs_6_), channel_id=1, source_target_pairs={{8,0},{16,8},{24,16},{28,24},{20,28},{12,20},{4,12},{0,4},{9,1},{1... | collective-permute-start | bytes 702728 | tf_op jit(solution)/shard_map/ppermute | solution.py:277
  79.5 1.9 %collective-permute-start.15 = (s16[2,15,32,256]{3,2,1,0:T(8,128)(2,1)S(1)}, s16[2,15,32,256]{3,2,1,0:T(8,128)(2,1)S(1)}, u32[]{:S(2)}, u32[]{:S(2)}) collective-permute-start(s16[2,15,32,256]{3,2,1,0:T(8,128)(2,1)S(1)} %get-tuple-element.19), channel_id=1, source_target_pairs={{0,1},{1,0},{2,3},{3,2},{4,5},{5,4},{6,7},{7,6},{8,9},{9,8},{10,11... | collective-permute-start | bytes 1474568 | tf_op jit(solution)/shard_map/ppermute | solution.py:356
  79.6 17.7 %collective-permute-start.14 = (s16[2,15,32,256]{3,2,1,0:T(8,128)(2,1)S(1)}, s16[2,15,32,256]{3,2,1,0:T(8,128)(2,1)S(1)}, u32[]{:S(2)}, u32[]{:S(2)}) collective-permute-start(s16[2,15,32,256]{3,2,1,0:T(8,128)(2,1)S(1)} %get-tuple-element.15), channel_id=1, source_target_pairs={{0,1},{1,0},{2,3},{3,2},{4,5},{5,4},{6,7},{7,6},{8,9},{9,8},{10,11... | collective-permute-start | bytes 1474568 | tf_op jit(solution)/shard_map/ppermute | solution.py:356
  82.2 8.1 %collective-permute-start.17 = (s16[15,32,256]{2,1,0:T(8,128)(2,1)S(1)}, s16[15,32,256]{2,1,0:T(8,128)(2,1)S(1)}, u32[]{:S(2)}, u32[]{:S(2)}) collective-permute-start(s16[15,32,256]{2,1,0:T(8,128)(2,1)S(1)} %second_send_kernel.2), channel_id=1, source_target_pairs={{0,2},{1,3},{2,0},{3,1},{4,6},{5,7},{6,4},{7,5},{8,10},{9,11},{10,... | collective-permute-start | bytes 737288 | tf_op jit(solution)/shard_map/ppermute | solution.py:375
  91.9 14.8 %all-to-all-start.1 = ((s16[8,4,32,128]{3,2,1,0:T(8,128)(2,1)}), s16[8,4,32,128]{3,2,1,0:T(8,128)(2,1)S(1)}, u32[]{:S(2)}, u32[]{:S(2)}) async-start(s16[8,4,32,128]{3,2,1,0:T(8,128)(2,1)} %third_send_kernel.3), calls=%async_computation.1 | async-start | bytes 524288 | tf_op jit(solution)/shard_map/all_to_all | solution.py:387
  98.1 22.5 %copy-start.13 = (f32[480]{0:T(512)S(1)}, f32[480]{0:T(512)}, u32[]{:S(2)}) copy-start(f32[480]{0:T(512)} %param.14) | copy-start | bytes 5764
  98.1 22.5 %copy-start.14 = (s32[480]{0:T(512)S(1)}, s32[480]{0:T(512)}, u32[]{:S(2)}) copy-start(s32[480]{0:T(512)} %param.17) | copy-start | bytes 5764
  98.1 22.5 %copy-start.15 = (f32[15]{0:T(128)S(1)}, f32[15]{0:T(128)}, u32[]{:S(2)}) copy-start(f32[15]{0:T(128)} %occ_energy_ref.1) | copy-start | bytes 184
  98.2 22.5 %copy-start.16 = (s32[15]{0:T(128)S(1)}, s32[15]{0:T(128)}, u32[]{:S(2)}) copy-start(s32[15]{0:T(128)} %occ_irrep_ref.1) | copy-start | bytes 184
  98.2 7.0 %collective-permute-start.16 = (s16[15,32,256]{2,1,0:T(8,128)(2,1)S(1)}, s16[15,32,256]{2,1,0:T(8,128)(2,1)S(1)}, u32[]{:S(2)}, u32[]{:S(2)}) collective-permute-start(s16[15,32,256]{2,1,0:T(8,128)(2,1)S(1)} %second_send_kernel.3), channel_id=1, source_target_pairs={{0,2},{1,3},{2,0},{3,1},{4,6},{5,7},{6,4},{7,5},{8,10},{9,11},{10,... | collective-permute-start | bytes 737288 | tf_op jit(solution)/shard_map/ppermute | solution.py:375
  106.7 13.9 %all-to-all-start = ((s16[8,4,32,128]{3,2,1,0:T(8,128)(2,1)}), s16[8,4,32,128]{3,2,1,0:T(8,128)(2,1)S(1)}, u32[]{:S(2)}, u32[]{:S(2)}) async-start(s16[8,4,32,128]{3,2,1,0:T(8,128)(2,1)} %third_send_kernel.2), calls=%async_computation | async-start | bytes 524288 | tf_op jit(solution)/shard_map/all_to_all | solution.py:387
  (15 other events, 136.3 us)

commit v4 on v3

--- a/solution.py
+++ b/solution.py
@@ -11,6 +11,7 @@
 LANES = 128
 K_BLOCK = 3840
 C_BLOCK = 480
+SPLIT = 4
 B_ROWS = 32
 STEPS = 8.0
 TOP = 32767.0
@@ -52,34 +53,46 @@
     return jnp.where(index % 2 == 0, index // 2, size - 1 - index // 2)
 
 
-def gather_pieces(me_ref, offsets, pieces, gathered, turned):
+def gather_pieces(me_ref, offsets, pieces, gathered, turned, sems):
     blocks = len(offsets)
-    rows, width = pieces[0].shape
+    rows = pieces[0].shape[0]
     place = walk_place(me_ref[0], blocks)
-    for offset, piece in zip(offsets, pieces):
+    copies = []
+    for number, (offset, piece) in enumerate(zip(offsets, pieces)):
         source = walk_index(lax.rem(place + offset + blocks, blocks), blocks)
         at = pl.multiple_of(source * rows, rows)
-        gathered[pl.ds(at, rows), :width] = piece[...]
+        copies.append(
+            pltpu.make_async_copy(piece, gathered.at[pl.ds(at, rows), :], sems.at[number])
+        )
+    for copy in copies:
+        copy.start()
+    for copy in copies:
+        copy.wait()
     for at in range(0, turned.shape[0], LANES):
-        tile = gathered[:, at : at + LANES].T
-        if at + LANES > width:
-            index = lax.broadcasted_iota(jnp.int32, tile.shape, 0)
-            tile = jnp.where(index < width - at, tile, jnp.zeros_like(tile))
-        turned[at : at + LANES, :] = tile
-
-
-def add_products(coupling_ref, edge_ref, at, width, turned, total_in, total_out, columns):
+        turned[at : at + LANES, :] = gathered[:, at : at + LANES].T
+
+
+def add_products(coupling_ref, edge_ref, at, whole, turned, total_in, total_out, columns):
     all_columns = coupling_ref.shape[0]
     block = C_BLOCK if all_columns % 16 == 0 else all_columns
     low, many = columns
-    whole = width // LANES * LANES
+    deep = turned.shape[0]
+    quarter = ceil_to(-(-whole // SPLIT), 256)
 
     def step(coupling_block, edge_block=None):
-        total = jnp.dot(coupling_block[...], turned[:whole, :], preferred_element_type=jnp.float32)
-        if whole < width:
-            total += jnp.dot(
-                edge_block[...], turned[whole:, :], preferred_element_type=jnp.float32
+        terms = [
+            jnp.dot(
+                coupling_block[:, k : min(k + quarter, whole)],
+                turned[k : min(k + quarter, whole), :],
+                preferred_element_type=jnp.float32,
             )
+            for k in range(0, whole, quarter)
+        ]
+        if whole < deep:
+            terms.append(
+                jnp.dot(edge_block[...], turned[whole:, :], preferred_element_type=jnp.float32)
+            )
+        total = sum(terms[1:], terms[0])
         rows = pl.ds(pl.program_id(0) * block, block)
         for part in range(total_out.shape[0]):
             own = total[:, part * LANES : (part + 1) * LANES]
@@ -88,37 +101,30 @@
     index_map = lambda i: (i, 0)
     specs = [pl.BlockSpec((block, whole), index_map)]
     args = [coupling_ref.at[low : low + many, at : at + whole]]
-    if whole < width:
+    if whole < deep:
         specs.append(pl.BlockSpec((block, LANES), index_map))
         args.append(edge_ref.at[low : low + many])
     pltpu.emit_pipeline(step, grid=(pl.cdiv(many, block),), in_specs=specs)(*args)
 
 
-def start_kernel(offsets, at, columns, me_ref, *refs):
-    pieces, refs = refs[: len(offsets)], refs[len(offsets) :]
+def lead_kernel(offsets, at, whole, columns, span, begin, me_ref, rep_ref, *refs):
+    pieces, refs = refs[: len(offsets)], list(refs[len(offsets) :])
     coupling_ref, edge_ref = refs[:2]
-    totals, (gathered, turned) = refs[2:-2], refs[-2:]
-    gather_pieces(me_ref, offsets, pieces, gathered, turned)
-    width = pieces[0].shape[1]
-    outs = totals[-len(columns) :]
-    ins = totals[: -len(columns)] or [None] * len(columns)
-    for span, total_in, total_out in zip(columns, ins, outs):
-        add_products(coupling_ref, edge_ref, at, width, turned, total_in, total_out, span)
-
-
-def last_kernel(offsets, at, columns, span, me_ref, rep_ref, *refs):
-    pieces = refs[: len(offsets)]
-    coupling_ref, edge_ref, total_in, total_out, turned, send_ref, gathered = refs[len(offsets) :]
-    gather_pieces(me_ref, offsets, pieces, gathered, turned)
-    width = pieces[0].shape[1]
-    add_products(coupling_ref, edge_ref, at, width, turned, total_in, total_out, columns)
-    first_send(span, rep_ref, total_out, send_ref)
-
-
-def rest_kernel(at, width, columns, span, rep_ref, turned, *refs):
-    coupling_ref, edge_ref, total_in, total_out, send = refs
-    add_products(coupling_ref, edge_ref, at, width, turned, total_in, total_out, columns)
-    first_send(span, rep_ref, total_out, send)
+    gathered, sems = refs[-2:]
+    total_in = None if begin else refs[2]
+    total_out, turned, *send = refs[2 if begin else 3 : -2]
+    gather_pieces(me_ref, offsets, pieces, gathered, turned, sems)
+    add_products(coupling_ref, edge_ref, at, whole, turned, total_in, total_out, columns)
+    if span is not None:
+        first_send(span, rep_ref, total_out, *send)
+
+
+def rest_kernel(at, whole, columns, span, begin, rep_ref, turned, coupling_ref, edge_ref, *refs):
+    total_in = None if begin else refs[0]
+    total_out, *send = refs[0 if begin else 1 :]
+    add_products(coupling_ref, edge_ref, at, whole, turned, total_in, total_out, columns)
+    if span is not None:
+        first_send(span, rep_ref, total_out, *send)
 
 
 def column_rows(total_ref, width, part, j, offset, bp):
@@ -261,9 +267,14 @@
 
     longer = grid_size // 2
     jobs = []
+    halfway = None
     for number, at in enumerate(range(0, depth, K_BLOCK)):
         own = amplitudes[:, at : at + K_BLOCK]
-        pieces, offsets = [own], [0]
+        size = own.shape[1]
+        own = jnp.pad(own, ((0, 0), (0, ceil_to(size, LANES) - size)))
+        if halfway is not None:
+            own, *_ = lax.optimization_barrier((own, *halfway))
+        pieces, offsets, hop_ends = [own], [0], []
         hops = (longer, grid_size - 1 - longer)
         if number % 2:
             hops = hops[::-1]
@@ -277,7 +288,9 @@
                 behind = lax.ppermute(behind, "grid", back)
                 pieces.append(behind)
                 offsets.append(hop)
-        jobs.append((at, tuple(offsets), pieces))
+            hop_ends.append((ahead, behind))
+        halfway = hop_ends[longer // 2 - 1]
+        jobs.append((at, size // LANES * LANES, tuple(offsets), pieces, hop_ends))
 
     firsts = list(range(0, count, B_ROWS - 1))
     counts = [min(B_ROWS - 1, count - first) for first in firsts]
@@ -304,49 +317,51 @@
 
     room = 4 * K_BLOCK * ((C_BLOCK if columns % 16 == 0 else columns) + slab)
     sends = []
-    totals = []
-    for number, (at, offsets, pieces) in enumerate(jobs):
-        size = pieces[0].shape[1]
-        deep = ceil_to(size, LANES)
-        holder = pltpu.VMEM((slab, deep), jnp.bfloat16)
-        turned = jax.ShapeDtypeStruct((deep, slab), jnp.bfloat16)
-        pieces_specs = "v" * len(pieces)
-        if number + 1 < len(jobs):
-            args = (me, *pieces, coupling, edge, *totals)
-            totals = local_call(
-                functools.partial(start_kernel, offsets, at, parts),
-                tuple(total_shapes),
-                "s" + pieces_specs + "aa" + "v" * len(totals),
-                args,
-                [holder, pltpu.VMEM((deep, slab), jnp.bfloat16)],
-                {len(args) - len(totals) + i: i for i in range(len(totals))},
-                work(columns, size),
-                room,
-            )
-            totals = list(totals)
-            continue
-        totals[0], turned, send = local_call(
-            functools.partial(last_kernel, offsets, at, parts[0], spans[0]),
-            (total_shapes[0], turned, send_shape),
-            "ss" + pieces_specs + "aav",
-            (me, rep, *pieces, coupling, edge, totals[0]),
-            [holder],
-            {len(pieces) + 4: 0},
-            work(parts[0][1], size),
-            room,
-        )
-        sends.append(send)
-        for part in range(1, len(spans)):
-            totals[part], send = local_call(
-                functools.partial(rest_kernel, at, size, parts[part], spans[part]),
-                (total_shapes[part], send_shape),
-                "svaav",
-                (rep, turned, coupling, edge, totals[part]),
-                aliases={4: 0},
-                cost=work(parts[part][1], size),
-                room=room,
-            )
-            sends.append(send)
+    totals = [()] * len(parts)
+    for number, (at, whole, offsets, pieces, _) in enumerate(jobs):
+        begin, last = number == 0, number + 1 == len(jobs)
+        deep = pieces[0].shape[1]
+        turned_shape = jax.ShapeDtypeStruct((deep, slab), jnp.bfloat16)
+        scratch = [
+            pltpu.VMEM((slab, deep), jnp.bfloat16),
+            pltpu.SemaphoreType.DMA((len(pieces),)),
+        ]
+        if not last:
+            ends = jobs[number + 1][4][longer // 2 - 1 :]
+            pieces = lax.optimization_barrier((*pieces, *ends[0]))[: len(pieces)]
+        for part, cols in enumerate(parts):
+            span = spans[part] if last else None
+            extra = (send_shape,) if last else ()
+            cost = work(cols[1], deep)
+            if part == 0:
+                args = (me, rep, *pieces, coupling, edge, *totals[part])
+                total, turned, *send = local_call(
+                    functools.partial(lead_kernel, offsets, at, whole, cols, span, begin),
+                    (total_shapes[part], turned_shape, *extra),
+                    "ss" + "a" * (len(pieces) + 2) + "v" * len(totals[part]),
+                    args,
+                    scratch,
+                    {} if begin else {len(args) - 1: 0},
+                    cost,
+                    room,
+                )
+            else:
+                if not last:
+                    turned, *_ = lax.optimization_barrier((turned, *ends[min(part, 1)]))
+                args = (rep, turned, coupling, edge, *totals[part])
+                total, *send = local_call(
+                    functools.partial(rest_kernel, at, whole, cols, span, begin),
+                    (total_shapes[part], *extra),
+                    "svaa" + "v" * len(totals[part]),
+                    args,
+                    (),
+                    {} if begin else {len(args) - 1: 0},
+                    cost,
+                    room,
+                )
+            totals[part] = (total,)
+            sends.extend(send)
+    totals = [total for total, in totals]
 
     low_pairs = [(i, i ^ 1) for i in range(lax.axis_size("rep"))]
     high_pairs = [(i, i ^ 2) for i in range(lax.axis_size("rep"))]
@@ -354,28 +369,34 @@
     groups = -(-width // pack)
     shape = (width, bp, slab)
     got = [lax.ppermute(send, "rep", low_pairs) for send in sends]
-    sends = [
-        local_call(
-            functools.partial(second_send_kernel, span),
-            jax.ShapeDtypeStruct(shape, jnp.int16),
-            "svv",
-            (rep, total, mine),
+    sends, kept = [], []
+    for span, total, mine in zip(spans, totals, got):
+        if sends:
+            mine, _ = lax.optimization_barrier((mine, sends[-1]))
+        args = (rep, total, mine)
+        sends.append(
+            local_call(
+                functools.partial(second_send_kernel, span),
+                jax.ShapeDtypeStruct(shape, jnp.int16),
+                "svv",
+                args,
+            )
         )
-        for span, total, mine in zip(spans, totals, got)
-    ]
-    kept = [
-        local_call(
-            functools.partial(keep_kernel, span),
-            jax.ShapeDtypeStruct(shape, jnp.float32),
-            "svv",
-            (rep, total, mine),
+        kept.append(
+            local_call(
+                functools.partial(keep_kernel, span),
+                jax.ShapeDtypeStruct(shape, jnp.float32),
+                "svv",
+                args,
+            )
         )
-        for span, total, mine in zip(spans, totals, got)
-    ]
     got = [lax.ppermute(send, "rep", high_pairs) for send in sends]
     arrived = []
+    send = None
     for part, span in enumerate(spans):
         mine = kept[part]
+        if send is not None:
+            mine, _ = lax.optimization_barrier((mine, send))
         if part + 1 < len(spans):
             mine, _ = lax.optimization_barrier((mine, sends[part + 1]))
         send = local_call(

time: 125 us -> 122 us (0.976)
  blocking collectives: 0 us -> 13.6 us
  starting transfers between devices: 30.7 us -> 21.6 us
  local copies, waits for them, and re-layouts: 11.1 us -> 3.58 us
  Pallas kernels: 41.7 us -> 44.1 us
  waiting for transfers between devices: 40.3 us -> 38.6 us
    all_to_all x0 -> x1, blocking collectives: none -> 13.6 us  [body(): lax.all_to_all(send, 'grid', split_axis=0, concat_axis=0, tiled=True)]
    all_to_all x2 -> x1, starting transfers between devices: 11.1 us -> 3.44 us  [body(): lax.all_to_all(send, 'grid', split_axis=0, concat_axis=0, tiled=True)]
    ppermute x7, waiting for transfers between devices: 12.8 us -> 19.6 us  [body(): ahead = lax.ppermute(ahead, 'grid', onward)]
    unnamed x38 -> x14, local copies, waits for them, and re-layouts: 5.47 us -> 0.04 us
    ppermute x7, waiting for transfers between devices: 6.38 us -> 2.61 us  [body(): behind = lax.ppermute(behind, 'grid', back)]
    ppermute x2, waiting for transfers between devices: 11.8 us -> 8.06 us  [body(): got = [lax.ppermute(send, 'rep', high_pairs) for send in sends]]
    pallas_call x10 -> x11, Pallas kernels: 41.7 us -> 44.1 us  [local_call(): pl.pallas_call(kernel, out_shape=out_shape, in_specs=[pl.BlockSpec(memory...]
    ppermute x2, waiting for transfers between devices: 1.36 us -> 0.01 us  [body(): got = [lax.ppermute(send, 'rep', low_pairs) for send in sends]]
  transfers between devices with their start and end apart: 20 -> 19, of which waited for: 10 -> 10; matrix products, arithmetic and copies ran while one was open for 4% -> 2% of each run, Pallas kernels for 17% -> 25%
where the time goes in v4:
time: 122 us
  Pallas kernels  44.1 us (36%)
  waiting for transfers between devices  38.6 us (32%)
  starting transfers between devices  21.6 us (18%)
  blocking collectives  13.6 us (11%)
  local copies, waits for them, and re-layouts  3.58 us (3%)
    pallas_call x11, Pallas kernels, local_call(): pl.pallas_call(kernel, out_shape=out_shape, in_specs=[pl.BlockSpec(memory...  44.1 us
    ppermute x7, waiting for transfers between devices, body(): ahead = lax.ppermute(ahead, 'grid', onward)  19.6 us
    all_to_all x1, blocking collectives, body(): lax.all_to_all(send, 'grid', split_axis=0, concat_axis=0, tiled=True)  13.6 us
    ppermute x7, starting transfers between devices, body(): ahead = lax.ppermute(ahead, 'grid', onward)  11.9 us
    all_to_all x1, waiting for transfers between devices, body(): lax.all_to_all(send, 'grid', split_axis=0, concat_axis=0, tiled=True)  8.34 us
    ppermute x2, waiting for transfers between devices, body(): got = [lax.ppermute(send, 'rep', high_pairs) for send in sends]  8.06 us
    all_to_all x1, starting transfers between devices, body(): lax.all_to_all(send, 'grid', split_axis=0, concat_axis=0, tiled=True)  3.44 us
    ppermute x7, starting transfers between devices, body(): behind = lax.ppermute(behind, 'grid', back)  3.43 us
  transfers between devices with their start and end apart: 19, of which 10 were waited for; matrix products, arithmetic and copies ran while one was open for 2% of the time, Pallas kernels for 25%

profile of v4, /device:TPU:0, one launch (start us, length us, event | category | flops | bytes accessed | tf_op | source)
XLA Modules:
  0.0 121.7 jit_solution(16630217698375064712)
XLA Ops:
  1.0 3.1 %collective-permute-start = (bf16[32,3840]{1,0:T(8,128)(2,1)S(1)}, bf16[32,3840]{1,0:T(8,128)(2,1)S(1)}, u32[]{:S(2)}, u32[]{:S(2)}) collective-permute-start(bf16[32,3840]{1,0:T(8,128)(2,1)S(1)} %slice.10.refs_0_), channel_id=1, source_target_pairs={{0,8},{8,16},{16,24},{24,28},{28,20},{20,12},{12,4},{4,0},{1,9},{9... | collective-permute-start | bytes 737288 | tf_op jit(solution)/shard_map/ppermute | solution.py:284
  4.0 5.9 %collective-permute-done.refs_1_ = bf16[32,3840]{1,0:T(8,128)(2,1)S(1)} collective-permute-done((bf16[32,3840]{1,0:T(8,128)(2,1)S(1)}, bf16[32,3840]{1,0:T(8,128)(2,1)S(1)}, u32[]{:S(2)}, u32[]{:S(2)}) %collective-permute-start) | collective-permute-done | bytes 245792 | tf_op jit(solution)/shard_map/ppermute | solution.py:284
  9.9 1.8 %collective-permute-start.1 = (bf16[32,3840]{1,0:T(8,128)(2,1)S(1)}, bf16[32,3840]{1,0:T(8,128)(2,1)S(1)}, u32[]{:S(2)}, u32[]{:S(2)}) collective-permute-start(bf16[32,3840]{1,0:T(8,128)(2,1)S(1)} %collective-permute-done.refs_1_), channel_id=1, source_target_pairs={{0,8},{8,16},{16,24},{24,28},{28,20},{20,12},{12,4},{4,0},{1,9},{9... | collective-permute-start | bytes 737288 | tf_op jit(solution)/shard_map/ppermute | solution.py:284
  12.0 5.1 %collective-permute-done.1.refs_3_ = bf16[32,3840]{1,0:T(8,128)(2,1)S(1)} collective-permute-done((bf16[32,3840]{1,0:T(8,128)(2,1)S(1)}, bf16[32,3840]{1,0:T(8,128)(2,1)S(1)}, u32[]{:S(2)}, u32[]{:S(2)}) %collective-permute-start.1) | collective-permute-done | bytes 245792 | tf_op jit(solution)/shard_map/ppermute | solution.py:284
  17.1 1.5 %collective-permute-start.11 = (bf16[32,3840]{1,0:T(8,128)(2,1)S(1)}, bf16[32,3840]{1,0:T(8,128)(2,1)S(1)}, u32[]{:S(2)}, u32[]{:S(2)}) collective-permute-start(bf16[32,3840]{1,0:T(8,128)(2,1)S(1)} %collective-permute-done.1.refs_3_), channel_id=1, source_target_pairs={{0,8},{8,16},{16,24},{24,28},{28,20},{20,12},{12,4},{4,0},{1,9},{9... | collective-permute-start | bytes 737288 | tf_op jit(solution)/shard_map/ppermute | solution.py:284
  20.2 1.5 %collective-permute-start.4 = (bf16[32,3712]{1,0:T(8,128)(2,1)S(1)}, bf16[32,3712]{1,0:T(8,128)(2,1)}, u32[]{:S(2)}, u32[]{:S(2)}) collective-permute-start(bf16[32,3712]{1,0:T(8,128)(2,1)S(1)} %pad.8.refs_0_), channel_id=1, source_target_pairs={{0,8},{8,16},{16,24},{24,28},{28,20},{20,12},{12,4},{4,0},{1,9},{9... | collective-permute-start | bytes 712712 | tf_op jit(solution)/shard_map/ppermute | solution.py:284
  22.2 3.8 %collective-permute-done.11.refs_5_ = bf16[32,3840]{1,0:T(8,128)(2,1)S(1)} collective-permute-done((bf16[32,3840]{1,0:T(8,128)(2,1)S(1)}, bf16[32,3840]{1,0:T(8,128)(2,1)S(1)}, u32[]{:S(2)}, u32[]{:S(2)}) %collective-permute-start.11) | collective-permute-done | bytes 245792 | tf_op jit(solution)/shard_map/ppermute | solution.py:284
  26.0 1.5 %collective-permute-start.13 = (bf16[32,3840]{1,0:T(8,128)(2,1)S(1)}, bf16[32,3840]{1,0:T(8,128)(2,1)S(1)}, u32[]{:S(2)}, u32[]{:S(2)}) collective-permute-start(bf16[32,3840]{1,0:T(8,128)(2,1)S(1)} %collective-permute-done.11.refs_5_), channel_id=1, source_target_pairs={{0,8},{8,16},{16,24},{24,28},{28,20},{20,12},{12,4},{4,0},{1,9},{9... | collective-permute-start | bytes 737288 | tf_op jit(solution)/shard_map/ppermute | solution.py:284
  28.9 2.3 %collective-permute-done.4.refs_1_ = bf16[32,3712]{1,0:T(8,128)(2,1)} collective-permute-done((bf16[32,3712]{1,0:T(8,128)(2,1)S(1)}, bf16[32,3712]{1,0:T(8,128)(2,1)}, u32[]{:S(2)}, u32[]{:S(2)}) %collective-permute-start.4) | collective-permute-done | bytes 237600 | tf_op jit(solution)/shard_map/ppermute | solution.py:284
  31.2 1.5 %collective-permute-start.6 = (bf16[32,3712]{1,0:T(8,128)(2,1)}, bf16[32,3712]{1,0:T(8,128)(2,1)}, u32[]{:S(2)}, u32[]{:S(2)}) collective-permute-start(bf16[32,3712]{1,0:T(8,128)(2,1)} %collective-permute-done.4.refs_1_), channel_id=1, source_target_pairs={{0,8},{8,16},{16,24},{24,28},{28,20},{20,12},{12,4},{4,0},{1,9},{9... | collective-permute-start | bytes 712712 | tf_op jit(solution)/shard_map/ppermute | solution.py:284
  32.6 1.2 %slice.12 = bf16[3600,76]{1,0:T(8,128)(2,1)S(1)} slice(bf16[3600,7500]{1,0:T(8,128)(2,1)} %bitcast.12), slice={[0:3600], [7424:7500]} | slice | bytes 1094400 | tf_op jit(solution)/shard_map/slice | solution.py:259
  34.1 1.7 %collective-permute-done.7.refs_4_ = bf16[32,3712]{1,0:T(8,128)(2,1)} collective-permute-done((bf16[32,3712]{1,0:T(8,128)(2,1)S(1)}, bf16[32,3712]{1,0:T(8,128)(2,1)}, u32[]{:S(2)}, u32[]{:S(2)}) %collective-permute-start.7) | collective-permute-done | bytes 237600 | tf_op jit(solution)/shard_map/ppermute | solution.py:288
  36.4 2.5 %collective-permute-done.6.refs_3_ = bf16[32,3712]{1,0:T(8,128)(2,1)} collective-permute-done((bf16[32,3712]{1,0:T(8,128)(2,1)}, bf16[32,3712]{1,0:T(8,128)(2,1)}, u32[]{:S(2)}, u32[]{:S(2)}) %collective-permute-start.6) | collective-permute-done | bytes 237600 | tf_op jit(solution)/shard_map/ppermute | solution.py:284
  40.0 10.8 %lead_kernel.2 = (f32[2,1920,128]{2,1,0:T(8,128)S(1)}, bf16[3840,256]{1,0:T(8,128)(2,1)S(1)}) custom-call(s32[1]{0:T(128)} %bitcast.1.me_ref, s32[1]{0:T(128)} %bitcast.rep_ref, bf16[32,3840]{1,0:T(8,128)(2,1)S(1)} %slice.10.refs_0_, bf16[32,3840]{1,0:T(8,128)(2,1)S(1)} %collective-permute-done.refs_1_, bf16[32,3840]{1,0:T(8,128)(2,1)S(1)} %collective-permute-done.2.refs_2_, ...), custom_call_target="tpu_custom_call" | custom-call | flops 3680501760 | bytes 18210816 | tf_op jit(solution)/shard_map/lead_kernel/pallas_call | solution.py:226
  51.8 7.5 %rest_kernel.2.refs_0_ = f32[2,1924,128]{2,1,0:T(8,128)S(1)} custom-call(s32[1]{0:T(128)} %bitcast.rep_ref, bf16[3840,256]{1,0:T(8,128)(2,1)S(1)} %get-tuple-element.39.turned, bf16[3600,7500]{1,0:T(8,128)(2,1)} %bitcast.14, bf16[3600,128]{1,0:T(8,128)(2,1)S(1)} %pad.9.refs_9_.edge_ref), custom_call_target="tpu_custom_call" | custom-call | flops 3428843520 | bytes 16965632 | tf_op jit(solution)/shard_map/rest_kernel/pallas_call | solution.py:226
  59.4 10.8 %lead_kernel.3 = (f32[2,1920,128]{2,1,0:T(8,128)S(1)}, bf16[3712,256]{1,0:T(8,128)(2,1)S(1)}, s16[2,15,32,256]{3,2,1,0:T(8,128)(2,1)S(1)}) custom-call(s32[1]{0:T(128)} %bitcast.1.me_ref, s32[1]{0:T(128)} %bitcast.rep_ref, bf16[32,3712]{1,0:T(8,128)(2,1)S(1)} %pad.8.refs_0_, ...), custom_call_target="tpu_custom_call", output_to_operand_aliasing={{0}: (12, {})} | custom-call | flops 3557818368 | bytes 17731584 | tf_op jit(solution)/shard_map/lead_kernel/pallas_call | solution.py:226
  70.3 8.3 %rest_kernel.3 = (f32[2,1924,128]{2,1,0:T(8,128)S(1)}, s16[2,15,32,256]{3,2,1,0:T(8,128)(2,1)S(1)}) custom-call(s32[1]{0:T(128)} %bitcast.rep_ref, bf16[3712,256]{1,0:T(8,128)(2,1)S(1)} %get-tuple-element.37.turned, bf16[3600,7500]{1,0:T(8,128)(2,1)} %bitcast.16, bf16[3600,128]{1,0:T(8,128)(2,1)S(1)} %pad.9.refs_9_.edge_ref, ...), custom_call_target="tpu_custom_call", output_to_operand_aliasing={{0}: (4, {})} | custom-call | flops 3314548736 | bytes 16519168 | tf_op jit(solution)/shard_map/rest_kernel/pallas_call | solution.py:226
  83.5 5.3 %collective-permute-done.16.got_ref = s16[15,32,256]{2,1,0:T(8,128)(2,1)S(1)} collective-permute-done((s16[15,32,256]{2,1,0:T(8,128)(2,1)S(1)}, s16[15,32,256]{2,1,0:T(8,128)(2,1)S(1)}, u32[]{:S(2)}, u32[]{:S(2)}) %collective-permute-start.16) | collective-permute-done | bytes 245792 | tf_op jit(solution)/shard_map/ppermute | solution.py:393
  88.8 1.6 %third_send_kernel.2 = s16[8,4,32,128]{3,2,1,0:T(8,128)(2,1)} custom-call(f32[15,32,256]{2,1,0:T(8,128)S(1)} %keep_kernel.2.kept_ref, s16[15,32,256]{2,1,0:T(8,128)(2,1)S(1)} %collective-permute-done.16.got_ref), custom_call_target="tpu_custom_call" | custom-call | flops 10000000 | bytes 4000000 | tf_op jit(solution)/shard_map/third_send_kernel/pallas_call | solution.py:226
  90.4 2.8 %collective-permute-done.17.got_ref = s16[15,32,256]{2,1,0:T(8,128)(2,1)S(1)} collective-permute-done((s16[15,32,256]{2,1,0:T(8,128)(2,1)S(1)}, s16[15,32,256]{2,1,0:T(8,128)(2,1)S(1)}, u32[]{:S(2)}, u32[]{:S(2)}) %collective-permute-start.17) | collective-permute-done | bytes 245792 | tf_op jit(solution)/shard_map/ppermute | solution.py:393
  94.0 13.6 %all_to_all.10.refs_1_ = s16[8,4,32,128]{3,2,1,0:T(8,128)(2,1)S(1)} all-to-all(s16[8,4,32,128]{3,2,1,0:T(8,128)(2,1)S(1)} %third_send_kernel.3), channel_id=1, replica_groups=mesh['grid'=8,'rep'=4] {'grid'}, dimensions={0} | all-to-all | bytes 524288 | tf_op jit(solution)/shard_map/all_to_all | solution.py:408
  107.6 3.4 %all-to-all-start = ((s16[8,4,32,128]{3,2,1,0:T(8,128)(2,1)}), s16[8,4,32,128]{3,2,1,0:T(8,128)(2,1)S(1)}, u32[]{:S(2)}, u32[]{:S(2)}) async-start(s16[8,4,32,128]{3,2,1,0:T(8,128)(2,1)} %third_send_kernel.2), calls=%async_computation | async-start | bytes 524288 | tf_op jit(solution)/shard_map/all_to_all | solution.py:408
  111.2 8.3 %all-to-all-done.refs_0_ = s16[8,4,32,128]{3,2,1,0:T(8,128)(2,1)S(1)} async-done(((s16[8,4,32,128]{3,2,1,0:T(8,128)(2,1)}), s16[8,4,32,128]{3,2,1,0:T(8,128)(2,1)S(1)}, u32[]{:S(2)}, u32[]{:S(2)}) %all-to-all-start) | async-done | bytes 262176 | tf_op jit(solution)/shard_map/all_to_all | solution.py:408
  119.6 2.1 %update_kernel.1 = f32[15,32,480]{2,1,0:T(8,128)} custom-call(f32[15]{0:T(128)S(1)} %copy-done.3, s32[15]{0:T(128)S(1)} %copy-done.4, s16[8,4,32,128]{3,2,1,0:T(8,128)(2,1)S(1)} %all-to-all-done.refs_0_, s16[8,4,32,128]{3,2,1,0:T(8,128)(2,1)S(1)} %all_to_all.10.refs_1_, f32[15,32,480]{2,1,0:T(8,128)S(1)} %bitcast.9, f32[32,1]{1,0:T(8,128)S(1)} %copy.12.refs_3_, ...), custom_call_target="tpu_custom_call" | custom-call | flops 10000000 | bytes 4000000 | tf_op jit(solution)/shard_map/update_kernel/pallas_call | solution.py:226
  (47 shorter events, 13.6 us)
Async XLA Ops:
  1.0 9.0 %collective-permute-start = (bf16[32,3840]{1,0:T(8,128)(2,1)S(1)}, bf16[32,3840]{1,0:T(8,128)(2,1)S(1)}, u32[]{:S(2)}, u32[]{:S(2)}) collective-permute-start(bf16[32,3840]{1,0:T(8,128)(2,1)S(1)} %slice.10.refs_0_), channel_id=1, source_target_pairs={{0,8},{8,16},{16,24},{24,28},{28,20},{20,12},{12,4},{4,0},{1,9},{9... | collective-permute-start | bytes 737288 | tf_op jit(solution)/shard_map/ppermute | solution.py:284
  4.0 7.7 %collective-permute-start.2 = (bf16[32,3840]{1,0:T(8,128)(2,1)S(1)}, bf16[32,3840]{1,0:T(8,128)(2,1)S(1)}, u32[]{:S(2)}, u32[]{:S(2)}) collective-permute-start(bf16[32,3840]{1,0:T(8,128)(2,1)S(1)} %slice.10.refs_0_), channel_id=1, source_target_pairs={{8,0},{16,8},{24,16},{28,24},{20,28},{12,20},{4,12},{0,4},{9,1},{1... | collective-permute-start | bytes 737288 | tf_op jit(solution)/shard_map/ppermute | solution.py:288
  9.9 7.1 %collective-permute-start.1 = (bf16[32,3840]{1,0:T(8,128)(2,1)S(1)}, bf16[32,3840]{1,0:T(8,128)(2,1)S(1)}, u32[]{:S(2)}, u32[]{:S(2)}) collective-permute-start(bf16[32,3840]{1,0:T(8,128)(2,1)S(1)} %collective-permute-done.refs_1_), channel_id=1, source_target_pairs={{0,8},{8,16},{16,24},{24,28},{28,20},{20,12},{12,4},{4,0},{1,9},{9... | collective-permute-start | bytes 737288 | tf_op jit(solution)/shard_map/ppermute | solution.py:284
  11.7 7.8 %collective-permute-start.3 = (bf16[32,3840]{1,0:T(8,128)(2,1)S(1)}, bf16[32,3840]{1,0:T(8,128)(2,1)S(1)}, u32[]{:S(2)}, u32[]{:S(2)}) collective-permute-start(bf16[32,3840]{1,0:T(8,128)(2,1)S(1)} %collective-permute-done.2.refs_2_), channel_id=1, source_target_pairs={{8,0},{16,8},{24,16},{28,24},{20,28},{12,20},{4,12},{0,4},{9,1},{1... | collective-permute-start | bytes 737288 | tf_op jit(solution)/shard_map/ppermute | solution.py:288
  17.1 8.9 %collective-permute-start.11 = (bf16[32,3840]{1,0:T(8,128)(2,1)S(1)}, bf16[32,3840]{1,0:T(8,128)(2,1)S(1)}, u32[]{:S(2)}, u32[]{:S(2)}) collective-permute-start(bf16[32,3840]{1,0:T(8,128)(2,1)S(1)} %collective-permute-done.1.refs_3_), channel_id=1, source_target_pairs={{0,8},{8,16},{16,24},{24,28},{28,20},{20,12},{12,4},{4,0},{1,9},{9... | collective-permute-start | bytes 737288 | tf_op jit(solution)/shard_map/ppermute | solution.py:284
  19.6 8.8 %collective-permute-start.5 = (bf16[32,3712]{1,0:T(8,128)(2,1)S(1)}, bf16[32,3712]{1,0:T(8,128)(2,1)S(1)}, u32[]{:S(2)}, u32[]{:S(2)}) collective-permute-start(bf16[32,3712]{1,0:T(8,128)(2,1)S(1)} %pad.8.refs_0_), channel_id=1, source_target_pairs={{8,0},{16,8},{24,16},{28,24},{20,28},{12,20},{4,12},{0,4},{9,1},{1... | collective-permute-start | bytes 712712 | tf_op jit(solution)/shard_map/ppermute | solution.py:288
  20.2 11.0 %collective-permute-start.4 = (bf16[32,3712]{1,0:T(8,128)(2,1)S(1)}, bf16[32,3712]{1,0:T(8,128)(2,1)}, u32[]{:S(2)}, u32[]{:S(2)}) collective-permute-start(bf16[32,3712]{1,0:T(8,128)(2,1)S(1)} %pad.8.refs_0_), channel_id=1, source_target_pairs={{0,8},{8,16},{16,24},{24,28},{28,20},{20,12},{12,4},{4,0},{1,9},{9... | collective-permute-start | bytes 712712 | tf_op jit(solution)/shard_map/ppermute | solution.py:284
  21.6 18.4 %collective-permute-start.12 = (bf16[32,3840]{1,0:T(8,128)(2,1)S(1)}, bf16[32,3840]{1,0:T(8,128)(2,1)S(1)}, u32[]{:S(2)}, u32[]{:S(2)}) collective-permute-start(bf16[32,3840]{1,0:T(8,128)(2,1)S(1)} %collective-permute-done.3.refs_4_), channel_id=1, source_target_pairs={{8,0},{16,8},{24,16},{28,24},{20,28},{12,20},{4,12},{0,4},{9,1},{1... | collective-permute-start | bytes 737288 | tf_op jit(solution)/shard_map/ppermute | solution.py:288
  26.0 14.0 %collective-permute-start.13 = (bf16[32,3840]{1,0:T(8,128)(2,1)S(1)}, bf16[32,3840]{1,0:T(8,128)(2,1)S(1)}, u32[]{:S(2)}, u32[]{:S(2)}) collective-permute-start(bf16[32,3840]{1,0:T(8,128)(2,1)S(1)} %collective-permute-done.11.refs_5_), channel_id=1, source_target_pairs={{0,8},{8,16},{16,24},{24,28},{28,20},{20,12},{12,4},{4,0},{1,9},{9... | collective-permute-start | bytes 737288 | tf_op jit(solution)/shard_map/ppermute | solution.py:284
  28.3 7.5 %collective-permute-start.7 = (bf16[32,3712]{1,0:T(8,128)(2,1)S(1)}, bf16[32,3712]{1,0:T(8,128)(2,1)}, u32[]{:S(2)}, u32[]{:S(2)}) collective-permute-start(bf16[32,3712]{1,0:T(8,128)(2,1)S(1)} %collective-permute-done.5.refs_2_), channel_id=1, source_target_pairs={{8,0},{16,8},{24,16},{28,24},{20,28},{12,20},{4,12},{0,4},{9,1},{1... | collective-permute-start | bytes 712712 | tf_op jit(solution)/shard_map/ppermute | solution.py:288
  31.2 7.7 %collective-permute-start.6 = (bf16[32,3712]{1,0:T(8,128)(2,1)}, bf16[32,3712]{1,0:T(8,128)(2,1)}, u32[]{:S(2)}, u32[]{:S(2)}) collective-permute-start(bf16[32,3712]{1,0:T(8,128)(2,1)} %collective-permute-done.4.refs_1_), channel_id=1, source_target_pairs={{0,8},{8,16},{16,24},{24,28},{28,20},{20,12},{12,4},{4,0},{1,9},{9... | collective-permute-start | bytes 712712 | tf_op jit(solution)/shard_map/ppermute | solution.py:284
  35.8 15.1 %collective-permute-start.9 = (bf16[32,3712]{1,0:T(8,128)(2,1)}, bf16[32,3712]{1,0:T(8,128)(2,1)S(1)}, u32[]{:S(2)}, u32[]{:S(2)}) collective-permute-start(bf16[32,3712]{1,0:T(8,128)(2,1)} %collective-permute-done.7.refs_4_), channel_id=1, source_target_pairs={{8,0},{16,8},{24,16},{28,24},{20,28},{12,20},{4,12},{0,4},{9,1},{1... | collective-permute-start | bytes 712712 | tf_op jit(solution)/shard_map/ppermute | solution.py:288
  38.9 12.0 %collective-permute-start.8 = (bf16[32,3712]{1,0:T(8,128)(2,1)}, bf16[32,3712]{1,0:T(8,128)(2,1)S(1)}, u32[]{:S(2)}, u32[]{:S(2)}) collective-permute-start(bf16[32,3712]{1,0:T(8,128)(2,1)} %collective-permute-done.6.refs_3_), channel_id=1, source_target_pairs={{0,8},{8,16},{16,24},{24,28},{28,20},{20,12},{12,4},{4,0},{1,9},{9... | collective-permute-start | bytes 712712 | tf_op jit(solution)/shard_map/ppermute | solution.py:284
  50.9 8.5 %collective-permute-start.10 = (bf16[32,3712]{1,0:T(8,128)(2,1)S(1)}, bf16[32,3712]{1,0:T(8,128)(2,1)S(1)}, u32[]{:S(2)}, u32[]{:S(2)}) collective-permute-start(bf16[32,3712]{1,0:T(8,128)(2,1)S(1)} %collective-permute-done.9.refs_6_), channel_id=1, source_target_pairs={{8,0},{16,8},{24,16},{28,24},{20,28},{12,20},{4,12},{0,4},{9,1},{1... | collective-permute-start | bytes 712712 | tf_op jit(solution)/shard_map/ppermute | solution.py:288
  70.2 8.9 %collective-permute-start.14 = (s16[2,15,32,256]{3,2,1,0:T(8,128)(2,1)S(1)}, s16[2,15,32,256]{3,2,1,0:T(8,128)(2,1)S(1)}, u32[]{:S(2)}, u32[]{:S(2)}) collective-permute-start(s16[2,15,32,256]{3,2,1,0:T(8,128)(2,1)S(1)} %get-tuple-element.36), channel_id=1, source_target_pairs={{0,1},{1,0},{2,3},{3,2},{4,5},{5,4},{6,7},{7,6},{8,9},{9,8},{10,11... | collective-permute-start | bytes 1474568 | tf_op jit(solution)/shard_map/ppermute | solution.py:371
  78.6 2.5 %collective-permute-start.15 = (s16[2,15,32,256]{3,2,1,0:T(8,128)(2,1)S(1)}, s16[2,15,32,256]{3,2,1,0:T(8,128)(2,1)S(1)}, u32[]{:S(2)}, u32[]{:S(2)}) collective-permute-start(s16[2,15,32,256]{3,2,1,0:T(8,128)(2,1)S(1)} %get-tuple-element.41), channel_id=1, source_target_pairs={{0,1},{1,0},{2,3},{3,2},{4,5},{5,4},{6,7},{7,6},{8,9},{9,8},{10,11... | collective-permute-start | bytes 1474568 | tf_op jit(solution)/shard_map/ppermute | solution.py:371
  79.9 8.9 %collective-permute-start.16 = (s16[15,32,256]{2,1,0:T(8,128)(2,1)S(1)}, s16[15,32,256]{2,1,0:T(8,128)(2,1)S(1)}, u32[]{:S(2)}, u32[]{:S(2)}) collective-permute-start(s16[15,32,256]{2,1,0:T(8,128)(2,1)S(1)} %second_send_kernel.2), channel_id=1, source_target_pairs={{0,2},{1,3},{2,0},{3,1},{4,6},{5,7},{6,4},{7,5},{8,10},{9,11},{10,... | collective-permute-start | bytes 737288 | tf_op jit(solution)/shard_map/ppermute | solution.py:393
  81.8 11.3 %collective-permute-start.17 = (s16[15,32,256]{2,1,0:T(8,128)(2,1)S(1)}, s16[15,32,256]{2,1,0:T(8,128)(2,1)S(1)}, u32[]{:S(2)}, u32[]{:S(2)}) collective-permute-start(s16[15,32,256]{2,1,0:T(8,128)(2,1)S(1)} %second_send_kernel.3), channel_id=1, source_target_pairs={{0,2},{1,3},{2,0},{3,1},{4,6},{5,7},{6,4},{7,5},{8,10},{9,11},{10,... | collective-permute-start | bytes 737288 | tf_op jit(solution)/shard_map/ppermute | solution.py:393
  83.4 36.2 %copy-start = (f32[32,15,480]{2,0,1:T(8,128)S(1)}, f32[32,15,480]{2,0,1:T(8,128)}, u32[]{:S(2)}) copy-start(f32[32,15,480]{2,0,1:T(8,128)} %param.11) | copy-start | bytes 2764804
  83.4 36.2 %copy-start.1 = (f32[480]{0:T(512)S(1)}, f32[480]{0:T(512)}, u32[]{:S(2)}) copy-start(f32[480]{0:T(512)} %param.14) | copy-start | bytes 5764
  83.4 36.1 %copy-start.2 = (s32[480]{0:T(512)S(1)}, s32[480]{0:T(512)}, u32[]{:S(2)}) copy-start(s32[480]{0:T(512)} %param.17) | copy-start | bytes 5764
  83.5 36.1 %copy-start.3 = (f32[15]{0:T(128)S(1)}, f32[15]{0:T(128)}, u32[]{:S(2)}) copy-start(f32[15]{0:T(128)} %occ_energy_ref.1) | copy-start | bytes 184
  83.5 36.1 %copy-start.4 = (s32[15]{0:T(128)S(1)}, s32[15]{0:T(128)}, u32[]{:S(2)}) copy-start(s32[15]{0:T(128)} %occ_irrep_ref.1) | copy-start | bytes 184
  107.6 12.0 %all-to-all-start = ((s16[8,4,32,128]{3,2,1,0:T(8,128)(2,1)}), s16[8,4,32,128]{3,2,1,0:T(8,128)(2,1)S(1)}, u32[]{:S(2)}, u32[]{:S(2)}) async-start(s16[8,4,32,128]{3,2,1,0:T(8,128)(2,1)} %third_send_kernel.2), calls=%async_computation | async-start | bytes 524288 | tf_op jit(solution)/shard_map/all_to_all | solution.py:408
  (2 other events, 55.4 us)

commit v5 on v3

v5 whole, which is shorter than its diff:
```python
import functools

import jax
import jax.numpy as jnp
from jax import lax
from jax.experimental import pallas as pl
from jax.experimental.pallas import tpu as pltpu
from jax.sharding import PartitionSpec as P

NOCC = 60
LANES = 128
K_BLOCK = 3840
C_BLOCK = 480
COPIES = 4
FIRST_PART = 47
STEPS = 8.0
TOP = 32767.0
MIB = 1024 * 1024


def ceil_to(value, unit):
    return -(-value // unit) * unit


def encode(rows, count):
    index = lax.broadcasted_iota(jnp.int32, rows.shape, 0)
    rows = jnp.where(index < count, rows, 0.0)
    largest = jnp.max(jnp.abs(rows), axis=0, keepdims=True)
    level = jnp.ceil(jnp.log2(jnp.maximum(largest, 1e-30)) * STEPS) + 1.0
    coded = jnp.floor(rows * (jnp.exp2(level * (-1.0 / STEPS)) * TOP) + 0.5)
    return jnp.where(index == count, level, coded)


def decode(block, count):
    index = lax.broadcasted_iota(jnp.int32, block.shape, 0)
    scale = jnp.exp2(block[count : count + 1] * (1.0 / STEPS)) * (1.0 / TOP)
    return jnp.where(index < count, block * scale, 0.0)


def to_code(block):
    return block.astype(jnp.int32).astype(jnp.int16)


def from_code(block):
    return block.astype(jnp.int32).astype(jnp.float32)


def walk_index(place, size):
    return jnp.where(place < size // 2, 2 * place, 2 * (size - 1 - place) + 1)


def walk_place(index, size):
    return jnp.where(index % 2 == 0, index // 2, size - 1 - index // 2)


def coupling_copies(coupling_ref, edge_ref, buffer, sems, low, start, slot):
    block = buffer.shape[1]
    whole = buffer.shape[2] - LANES
    rows = pl.ds(pl.multiple_of(low + start, 16), block)
    quarter = ceil_to(-(-whole // COPIES), 256)
    copies = []
    for number, k in enumerate(range(0, whole, quarter)):
        pairs = pl.ds(k, min(quarter, whole - k))
        copies.append(
            pltpu.make_async_copy(
                coupling_ref.at[rows, pairs], buffer.at[slot, :, pairs], sems.at[slot, number]
            )
        )
    copies.append(
        pltpu.make_async_copy(
            edge_ref.at[rows, :], buffer.at[slot, :, pl.ds(whole, LANES)], sems.at[slot, COPIES]
        )
    )
    return copies


def multiply(coupling_ref, edge_ref, buffer, sems, turned, total_ref, columns, before=None):
    low, many = columns
    block = buffer.shape[1]
    steps = -(-many // block)

    def copies(step):
        start = jnp.minimum(step * block, many - block)
        return coupling_copies(coupling_ref, edge_ref, buffer, sems, low, start, lax.rem(step, 2))

    for copy in copies(jnp.int32(0)):
        copy.start()
    if before is not None:
        before()

    def step(number, carry):
        @pl.when(number + 1 < steps)
        def _():
            for copy in copies(number + 1):
                copy.start()

        for copy in copies(number):
            copy.wait()
        total = jnp.dot(
            buffer[lax.rem(number, 2)], turned[...], preferred_element_type=jnp.float32
        )
        rows = pl.ds(pl.multiple_of(jnp.minimum(number * block, many - block), 4), block)
        for part in range(total_ref.shape[0]):
            total_ref[part, rows, :] = total[:, part * LANES : (part + 1) * LANES]
        return carry

    lax.fori_loop(0, steps, step, 0)


def gather_pieces(me_ref, offsets, edges, pieces, gathered, turned, sems):
    rows = pieces[0].shape[0]
    grid_size = gathered.shape[0] // rows
    place = walk_place(me_ref[0], grid_size)
    copies = []
    for number, (offset, edge, piece) in enumerate(zip(offsets, edges, pieces)):
        source = walk_index(lax.rem(place + offset + grid_size, grid_size), grid_size)
        target = gathered.at[
            pl.ds(pl.multiple_of(source * rows, rows), rows), pl.ds(edge, piece.shape[1])
        ]
        copies.append(pltpu.make_async_copy(piece, target, sems.at[number]))
    for copy in copies:
        copy.start()
    for copy in copies:
        copy.wait()
    for at in range(0, turned.shape[0], LANES):
        turned[at : at + LANES, :] = gathered[:, at : at + LANES].T


def lead_kernel(offsets, edges, columns, span, me_ref, rep_ref, *refs):
    pieces, refs = refs[: len(offsets)], refs[len(offsets) :]
    coupling_ref, edge_ref, total, turned, send, gathered, sems, buffer, buffer_sems = refs
    multiply(
        coupling_ref,
        edge_ref,
        buffer,
        buffer_sems,
        turned,
        total,
        columns,
        lambda: gather_pieces(me_ref, offsets, edges, pieces, gathered, turned, sems),
    )
    first_send(span, rep_ref, total, send)


def rest_kernel(columns, span, rep_ref, turned, coupling_ref, edge_ref, total, send, buffer, sems):
    multiply(coupling_ref, edge_ref, buffer, sems, turned, total, columns)
    first_send(span, rep_ref, total, send)


def column_rows(total_ref, width, part, j, offset, bp):
    rows = pl.ds(offset + part * width + j, bp, stride=NOCC)
    return jnp.concatenate([total_ref[h, rows, :] for h in range(total_ref.shape[0])], axis=1)


def first_send(span, rep_ref, total_ref, out_ref):
    offset, count, width = span
    low = rep_ref[0] % 2

    def step(j, carry):
        for high in range(2):
            rows = column_rows(total_ref, width, 2 * high + 1 - low, j, offset, out_ref.shape[2])
            out_ref[high, j] = to_code(encode(rows, count))
        return carry

    lax.fori_loop(0, width, step, 0)


def second_send_kernel(span, rep_ref, total_ref, got_ref, out_ref):
    offset, count, width = span
    low, high = rep_ref[0] % 2, 1 - rep_ref[0] // 2

    def step(j, carry):
        rows = column_rows(total_ref, width, 2 * high + low, j, offset, out_ref.shape[1])
        rows = rows + decode(from_code(got_ref[high, j]), count)
        out_ref[j] = to_code(encode(rows, count))
        return carry

    lax.fori_loop(0, width, step, 0)


def keep_kernel(span, rep_ref, total_ref, got_ref, out_ref):
    offset, count, width = span
    low, high = rep_ref[0] % 2, rep_ref[0] // 2

    def step(j, carry):
        rows = column_rows(total_ref, width, 2 * high + low, j, offset, out_ref.shape[1])
        out_ref[j] = rows + decode(from_code(got_ref[high, j]), count)
        return carry

    lax.fori_loop(0, width, step, 0)


def pack_rows(count, rows_dev, kept_ref, got_ref, stage):
    pack = LANES // rows_dev
    groups = stage.shape[1]
    size, _, slab = kept_ref.shape

    def step(jj, carry):
        coded = []
        for jq in range(pack):
            j = jnp.minimum(jq * groups + jj, size - 1)
            coded.append(encode(kept_ref[j] + decode(from_code(got_ref[j]), count), count))
        for g in range(slab // rows_dev):
            own = [block[:, g * rows_dev : (g + 1) * rows_dev] for block in coded]
            stage[g, jj] = to_code(jnp.concatenate(own, axis=1))
        return carry

    lax.fori_loop(0, groups, step, 0)


def third_send_kernel(count, rows_dev, kept_ref, got_ref, stage):
    pack_rows(count, rows_dev, kept_ref, got_ref, stage)


def last_send_kernel(count, rows_dev, parts, me_ref, kept_ref, got_ref, *refs):
    earlier, targets, stage = refs[: parts - 1], refs[parts - 1 : -1], refs[-1]
    pack_rows(count, rows_dev, kept_ref, got_ref, stage)
    for number, target in enumerate(targets):
        at = 0
        for source in (*earlier, stage):
            bp = source.shape[2]
            target[:, at : at + bp, :] = source[me_ref[0] ^ number]
            at += bp


def update_kernel(counts, bps, width, rows_dev, me_ref, occ_energy_ref, occ_irrep_ref, *refs):
    (
        integrals_ref,
        row_energy_ref,
        vir_energy_ref,
        row_irrep_ref,
        vir_irrep_ref,
        out_ref,
        blocks,
        stage,
    ) = refs[-8:]
    arrived = refs[:-8]
    for number, got_ref in enumerate(arrived):
        blocks[me_ref[0] ^ number] = got_ref[...]
    pack = LANES // rows_dev
    for jj in range(blocks.shape[1]):
        at = 0
        for g in range(len(arrived)):
            row = 0
            for count, bp in zip(counts, bps):
                block = decode(from_code(blocks[g, jj, row : row + bp, :]), count)
                stage[at : at + count, :] = block[:count]
                at += count
                row += bp
        turned = stage[...].T
        for jq in range(pack):
            j = jq * blocks.shape[1] + jj
            if j >= width:
                continue
            cycle = turned[jq * rows_dev : (jq + 1) * rows_dev]
            denominator = row_energy_ref[...] + occ_energy_ref[j] - vir_energy_ref[...]
            labels = row_irrep_ref[...] ^ occ_irrep_ref[j] ^ vir_irrep_ref[...]
            out_ref[j] = jnp.where(
                labels == 0, (integrals_ref[j] + cycle) / denominator, jnp.float32(0.0)
            )


def local_call(kernel, out_shape, specs, args, scratch=(), aliases={}, cost=(10**7, 4 * 10**6), room=0):
    spaces = {"s": pltpu.SMEM, "v": pltpu.VMEM, "a": pl.ANY}
    return pl.pallas_call(
        kernel,
        out_shape=out_shape,
        in_specs=[pl.BlockSpec(memory_space=spaces[letter]) for letter in specs],
        out_specs=jax.tree.map(lambda _: pl.BlockSpec(memory_space=pltpu.VMEM), out_shape),
        scratch_shapes=list(scratch),
        input_output_aliases=aliases,
        compiler_params=pltpu.CompilerParams(vmem_limit_bytes=8 * MIB + room),
        cost_estimate=pl.CostEstimate(
            flops=cost[0], bytes_accessed=cost[1], transcendentals=0
        ),
        name=kernel.func.__name__,
    )(*args)


def body(
    amplitudes,
    coupling,
    integrals,
    row_energy,
    occ_energy,
    vir_energy,
    row_irrep,
    occ_irrep,
    vir_irrep,
):
    grid_size = lax.axis_size("grid")
    me = lax.axis_index("grid").astype(jnp.int32).reshape(1)
    rep = lax.axis_index("rep").astype(jnp.int32).reshape(1)
    rows_dev, depth = amplitudes.shape
    coupling = coupling.T
    columns = coupling.shape[0]
    count = columns // NOCC
    ragged = ceil_to(columns, 16) - columns
    if ragged:
        coupling = jnp.pad(coupling, ((0, ragged), (0, 0)))
        columns += ragged
    edge = depth % LANES
    edge = jnp.pad(coupling[:, depth - edge :], ((0, 0), (0, LANES - edge)))
    slab = rows_dev * grid_size
    width = NOCC // lax.axis_size("rep")

    walk = [*range(0, grid_size, 2), *range(1, grid_size, 2)[::-1]]
    onward = [(walk[i], walk[(i + 1) % grid_size]) for i in range(grid_size)]
    back = [(b, a) for a, b in onward]

    longer = grid_size // 2
    pieces, offsets, edges = [], [], []
    for number, at in enumerate(range(0, depth, K_BLOCK)):
        own = amplitudes[:, at : at + K_BLOCK]
        size = own.shape[1]
        own = jnp.pad(own, ((0, 0), (0, ceil_to(size, LANES) - size)))
        hops = (longer, grid_size - 1 - longer)
        if number % 2:
            hops = hops[::-1]
        ahead = behind = own
        pieces.append(own)
        offsets.append(0)
        for hop in range(1, longer + 1):
            if hop <= hops[0]:
                ahead = lax.ppermute(ahead, "grid", onward)
                pieces.append(ahead)
                offsets.append(-hop)
            if hop <= hops[1]:
                behind = lax.ppermute(behind, "grid", back)
                pieces.append(behind)
                offsets.append(hop)
        edges += [at] * grid_size

    counts = [FIRST_PART, count - FIRST_PART] if count > FIRST_PART else [count]
    firsts = [0, FIRST_PART][: len(counts)]
    bps = [ceil_to(number + 1, 16) for number in counts]
    lows = [first * NOCC // 16 * 16 for first in firsts]
    highs = [
        min(columns, ceil_to((first + number) * NOCC, 16)) for first, number in zip(firsts, counts)
    ]
    parts = [(low, high - low) for low, high in zip(lows, highs)]
    spans = [
        (first * NOCC - low, number, width) for first, low, number in zip(firsts, lows, counts)
    ]
    total_shapes = [
        jax.ShapeDtypeStruct((slab // LANES, max(span[0] + bp * NOCC, part[1]), LANES), jnp.float32)
        for span, part, bp in zip(spans, parts, bps)
    ]
    send_shapes = [jax.ShapeDtypeStruct((2, width, bp, slab), jnp.int16) for bp in bps]
    deep = ceil_to(depth, LANES)
    low_pairs = [(i, i ^ 1) for i in range(lax.axis_size("rep"))]
    high_pairs = [(i, i ^ 2) for i in range(lax.axis_size("rep"))]

    totals, sends, got = [], [], []
    for part, (cols, span, bp) in enumerate(zip(parts, spans, bps)):
        block = min(C_BLOCK, ceil_to(cols[1] // 2, 16))
        scratch = [
            pltpu.VMEM((2, block, deep), jnp.bfloat16),
            pltpu.SemaphoreType.DMA((2, COPIES + 1)),
        ]
        cost = (2 * cols[1] * deep * slab, 2 * cols[1] * deep)
        room = 4 * block * deep + (2 * slab * deep if part == 0 else 0)
        if slab > 2 * LANES:
            room += 2 * slab * deep + 4 * slab * total_shapes[part].shape[1]
        if part == 0:
            total, turned, send = local_call(
                functools.partial(lead_kernel, tuple(offsets), tuple(edges), cols, span),
                (
                    total_shapes[0],
                    jax.ShapeDtypeStruct((deep, slab), jnp.bfloat16),
                    send_shapes[0],
                ),
                "ss" + "a" * (len(pieces) + 2),
                (me, rep, *pieces, coupling, edge),
                [
                    pltpu.VMEM((slab, deep), jnp.bfloat16),
                    pltpu.SemaphoreType.DMA((len(pieces),)),
                    *scratch,
                ],
                cost=cost,
                room=room,
            )
        else:
            turned, _ = lax.optimization_barrier((turned, sends[0]))
            total, send = local_call(
                functools.partial(rest_kernel, cols, span),
                (total_shapes[part], send_shapes[part]),
                "svaa",
                (rep, turned, coupling, edge),
                scratch,
                cost=cost,
                room=room,
            )
        arrived = lax.ppermute(send, "rep", low_pairs)
        totals.append(total)
        got.append(arrived)
        sends.append(
            local_call(
                functools.partial(second_send_kernel, span),
                jax.ShapeDtypeStruct((width, bp, slab), jnp.int16),
                "svv",
                (rep, total, arrived),
            )
        )
    kept = [
        local_call(
            functools.partial(keep_kernel, span),
            jax.ShapeDtypeStruct((width, bp, slab), jnp.float32),
            "svv",
            (rep, total, arrived),
        )
        for span, bp, total, arrived in zip(spans, bps, totals, got)
    ]
    got = [lax.ppermute(send, "rep", high_pairs) for send in sends]

    groups = -(-width // (LANES // rows_dev))
    staged = []
    for part, span in enumerate(spans[:-1]):
        mine, _ = lax.optimization_barrier((kept[part], sends[-1]))
        staged.append(
            local_call(
                functools.partial(third_send_kernel, span[1], rows_dev),
                jax.ShapeDtypeStruct((grid_size, groups, bps[part], LANES), jnp.int16),
                "vv",
                (mine, got[part]),
            )
        )
    targets = local_call(
        functools.partial(last_send_kernel, counts[-1], rows_dev, len(counts)),
        (jax.ShapeDtypeStruct((groups, sum(bps), LANES), jnp.int16),) * grid_size,
        "svv" + "v" * len(staged),
        (me, kept[-1], got[-1], *staged),
        [pltpu.VMEM((grid_size, groups, bps[-1], LANES), jnp.int16)],
    )
    arrived = [targets[0]] + [
        lax.ppermute(target, "grid", [(g, g ^ number) for g in range(grid_size)])
        for number, target in list(enumerate(targets))[1:]
    ]

    updated = local_call(
        functools.partial(update_kernel, counts, bps, width, rows_dev),
        jax.ShapeDtypeStruct((width, rows_dev, count * grid_size), jnp.float32),
        "sss" + "v" * (len(arrived) + 5),
        (
            me,
            occ_energy,
            occ_irrep,
            *arrived,
            jnp.transpose(integrals, (1, 0, 2)),
            row_energy[:, None],
            vir_energy[None, :],
            row_irrep[:, None],
            vir_irrep[None, :],
        ),
        [
            pltpu.VMEM((grid_size, groups, sum(bps), LANES), jnp.int16),
            pltpu.VMEM((count * grid_size, LANES), jnp.float32),
        ],
    )
    return jnp.transpose(updated, (1, 0, 2))


def solution(mesh):
    return jax.shard_map(
        body,
        mesh=mesh,
        in_specs=(
            P("grid", "rep"),
            P("rep", "grid"),
            P("grid", "rep", None),
            P("grid"),
            P("rep"),
            P(),
            P("grid"),
            P("rep"),
            P(),
        ),
        out_specs=P("grid", "rep", None),
        check_vma=False,
    )
```

time: 125 us -> 107 us (0.86)
  Pallas kernels: 41.7 us -> 34.1 us
  waiting for transfers between devices: 40.3 us -> 35.1 us
  local copies, waits for them, and re-layouts: 11.1 us -> 6.85 us
    all_to_all x2 -> x0, starting transfers between devices: 11.1 us -> none  [body(): lax.all_to_all(send, 'grid', split_axis=0, concat_axis=0, tiled=True)]
    ppermute x2 -> x9, starting transfers between devices: 0.57 us -> 11.3 us  [the longest x7 11.2 us: body(): lax.ppermute(target, 'grid', [(g, g ^ number) for g in range(grid_size)])]
    ppermute x2, waiting for transfers between devices: 11.8 us -> 3.15 us  [body(): got = [lax.ppermute(send, 'rep', high_pairs) for send in sends]]
    ppermute x2 -> x9, waiting for transfers between devices: 1.36 us -> 9.83 us  [the longest x7 6.13 us: body(): lax.ppermute(target, 'grid', [(g, g ^ number) for g in range(grid_size)])]
    all_to_all x2 -> x0, waiting for transfers between devices: 8.04 us -> none  [body(): lax.all_to_all(send, 'grid', split_axis=0, concat_axis=0, tiled=True)]
    pallas_call x10 -> x9, Pallas kernels: 41.7 us -> 34.1 us  [local_call(): pl.pallas_call(kernel, out_shape=out_shape, in_specs=[pl.BlockSpec(memory...]
    unnamed x38 -> x22, local copies, waits for them, and re-layouts: 5.47 us -> 3.31 us
    ppermute x7, waiting for transfers between devices: 6.38 us -> 8.32 us  [body(): behind = lax.ppermute(behind, 'grid', back)]
  transfers between devices with their start and end apart: 20 -> 25, of which waited for: 10 -> 14; matrix products, arithmetic and copies ran while one was open for 4% -> 2% of each run, Pallas kernels for 17% -> 9%
where the time goes in v5:
time: 107 us; the launch traced here: 106 us
  waiting for transfers between devices  35.1 us (33%)
  Pallas kernels  34.1 us (32%)
  starting transfers between devices  30.1 us (28%)
  local copies, waits for them, and re-layouts  6.85 us (6%)
    pallas_call x9, Pallas kernels, local_call(): pl.pallas_call(kernel, out_shape=out_shape, in_specs=[pl.BlockSpec(memory...  34.1 us
    ppermute x7, starting transfers between devices, body(): ahead = lax.ppermute(ahead, 'grid', onward)  14.1 us
    ppermute x7, waiting for transfers between devices, body(): ahead = lax.ppermute(ahead, 'grid', onward)  13.8 us
    ppermute x7, starting transfers between devices, body(): lax.ppermute(target, 'grid', [(g, g ^ number) for g in range(grid_size)])  11.2 us
    ppermute x7, waiting for transfers between devices, body(): behind = lax.ppermute(behind, 'grid', back)  8.32 us
    ppermute x7, waiting for transfers between devices, body(): lax.ppermute(target, 'grid', [(g, g ^ number) for g in range(grid_size)])  6.13 us
    ppermute x2, waiting for transfers between devices, body(): arrived = lax.ppermute(send, 'rep', low_pairs)  3.7 us
    unnamed x22, local copies, waits for them, and re-layouts  3.31 us
  transfers between devices with their start and end apart: 25, of which 14 were waited for; matrix products, arithmetic and copies ran while one was open for 2% of the time, Pallas kernels for 9%

profile of v5, /device:TPU:0, one launch (start us, length us, event | category | flops | bytes accessed | tf_op | source)
XLA Modules:
  0.0 106.4 jit_solution(16761666211864651238)
XLA Ops:
  1.0 3.1 %collective-permute-start = (bf16[32,3840]{1,0:T(8,128)(2,1)S(1)}, bf16[32,3840]{1,0:T(8,128)(2,1)S(1)}, u32[]{:S(2)}, u32[]{:S(2)}) collective-permute-start(bf16[32,3840]{1,0:T(8,128)(2,1)S(1)} %slice.9.refs_0_), channel_id=1, source_target_pairs={{0,8},{8,16},{16,24},{24,28},{28,20},{20,12},{12,4},{4,0},{1,9},{9... | collective-permute-start | bytes 737288 | tf_op jit(solution)/shard_map/ppermute | solution.py:325
  5.1 2.0 %collective-permute-start.1 = (bf16[32,3840]{1,0:T(8,128)(2,1)S(1)}, bf16[32,3840]{1,0:T(8,128)(2,1)S(1)}, u32[]{:S(2)}, u32[]{:S(2)}) collective-permute-start(bf16[32,3840]{1,0:T(8,128)(2,1)S(1)} %slice.9.refs_0_), channel_id=1, source_target_pairs={{8,0},{16,8},{24,16},{28,24},{20,28},{12,20},{4,12},{0,4},{9,1},{1... | collective-permute-start | bytes 737288 | tf_op jit(solution)/shard_map/ppermute | solution.py:329
  7.1 2.9 %collective-permute-done.refs_1_ = bf16[32,3840]{1,0:T(8,128)(2,1)S(1)} collective-permute-done((bf16[32,3840]{1,0:T(8,128)(2,1)S(1)}, bf16[32,3840]{1,0:T(8,128)(2,1)S(1)}, u32[]{:S(2)}, u32[]{:S(2)}) %collective-permute-start) | collective-permute-done | bytes 245792 | tf_op jit(solution)/shard_map/ppermute | solution.py:325
  9.9 1.8 %collective-permute-start.2 = (bf16[32,3840]{1,0:T(8,128)(2,1)S(1)}, bf16[32,3840]{1,0:T(8,128)(2,1)S(1)}, u32[]{:S(2)}, u32[]{:S(2)}) collective-permute-start(bf16[32,3840]{1,0:T(8,128)(2,1)S(1)} %collective-permute-done.refs_1_), channel_id=1, source_target_pairs={{0,8},{8,16},{16,24},{24,28},{28,20},{20,12},{12,4},{4,0},{1,9},{9... | collective-permute-start | bytes 737288 | tf_op jit(solution)/shard_map/ppermute | solution.py:325
  11.7 1.6 %collective-permute-start.7 = (bf16[32,3712]{1,0:T(8,128)(2,1)S(1)}, bf16[32,3712]{1,0:T(8,128)(2,1)S(1)}, u32[]{:S(2)}, u32[]{:S(2)}) collective-permute-start(bf16[32,3712]{1,0:T(8,128)(2,1)S(1)} %pad.8.refs_8_), channel_id=1, source_target_pairs={{0,8},{8,16},{16,24},{24,28},{28,20},{20,12},{12,4},{4,0},{1,9},{9... | collective-permute-start | bytes 712712 | tf_op jit(solution)/shard_map/ppermute | solution.py:325
  13.8 5.3 %collective-permute-done.1.refs_2_ = bf16[32,3840]{1,0:T(8,128)(2,1)S(1)} collective-permute-done((bf16[32,3840]{1,0:T(8,128)(2,1)S(1)}, bf16[32,3840]{1,0:T(8,128)(2,1)S(1)}, u32[]{:S(2)}, u32[]{:S(2)}) %collective-permute-start.1) | collective-permute-done | bytes 245792 | tf_op jit(solution)/shard_map/ppermute | solution.py:329
  19.1 2.0 %collective-permute-start.4 = (bf16[32,3840]{1,0:T(8,128)(2,1)S(1)}, bf16[32,3840]{1,0:T(8,128)(2,1)S(1)}, u32[]{:S(2)}, u32[]{:S(2)}) collective-permute-start(bf16[32,3840]{1,0:T(8,128)(2,1)S(1)} %collective-permute-done.2.refs_3_), channel_id=1, source_target_pairs={{0,8},{8,16},{16,24},{24,28},{28,20},{20,12},{12,4},{4,0},{1,9},{9... | collective-permute-start | bytes 737288 | tf_op jit(solution)/shard_map/ppermute | solution.py:325
  21.1 2.8 %collective-permute-done.7.refs_9_ = bf16[32,3712]{1,0:T(8,128)(2,1)S(1)} collective-permute-done((bf16[32,3712]{1,0:T(8,128)(2,1)S(1)}, bf16[32,3712]{1,0:T(8,128)(2,1)S(1)}, u32[]{:S(2)}, u32[]{:S(2)}) %collective-permute-start.7) | collective-permute-done | bytes 237600 | tf_op jit(solution)/shard_map/ppermute | solution.py:325
  23.9 1.8 %collective-permute-start.9 = (bf16[32,3712]{1,0:T(8,128)(2,1)S(1)}, bf16[32,3712]{1,0:T(8,128)(2,1)}, u32[]{:S(2)}, u32[]{:S(2)}) collective-permute-start(bf16[32,3712]{1,0:T(8,128)(2,1)S(1)} %collective-permute-done.7.refs_9_), channel_id=1, source_target_pairs={{0,8},{8,16},{16,24},{24,28},{28,20},{20,12},{12,4},{4,0},{1,9},{9... | collective-permute-start | bytes 712712 | tf_op jit(solution)/shard_map/ppermute | solution.py:325
  27.3 2.1 %collective-permute-done.3.refs_4_ = bf16[32,3840]{1,0:T(8,128)(2,1)S(1)} collective-permute-done((bf16[32,3840]{1,0:T(8,128)(2,1)S(1)}, bf16[32,3840]{1,0:T(8,128)(2,1)S(1)}, u32[]{:S(2)}, u32[]{:S(2)}) %collective-permute-start.3) | collective-permute-done | bytes 245792 | tf_op jit(solution)/shard_map/ppermute | solution.py:329
  29.4 2.0 %collective-permute-start.6 = (bf16[32,3840]{1,0:T(8,128)(2,1)S(1)}, bf16[32,3840]{1,0:T(8,128)(2,1)S(1)}, u32[]{:S(2)}, u32[]{:S(2)}) collective-permute-start(bf16[32,3840]{1,0:T(8,128)(2,1)S(1)} %collective-permute-done.4.refs_5_), channel_id=1, source_target_pairs={{0,8},{8,16},{16,24},{24,28},{28,20},{20,12},{12,4},{4,0},{1,9},{9... | collective-permute-start | bytes 737288 | tf_op jit(solution)/shard_map/ppermute | solution.py:325
  31.4 2.9 %collective-permute-done.9.refs_11_ = bf16[32,3712]{1,0:T(8,128)(2,1)} collective-permute-done((bf16[32,3712]{1,0:T(8,128)(2,1)S(1)}, bf16[32,3712]{1,0:T(8,128)(2,1)}, u32[]{:S(2)}, u32[]{:S(2)}) %collective-permute-start.9) | collective-permute-done | bytes 237600 | tf_op jit(solution)/shard_map/ppermute | solution.py:325
  34.4 1.8 %collective-permute-start.11 = (bf16[32,3712]{1,0:T(8,128)(2,1)}, bf16[32,3712]{1,0:T(8,128)(2,1)}, u32[]{:S(2)}, u32[]{:S(2)}) collective-permute-start(bf16[32,3712]{1,0:T(8,128)(2,1)} %collective-permute-done.9.refs_11_), channel_id=1, source_target_pairs={{0,8},{8,16},{16,24},{24,28},{28,20},{20,12},{12,4},{4,0},{1,9},{9... | collective-permute-start | bytes 712712 | tf_op jit(solution)/shard_map/ppermute | solution.py:325
  37.9 5.1 %collective-permute-done.11.refs_13_ = bf16[32,3712]{1,0:T(8,128)(2,1)} collective-permute-done((bf16[32,3712]{1,0:T(8,128)(2,1)}, bf16[32,3712]{1,0:T(8,128)(2,1)}, u32[]{:S(2)}, u32[]{:S(2)}) %collective-permute-start.11) | collective-permute-done | bytes 237600 | tf_op jit(solution)/shard_map/ppermute | solution.py:325
  45.4 21.1 %lead_kernel.1 = (f32[2,2880,128]{2,1,0:T(8,128)S(1)}, bf16[7552,256]{1,0:T(8,128)(2,1)S(1)}, s16[2,15,48,256]{3,2,1,0:T(8,128)(2,1)S(1)}) custom-call(s32[1]{0:T(128)} %bitcast.me_ref, s32[1]{0:T(128)} %bitcast.1.rep_ref, bf16[32,3840]{1,0:T(8,128)(2,1)S(1)} %slice.9.refs_0_, bf16[32,3840]{1,0:T(8,128)(2,1)S(1)} %collective-permute-done.refs_1_, ...), custom_call_target="tpu_custom_call" | custom-call | flops 10950279168 | bytes 42774528 | tf_op jit(solution)/shard_map/lead_kernel/pallas_call | solution.py:265
  66.6 2.2 %collective-permute-done.14.got_ref = s16[2,15,48,256]{3,2,1,0:T(8,128)(2,1)S(1)} collective-permute-done((s16[2,15,48,256]{3,2,1,0:T(8,128)(2,1)S(1)}, s16[2,15,48,256]{3,2,1,0:T(8,128)(2,1)S(1)}, u32[]{:S(2)}, u32[]{:S(2)}) %collective-permute-start.14) | collective-permute-done | bytes 737312 | tf_op jit(solution)/shard_map/ppermute | solution.py:394
  71.2 6.9 %rest_kernel.1 = (f32[2,964,128]{2,1,0:T(8,128)S(1)}, s16[2,15,16,256]{3,2,1,0:T(8,128)(2,1)S(1)}) custom-call(s32[1]{0:T(128)} %bitcast.1.rep_ref, bf16[7552,256]{1,0:T(8,128)(2,1)S(1)} %get-tuple-element.23.turned, bf16[3600,7500]{1,0:T(8,128)(2,1)} %bitcast.14, bf16[3600,128]{1,0:T(8,128)(2,1)S(1)} %pad.9.refs_17_.edge_ref), custom_call_target="tpu_custom_call" | custom-call | flops 3031433216 | bytes 11841536 | tf_op jit(solution)/shard_map/rest_kernel/pallas_call | solution.py:265
  82.8 3.1 %collective-permute-done.16.got_ref = s16[15,16,256]{2,1,0:T(8,128)(2,1)S(1)} collective-permute-done((s16[15,16,256]{2,1,0:T(8,128)(2,1)S(1)}, s16[15,16,256]{2,1,0:T(8,128)(2,1)S(1)}, u32[]{:S(2)}, u32[]{:S(2)}) %collective-permute-start.16) | collective-permute-done | bytes 122912 | tf_op jit(solution)/shard_map/ppermute | solution.py:414
  87.7 1.6 %collective-permute-start.19 = (s16[4,64,128]{2,1,0:T(8,128)(2,1)S(1)}, s16[4,64,128]{2,1,0:T(8,128)(2,1)S(1)}, u32[]{:S(2)}, u32[]{:S(2)}) collective-permute-start(s16[4,64,128]{2,1,0:T(8,128)(2,1)S(1)} %get-tuple-element.29), channel_id=1, source_target_pairs={{0,8},{4,12},{8,0},{12,4},{16,24},{20,28},{24,16},{28,20},{1,9},{5... | collective-permute-start | bytes 196616 | tf_op jit(solution)/shard_map/ppermute | solution.py:436
  90.2 2.6 %collective-permute-start.21 = (s16[4,64,128]{2,1,0:T(8,128)(2,1)S(1)}, s16[4,64,128]{2,1,0:T(8,128)(2,1)S(1)}, u32[]{:S(2)}, u32[]{:S(2)}) collective-permute-start(s16[4,64,128]{2,1,0:T(8,128)(2,1)S(1)} %get-tuple-element.31), channel_id=1, source_target_pairs={{0,16},{4,20},{8,24},{12,28},{16,0},{20,4},{24,8},{28,12},{1,17},{... | collective-permute-start | bytes 196616 | tf_op jit(solution)/shard_map/ppermute | solution.py:436
  93.5 3.6 %collective-permute-start.23 = (s16[4,64,128]{2,1,0:T(8,128)(2,1)S(1)}, s16[4,64,128]{2,1,0:T(8,128)(2,1)S(1)}, u32[]{:S(2)}, u32[]{:S(2)}) collective-permute-start(s16[4,64,128]{2,1,0:T(8,128)(2,1)S(1)} %get-tuple-element.33), channel_id=1, source_target_pairs={{0,24},{4,28},{8,16},{12,20},{16,8},{20,12},{24,0},{28,4},{1,25},{... | collective-permute-start | bytes 196616 | tf_op jit(solution)/shard_map/ppermute | solution.py:436
  98.7 3.7 %collective-permute-done.22.refs_5_ = s16[4,64,128]{2,1,0:T(8,128)(2,1)S(1)} collective-permute-done((s16[4,64,128]{2,1,0:T(8,128)(2,1)S(1)}, s16[4,64,128]{2,1,0:T(8,128)(2,1)S(1)}, u32[]{:S(2)}, u32[]{:S(2)}) %collective-permute-start.22) | collective-permute-done | bytes 65568 | tf_op jit(solution)/shard_map/ppermute | solution.py:436
  102.4 1.8 %collective-permute-done.24.refs_7_ = s16[4,64,128]{2,1,0:T(8,128)(2,1)S(1)} collective-permute-done((s16[4,64,128]{2,1,0:T(8,128)(2,1)S(1)}, s16[4,64,128]{2,1,0:T(8,128)(2,1)S(1)}, u32[]{:S(2)}, u32[]{:S(2)}) %collective-permute-start.24) | collective-permute-done | bytes 65568 | tf_op jit(solution)/shard_map/ppermute | solution.py:436
  104.2 2.2 %update_kernel.1 = f32[15,32,480]{2,1,0:T(8,128)} custom-call(s32[1]{0:T(128)} %bitcast.me_ref, f32[15]{0:T(128)S(1)} %copy-done.7, s32[15]{0:T(128)S(1)} %copy-done.8, s16[4,64,128]{2,1,0:T(8,128)(2,1)S(1)} %get-tuple-element.27.refs_0_, s16[4,64,128]{2,1,0:T(8,128)(2,1)S(1)} %collective-permute-done.18.refs_1_, ...), custom_call_target="tpu_custom_call" | custom-call | flops 10000000 | bytes 4000000 | tf_op jit(solution)/shard_map/update_kernel/pallas_call | solution.py:265
  (64 shorter events, 20.2 us)
Async XLA Ops:
  1.0 9.0 %collective-permute-start = (bf16[32,3840]{1,0:T(8,128)(2,1)S(1)}, bf16[32,3840]{1,0:T(8,128)(2,1)S(1)}, u32[]{:S(2)}, u32[]{:S(2)}) collective-permute-start(bf16[32,3840]{1,0:T(8,128)(2,1)S(1)} %slice.9.refs_0_), channel_id=1, source_target_pairs={{0,8},{8,16},{16,24},{24,28},{28,20},{20,12},{12,4},{4,0},{1,9},{9... | collective-permute-start | bytes 737288 | tf_op jit(solution)/shard_map/ppermute | solution.py:325
  5.0 8.8 %collective-permute-start.8 = (bf16[32,3712]{1,0:T(8,128)(2,1)S(1)}, bf16[32,3712]{1,0:T(8,128)(2,1)S(1)}, u32[]{:S(2)}, u32[]{:S(2)}) collective-permute-start(bf16[32,3712]{1,0:T(8,128)(2,1)S(1)} %pad.8.refs_8_), channel_id=1, source_target_pairs={{8,0},{16,8},{24,16},{28,24},{20,28},{12,20},{4,12},{0,4},{9,1},{1... | collective-permute-start | bytes 712712 | tf_op jit(solution)/shard_map/ppermute | solution.py:329
  5.1 14.0 %collective-permute-start.1 = (bf16[32,3840]{1,0:T(8,128)(2,1)S(1)}, bf16[32,3840]{1,0:T(8,128)(2,1)S(1)}, u32[]{:S(2)}, u32[]{:S(2)}) collective-permute-start(bf16[32,3840]{1,0:T(8,128)(2,1)S(1)} %slice.9.refs_0_), channel_id=1, source_target_pairs={{8,0},{16,8},{24,16},{28,24},{20,28},{12,20},{4,12},{0,4},{9,1},{1... | collective-permute-start | bytes 737288 | tf_op jit(solution)/shard_map/ppermute | solution.py:329
  9.9 9.1 %collective-permute-start.2 = (bf16[32,3840]{1,0:T(8,128)(2,1)S(1)}, bf16[32,3840]{1,0:T(8,128)(2,1)S(1)}, u32[]{:S(2)}, u32[]{:S(2)}) collective-permute-start(bf16[32,3840]{1,0:T(8,128)(2,1)S(1)} %collective-permute-done.refs_1_), channel_id=1, source_target_pairs={{0,8},{8,16},{16,24},{24,28},{28,20},{20,12},{12,4},{4,0},{1,9},{9... | collective-permute-start | bytes 737288 | tf_op jit(solution)/shard_map/ppermute | solution.py:325
  11.7 12.2 %collective-permute-start.7 = (bf16[32,3712]{1,0:T(8,128)(2,1)S(1)}, bf16[32,3712]{1,0:T(8,128)(2,1)S(1)}, u32[]{:S(2)}, u32[]{:S(2)}) collective-permute-start(bf16[32,3712]{1,0:T(8,128)(2,1)S(1)} %pad.8.refs_8_), channel_id=1, source_target_pairs={{0,8},{8,16},{16,24},{24,28},{28,20},{20,12},{12,4},{4,0},{1,9},{9... | collective-permute-start | bytes 712712 | tf_op jit(solution)/shard_map/ppermute | solution.py:325
  13.8 12.6 %collective-permute-start.10 = (bf16[32,3712]{1,0:T(8,128)(2,1)S(1)}, bf16[32,3712]{1,0:T(8,128)(2,1)S(1)}, u32[]{:S(2)}, u32[]{:S(2)}) collective-permute-start(bf16[32,3712]{1,0:T(8,128)(2,1)S(1)} %collective-permute-done.8.refs_10_), channel_id=1, source_target_pairs={{8,0},{16,8},{24,16},{28,24},{20,28},{12,20},{4,12},{0,4},{9,1},{1... | collective-permute-start | bytes 712712 | tf_op jit(solution)/shard_map/ppermute | solution.py:329
  19.1 10.4 %collective-permute-start.3 = (bf16[32,3840]{1,0:T(8,128)(2,1)S(1)}, bf16[32,3840]{1,0:T(8,128)(2,1)S(1)}, u32[]{:S(2)}, u32[]{:S(2)}) collective-permute-start(bf16[32,3840]{1,0:T(8,128)(2,1)S(1)} %collective-permute-done.1.refs_2_), channel_id=1, source_target_pairs={{8,0},{16,8},{24,16},{28,24},{20,28},{12,20},{4,12},{0,4},{9,1},{1... | collective-permute-start | bytes 737288 | tf_op jit(solution)/shard_map/ppermute | solution.py:329
  19.1 10.4 %collective-permute-start.4 = (bf16[32,3840]{1,0:T(8,128)(2,1)S(1)}, bf16[32,3840]{1,0:T(8,128)(2,1)S(1)}, u32[]{:S(2)}, u32[]{:S(2)}) collective-permute-start(bf16[32,3840]{1,0:T(8,128)(2,1)S(1)} %collective-permute-done.2.refs_3_), channel_id=1, source_target_pairs={{0,8},{8,16},{16,24},{24,28},{28,20},{20,12},{12,4},{4,0},{1,9},{9... | collective-permute-start | bytes 737288 | tf_op jit(solution)/shard_map/ppermute | solution.py:325
  23.9 10.5 %collective-permute-start.9 = (bf16[32,3712]{1,0:T(8,128)(2,1)S(1)}, bf16[32,3712]{1,0:T(8,128)(2,1)}, u32[]{:S(2)}, u32[]{:S(2)}) collective-permute-start(bf16[32,3712]{1,0:T(8,128)(2,1)S(1)} %collective-permute-done.7.refs_9_), channel_id=1, source_target_pairs={{0,8},{8,16},{16,24},{24,28},{28,20},{20,12},{12,4},{4,0},{1,9},{9... | collective-permute-start | bytes 712712 | tf_op jit(solution)/shard_map/ppermute | solution.py:325
  26.4 9.8 %collective-permute-start.12 = (bf16[32,3712]{1,0:T(8,128)(2,1)S(1)}, bf16[32,3712]{1,0:T(8,128)(2,1)}, u32[]{:S(2)}, u32[]{:S(2)}) collective-permute-start(bf16[32,3712]{1,0:T(8,128)(2,1)S(1)} %collective-permute-done.10.refs_12_), channel_id=1, source_target_pairs={{8,0},{16,8},{24,16},{28,24},{20,28},{12,20},{4,12},{0,4},{9,1},{1... | collective-permute-start | bytes 712712 | tf_op jit(solution)/shard_map/ppermute | solution.py:329
  29.4 13.6 %collective-permute-start.5 = (bf16[32,3840]{1,0:T(8,128)(2,1)S(1)}, bf16[32,3840]{1,0:T(8,128)(2,1)S(1)}, u32[]{:S(2)}, u32[]{:S(2)}) collective-permute-start(bf16[32,3840]{1,0:T(8,128)(2,1)S(1)} %collective-permute-done.3.refs_4_), channel_id=1, source_target_pairs={{8,0},{16,8},{24,16},{28,24},{20,28},{12,20},{4,12},{0,4},{9,1},{1... | collective-permute-start | bytes 737288 | tf_op jit(solution)/shard_map/ppermute | solution.py:329
  29.4 14.1 %collective-permute-start.6 = (bf16[32,3840]{1,0:T(8,128)(2,1)S(1)}, bf16[32,3840]{1,0:T(8,128)(2,1)S(1)}, u32[]{:S(2)}, u32[]{:S(2)}) collective-permute-start(bf16[32,3840]{1,0:T(8,128)(2,1)S(1)} %collective-permute-done.4.refs_5_), channel_id=1, source_target_pairs={{0,8},{8,16},{16,24},{24,28},{28,20},{20,12},{12,4},{4,0},{1,9},{9... | collective-permute-start | bytes 737288 | tf_op jit(solution)/shard_map/ppermute | solution.py:325
  34.4 8.6 %collective-permute-start.11 = (bf16[32,3712]{1,0:T(8,128)(2,1)}, bf16[32,3712]{1,0:T(8,128)(2,1)}, u32[]{:S(2)}, u32[]{:S(2)}) collective-permute-start(bf16[32,3712]{1,0:T(8,128)(2,1)} %collective-permute-done.9.refs_11_), channel_id=1, source_target_pairs={{0,8},{8,16},{16,24},{24,28},{28,20},{20,12},{12,4},{4,0},{1,9},{9... | collective-permute-start | bytes 712712 | tf_op jit(solution)/shard_map/ppermute | solution.py:325
  36.2 7.3 %collective-permute-start.13 = (bf16[32,3712]{1,0:T(8,128)(2,1)}, bf16[32,3712]{1,0:T(8,128)(2,1)}, u32[]{:S(2)}, u32[]{:S(2)}) collective-permute-start(bf16[32,3712]{1,0:T(8,128)(2,1)} %collective-permute-done.12.refs_14_), channel_id=1, source_target_pairs={{8,0},{16,8},{24,16},{28,24},{20,28},{12,20},{4,12},{0,4},{9,1},{1... | collective-permute-start | bytes 712712 | tf_op jit(solution)/shard_map/ppermute | solution.py:329
  66.5 2.3 %collective-permute-start.14 = (s16[2,15,48,256]{3,2,1,0:T(8,128)(2,1)S(1)}, s16[2,15,48,256]{3,2,1,0:T(8,128)(2,1)S(1)}, u32[]{:S(2)}, u32[]{:S(2)}) collective-permute-start(s16[2,15,48,256]{3,2,1,0:T(8,128)(2,1)S(1)} %get-tuple-element.22), channel_id=1, source_target_pairs={{0,1},{1,0},{2,3},{3,2},{4,5},{5,4},{6,7},{7,6},{8,9},{9,8},{10,11... | collective-permute-start | bytes 2211848 | tf_op jit(solution)/shard_map/ppermute | solution.py:394
  69.6 12.1 %collective-permute-start.17 = (s16[15,48,256]{2,1,0:T(8,128)(2,1)S(1)}, s16[15,48,256]{2,1,0:T(8,128)(2,1)S(1)}, u32[]{:S(2)}, u32[]{:S(2)}) collective-permute-start(s16[15,48,256]{2,1,0:T(8,128)(2,1)S(1)} %second_send_kernel.2), channel_id=1, source_target_pairs={{0,2},{1,3},{2,0},{3,1},{4,6},{5,7},{6,4},{7,5},{8,10},{9,11},{10,... | collective-permute-start | bytes 1105928 | tf_op jit(solution)/shard_map/ppermute | solution.py:414
  80.5 5.4 %collective-permute-start.16 = (s16[15,16,256]{2,1,0:T(8,128)(2,1)S(1)}, s16[15,16,256]{2,1,0:T(8,128)(2,1)S(1)}, u32[]{:S(2)}, u32[]{:S(2)}) collective-permute-start(s16[15,16,256]{2,1,0:T(8,128)(2,1)S(1)} %second_send_kernel.3), channel_id=1, source_target_pairs={{0,2},{1,3},{2,0},{3,1},{4,6},{5,7},{6,4},{7,5},{8,10},{9,11},{10,... | collective-permute-start | bytes 368648 | tf_op jit(solution)/shard_map/ppermute | solution.py:414
  86.7 6.8 %collective-permute-start.18 = (s16[4,64,128]{2,1,0:T(8,128)(2,1)S(1)}, s16[4,64,128]{2,1,0:T(8,128)(2,1)S(1)}, u32[]{:S(2)}, u32[]{:S(2)}) collective-permute-start(s16[4,64,128]{2,1,0:T(8,128)(2,1)S(1)} %get-tuple-element.28), channel_id=1, source_target_pairs={{0,4},{4,0},{8,12},{12,8},{16,20},{20,16},{24,28},{28,24},{1,5},{5... | collective-permute-start | bytes 196616 | tf_op jit(solution)/shard_map/ppermute | solution.py:436
  87.7 9.5 %collective-permute-start.19 = (s16[4,64,128]{2,1,0:T(8,128)(2,1)S(1)}, s16[4,64,128]{2,1,0:T(8,128)(2,1)S(1)}, u32[]{:S(2)}, u32[]{:S(2)}) collective-permute-start(s16[4,64,128]{2,1,0:T(8,128)(2,1)S(1)} %get-tuple-element.29), channel_id=1, source_target_pairs={{0,8},{4,12},{8,0},{12,4},{16,24},{20,28},{24,16},{28,20},{1,9},{5... | collective-permute-start | bytes 196616 | tf_op jit(solution)/shard_map/ppermute | solution.py:436
  89.2 8.8 %collective-permute-start.20 = (s16[4,64,128]{2,1,0:T(8,128)(2,1)S(1)}, s16[4,64,128]{2,1,0:T(8,128)(2,1)S(1)}, u32[]{:S(2)}, u32[]{:S(2)}) collective-permute-start(s16[4,64,128]{2,1,0:T(8,128)(2,1)S(1)} %get-tuple-element.30), channel_id=1, source_target_pairs={{0,12},{4,8},{8,4},{12,0},{16,28},{20,24},{24,20},{28,16},{1,13},{... | collective-permute-start | bytes 196616 | tf_op jit(solution)/shard_map/ppermute | solution.py:436
  90.2 8.5 %collective-permute-start.21 = (s16[4,64,128]{2,1,0:T(8,128)(2,1)S(1)}, s16[4,64,128]{2,1,0:T(8,128)(2,1)S(1)}, u32[]{:S(2)}, u32[]{:S(2)}) collective-permute-start(s16[4,64,128]{2,1,0:T(8,128)(2,1)S(1)} %get-tuple-element.31), channel_id=1, source_target_pairs={{0,16},{4,20},{8,24},{12,28},{16,0},{20,4},{24,8},{28,12},{1,17},{... | collective-permute-start | bytes 196616 | tf_op jit(solution)/shard_map/ppermute | solution.py:436
  92.8 9.6 %collective-permute-start.22 = (s16[4,64,128]{2,1,0:T(8,128)(2,1)S(1)}, s16[4,64,128]{2,1,0:T(8,128)(2,1)S(1)}, u32[]{:S(2)}, u32[]{:S(2)}) collective-permute-start(s16[4,64,128]{2,1,0:T(8,128)(2,1)S(1)} %get-tuple-element.32), channel_id=1, source_target_pairs={{0,20},{4,16},{8,28},{12,24},{16,4},{20,0},{24,12},{28,8},{1,21},{... | collective-permute-start | bytes 196616 | tf_op jit(solution)/shard_map/ppermute | solution.py:436
  93.5 8.9 %collective-permute-start.23 = (s16[4,64,128]{2,1,0:T(8,128)(2,1)S(1)}, s16[4,64,128]{2,1,0:T(8,128)(2,1)S(1)}, u32[]{:S(2)}, u32[]{:S(2)}) collective-permute-start(s16[4,64,128]{2,1,0:T(8,128)(2,1)S(1)} %get-tuple-element.33), channel_id=1, source_target_pairs={{0,24},{4,28},{8,16},{12,20},{16,8},{20,12},{24,0},{28,4},{1,25},{... | collective-permute-start | bytes 196616 | tf_op jit(solution)/shard_map/ppermute | solution.py:436
  97.1 7.1 %collective-permute-start.24 = (s16[4,64,128]{2,1,0:T(8,128)(2,1)S(1)}, s16[4,64,128]{2,1,0:T(8,128)(2,1)S(1)}, u32[]{:S(2)}, u32[]{:S(2)}) collective-permute-start(s16[4,64,128]{2,1,0:T(8,128)(2,1)S(1)} %get-tuple-element.34), channel_id=1, source_target_pairs={{0,28},{4,24},{8,20},{12,16},{16,12},{20,8},{24,4},{28,0},{1,29},{... | collective-permute-start | bytes 196616 | tf_op jit(solution)/shard_map/ppermute | solution.py:436
  (12 other events, 158.2 us)

commit v6 on v5

--- a/solution.py
+++ b/solution.py
@@ -11,6 +11,7 @@
 LANES = 128
 K_BLOCK = 3840
 C_BLOCK = 480
+SLOTS = 3
 COPIES = 4
 FIRST_PART = 47
 STEPS = 8.0
@@ -81,23 +82,24 @@
 
     def copies(step):
         start = jnp.minimum(step * block, many - block)
-        return coupling_copies(coupling_ref, edge_ref, buffer, sems, low, start, lax.rem(step, 2))
-
-    for copy in copies(jnp.int32(0)):
-        copy.start()
+        return coupling_copies(coupling_ref, edge_ref, buffer, sems, low, start, lax.rem(step, SLOTS))
+
+    for ahead in range(min(SLOTS - 1, steps)):
+        for copy in copies(jnp.int32(ahead)):
+            copy.start()
     if before is not None:
         before()
 
     def step(number, carry):
-        @pl.when(number + 1 < steps)
+        @pl.when(number + SLOTS - 1 < steps)
         def _():
-            for copy in copies(number + 1):
+            for copy in copies(number + SLOTS - 1):
                 copy.start()
 
         for copy in copies(number):
             copy.wait()
         total = jnp.dot(
-            buffer[lax.rem(number, 2)], turned[...], preferred_element_type=jnp.float32
+            buffer[lax.rem(number, SLOTS)], turned[...], preferred_element_type=jnp.float32
         )
         rows = pl.ds(pl.multiple_of(jnp.minimum(number * block, many - block), 4), block)
         for part in range(total_ref.shape[0]):
@@ -107,15 +109,13 @@
     lax.fori_loop(0, steps, step, 0)
 
 
-def gather_pieces(me_ref, offsets, edges, pieces, gathered, turned, sems):
+def turn_pieces(edges, pieces, gathered, sems, turned, lanes):
     rows = pieces[0].shape[0]
-    grid_size = gathered.shape[0] // rows
-    place = walk_place(me_ref[0], grid_size)
+    slots = gathered.shape[0] // rows
     copies = []
-    for number, (offset, edge, piece) in enumerate(zip(offsets, edges, pieces)):
-        source = walk_index(lax.rem(place + offset + grid_size, grid_size), grid_size)
+    for number, (edge, piece) in enumerate(zip(edges, pieces)):
         target = gathered.at[
-            pl.ds(pl.multiple_of(source * rows, rows), rows), pl.ds(edge, piece.shape[1])
+            pl.ds(number % slots * rows, rows), pl.ds(edge, piece.shape[1])
         ]
         copies.append(pltpu.make_async_copy(piece, target, sems.at[number]))
     for copy in copies:
@@ -123,22 +123,24 @@
     for copy in copies:
         copy.wait()
     for at in range(0, turned.shape[0], LANES):
-        turned[at : at + LANES, :] = gathered[:, at : at + LANES].T
-
-
-def lead_kernel(offsets, edges, columns, span, me_ref, rep_ref, *refs):
-    pieces, refs = refs[: len(offsets)], refs[len(offsets) :]
+        turned[at : at + LANES, lanes : lanes + slots * rows] = gathered[:, at : at + LANES].T
+
+
+def near_kernel(edges, *refs):
+    *pieces, turned, gathered, sems = refs
+    turn_pieces(edges, pieces, gathered, sems, turned, 0)
+
+
+def lead_kernel(edges, columns, span, rep_ref, near, *refs):
+    pieces, refs = refs[: len(edges)], refs[len(edges) :]
     coupling_ref, edge_ref, total, turned, send, gathered, sems, buffer, buffer_sems = refs
-    multiply(
-        coupling_ref,
-        edge_ref,
-        buffer,
-        buffer_sems,
-        turned,
-        total,
-        columns,
-        lambda: gather_pieces(me_ref, offsets, edges, pieces, gathered, turned, sems),
-    )
+
+    def before():
+        lanes = near.shape[1]
+        turned[:, :lanes] = near[...]
+        turn_pieces(edges, pieces, gathered, sems, turned, lanes)
+
+    multiply(coupling_ref, edge_ref, buffer, buffer_sems, turned, total, columns, before)
     first_send(span, rep_ref, total, send)
 
 
@@ -212,18 +214,18 @@
     pack_rows(count, rows_dev, kept_ref, got_ref, stage)
 
 
-def last_send_kernel(count, rows_dev, parts, me_ref, kept_ref, got_ref, *refs):
+def last_send_kernel(count, rows_dev, parts, kept_ref, got_ref, *refs):
     earlier, targets, stage = refs[: parts - 1], refs[parts - 1 : -1], refs[-1]
     pack_rows(count, rows_dev, kept_ref, got_ref, stage)
     for number, target in enumerate(targets):
         at = 0
         for source in (*earlier, stage):
             bp = source.shape[2]
-            target[:, at : at + bp, :] = source[me_ref[0] ^ number]
+            target[:, at : at + bp, :] = source[number]
             at += bp
 
 
-def update_kernel(counts, bps, width, rows_dev, me_ref, occ_energy_ref, occ_irrep_ref, *refs):
+def update_kernel(counts, bps, width, rows_dev, order, me_ref, occ_energy_ref, occ_irrep_ref, *refs):
     (
         integrals_ref,
         row_energy_ref,
@@ -235,8 +237,11 @@
         stage,
     ) = refs[-8:]
     arrived = refs[:-8]
-    for number, got_ref in enumerate(arrived):
-        blocks[me_ref[0] ^ number] = got_ref[...]
+    grid_size = len(arrived)
+    place = walk_place(me_ref[0], grid_size)
+    for offset, got_ref in zip(order, arrived):
+        source = walk_index(lax.rem(place - offset + grid_size, grid_size), grid_size)
+        blocks[source] = got_ref[...]
     pack = LANES // rows_dev
     for jj in range(blocks.shape[1]):
         at = 0
@@ -309,27 +314,28 @@
     back = [(b, a) for a, b in onward]
 
     longer = grid_size // 2
-    pieces, offsets, edges = [], [], []
+    order = [0]
+    for hop in range(1, longer):
+        order += [-hop, hop]
+    order.append(longer)
+    near, far, near_edges, far_edges = [], [], [], []
     for number, at in enumerate(range(0, depth, K_BLOCK)):
         own = amplitudes[:, at : at + K_BLOCK]
         size = own.shape[1]
         own = jnp.pad(own, ((0, 0), (0, ceil_to(size, LANES) - size)))
-        hops = (longer, grid_size - 1 - longer)
-        if number % 2:
-            hops = hops[::-1]
         ahead = behind = own
-        pieces.append(own)
-        offsets.append(0)
+        pieces = [own]
         for hop in range(1, longer + 1):
-            if hop <= hops[0]:
+            if hop < longer or number % 2 == 0:
                 ahead = lax.ppermute(ahead, "grid", onward)
                 pieces.append(ahead)
-                offsets.append(-hop)
-            if hop <= hops[1]:
+            if hop < longer or number % 2 == 1:
                 behind = lax.ppermute(behind, "grid", back)
                 pieces.append(behind)
-                offsets.append(hop)
-        edges += [at] * grid_size
+        near += pieces[:longer]
+        far += pieces[longer:]
+        near_edges += [at] * longer
+        far_edges += [at] * longer
 
     counts = [FIRST_PART, count - FIRST_PART] if count > FIRST_PART else [count]
     firsts = [0, FIRST_PART][: len(counts)]
@@ -351,32 +357,42 @@
     low_pairs = [(i, i ^ 1) for i in range(lax.axis_size("rep"))]
     high_pairs = [(i, i ^ 2) for i in range(lax.axis_size("rep"))]
 
+    half = slab // 2
+    turn_scratch = [
+        pltpu.VMEM((half, deep), jnp.bfloat16),
+        pltpu.SemaphoreType.DMA((len(near),)),
+    ]
+    near = local_call(
+        functools.partial(near_kernel, tuple(near_edges)),
+        jax.ShapeDtypeStruct((deep, half), jnp.bfloat16),
+        "a" * len(near),
+        near,
+        turn_scratch,
+        cost=(10**8, 4 * half * deep),
+        room=2 * half * deep + (2 * half * deep if slab > 2 * LANES else 0),
+    )
     totals, sends, got = [], [], []
     for part, (cols, span, bp) in enumerate(zip(parts, spans, bps)):
         block = min(C_BLOCK, ceil_to(cols[1] // 2, 16))
         scratch = [
-            pltpu.VMEM((2, block, deep), jnp.bfloat16),
-            pltpu.SemaphoreType.DMA((2, COPIES + 1)),
+            pltpu.VMEM((SLOTS, block, deep), jnp.bfloat16),
+            pltpu.SemaphoreType.DMA((SLOTS, COPIES + 1)),
         ]
         cost = (2 * cols[1] * deep * slab, 2 * cols[1] * deep)
-        room = 4 * block * deep + (2 * slab * deep if part == 0 else 0)
+        room = 2 * SLOTS * block * deep + (slab * deep if part == 0 else 0)
         if slab > 2 * LANES:
-            room += 2 * slab * deep + 4 * slab * total_shapes[part].shape[1]
+            room += 3 * slab * deep + 4 * slab * total_shapes[part].shape[1]
         if part == 0:
             total, turned, send = local_call(
-                functools.partial(lead_kernel, tuple(offsets), tuple(edges), cols, span),
+                functools.partial(lead_kernel, tuple(far_edges), cols, span),
                 (
                     total_shapes[0],
                     jax.ShapeDtypeStruct((deep, slab), jnp.bfloat16),
                     send_shapes[0],
                 ),
-                "ss" + "a" * (len(pieces) + 2),
-                (me, rep, *pieces, coupling, edge),
-                [
-                    pltpu.VMEM((slab, deep), jnp.bfloat16),
-                    pltpu.SemaphoreType.DMA((len(pieces),)),
-                    *scratch,
-                ],
+                "sv" + "a" * (len(far) + 2),
+                (rep, near, *far, coupling, edge),
+                [*turn_scratch, *scratch],
                 cost=cost,
                 room=room,
             )
@@ -428,17 +444,20 @@
     targets = local_call(
         functools.partial(last_send_kernel, counts[-1], rows_dev, len(counts)),
         (jax.ShapeDtypeStruct((groups, sum(bps), LANES), jnp.int16),) * grid_size,
-        "svv" + "v" * len(staged),
-        (me, kept[-1], got[-1], *staged),
+        "vv" + "v" * len(staged),
+        (kept[-1], got[-1], *staged),
         [pltpu.VMEM((grid_size, groups, bps[-1], LANES), jnp.int16)],
     )
-    arrived = [targets[0]] + [
-        lax.ppermute(target, "grid", [(g, g ^ number) for g in range(grid_size)])
-        for number, target in list(enumerate(targets))[1:]
-    ]
+    arrived = list(targets)
+    for number in range(1, grid_size)[::-1]:
+        arrived[number] = lax.ppermute(
+            targets[number],
+            "grid",
+            [(walk[i], walk[(i + order[number]) % grid_size]) for i in range(grid_size)],
+        )
 
     updated = local_call(
-        functools.partial(update_kernel, counts, bps, width, rows_dev),
+        functools.partial(update_kernel, counts, bps, width, rows_dev, order),
         jax.ShapeDtypeStruct((width, rows_dev, count * grid_size), jnp.float32),
         "sss" + "v" * (len(arrived) + 5),
         (

time: 107 us -> 99.8 us (0.933)
  waiting for transfers between devices: 35.1 us -> 30.3 us
  Pallas kernels: 34.1 us -> 32.1 us
  local copies, waits for them, and re-layouts: 6.85 us -> 5.21 us
  starting transfers between devices: 30.1 us -> 31.7 us
    ppermute x7, waiting for transfers between devices: 13.8 us -> 10.7 us  [body(): ahead = lax.ppermute(ahead, 'grid', onward)]
    ppermute x7, waiting for transfers between devices: 6.13 us -> 3.8 us  [body(): lax.ppermute(targets[number], 'grid', [(walk[i], walk[(i + order[number])...]
    pallas_call x9 -> x10, Pallas kernels: 34.1 us -> 32.1 us  [local_call(): pl.pallas_call(kernel, out_shape=out_shape, in_specs=[pl.BlockSpec(memory...]
    unnamed x22 -> x18, local copies, waits for them, and re-layouts: 3.31 us -> 1.67 us
    ppermute x7, starting transfers between devices: 11.2 us -> 12.8 us  [body(): lax.ppermute(targets[number], 'grid', [(walk[i], walk[(i + order[number])...]
  transfers between devices with their start and end apart: 25 -> 25, of which waited for: 14 -> 12; matrix products, arithmetic and copies ran while one was open for 2% -> 3% of each run, Pallas kernels for 9% -> 12%
where the time goes in v6:
time: 99.8 us; the launch traced here: 99.6 us
  Pallas kernels  32.1 us (32%)
  starting transfers between devices  31.7 us (32%)
  waiting for transfers between devices  30.3 us (30%)
  local copies, waits for them, and re-layouts  5.21 us (5%)
    pallas_call x10, Pallas kernels, local_call(): pl.pallas_call(kernel, out_shape=out_shape, in_specs=[pl.BlockSpec(memory...  32.1 us
    ppermute x7, starting transfers between devices, body(): ahead = lax.ppermute(ahead, 'grid', onward)  14.1 us
    ppermute x7, starting transfers between devices, body(): lax.ppermute(targets[number], 'grid', [(walk[i], walk[(i + order[number])...  12.8 us
    ppermute x7, waiting for transfers between devices, body(): ahead = lax.ppermute(ahead, 'grid', onward)  10.7 us
    ppermute x7, waiting for transfers between devices, body(): behind = lax.ppermute(behind, 'grid', back)  9.02 us
    ppermute x7, waiting for transfers between devices, body(): lax.ppermute(targets[number], 'grid', [(walk[i], walk[(i + order[number])...  3.8 us
    ppermute x2, waiting for transfers between devices, body(): arrived = lax.ppermute(send, 'rep', low_pairs)  3.7 us
    ppermute x2, waiting for transfers between devices, body(): got = [lax.ppermute(send, 'rep', high_pairs) for send in sends]  3.15 us
  transfers between devices with their start and end apart: 25, of which 12 were waited for; matrix products, arithmetic and copies ran while one was open for 3% of the time, Pallas kernels for 12%

profile of v6, /device:TPU:0, one launch (start us, length us, event | category | flops | bytes accessed | tf_op | source)
XLA Modules:
  0.0 99.6 jit_solution(5926986242660189386)
XLA Ops:
  1.0 3.1 %collective-permute-start = (bf16[32,3840]{1,0:T(8,128)(2,1)S(1)}, bf16[32,3840]{1,0:T(8,128)(2,1)S(1)}, u32[]{:S(2)}, u32[]{:S(2)}) collective-permute-start(bf16[32,3840]{1,0:T(8,128)(2,1)S(1)} %slice.9.refs_0_), channel_id=1, source_target_pairs={{0,8},{8,16},{16,24},{24,28},{28,20},{20,12},{12,4},{4,0},{1,9},{9... | collective-permute-start | bytes 737288 | tf_op jit(solution)/shard_map/ppermute | solution.py:330
  5.1 2.0 %collective-permute-start.1 = (bf16[32,3840]{1,0:T(8,128)(2,1)S(1)}, bf16[32,3840]{1,0:T(8,128)(2,1)S(1)}, u32[]{:S(2)}, u32[]{:S(2)}) collective-permute-start(bf16[32,3840]{1,0:T(8,128)(2,1)S(1)} %slice.9.refs_0_), channel_id=1, source_target_pairs={{8,0},{16,8},{24,16},{28,24},{20,28},{12,20},{4,12},{0,4},{9,1},{1... | collective-permute-start | bytes 737288 | tf_op jit(solution)/shard_map/ppermute | solution.py:333
  7.1 2.9 %collective-permute-done.refs_1_ = bf16[32,3840]{1,0:T(8,128)(2,1)S(1)} collective-permute-done((bf16[32,3840]{1,0:T(8,128)(2,1)S(1)}, bf16[32,3840]{1,0:T(8,128)(2,1)S(1)}, u32[]{:S(2)}, u32[]{:S(2)}) %collective-permute-start) | collective-permute-done | bytes 245792 | tf_op jit(solution)/shard_map/ppermute | solution.py:330
  9.9 1.8 %collective-permute-start.2 = (bf16[32,3840]{1,0:T(8,128)(2,1)S(1)}, bf16[32,3840]{1,0:T(8,128)(2,1)S(1)}, u32[]{:S(2)}, u32[]{:S(2)}) collective-permute-start(bf16[32,3840]{1,0:T(8,128)(2,1)S(1)} %collective-permute-done.refs_1_), channel_id=1, source_target_pairs={{0,8},{8,16},{16,24},{24,28},{28,20},{20,12},{12,4},{4,0},{1,9},{9... | collective-permute-start | bytes 737288 | tf_op jit(solution)/shard_map/ppermute | solution.py:330
  11.7 1.6 %collective-permute-start.3 = (bf16[32,3712]{1,0:T(8,128)(2,1)S(1)}, bf16[32,3712]{1,0:T(8,128)(2,1)S(1)}, u32[]{:S(2)}, u32[]{:S(2)}) collective-permute-start(bf16[32,3712]{1,0:T(8,128)(2,1)S(1)} %pad.8.refs_4_), channel_id=1, source_target_pairs={{0,8},{8,16},{16,24},{24,28},{28,20},{20,12},{12,4},{4,0},{1,9},{9... | collective-permute-start | bytes 712712 | tf_op jit(solution)/shard_map/ppermute | solution.py:330
  13.8 5.3 %collective-permute-done.1.refs_2_ = bf16[32,3840]{1,0:T(8,128)(2,1)S(1)} collective-permute-done((bf16[32,3840]{1,0:T(8,128)(2,1)S(1)}, bf16[32,3840]{1,0:T(8,128)(2,1)S(1)}, u32[]{:S(2)}, u32[]{:S(2)}) %collective-permute-start.1) | collective-permute-done | bytes 245792 | tf_op jit(solution)/shard_map/ppermute | solution.py:333
  19.1 2.0 %collective-permute-start.7 = (bf16[32,3840]{1,0:T(8,128)(2,1)S(1)}, bf16[32,3840]{1,0:T(8,128)(2,1)S(1)}, u32[]{:S(2)}, u32[]{:S(2)}) collective-permute-start(bf16[32,3840]{1,0:T(8,128)(2,1)S(1)} %collective-permute-done.2.refs_3_), channel_id=1, source_target_pairs={{0,8},{8,16},{16,24},{24,28},{28,20},{20,12},{12,4},{4,0},{1,9},{9... | collective-permute-start | bytes 737288 | tf_op jit(solution)/shard_map/ppermute | solution.py:330
  21.1 2.8 %collective-permute-done.3.refs_5_ = bf16[32,3712]{1,0:T(8,128)(2,1)S(1)} collective-permute-done((bf16[32,3712]{1,0:T(8,128)(2,1)S(1)}, bf16[32,3712]{1,0:T(8,128)(2,1)S(1)}, u32[]{:S(2)}, u32[]{:S(2)}) %collective-permute-start.3) | collective-permute-done | bytes 237600 | tf_op jit(solution)/shard_map/ppermute | solution.py:330
  23.9 1.8 %collective-permute-start.5 = (bf16[32,3712]{1,0:T(8,128)(2,1)S(1)}, bf16[32,3712]{1,0:T(8,128)(2,1)}, u32[]{:S(2)}, u32[]{:S(2)}) collective-permute-start(bf16[32,3712]{1,0:T(8,128)(2,1)S(1)} %collective-permute-done.3.refs_5_), channel_id=1, source_target_pairs={{0,8},{8,16},{16,24},{24,28},{28,20},{20,12},{12,4},{4,0},{1,9},{9... | collective-permute-start | bytes 712712 | tf_op jit(solution)/shard_map/ppermute | solution.py:330
  26.6 2.8 %collective-permute-done.6.refs_0_ = bf16[32,3840]{1,0:T(8,128)(2,1)S(1)} collective-permute-done((bf16[32,3840]{1,0:T(8,128)(2,1)S(1)}, bf16[32,3840]{1,0:T(8,128)(2,1)S(1)}, u32[]{:S(2)}, u32[]{:S(2)}) %collective-permute-start.6) | collective-permute-done | bytes 245792 | tf_op jit(solution)/shard_map/ppermute | solution.py:333
  29.4 2.0 %collective-permute-start.9 = (bf16[32,3840]{1,0:T(8,128)(2,1)S(1)}, bf16[32,3840]{1,0:T(8,128)(2,1)S(1)}, u32[]{:S(2)}, u32[]{:S(2)}) collective-permute-start(bf16[32,3840]{1,0:T(8,128)(2,1)S(1)} %collective-permute-done.7.refs_1_), channel_id=1, source_target_pairs={{0,8},{8,16},{16,24},{24,28},{28,20},{20,12},{12,4},{4,0},{1,9},{9... | collective-permute-start | bytes 737288 | tf_op jit(solution)/shard_map/ppermute | solution.py:330
  31.4 2.9 %collective-permute-done.5.refs_7_ = bf16[32,3712]{1,0:T(8,128)(2,1)} collective-permute-done((bf16[32,3712]{1,0:T(8,128)(2,1)S(1)}, bf16[32,3712]{1,0:T(8,128)(2,1)}, u32[]{:S(2)}, u32[]{:S(2)}) %collective-permute-start.5) | collective-permute-done | bytes 237600 | tf_op jit(solution)/shard_map/ppermute | solution.py:330
  34.4 1.8 %collective-permute-start.11 = (bf16[32,3712]{1,0:T(8,128)(2,1)}, bf16[32,3712]{1,0:T(8,128)(2,1)S(1)}, u32[]{:S(2)}, u32[]{:S(2)}) collective-permute-start(bf16[32,3712]{1,0:T(8,128)(2,1)} %collective-permute-done.5.refs_7_), channel_id=1, source_target_pairs={{0,8},{8,16},{16,24},{24,28},{28,20},{20,12},{12,4},{4,0},{1,9},{9... | collective-permute-start | bytes 712712 | tf_op jit(solution)/shard_map/ppermute | solution.py:330
  38.8 2.1 %near_kernel.1.near = bf16[7552,128]{1,0:T(8,128)(2,1)S(1)} custom-call(bf16[32,3840]{1,0:T(8,128)(2,1)S(1)} %slice.9.refs_0_, bf16[32,3840]{1,0:T(8,128)(2,1)S(1)} %collective-permute-done.refs_1_, bf16[32,3840]{1,0:T(8,128)(2,1)S(1)} %collective-permute-done.1.refs_2_, bf16[32,3840]{1,0:T(8,128)(2,1)S(1)} %collective-permute-done.2.refs_3_, ...), custom_call_target="tpu_custom_call" | custom-call | flops 100000000 | bytes 3866624 | tf_op jit(solution)/shard_map/near_kernel/pallas_call | solution.py:270
  40.9 2.0 %collective-permute-done.11.refs_5_ = bf16[32,3712]{1,0:T(8,128)(2,1)S(1)} collective-permute-done((bf16[32,3712]{1,0:T(8,128)(2,1)}, bf16[32,3712]{1,0:T(8,128)(2,1)S(1)}, u32[]{:S(2)}, u32[]{:S(2)}) %collective-permute-start.11) | collective-permute-done | bytes 237600 | tf_op jit(solution)/shard_map/ppermute | solution.py:330
  43.4 16.9 %lead_kernel.1 = (f32[2,2880,128]{2,1,0:T(8,128)S(1)}, bf16[7552,256]{1,0:T(8,128)(2,1)S(1)}, s16[2,15,48,256]{3,2,1,0:T(8,128)(2,1)S(1)}) custom-call(s32[1]{0:T(128)} %bitcast.1.rep_ref, bf16[7552,128]{1,0:T(8,128)(2,1)S(1)} %near_kernel.1.near, bf16[32,3840]{1,0:T(8,128)(2,1)S(1)} %collective-permute-done.6.refs_0_, ...), custom_call_target="tpu_custom_call" | custom-call | flops 10950279168 | bytes 42774528 | tf_op jit(solution)/shard_map/lead_kernel/pallas_call | solution.py:270
  60.4 2.2 %collective-permute-done.14.got_ref = s16[2,15,48,256]{3,2,1,0:T(8,128)(2,1)S(1)} collective-permute-done((s16[2,15,48,256]{3,2,1,0:T(8,128)(2,1)S(1)}, s16[2,15,48,256]{3,2,1,0:T(8,128)(2,1)S(1)}, u32[]{:S(2)}, u32[]{:S(2)}) %collective-permute-start.14) | collective-permute-done | bytes 737312 | tf_op jit(solution)/shard_map/ppermute | solution.py:410
  65.0 7.0 %rest_kernel.1 = (f32[2,964,128]{2,1,0:T(8,128)S(1)}, s16[2,15,16,256]{3,2,1,0:T(8,128)(2,1)S(1)}) custom-call(s32[1]{0:T(128)} %bitcast.1.rep_ref, bf16[7552,256]{1,0:T(8,128)(2,1)S(1)} %get-tuple-element.23.turned, bf16[3600,7500]{1,0:T(8,128)(2,1)} %bitcast.14, bf16[3600,128]{1,0:T(8,128)(2,1)S(1)} %pad.9.refs_9_.edge_ref), custom_call_target="tpu_custom_call" | custom-call | flops 3031433216 | bytes 11841536 | tf_op jit(solution)/shard_map/rest_kernel/pallas_call | solution.py:270
  76.7 3.1 %collective-permute-done.16.got_ref = s16[15,16,256]{2,1,0:T(8,128)(2,1)S(1)} collective-permute-done((s16[15,16,256]{2,1,0:T(8,128)(2,1)S(1)}, s16[15,16,256]{2,1,0:T(8,128)(2,1)S(1)}, u32[]{:S(2)}, u32[]{:S(2)}) %collective-permute-start.16) | collective-permute-done | bytes 122912 | tf_op jit(solution)/shard_map/ppermute | solution.py:430
  82.6 1.9 %collective-permute-start.20 = (s16[4,64,128]{2,1,0:T(8,128)(2,1)S(1)}, s16[4,64,128]{2,1,0:T(8,128)(2,1)S(1)}, u32[]{:S(2)}, u32[]{:S(2)}) collective-permute-start(s16[4,64,128]{2,1,0:T(8,128)(2,1)S(1)} %get-tuple-element.30), channel_id=1, source_target_pairs={{0,12},{8,4},{16,0},{24,8},{28,16},{20,24},{12,28},{4,20},{1,13},{... | collective-permute-start | bytes 196616 | tf_op jit(solution)/shard_map/ppermute | solution.py:453
  85.6 2.9 %collective-permute-start.22 = (s16[4,64,128]{2,1,0:T(8,128)(2,1)S(1)}, s16[4,64,128]{2,1,0:T(8,128)(2,1)S(1)}, u32[]{:S(2)}, u32[]{:S(2)}) collective-permute-start(s16[4,64,128]{2,1,0:T(8,128)(2,1)S(1)} %get-tuple-element.32), channel_id=1, source_target_pairs={{0,20},{8,12},{16,4},{24,0},{28,8},{20,16},{12,24},{4,28},{1,21},{... | collective-permute-start | bytes 196616 | tf_op jit(solution)/shard_map/ppermute | solution.py:453
  89.4 4.0 %collective-permute-start.24 = (s16[4,64,128]{2,1,0:T(8,128)(2,1)S(1)}, s16[4,64,128]{2,1,0:T(8,128)(2,1)S(1)}, u32[]{:S(2)}, u32[]{:S(2)}) collective-permute-start(s16[4,64,128]{2,1,0:T(8,128)(2,1)S(1)} %get-tuple-element.34), channel_id=1, source_target_pairs={{0,28},{8,20},{16,12},{24,4},{28,0},{20,8},{12,16},{4,24},{1,29},{... | collective-permute-start | bytes 196616 | tf_op jit(solution)/shard_map/ppermute | solution.py:453
  93.5 3.8 %collective-permute-done.23.refs_6_ = s16[4,64,128]{2,1,0:T(8,128)(2,1)S(1)} collective-permute-done((s16[4,64,128]{2,1,0:T(8,128)(2,1)S(1)}, s16[4,64,128]{2,1,0:T(8,128)(2,1)S(1)}, u32[]{:S(2)}, u32[]{:S(2)}) %collective-permute-start.23) | collective-permute-done | bytes 65568 | tf_op jit(solution)/shard_map/ppermute | solution.py:453
  97.4 2.2 %update_kernel.1 = f32[15,32,480]{2,1,0:T(8,128)} custom-call(s32[1]{0:T(128)} %bitcast.me_ref, f32[15]{0:T(128)S(1)} %copy-done.5, s32[15]{0:T(128)S(1)} %copy-done.6, s16[4,64,128]{2,1,0:T(8,128)(2,1)S(1)} %get-tuple-element.27.refs_0_, s16[4,64,128]{2,1,0:T(8,128)(2,1)S(1)} %collective-permute-done.18.refs_1_, ...), custom_call_target="tpu_custom_call" | custom-call | flops 10000000 | bytes 4000000 | tf_op jit(solution)/shard_map/update_kernel/pallas_call | solution.py:270
  (61 shorter events, 18.4 us)
Async XLA Ops:
  1.0 9.0 %collective-permute-start = (bf16[32,3840]{1,0:T(8,128)(2,1)S(1)}, bf16[32,3840]{1,0:T(8,128)(2,1)S(1)}, u32[]{:S(2)}, u32[]{:S(2)}) collective-permute-start(bf16[32,3840]{1,0:T(8,128)(2,1)S(1)} %slice.9.refs_0_), channel_id=1, source_target_pairs={{0,8},{8,16},{16,24},{24,28},{28,20},{20,12},{12,4},{4,0},{1,9},{9... | collective-permute-start | bytes 737288 | tf_op jit(solution)/shard_map/ppermute | solution.py:330
  5.0 8.8 %collective-permute-start.4 = (bf16[32,3712]{1,0:T(8,128)(2,1)S(1)}, bf16[32,3712]{1,0:T(8,128)(2,1)S(1)}, u32[]{:S(2)}, u32[]{:S(2)}) collective-permute-start(bf16[32,3712]{1,0:T(8,128)(2,1)S(1)} %pad.8.refs_4_), channel_id=1, source_target_pairs={{8,0},{16,8},{24,16},{28,24},{20,28},{12,20},{4,12},{0,4},{9,1},{1... | collective-permute-start | bytes 712712 | tf_op jit(solution)/shard_map/ppermute | solution.py:333
  5.1 14.0 %collective-permute-start.1 = (bf16[32,3840]{1,0:T(8,128)(2,1)S(1)}, bf16[32,3840]{1,0:T(8,128)(2,1)S(1)}, u32[]{:S(2)}, u32[]{:S(2)}) collective-permute-start(bf16[32,3840]{1,0:T(8,128)(2,1)S(1)} %slice.9.refs_0_), channel_id=1, source_target_pairs={{8,0},{16,8},{24,16},{28,24},{20,28},{12,20},{4,12},{0,4},{9,1},{1... | collective-permute-start | bytes 737288 | tf_op jit(solution)/shard_map/ppermute | solution.py:333
  9.9 9.1 %collective-permute-start.2 = (bf16[32,3840]{1,0:T(8,128)(2,1)S(1)}, bf16[32,3840]{1,0:T(8,128)(2,1)S(1)}, u32[]{:S(2)}, u32[]{:S(2)}) collective-permute-start(bf16[32,3840]{1,0:T(8,128)(2,1)S(1)} %collective-permute-done.refs_1_), channel_id=1, source_target_pairs={{0,8},{8,16},{16,24},{24,28},{28,20},{20,12},{12,4},{4,0},{1,9},{9... | collective-permute-start | bytes 737288 | tf_op jit(solution)/shard_map/ppermute | solution.py:330
  11.7 12.2 %collective-permute-start.3 = (bf16[32,3712]{1,0:T(8,128)(2,1)S(1)}, bf16[32,3712]{1,0:T(8,128)(2,1)S(1)}, u32[]{:S(2)}, u32[]{:S(2)}) collective-permute-start(bf16[32,3712]{1,0:T(8,128)(2,1)S(1)} %pad.8.refs_4_), channel_id=1, source_target_pairs={{0,8},{8,16},{16,24},{24,28},{28,20},{20,12},{12,4},{4,0},{1,9},{9... | collective-permute-start | bytes 712712 | tf_op jit(solution)/shard_map/ppermute | solution.py:330
  13.8 12.6 %collective-permute-start.10 = (bf16[32,3712]{1,0:T(8,128)(2,1)S(1)}, bf16[32,3712]{1,0:T(8,128)(2,1)S(1)}, u32[]{:S(2)}, u32[]{:S(2)}) collective-permute-start(bf16[32,3712]{1,0:T(8,128)(2,1)S(1)} %collective-permute-done.4.refs_6_), channel_id=1, source_target_pairs={{8,0},{16,8},{24,16},{28,24},{20,28},{12,20},{4,12},{0,4},{9,1},{1... | collective-permute-start | bytes 712712 | tf_op jit(solution)/shard_map/ppermute | solution.py:333
  19.1 10.4 %collective-permute-start.6 = (bf16[32,3840]{1,0:T(8,128)(2,1)S(1)}, bf16[32,3840]{1,0:T(8,128)(2,1)S(1)}, u32[]{:S(2)}, u32[]{:S(2)}) collective-permute-start(bf16[32,3840]{1,0:T(8,128)(2,1)S(1)} %collective-permute-done.1.refs_2_), channel_id=1, source_target_pairs={{8,0},{16,8},{24,16},{28,24},{20,28},{12,20},{4,12},{0,4},{9,1},{1... | collective-permute-start | bytes 737288 | tf_op jit(solution)/shard_map/ppermute | solution.py:333
  19.1 10.4 %collective-permute-start.7 = (bf16[32,3840]{1,0:T(8,128)(2,1)S(1)}, bf16[32,3840]{1,0:T(8,128)(2,1)S(1)}, u32[]{:S(2)}, u32[]{:S(2)}) collective-permute-start(bf16[32,3840]{1,0:T(8,128)(2,1)S(1)} %collective-permute-done.2.refs_3_), channel_id=1, source_target_pairs={{0,8},{8,16},{16,24},{24,28},{28,20},{20,12},{12,4},{4,0},{1,9},{9... | collective-permute-start | bytes 737288 | tf_op jit(solution)/shard_map/ppermute | solution.py:330
  23.9 10.5 %collective-permute-start.5 = (bf16[32,3712]{1,0:T(8,128)(2,1)S(1)}, bf16[32,3712]{1,0:T(8,128)(2,1)}, u32[]{:S(2)}, u32[]{:S(2)}) collective-permute-start(bf16[32,3712]{1,0:T(8,128)(2,1)S(1)} %collective-permute-done.3.refs_5_), channel_id=1, source_target_pairs={{0,8},{8,16},{16,24},{24,28},{28,20},{20,12},{12,4},{4,0},{1,9},{9... | collective-permute-start | bytes 712712 | tf_op jit(solution)/shard_map/ppermute | solution.py:330
  26.4 9.8 %collective-permute-start.12 = (bf16[32,3712]{1,0:T(8,128)(2,1)S(1)}, bf16[32,3712]{1,0:T(8,128)(2,1)S(1)}, u32[]{:S(2)}, u32[]{:S(2)}) collective-permute-start(bf16[32,3712]{1,0:T(8,128)(2,1)S(1)} %collective-permute-done.10.refs_4_), channel_id=1, source_target_pairs={{8,0},{16,8},{24,16},{28,24},{20,28},{12,20},{4,12},{0,4},{9,1},{1... | collective-permute-start | bytes 712712 | tf_op jit(solution)/shard_map/ppermute | solution.py:333
  29.4 13.5 %collective-permute-start.8 = (bf16[32,3840]{1,0:T(8,128)(2,1)S(1)}, bf16[32,3840]{1,0:T(8,128)(2,1)S(1)}, u32[]{:S(2)}, u32[]{:S(2)}) collective-permute-start(bf16[32,3840]{1,0:T(8,128)(2,1)S(1)} %collective-permute-done.6.refs_0_), channel_id=1, source_target_pairs={{8,0},{16,8},{24,16},{28,24},{20,28},{12,20},{4,12},{0,4},{9,1},{1... | collective-permute-start | bytes 737288 | tf_op jit(solution)/shard_map/ppermute | solution.py:333
  29.4 14.0 %collective-permute-start.9 = (bf16[32,3840]{1,0:T(8,128)(2,1)S(1)}, bf16[32,3840]{1,0:T(8,128)(2,1)S(1)}, u32[]{:S(2)}, u32[]{:S(2)}) collective-permute-start(bf16[32,3840]{1,0:T(8,128)(2,1)S(1)} %collective-permute-done.7.refs_1_), channel_id=1, source_target_pairs={{0,8},{8,16},{16,24},{24,28},{28,20},{20,12},{12,4},{4,0},{1,9},{9... | collective-permute-start | bytes 737288 | tf_op jit(solution)/shard_map/ppermute | solution.py:330
  34.4 8.5 %collective-permute-start.11 = (bf16[32,3712]{1,0:T(8,128)(2,1)}, bf16[32,3712]{1,0:T(8,128)(2,1)S(1)}, u32[]{:S(2)}, u32[]{:S(2)}) collective-permute-start(bf16[32,3712]{1,0:T(8,128)(2,1)} %collective-permute-done.5.refs_7_), channel_id=1, source_target_pairs={{0,8},{8,16},{16,24},{24,28},{28,20},{20,12},{12,4},{4,0},{1,9},{9... | collective-permute-start | bytes 712712 | tf_op jit(solution)/shard_map/ppermute | solution.py:330
  36.2 7.2 %collective-permute-start.13 = (bf16[32,3712]{1,0:T(8,128)(2,1)S(1)}, bf16[32,3712]{1,0:T(8,128)(2,1)S(1)}, u32[]{:S(2)}, u32[]{:S(2)}) collective-permute-start(bf16[32,3712]{1,0:T(8,128)(2,1)S(1)} %collective-permute-done.12.refs_6_), channel_id=1, source_target_pairs={{8,0},{16,8},{24,16},{28,24},{20,28},{12,20},{4,12},{0,4},{9,1},{1... | collective-permute-start | bytes 712712 | tf_op jit(solution)/shard_map/ppermute | solution.py:333
  60.3 2.3 %collective-permute-start.14 = (s16[2,15,48,256]{3,2,1,0:T(8,128)(2,1)S(1)}, s16[2,15,48,256]{3,2,1,0:T(8,128)(2,1)S(1)}, u32[]{:S(2)}, u32[]{:S(2)}) collective-permute-start(s16[2,15,48,256]{3,2,1,0:T(8,128)(2,1)S(1)} %get-tuple-element.22), channel_id=1, source_target_pairs={{0,1},{1,0},{2,3},{3,2},{4,5},{5,4},{6,7},{7,6},{8,9},{9,8},{10,11... | collective-permute-start | bytes 2211848 | tf_op jit(solution)/shard_map/ppermute | solution.py:410
  63.4 12.2 %collective-permute-start.17 = (s16[15,48,256]{2,1,0:T(8,128)(2,1)S(1)}, s16[15,48,256]{2,1,0:T(8,128)(2,1)S(1)}, u32[]{:S(2)}, u32[]{:S(2)}) collective-permute-start(s16[15,48,256]{2,1,0:T(8,128)(2,1)S(1)} %second_send_kernel.2), channel_id=1, source_target_pairs={{0,2},{1,3},{2,0},{3,1},{4,6},{5,7},{6,4},{7,5},{8,10},{9,11},{10,... | collective-permute-start | bytes 1105928 | tf_op jit(solution)/shard_map/ppermute | solution.py:430
  74.4 5.4 %collective-permute-start.16 = (s16[15,16,256]{2,1,0:T(8,128)(2,1)S(1)}, s16[15,16,256]{2,1,0:T(8,128)(2,1)S(1)}, u32[]{:S(2)}, u32[]{:S(2)}) collective-permute-start(s16[15,16,256]{2,1,0:T(8,128)(2,1)S(1)} %second_send_kernel.3), channel_id=1, source_target_pairs={{0,2},{1,3},{2,0},{3,1},{4,6},{5,7},{6,4},{7,5},{8,10},{9,11},{10,... | collective-permute-start | bytes 368648 | tf_op jit(solution)/shard_map/ppermute | solution.py:430
  80.5 8.0 %collective-permute-start.18 = (s16[4,64,128]{2,1,0:T(8,128)(2,1)S(1)}, s16[4,64,128]{2,1,0:T(8,128)(2,1)S(1)}, u32[]{:S(2)}, u32[]{:S(2)}) collective-permute-start(s16[4,64,128]{2,1,0:T(8,128)(2,1)S(1)} %get-tuple-element.28), channel_id=1, source_target_pairs={{0,4},{8,0},{16,8},{24,16},{28,24},{20,28},{12,20},{4,12},{1,5},{9... | collective-permute-start | bytes 196616 | tf_op jit(solution)/shard_map/ppermute | solution.py:453
  81.5 7.9 %collective-permute-start.19 = (s16[4,64,128]{2,1,0:T(8,128)(2,1)S(1)}, s16[4,64,128]{2,1,0:T(8,128)(2,1)S(1)}, u32[]{:S(2)}, u32[]{:S(2)}) collective-permute-start(s16[4,64,128]{2,1,0:T(8,128)(2,1)S(1)} %get-tuple-element.29), channel_id=1, source_target_pairs={{0,8},{8,16},{16,24},{24,28},{28,20},{20,12},{12,4},{4,0},{1,9},{9... | collective-permute-start | bytes 196616 | tf_op jit(solution)/shard_map/ppermute | solution.py:453
  82.6 10.9 %collective-permute-start.20 = (s16[4,64,128]{2,1,0:T(8,128)(2,1)S(1)}, s16[4,64,128]{2,1,0:T(8,128)(2,1)S(1)}, u32[]{:S(2)}, u32[]{:S(2)}) collective-permute-start(s16[4,64,128]{2,1,0:T(8,128)(2,1)S(1)} %get-tuple-element.30), channel_id=1, source_target_pairs={{0,12},{8,4},{16,0},{24,8},{28,16},{20,24},{12,28},{4,20},{1,13},{... | collective-permute-start | bytes 196616 | tf_op jit(solution)/shard_map/ppermute | solution.py:453
  84.6 9.0 %collective-permute-start.21 = (s16[4,64,128]{2,1,0:T(8,128)(2,1)S(1)}, s16[4,64,128]{2,1,0:T(8,128)(2,1)S(1)}, u32[]{:S(2)}, u32[]{:S(2)}) collective-permute-start(s16[4,64,128]{2,1,0:T(8,128)(2,1)S(1)} %get-tuple-element.31), channel_id=1, source_target_pairs={{0,16},{8,24},{16,28},{24,20},{28,12},{20,4},{12,0},{4,8},{1,17},{... | collective-permute-start | bytes 196616 | tf_op jit(solution)/shard_map/ppermute | solution.py:453
  85.6 8.0 %collective-permute-start.22 = (s16[4,64,128]{2,1,0:T(8,128)(2,1)S(1)}, s16[4,64,128]{2,1,0:T(8,128)(2,1)S(1)}, u32[]{:S(2)}, u32[]{:S(2)}) collective-permute-start(s16[4,64,128]{2,1,0:T(8,128)(2,1)S(1)} %get-tuple-element.32), channel_id=1, source_target_pairs={{0,20},{8,12},{16,4},{24,0},{28,8},{20,16},{12,24},{4,28},{1,21},{... | collective-permute-start | bytes 196616 | tf_op jit(solution)/shard_map/ppermute | solution.py:453
  88.5 8.8 %collective-permute-start.23 = (s16[4,64,128]{2,1,0:T(8,128)(2,1)S(1)}, s16[4,64,128]{2,1,0:T(8,128)(2,1)S(1)}, u32[]{:S(2)}, u32[]{:S(2)}) collective-permute-start(s16[4,64,128]{2,1,0:T(8,128)(2,1)S(1)} %get-tuple-element.33), channel_id=1, source_target_pairs={{0,24},{8,28},{16,20},{24,12},{28,4},{20,0},{12,8},{4,16},{1,25},{... | collective-permute-start | bytes 196616 | tf_op jit(solution)/shard_map/ppermute | solution.py:453
  89.4 8.0 %collective-permute-start.24 = (s16[4,64,128]{2,1,0:T(8,128)(2,1)S(1)}, s16[4,64,128]{2,1,0:T(8,128)(2,1)S(1)}, u32[]{:S(2)}, u32[]{:S(2)}) collective-permute-start(s16[4,64,128]{2,1,0:T(8,128)(2,1)S(1)} %get-tuple-element.34), channel_id=1, source_target_pairs={{0,28},{8,20},{16,12},{24,4},{28,0},{20,8},{12,16},{4,24},{1,29},{... | collective-permute-start | bytes 196616 | tf_op jit(solution)/shard_map/ppermute | solution.py:453
  (10 other events, 156.2 us)

commit v7 on v6

--- a/solution.py
+++ b/solution.py
@@ -12,6 +12,7 @@
 K_BLOCK = 3840
 C_BLOCK = 480
 SLOTS = 3
+EARLY = 3
 COPIES = 4
 FIRST_PART = 47
 STEPS = 8.0
@@ -126,26 +127,74 @@
         turned[at : at + LANES, lanes : lanes + slots * rows] = gathered[:, at : at + LANES].T
 
 
-def near_kernel(edges, *refs):
-    *pieces, turned, gathered, sems = refs
-    turn_pieces(edges, pieces, gathered, sems, turned, 0)
-
-
-def lead_kernel(edges, columns, span, rep_ref, near, *refs):
-    pieces, refs = refs[: len(edges)], refs[len(edges) :]
+def near_kernel(at, whole, columns, count, *refs):
+    pieces, refs = refs[:count], refs[count:]
+    if columns is None:
+        turned, gathered, sems = refs
+        turn_pieces((0,) * count, pieces, gathered, sems, turned, 0)
+        return
+    coupling_ref, edge_ref, turned, held, gathered, sems, held_sems = refs
+    low, many = columns
+    rows = pl.ds(low, many)
+    quarter = ceil_to(-(-whole // COPIES), LANES)
+    copies = []
+    for number, k in enumerate(range(0, whole, quarter)):
+        size = min(quarter, whole - k)
+        copies.append(
+            pltpu.make_async_copy(
+                coupling_ref.at[rows, pl.ds(at + k, size)],
+                held.at[:, pl.ds(k, size)],
+                held_sems.at[number],
+            )
+        )
+    if whole < held.shape[1]:
+        copies.append(
+            pltpu.make_async_copy(
+                edge_ref.at[rows, :], held.at[:, pl.ds(whole, LANES)], held_sems.at[COPIES]
+            )
+        )
+    for copy in copies:
+        copy.start()
+    turn_pieces((0,) * count, pieces, gathered, sems, turned, 0)
+    for copy in copies:
+        copy.wait()
+
+
+def lead_kernel(edges, columns, span, nears, rep_ref, *refs):
+    near, pieces, refs = refs[:nears], refs[nears : nears + len(edges)], refs[nears + len(edges) :]
     coupling_ref, edge_ref, total, turned, send, gathered, sems, buffer, buffer_sems = refs
 
     def before():
-        lanes = near.shape[1]
-        turned[:, :lanes] = near[...]
+        at, lanes = 0, near[0].shape[1]
+        for part in near:
+            turned[at : at + part.shape[0], :lanes] = part[...]
+            at += part.shape[0]
         turn_pieces(edges, pieces, gathered, sems, turned, lanes)
 
     multiply(coupling_ref, edge_ref, buffer, buffer_sems, turned, total, columns, before)
     first_send(span, rep_ref, total, send)
 
 
-def rest_kernel(columns, span, rep_ref, turned, coupling_ref, edge_ref, total, send, buffer, sems):
-    multiply(coupling_ref, edge_ref, buffer, sems, turned, total, columns)
+def rest_kernel(span, rep_ref, turned, *refs):
+    *held, total, send = refs
+    many = held[0].shape[0]
+    block = min(C_BLOCK, ceil_to(many // 2, 16))
+
+    def step(number, carry):
+        start = pl.multiple_of(jnp.minimum(number * block, many - block), 16)
+        rows = pl.ds(start, block)
+        at, products = 0, 0.0
+        for part in held:
+            size = part.shape[1]
+            products += jnp.dot(
+                part[rows, :], turned[at : at + size, :], preferred_element_type=jnp.float32
+            )
+            at += size
+        for part in range(total.shape[0]):
+            total[part, rows, :] = products[:, part * LANES : (part + 1) * LANES]
+        return carry
+
+    lax.fori_loop(0, -(-many // block), step, 0)
     first_send(span, rep_ref, total, send)
 
 
@@ -210,22 +259,25 @@
     lax.fori_loop(0, groups, step, 0)
 
 
-def third_send_kernel(count, rows_dev, kept_ref, got_ref, stage):
+def third_send_kernel(count, rows_dev, kept_ref, got_ref, *outs):
+    *early, stage = outs
     pack_rows(count, rows_dev, kept_ref, got_ref, stage)
-
-
-def last_send_kernel(count, rows_dev, parts, kept_ref, got_ref, *refs):
+    for number, target in enumerate(early):
+        target[...] = stage[stage.shape[0] - len(early) + number]
+
+
+def last_send_kernel(count, rows_dev, parts, early, kept_ref, got_ref, *refs):
     earlier, targets, stage = refs[: parts - 1], refs[parts - 1 : -1], refs[-1]
     pack_rows(count, rows_dev, kept_ref, got_ref, stage)
     for number, target in enumerate(targets):
         at = 0
-        for source in (*earlier, stage):
+        for source in (*earlier, stage) if number < len(targets) - early else (stage,):
             bp = source.shape[2]
             target[:, at : at + bp, :] = source[number]
             at += bp
 
 
-def update_kernel(counts, bps, width, rows_dev, order, me_ref, occ_energy_ref, occ_irrep_ref, *refs):
+def update_kernel(counts, bps, width, rows_dev, order, early, me_ref, occ_energy_ref, occ_irrep_ref, *refs):
     (
         integrals_ref,
         row_energy_ref,
@@ -236,12 +288,18 @@
         blocks,
         stage,
     ) = refs[-8:]
-    arrived = refs[:-8]
+    ahead, arrived = refs[:early], refs[early:-8]
     grid_size = len(arrived)
     place = walk_place(me_ref[0], grid_size)
-    for offset, got_ref in zip(order, arrived):
+    for number, (offset, got_ref) in enumerate(zip(order, arrived)):
         source = walk_index(lax.rem(place - offset + grid_size, grid_size), grid_size)
-        blocks[source] = got_ref[...]
+        ready = ahead[max(number - (grid_size - len(ahead)), 0) :][:1]
+        if number < grid_size - len(ahead):
+            ready = []
+        at = 0
+        for piece in (*ready, got_ref):
+            blocks[source, :, at : at + piece.shape[1], :] = piece[...]
+            at += piece.shape[1]
     pack = LANES // rows_dev
     for jj in range(blocks.shape[1]):
         at = 0
@@ -274,7 +332,7 @@
         out_specs=jax.tree.map(lambda _: pl.BlockSpec(memory_space=pltpu.VMEM), out_shape),
         scratch_shapes=list(scratch),
         input_output_aliases=aliases,
-        compiler_params=pltpu.CompilerParams(vmem_limit_bytes=8 * MIB + room),
+        compiler_params=pltpu.CompilerParams(vmem_limit_bytes=5 * MIB + room),
         cost_estimate=pl.CostEstimate(
             flops=cost[0], bytes_accessed=cost[1], transcendentals=0
         ),
@@ -318,7 +376,7 @@
     for hop in range(1, longer):
         order += [-hop, hop]
     order.append(longer)
-    near, far, near_edges, far_edges = [], [], [], []
+    near, far, far_edges = [], [], []
     for number, at in enumerate(range(0, depth, K_BLOCK)):
         own = amplitudes[:, at : at + K_BLOCK]
         size = own.shape[1]
@@ -332,9 +390,8 @@
             if hop < longer or number % 2 == 1:
                 behind = lax.ppermute(behind, "grid", back)
                 pieces.append(behind)
-        near += pieces[:longer]
+        near.append((at, size // LANES * LANES, pieces[:longer]))
         far += pieces[longer:]
-        near_edges += [at] * longer
         far_edges += [at] * longer
 
     counts = [FIRST_PART, count - FIRST_PART] if count > FIRST_PART else [count]
@@ -358,54 +415,66 @@
     high_pairs = [(i, i ^ 2) for i in range(lax.axis_size("rep"))]
 
     half = slab // 2
-    turn_scratch = [
-        pltpu.VMEM((half, deep), jnp.bfloat16),
-        pltpu.SemaphoreType.DMA((len(near),)),
-    ]
-    near = local_call(
-        functools.partial(near_kernel, tuple(near_edges)),
-        jax.ShapeDtypeStruct((deep, half), jnp.bfloat16),
-        "a" * len(near),
-        near,
-        turn_scratch,
-        cost=(10**8, 4 * half * deep),
-        room=2 * half * deep + (2 * half * deep if slab > 2 * LANES else 0),
-    )
+    large = slab > 2 * LANES
+    cols = parts[1] if len(parts) > 1 else None
+    turned_near, held = [], []
+    for at, whole, pieces in near:
+        size = pieces[0].shape[1]
+        out_shape = [jax.ShapeDtypeStruct((size, half), jnp.bfloat16)]
+        args = list(pieces)
+        scratch = [
+            pltpu.VMEM((half, size), jnp.bfloat16),
+            pltpu.SemaphoreType.DMA((len(pieces),)),
+        ]
+        if cols is not None:
+            out_shape.append(jax.ShapeDtypeStruct((cols[1], size), jnp.bfloat16))
+            args += [coupling, edge]
+            scratch.append(pltpu.SemaphoreType.DMA((COPIES + 1,)))
+        part, *rest = local_call(
+            functools.partial(near_kernel, at, whole, cols, len(pieces)),
+            tuple(out_shape),
+            "a" * len(args),
+            args,
+            scratch,
+            cost=(10**8, 4 * half * size + (2 * cols[1] * size if cols else 0)),
+            room=2 * half * size * (2 if large else 1),
+        )
+        turned_near.append(part)
+        held += rest
     totals, sends, got = [], [], []
     for part, (cols, span, bp) in enumerate(zip(parts, spans, bps)):
-        block = min(C_BLOCK, ceil_to(cols[1] // 2, 16))
-        scratch = [
-            pltpu.VMEM((SLOTS, block, deep), jnp.bfloat16),
-            pltpu.SemaphoreType.DMA((SLOTS, COPIES + 1)),
-        ]
         cost = (2 * cols[1] * deep * slab, 2 * cols[1] * deep)
-        room = 2 * SLOTS * block * deep + (slab * deep if part == 0 else 0)
-        if slab > 2 * LANES:
-            room += 3 * slab * deep + 4 * slab * total_shapes[part].shape[1]
         if part == 0:
+            block = min(C_BLOCK, ceil_to(cols[1] // 2, 16))
+            room = 2 * SLOTS * block * deep + slab * deep
+            if large:
+                room += 3 * slab * deep + 4 * slab * total_shapes[0].shape[1]
             total, turned, send = local_call(
-                functools.partial(lead_kernel, tuple(far_edges), cols, span),
+                functools.partial(lead_kernel, tuple(far_edges), cols, span, len(turned_near)),
                 (
                     total_shapes[0],
                     jax.ShapeDtypeStruct((deep, slab), jnp.bfloat16),
                     send_shapes[0],
                 ),
-                "sv" + "a" * (len(far) + 2),
-                (rep, near, *far, coupling, edge),
-                [*turn_scratch, *scratch],
+                "s" + "v" * len(turned_near) + "a" * (len(far) + 2),
+                (rep, *turned_near, *far, coupling, edge),
+                [
+                    pltpu.VMEM((half, deep), jnp.bfloat16),
+                    pltpu.SemaphoreType.DMA((len(far),)),
+                    pltpu.VMEM((SLOTS, block, deep), jnp.bfloat16),
+                    pltpu.SemaphoreType.DMA((SLOTS, COPIES + 1)),
+                ],
                 cost=cost,
                 room=room,
             )
         else:
             turned, _ = lax.optimization_barrier((turned, sends[0]))
             total, send = local_call(
-                functools.partial(rest_kernel, cols, span),
+                functools.partial(rest_kernel, span),
                 (total_shapes[part], send_shapes[part]),
-                "svaa",
-                (rep, turned, coupling, edge),
-                scratch,
+                "sv" + "v" * len(held),
+                (rep, turned, *held),
                 cost=cost,
-                room=room,
             )
         arrived = lax.ppermute(send, "rep", low_pairs)
         totals.append(total)
@@ -430,40 +499,46 @@
     got = [lax.ppermute(send, "rep", high_pairs) for send in sends]
 
     groups = -(-width // (LANES // rows_dev))
-    staged = []
+    staged, left = [], []
+    early = min(EARLY, grid_size - 1) if len(spans) > 1 else 0
     for part, span in enumerate(spans[:-1]):
         mine, _ = lax.optimization_barrier((kept[part], sends[-1]))
-        staged.append(
-            local_call(
-                functools.partial(third_send_kernel, span[1], rows_dev),
-                jax.ShapeDtypeStruct((grid_size, groups, bps[part], LANES), jnp.int16),
-                "vv",
-                (mine, got[part]),
-            )
-        )
+        *leaving, stage = local_call(
+            functools.partial(third_send_kernel, span[1], rows_dev),
+            (jax.ShapeDtypeStruct((groups, bps[part], LANES), jnp.int16),) * early
+            + (jax.ShapeDtypeStruct((grid_size, groups, bps[part], LANES), jnp.int16),),
+            "vv",
+            (mine, got[part]),
+        )
+        staged.append(stage)
+        left += leaving
+    rows = [sum(bps)] * (grid_size - early) + [bps[-1]] * early
     targets = local_call(
-        functools.partial(last_send_kernel, counts[-1], rows_dev, len(counts)),
-        (jax.ShapeDtypeStruct((groups, sum(bps), LANES), jnp.int16),) * grid_size,
+        functools.partial(last_send_kernel, counts[-1], rows_dev, len(counts), early),
+        tuple(jax.ShapeDtypeStruct((groups, many, LANES), jnp.int16) for many in rows),
         "vv" + "v" * len(staged),
         (kept[-1], got[-1], *staged),
         [pltpu.VMEM((grid_size, groups, bps[-1], LANES), jnp.int16)],
     )
+
+    def go_back(block, number):
+        pairs = [(walk[i], walk[(i + order[number]) % grid_size]) for i in range(grid_size)]
+        return lax.ppermute(block, "grid", pairs)
+
+    ahead = [go_back(block, grid_size - early + i) for i, block in enumerate(left)]
     arrived = list(targets)
     for number in range(1, grid_size)[::-1]:
-        arrived[number] = lax.ppermute(
-            targets[number],
-            "grid",
-            [(walk[i], walk[(i + order[number]) % grid_size]) for i in range(grid_size)],
-        )
+        arrived[number] = go_back(targets[number], number)
 
     updated = local_call(
-        functools.partial(update_kernel, counts, bps, width, rows_dev, order),
+        functools.partial(update_kernel, counts, bps, width, rows_dev, order, early),
         jax.ShapeDtypeStruct((width, rows_dev, count * grid_size), jnp.float32),
-        "sss" + "v" * (len(arrived) + 5),
+        "sss" + "v" * (early + len(arrived) + 5),
         (
             me,
             occ_energy,
             occ_irrep,
+            *ahead,
             *arrived,
             jnp.transpose(integrals, (1, 0, 2)),
             row_energy[:, None],

time: 99.8 us -> 109 us (1.092)
  starting transfers between devices: 31.7 us -> 40.6 us
  waiting for transfers between devices: 30.3 us -> 24.8 us
  Pallas kernels: 32.1 us -> 36.2 us
  local copies, waits for them, and re-layouts: 5.21 us -> 6.83 us
    ppermute x7 -> x10, starting transfers between devices: 12.8 us -> 21.7 us  [go_back(): return lax.ppermute(block, 'grid', pairs)]
    pallas_call x10 -> x11, Pallas kernels: 32.1 us -> 36.2 us  [local_call(): pl.pallas_call(kernel, out_shape=out_shape, in_specs=[pl.BlockSpec(memory...]
    ppermute x7, waiting for transfers between devices: 10.7 us -> 8.68 us  [body(): ahead = lax.ppermute(ahead, 'grid', onward)]
    unnamed x18 -> x22, local copies, waits for them, and re-layouts: 1.67 us -> 3.3 us
    ppermute x2, waiting for transfers between devices: 3.15 us -> 1.68 us  [body(): got = [lax.ppermute(send, 'rep', high_pairs) for send in sends]]
    ppermute x7, waiting for transfers between devices: 9.02 us -> 7.82 us  [body(): behind = lax.ppermute(behind, 'grid', back)]
    ppermute x7 -> x10, waiting for transfers between devices: 3.8 us -> 2.91 us  [go_back(): return lax.ppermute(block, 'grid', pairs)]
  transfers between devices with their start and end apart: 25 -> 28, of which waited for: 12 -> 12; matrix products, arithmetic and copies ran while one was open for 3% -> 2% of each run, Pallas kernels for 12% -> 12%
where the time goes in v7:
time: 109 us
  starting transfers between devices  40.6 us (37%)
  Pallas kernels  36.2 us (33%)
  waiting for transfers between devices  24.8 us (23%)
  local copies, waits for them, and re-layouts  6.83 us (6%)
    pallas_call x11, Pallas kernels, local_call(): pl.pallas_call(kernel, out_shape=out_shape, in_specs=[pl.BlockSpec(memory...  36.2 us
    ppermute x10, starting transfers between devices, go_back(): return lax.ppermute(block, 'grid', pairs)  21.7 us
    ppermute x7, starting transfers between devices, body(): ahead = lax.ppermute(ahead, 'grid', onward)  14.1 us
    ppermute x7, waiting for transfers between devices, body(): ahead = lax.ppermute(ahead, 'grid', onward)  8.68 us
    ppermute x7, waiting for transfers between devices, body(): behind = lax.ppermute(behind, 'grid', back)  7.82 us
    ppermute x2, waiting for transfers between devices, body(): arrived = lax.ppermute(send, 'rep', low_pairs)  3.7 us
    unnamed x22, local copies, waits for them, and re-layouts  3.3 us
    ppermute x10, waiting for transfers between devices, go_back(): return lax.ppermute(block, 'grid', pairs)  2.91 us
  transfers between devices with their start and end apart: 28, of which 12 were waited for; matrix products, arithmetic and copies ran while one was open for 2% of the time, Pallas kernels for 12%

profile of v7, /device:TPU:0, one launch (start us, length us, event | category | flops | bytes accessed | tf_op | source)
XLA Modules:
  0.0 108.7 jit_solution(9890130477392497634)
XLA Ops:
  1.0 3.1 %collective-permute-start = (bf16[32,3840]{1,0:T(8,128)(2,1)S(1)}, bf16[32,3840]{1,0:T(8,128)(2,1)S(1)}, u32[]{:S(2)}, u32[]{:S(2)}) collective-permute-start(bf16[32,3840]{1,0:T(8,128)(2,1)S(1)} %slice.9.refs_0_), channel_id=1, source_target_pairs={{0,8},{8,16},{16,24},{24,28},{28,20},{20,12},{12,4},{4,0},{1,9},{9... | collective-permute-start | bytes 737288 | tf_op jit(solution)/shard_map/ppermute | solution.py:388
  5.1 2.0 %collective-permute-start.1 = (bf16[32,3840]{1,0:T(8,128)(2,1)S(1)}, bf16[32,3840]{1,0:T(8,128)(2,1)S(1)}, u32[]{:S(2)}, u32[]{:S(2)}) collective-permute-start(bf16[32,3840]{1,0:T(8,128)(2,1)S(1)} %slice.9.refs_0_), channel_id=1, source_target_pairs={{8,0},{16,8},{24,16},{28,24},{20,28},{12,20},{4,12},{0,4},{9,1},{1... | collective-permute-start | bytes 737288 | tf_op jit(solution)/shard_map/ppermute | solution.py:391
  7.1 2.9 %collective-permute-done.refs_1_ = bf16[32,3840]{1,0:T(8,128)(2,1)S(1)} collective-permute-done((bf16[32,3840]{1,0:T(8,128)(2,1)S(1)}, bf16[32,3840]{1,0:T(8,128)(2,1)S(1)}, u32[]{:S(2)}, u32[]{:S(2)}) %collective-permute-start) | collective-permute-done | bytes 245792 | tf_op jit(solution)/shard_map/ppermute | solution.py:388
  9.9 1.8 %collective-permute-start.2 = (bf16[32,3840]{1,0:T(8,128)(2,1)S(1)}, bf16[32,3840]{1,0:T(8,128)(2,1)S(1)}, u32[]{:S(2)}, u32[]{:S(2)}) collective-permute-start(bf16[32,3840]{1,0:T(8,128)(2,1)S(1)} %collective-permute-done.refs_1_), channel_id=1, source_target_pairs={{0,8},{8,16},{16,24},{24,28},{28,20},{20,12},{12,4},{4,0},{1,9},{9... | collective-permute-start | bytes 737288 | tf_op jit(solution)/shard_map/ppermute | solution.py:388
  14.5 4.6 %collective-permute-done.1.refs_2_ = bf16[32,3840]{1,0:T(8,128)(2,1)S(1)} collective-permute-done((bf16[32,3840]{1,0:T(8,128)(2,1)S(1)}, bf16[32,3840]{1,0:T(8,128)(2,1)S(1)}, u32[]{:S(2)}, u32[]{:S(2)}) %collective-permute-start.1) | collective-permute-done | bytes 245792 | tf_op jit(solution)/shard_map/ppermute | solution.py:391
  19.1 2.0 %collective-permute-start.7 = (bf16[32,3840]{1,0:T(8,128)(2,1)S(1)}, bf16[32,3840]{1,0:T(8,128)(2,1)S(1)}, u32[]{:S(2)}, u32[]{:S(2)}) collective-permute-start(bf16[32,3840]{1,0:T(8,128)(2,1)S(1)} %collective-permute-done.2.refs_3_), channel_id=1, source_target_pairs={{0,8},{8,16},{16,24},{24,28},{28,20},{20,12},{12,4},{4,0},{1,9},{9... | collective-permute-start | bytes 737288 | tf_op jit(solution)/shard_map/ppermute | solution.py:388
  21.1 2.8 %collective-permute-done.3.refs_1_ = bf16[32,3712]{1,0:T(8,128)(2,1)S(1)} collective-permute-done((bf16[32,3712]{1,0:T(8,128)(2,1)S(1)}, bf16[32,3712]{1,0:T(8,128)(2,1)S(1)}, u32[]{:S(2)}, u32[]{:S(2)}) %collective-permute-start.3) | collective-permute-done | bytes 237600 | tf_op jit(solution)/shard_map/ppermute | solution.py:388
  23.9 1.8 %collective-permute-start.5 = (bf16[32,3712]{1,0:T(8,128)(2,1)S(1)}, bf16[32,3712]{1,0:T(8,128)(2,1)}, u32[]{:S(2)}, u32[]{:S(2)}) collective-permute-start(bf16[32,3712]{1,0:T(8,128)(2,1)S(1)} %collective-permute-done.3.refs_1_), channel_id=1, source_target_pairs={{0,8},{8,16},{16,24},{24,28},{28,20},{20,12},{12,4},{4,0},{1,9},{9... | collective-permute-start | bytes 712712 | tf_op jit(solution)/shard_map/ppermute | solution.py:388
  26.6 2.8 %collective-permute-done.6.refs_2_ = bf16[32,3840]{1,0:T(8,128)(2,1)S(1)} collective-permute-done((bf16[32,3840]{1,0:T(8,128)(2,1)S(1)}, bf16[32,3840]{1,0:T(8,128)(2,1)S(1)}, u32[]{:S(2)}, u32[]{:S(2)}) %collective-permute-start.6) | collective-permute-done | bytes 245792 | tf_op jit(solution)/shard_map/ppermute | solution.py:391
  29.4 2.0 %collective-permute-start.9 = (bf16[32,3840]{1,0:T(8,128)(2,1)S(1)}, bf16[32,3840]{1,0:T(8,128)(2,1)S(1)}, u32[]{:S(2)}, u32[]{:S(2)}) collective-permute-start(bf16[32,3840]{1,0:T(8,128)(2,1)S(1)} %collective-permute-done.7.refs_3_), channel_id=1, source_target_pairs={{0,8},{8,16},{16,24},{24,28},{28,20},{20,12},{12,4},{4,0},{1,9},{9... | collective-permute-start | bytes 737288 | tf_op jit(solution)/shard_map/ppermute | solution.py:388
  31.4 2.9 %collective-permute-done.5.refs_3_ = bf16[32,3712]{1,0:T(8,128)(2,1)} collective-permute-done((bf16[32,3712]{1,0:T(8,128)(2,1)S(1)}, bf16[32,3712]{1,0:T(8,128)(2,1)}, u32[]{:S(2)}, u32[]{:S(2)}) %collective-permute-start.5) | collective-permute-done | bytes 237600 | tf_op jit(solution)/shard_map/ppermute | solution.py:388
  34.4 1.8 %collective-permute-start.11 = (bf16[32,3712]{1,0:T(8,128)(2,1)}, bf16[32,3712]{1,0:T(8,128)(2,1)}, u32[]{:S(2)}, u32[]{:S(2)}) collective-permute-start(bf16[32,3712]{1,0:T(8,128)(2,1)} %collective-permute-done.5.refs_3_), channel_id=1, source_target_pairs={{0,8},{8,16},{16,24},{24,28},{28,20},{20,12},{12,4},{4,0},{1,9},{9... | collective-permute-start | bytes 712712 | tf_op jit(solution)/shard_map/ppermute | solution.py:388
  39.7 3.3 %near_kernel.3 = (bf16[3712,128]{1,0:T(8,128)(2,1)S(1)}, bf16[784,3712]{1,0:T(8,128)(2,1)S(1)}) custom-call(bf16[32,3712]{1,0:T(8,128)(2,1)S(1)} %pad.9.refs_0_, bf16[32,3712]{1,0:T(8,128)(2,1)S(1)} %copy-done.4, bf16[32,3712]{1,0:T(8,128)(2,1)S(1)} %copy-done.2, bf16[32,3712]{1,0:T(8,128)(2,1)} %collective-permute-done.5.refs_3_, ...), custom_call_target="tpu_custom_call" | custom-call | flops 100000000 | bytes 7720960 | tf_op jit(solution)/shard_map/near_kernel/pallas_call | solution.py:328
  43.0 2.8 %near_kernel.2 = (bf16[3840,128]{1,0:T(8,128)(2,1)S(1)}, bf16[784,3840]{1,0:T(8,128)(2,1)S(1)}) custom-call(bf16[32,3840]{1,0:T(8,128)(2,1)S(1)} %slice.9.refs_0_, bf16[32,3840]{1,0:T(8,128)(2,1)S(1)} %collective-permute-done.refs_1_, bf16[32,3840]{1,0:T(8,128)(2,1)S(1)} %collective-permute-done.1.refs_2_, ...), custom_call_target="tpu_custom_call" | custom-call | flops 100000000 | bytes 7987200 | tf_op jit(solution)/shard_map/near_kernel/pallas_call | solution.py:328
  45.9 19.8 %lead_kernel.1 = (f32[2,2880,128]{2,1,0:T(8,128)S(1)}, bf16[7552,256]{1,0:T(8,128)(2,1)S(1)}, s16[2,15,48,256]{3,2,1,0:T(8,128)(2,1)S(1)}) custom-call(s32[1]{0:T(128)} %bitcast.1.rep_ref, bf16[3840,128]{1,0:T(8,128)(2,1)S(1)} %get-tuple-element.28.refs_0_, bf16[3712,128]{1,0:T(8,128)(2,1)S(1)} %get-tuple-element.29.refs_1_, ...), custom_call_target="tpu_custom_call" | custom-call | flops 10950279168 | bytes 42774528 | tf_op jit(solution)/shard_map/lead_kernel/pallas_call | solution.py:328
  65.8 2.2 %collective-permute-done.14.got_ref = s16[2,15,48,256]{3,2,1,0:T(8,128)(2,1)S(1)} collective-permute-done((s16[2,15,48,256]{3,2,1,0:T(8,128)(2,1)S(1)}, s16[2,15,48,256]{3,2,1,0:T(8,128)(2,1)S(1)}, u32[]{:S(2)}, u32[]{:S(2)}) %collective-permute-start.14) | collective-permute-done | bytes 737312 | tf_op jit(solution)/shard_map/ppermute | solution.py:479
  68.9 1.8 %collective-permute-start.16 = (s16[15,48,256]{2,1,0:T(8,128)(2,1)S(1)}, s16[15,48,256]{2,1,0:T(8,128)(2,1)S(1)}, u32[]{:S(2)}, u32[]{:S(2)}) collective-permute-start(s16[15,48,256]{2,1,0:T(8,128)(2,1)S(1)} %second_send_kernel.2), channel_id=1, source_target_pairs={{0,2},{1,3},{2,0},{3,1},{4,6},{5,7},{6,4},{7,5},{8,10},{9,11},{10,... | collective-permute-start | bytes 1105928 | tf_op jit(solution)/shard_map/ppermute | solution.py:499
  70.6 4.1 %rest_kernel.1 = (f32[2,964,128]{2,1,0:T(8,128)S(1)}, s16[2,15,16,256]{3,2,1,0:T(8,128)(2,1)S(1)}) custom-call(s32[1]{0:T(128)} %bitcast.1.rep_ref, bf16[7552,256]{1,0:T(8,128)(2,1)S(1)} %get-tuple-element.33.turned, bf16[784,3840]{1,0:T(8,128)(2,1)S(1)} %get-tuple-element.34.refs_0_, bf16[784,3712]{1,0:T(8,128)(2,1)S(1)} %get-tuple-element.35.refs_1_), custom_call_target="tpu_custom_call" | custom-call | flops 3031433216 | bytes 11841536 | tf_op jit(solution)/shard_map/rest_kernel/pallas_call | solution.py:328
  80.7 3.8 %collective-permute-start.17 = (s16[4,48,128]{2,1,0:T(8,128)(2,1)S(1)}, s16[4,48,128]{2,1,0:T(8,128)(2,1)S(1)}, u32[]{:S(2)}, u32[]{:S(2)}) collective-permute-start(s16[4,48,128]{2,1,0:T(8,128)(2,1)S(1)} %get-tuple-element.39), channel_id=1, source_target_pairs={{0,20},{8,12},{16,4},{24,0},{28,8},{20,16},{12,24},{4,28},{1,21},{... | collective-permute-start | bytes 147464 | tf_op jit(solution)/shard_map/ppermute | solution.py:526
  85.6 3.8 %collective-permute-start.25 = (s16[4,16,128]{2,1,0:T(8,128)(2,1)S(1)}, s16[4,16,128]{2,1,0:T(8,128)(2,1)S(1)}, u32[]{:S(2)}, u32[]{:S(2)}) collective-permute-start(s16[4,16,128]{2,1,0:T(8,128)(2,1)S(1)} %get-tuple-element.48), channel_id=1, source_target_pairs={{0,20},{8,12},{16,4},{24,0},{28,8},{20,16},{12,24},{4,28},{1,21},{... | collective-permute-start | bytes 49160 | tf_op jit(solution)/shard_map/ppermute | solution.py:526
  89.4 4.7 %collective-permute-start.27 = (s16[4,16,128]{2,1,0:T(8,128)(2,1)S(1)}, s16[4,16,128]{2,1,0:T(8,128)(2,1)S(1)}, u32[]{:S(2)}, u32[]{:S(2)}) collective-permute-start(s16[4,16,128]{2,1,0:T(8,128)(2,1)S(1)} %get-tuple-element.50), channel_id=1, source_target_pairs={{0,28},{8,20},{16,12},{24,4},{28,0},{20,8},{12,16},{4,24},{1,29},{... | collective-permute-start | bytes 49160 | tf_op jit(solution)/shard_map/ppermute | solution.py:526
  99.2 4.5 %collective-permute-start.19 = (s16[4,48,128]{2,1,0:T(8,128)(2,1)S(1)}, s16[4,48,128]{2,1,0:T(8,128)(2,1)S(1)}, u32[]{:S(2)}, u32[]{:S(2)}) collective-permute-start(s16[4,48,128]{2,1,0:T(8,128)(2,1)S(1)} %get-tuple-element.41), channel_id=1, source_target_pairs={{0,28},{8,20},{16,12},{24,4},{28,0},{20,8},{12,16},{4,24},{1,29},{... | collective-permute-start | bytes 147464 | tf_op jit(solution)/shard_map/ppermute | solution.py:526
  103.9 2.6 %collective-permute-done.19.refs_2_ = s16[4,48,128]{2,1,0:T(8,128)(2,1)S(1)} collective-permute-done((s16[4,48,128]{2,1,0:T(8,128)(2,1)S(1)}, s16[4,48,128]{2,1,0:T(8,128)(2,1)S(1)}, u32[]{:S(2)}, u32[]{:S(2)}) %collective-permute-start.19) | collective-permute-done | bytes 49184 | tf_op jit(solution)/shard_map/ppermute | solution.py:526
  106.5 2.2 %update_kernel.1 = f32[15,32,480]{2,1,0:T(8,128)} custom-call(s32[1]{0:T(128)} %bitcast.me_ref, f32[15]{0:T(128)S(1)} %copy-done.7, s32[15]{0:T(128)S(1)} %copy-done.8, s16[4,48,128]{2,1,0:T(8,128)(2,1)S(1)} %collective-permute-done.17.refs_0_, s16[4,48,128]{2,1,0:T(8,128)(2,1)S(1)} %collective-permute-done.18.refs_1_, ...), custom_call_target="tpu_custom_call" | custom-call | flops 10000000 | bytes 4000000 | tf_op jit(solution)/shard_map/update_kernel/pallas_call | solution.py:328
  (72 shorter events, 22.4 us)
Async XLA Ops:
  1.0 9.0 %collective-permute-start = (bf16[32,3840]{1,0:T(8,128)(2,1)S(1)}, bf16[32,3840]{1,0:T(8,128)(2,1)S(1)}, u32[]{:S(2)}, u32[]{:S(2)}) collective-permute-start(bf16[32,3840]{1,0:T(8,128)(2,1)S(1)} %slice.9.refs_0_), channel_id=1, source_target_pairs={{0,8},{8,16},{16,24},{24,28},{28,20},{20,12},{12,4},{4,0},{1,9},{9... | collective-permute-start | bytes 737288 | tf_op jit(solution)/shard_map/ppermute | solution.py:388
  5.0 8.8 %collective-permute-start.4 = (bf16[32,3712]{1,0:T(8,128)(2,1)S(1)}, bf16[32,3712]{1,0:T(8,128)(2,1)S(1)}, u32[]{:S(2)}, u32[]{:S(2)}) collective-permute-start(bf16[32,3712]{1,0:T(8,128)(2,1)S(1)} %pad.9.refs_0_), channel_id=1, source_target_pairs={{8,0},{16,8},{24,16},{28,24},{20,28},{12,20},{4,12},{0,4},{9,1},{1... | collective-permute-start | bytes 712712 | tf_op jit(solution)/shard_map/ppermute | solution.py:391
  5.1 14.0 %collective-permute-start.1 = (bf16[32,3840]{1,0:T(8,128)(2,1)S(1)}, bf16[32,3840]{1,0:T(8,128)(2,1)S(1)}, u32[]{:S(2)}, u32[]{:S(2)}) collective-permute-start(bf16[32,3840]{1,0:T(8,128)(2,1)S(1)} %slice.9.refs_0_), channel_id=1, source_target_pairs={{8,0},{16,8},{24,16},{28,24},{20,28},{12,20},{4,12},{0,4},{9,1},{1... | collective-permute-start | bytes 737288 | tf_op jit(solution)/shard_map/ppermute | solution.py:391
  9.9 9.1 %collective-permute-start.2 = (bf16[32,3840]{1,0:T(8,128)(2,1)S(1)}, bf16[32,3840]{1,0:T(8,128)(2,1)S(1)}, u32[]{:S(2)}, u32[]{:S(2)}) collective-permute-start(bf16[32,3840]{1,0:T(8,128)(2,1)S(1)} %collective-permute-done.refs_1_), channel_id=1, source_target_pairs={{0,8},{8,16},{16,24},{24,28},{28,20},{20,12},{12,4},{4,0},{1,9},{9... | collective-permute-start | bytes 737288 | tf_op jit(solution)/shard_map/ppermute | solution.py:388
  11.7 12.2 %collective-permute-start.3 = (bf16[32,3712]{1,0:T(8,128)(2,1)S(1)}, bf16[32,3712]{1,0:T(8,128)(2,1)S(1)}, u32[]{:S(2)}, u32[]{:S(2)}) collective-permute-start(bf16[32,3712]{1,0:T(8,128)(2,1)S(1)} %pad.9.refs_0_), channel_id=1, source_target_pairs={{0,8},{8,16},{16,24},{24,28},{28,20},{20,12},{12,4},{4,0},{1,9},{9... | collective-permute-start | bytes 712712 | tf_op jit(solution)/shard_map/ppermute | solution.py:388
  13.8 12.6 %collective-permute-start.10 = (bf16[32,3712]{1,0:T(8,128)(2,1)S(1)}, bf16[32,3712]{1,0:T(8,128)(2,1)S(1)}, u32[]{:S(2)}, u32[]{:S(2)}) collective-permute-start(bf16[32,3712]{1,0:T(8,128)(2,1)S(1)} %collective-permute-done.4.refs_2_), channel_id=1, source_target_pairs={{8,0},{16,8},{24,16},{28,24},{20,28},{12,20},{4,12},{0,4},{9,1},{1... | collective-permute-start | bytes 712712 | tf_op jit(solution)/shard_map/ppermute | solution.py:391
  19.1 10.4 %collective-permute-start.6 = (bf16[32,3840]{1,0:T(8,128)(2,1)S(1)}, bf16[32,3840]{1,0:T(8,128)(2,1)S(1)}, u32[]{:S(2)}, u32[]{:S(2)}) collective-permute-start(bf16[32,3840]{1,0:T(8,128)(2,1)S(1)} %collective-permute-done.1.refs_2_), channel_id=1, source_target_pairs={{8,0},{16,8},{24,16},{28,24},{20,28},{12,20},{4,12},{0,4},{9,1},{1... | collective-permute-start | bytes 737288 | tf_op jit(solution)/shard_map/ppermute | solution.py:391
  19.1 10.4 %collective-permute-start.7 = (bf16[32,3840]{1,0:T(8,128)(2,1)S(1)}, bf16[32,3840]{1,0:T(8,128)(2,1)S(1)}, u32[]{:S(2)}, u32[]{:S(2)}) collective-permute-start(bf16[32,3840]{1,0:T(8,128)(2,1)S(1)} %collective-permute-done.2.refs_3_), channel_id=1, source_target_pairs={{0,8},{8,16},{16,24},{24,28},{28,20},{20,12},{12,4},{4,0},{1,9},{9... | collective-permute-start | bytes 737288 | tf_op jit(solution)/shard_map/ppermute | solution.py:388
  23.9 10.5 %collective-permute-start.5 = (bf16[32,3712]{1,0:T(8,128)(2,1)S(1)}, bf16[32,3712]{1,0:T(8,128)(2,1)}, u32[]{:S(2)}, u32[]{:S(2)}) collective-permute-start(bf16[32,3712]{1,0:T(8,128)(2,1)S(1)} %collective-permute-done.3.refs_1_), channel_id=1, source_target_pairs={{0,8},{8,16},{16,24},{24,28},{28,20},{20,12},{12,4},{4,0},{1,9},{9... | collective-permute-start | bytes 712712 | tf_op jit(solution)/shard_map/ppermute | solution.py:388
  26.4 9.8 %collective-permute-start.12 = (bf16[32,3712]{1,0:T(8,128)(2,1)S(1)}, bf16[32,3712]{1,0:T(8,128)(2,1)}, u32[]{:S(2)}, u32[]{:S(2)}) collective-permute-start(bf16[32,3712]{1,0:T(8,128)(2,1)S(1)} %collective-permute-done.10.refs_6_), channel_id=1, source_target_pairs={{8,0},{16,8},{24,16},{28,24},{20,28},{12,20},{4,12},{0,4},{9,1},{1... | collective-permute-start | bytes 712712 | tf_op jit(solution)/shard_map/ppermute | solution.py:391
  29.4 16.4 %collective-permute-start.8 = (bf16[32,3840]{1,0:T(8,128)(2,1)S(1)}, bf16[32,3840]{1,0:T(8,128)(2,1)S(1)}, u32[]{:S(2)}, u32[]{:S(2)}) collective-permute-start(bf16[32,3840]{1,0:T(8,128)(2,1)S(1)} %collective-permute-done.6.refs_2_), channel_id=1, source_target_pairs={{8,0},{16,8},{24,16},{28,24},{20,28},{12,20},{4,12},{0,4},{9,1},{1... | collective-permute-start | bytes 737288 | tf_op jit(solution)/shard_map/ppermute | solution.py:391
  29.4 16.5 %collective-permute-start.9 = (bf16[32,3840]{1,0:T(8,128)(2,1)S(1)}, bf16[32,3840]{1,0:T(8,128)(2,1)S(1)}, u32[]{:S(2)}, u32[]{:S(2)}) collective-permute-start(bf16[32,3840]{1,0:T(8,128)(2,1)S(1)} %collective-permute-done.7.refs_3_), channel_id=1, source_target_pairs={{0,8},{8,16},{16,24},{24,28},{28,20},{20,12},{12,4},{4,0},{1,9},{9... | collective-permute-start | bytes 737288 | tf_op jit(solution)/shard_map/ppermute | solution.py:388
  34.4 11.5 %collective-permute-start.11 = (bf16[32,3712]{1,0:T(8,128)(2,1)}, bf16[32,3712]{1,0:T(8,128)(2,1)}, u32[]{:S(2)}, u32[]{:S(2)}) collective-permute-start(bf16[32,3712]{1,0:T(8,128)(2,1)} %collective-permute-done.5.refs_3_), channel_id=1, source_target_pairs={{0,8},{8,16},{16,24},{24,28},{28,20},{20,12},{12,4},{4,0},{1,9},{9... | collective-permute-start | bytes 712712 | tf_op jit(solution)/shard_map/ppermute | solution.py:388
  36.2 9.7 %collective-permute-start.13 = (bf16[32,3712]{1,0:T(8,128)(2,1)}, bf16[32,3712]{1,0:T(8,128)(2,1)}, u32[]{:S(2)}, u32[]{:S(2)}) collective-permute-start(bf16[32,3712]{1,0:T(8,128)(2,1)} %collective-permute-done.12.refs_8_), channel_id=1, source_target_pairs={{8,0},{16,8},{24,16},{28,24},{20,28},{12,20},{4,12},{0,4},{9,1},{1... | collective-permute-start | bytes 712712 | tf_op jit(solution)/shard_map/ppermute | solution.py:391
  68.9 10.7 %collective-permute-start.16 = (s16[15,48,256]{2,1,0:T(8,128)(2,1)S(1)}, s16[15,48,256]{2,1,0:T(8,128)(2,1)S(1)}, u32[]{:S(2)}, u32[]{:S(2)}) collective-permute-start(s16[15,48,256]{2,1,0:T(8,128)(2,1)S(1)} %second_send_kernel.2), channel_id=1, source_target_pairs={{0,2},{1,3},{2,0},{3,1},{4,6},{5,7},{6,4},{7,5},{8,10},{9,11},{10,... | collective-permute-start | bytes 1105928 | tf_op jit(solution)/shard_map/ppermute | solution.py:499
  77.2 7.7 %collective-permute-start.20 = (s16[15,16,256]{2,1,0:T(8,128)(2,1)S(1)}, s16[15,16,256]{2,1,0:T(8,128)(2,1)S(1)}, u32[]{:S(2)}, u32[]{:S(2)}) collective-permute-start(s16[15,16,256]{2,1,0:T(8,128)(2,1)S(1)} %second_send_kernel.3), channel_id=1, source_target_pairs={{0,2},{1,3},{2,0},{3,1},{4,6},{5,7},{6,4},{7,5},{8,10},{9,11},{10,... | collective-permute-start | bytes 368648 | tf_op jit(solution)/shard_map/ppermute | solution.py:499
  80.7 17.3 %collective-permute-start.17 = (s16[4,48,128]{2,1,0:T(8,128)(2,1)S(1)}, s16[4,48,128]{2,1,0:T(8,128)(2,1)S(1)}, u32[]{:S(2)}, u32[]{:S(2)}) collective-permute-start(s16[4,48,128]{2,1,0:T(8,128)(2,1)S(1)} %get-tuple-element.39), channel_id=1, source_target_pairs={{0,20},{8,12},{16,4},{24,0},{28,8},{20,16},{12,24},{4,28},{1,21},{... | collective-permute-start | bytes 147464 | tf_op jit(solution)/shard_map/ppermute | solution.py:526
  84.5 14.8 %collective-permute-start.18 = (s16[4,48,128]{2,1,0:T(8,128)(2,1)S(1)}, s16[4,48,128]{2,1,0:T(8,128)(2,1)S(1)}, u32[]{:S(2)}, u32[]{:S(2)}) collective-permute-start(s16[4,48,128]{2,1,0:T(8,128)(2,1)S(1)} %get-tuple-element.40), channel_id=1, source_target_pairs={{0,24},{8,28},{16,20},{24,12},{28,4},{20,0},{12,8},{4,16},{1,25},{... | collective-permute-start | bytes 147464 | tf_op jit(solution)/shard_map/ppermute | solution.py:526
  85.6 8.6 %collective-permute-start.25 = (s16[4,16,128]{2,1,0:T(8,128)(2,1)S(1)}, s16[4,16,128]{2,1,0:T(8,128)(2,1)S(1)}, u32[]{:S(2)}, u32[]{:S(2)}) collective-permute-start(s16[4,16,128]{2,1,0:T(8,128)(2,1)S(1)} %get-tuple-element.48), channel_id=1, source_target_pairs={{0,20},{8,12},{16,4},{24,0},{28,8},{20,16},{12,24},{4,28},{1,21},{... | collective-permute-start | bytes 49160 | tf_op jit(solution)/shard_map/ppermute | solution.py:526
  94.2 12.3 %collective-permute-start.21 = (s16[4,64,128]{2,1,0:T(8,128)(2,1)S(1)}, s16[4,64,128]{2,1,0:T(8,128)(2,1)S(1)}, u32[]{:S(2)}, u32[]{:S(2)}) collective-permute-start(s16[4,64,128]{2,1,0:T(8,128)(2,1)S(1)} %get-tuple-element.44), channel_id=1, source_target_pairs={{0,4},{8,0},{16,8},{24,16},{28,24},{20,28},{12,20},{4,12},{1,5},{9... | collective-permute-start | bytes 196616 | tf_op jit(solution)/shard_map/ppermute | solution.py:526
  94.9 11.6 %collective-permute-start.22 = (s16[4,64,128]{2,1,0:T(8,128)(2,1)S(1)}, s16[4,64,128]{2,1,0:T(8,128)(2,1)S(1)}, u32[]{:S(2)}, u32[]{:S(2)}) collective-permute-start(s16[4,64,128]{2,1,0:T(8,128)(2,1)S(1)} %get-tuple-element.45), channel_id=1, source_target_pairs={{0,8},{8,16},{16,24},{24,28},{28,20},{20,12},{12,4},{4,0},{1,9},{9... | collective-permute-start | bytes 196616 | tf_op jit(solution)/shard_map/ppermute | solution.py:526
  96.3 10.2 %collective-permute-start.23 = (s16[4,64,128]{2,1,0:T(8,128)(2,1)S(1)}, s16[4,64,128]{2,1,0:T(8,128)(2,1)S(1)}, u32[]{:S(2)}, u32[]{:S(2)}) collective-permute-start(s16[4,64,128]{2,1,0:T(8,128)(2,1)S(1)} %get-tuple-element.46), channel_id=1, source_target_pairs={{0,12},{8,4},{16,0},{24,8},{28,16},{20,24},{12,28},{4,20},{1,13},{... | collective-permute-start | bytes 196616 | tf_op jit(solution)/shard_map/ppermute | solution.py:526
  98.0 8.5 %collective-permute-start.24 = (s16[4,64,128]{2,1,0:T(8,128)(2,1)S(1)}, s16[4,64,128]{2,1,0:T(8,128)(2,1)S(1)}, u32[]{:S(2)}, u32[]{:S(2)}) collective-permute-start(s16[4,64,128]{2,1,0:T(8,128)(2,1)S(1)} %get-tuple-element.47), channel_id=1, source_target_pairs={{0,16},{8,24},{16,28},{24,20},{28,12},{20,4},{12,0},{4,8},{1,17},{... | collective-permute-start | bytes 196616 | tf_op jit(solution)/shard_map/ppermute | solution.py:526
  99.2 7.2 %collective-permute-start.19 = (s16[4,48,128]{2,1,0:T(8,128)(2,1)S(1)}, s16[4,48,128]{2,1,0:T(8,128)(2,1)S(1)}, u32[]{:S(2)}, u32[]{:S(2)}) collective-permute-start(s16[4,48,128]{2,1,0:T(8,128)(2,1)S(1)} %get-tuple-element.41), channel_id=1, source_target_pairs={{0,28},{8,20},{16,12},{24,4},{28,0},{20,8},{12,16},{4,24},{1,29},{... | collective-permute-start | bytes 147464 | tf_op jit(solution)/shard_map/ppermute | solution.py:526
  (15 other events, 235.9 us)

commit v8 on v7

--- a/solution.py
+++ b/solution.py
@@ -12,7 +12,7 @@
 K_BLOCK = 3840
 C_BLOCK = 480
 SLOTS = 3
-EARLY = 3
+EARLY = 0
 COPIES = 4
 FIRST_PART = 47
 STEPS = 8.0
@@ -332,7 +332,7 @@
         out_specs=jax.tree.map(lambda _: pl.BlockSpec(memory_space=pltpu.VMEM), out_shape),
         scratch_shapes=list(scratch),
         input_output_aliases=aliases,
-        compiler_params=pltpu.CompilerParams(vmem_limit_bytes=5 * MIB + room),
+        compiler_params=pltpu.CompilerParams(vmem_limit_bytes=8 * MIB + room),
         cost_estimate=pl.CostEstimate(
             flops=cost[0], bytes_accessed=cost[1], transcendentals=0
         ),
@@ -371,29 +371,6 @@
     onward = [(walk[i], walk[(i + 1) % grid_size]) for i in range(grid_size)]
     back = [(b, a) for a, b in onward]
 
-    longer = grid_size // 2
-    order = [0]
-    for hop in range(1, longer):
-        order += [-hop, hop]
-    order.append(longer)
-    near, far, far_edges = [], [], []
-    for number, at in enumerate(range(0, depth, K_BLOCK)):
-        own = amplitudes[:, at : at + K_BLOCK]
-        size = own.shape[1]
-        own = jnp.pad(own, ((0, 0), (0, ceil_to(size, LANES) - size)))
-        ahead = behind = own
-        pieces = [own]
-        for hop in range(1, longer + 1):
-            if hop < longer or number % 2 == 0:
-                ahead = lax.ppermute(ahead, "grid", onward)
-                pieces.append(ahead)
-            if hop < longer or number % 2 == 1:
-                behind = lax.ppermute(behind, "grid", back)
-                pieces.append(behind)
-        near.append((at, size // LANES * LANES, pieces[:longer]))
-        far += pieces[longer:]
-        far_edges += [at] * longer
-
     counts = [FIRST_PART, count - FIRST_PART] if count > FIRST_PART else [count]
     firsts = [0, FIRST_PART][: len(counts)]
     bps = [ceil_to(number + 1, 16) for number in counts]
@@ -416,9 +393,9 @@
 
     half = slab // 2
     large = slab > 2 * LANES
-    cols = parts[1] if len(parts) > 1 else None
-    turned_near, held = [], []
-    for at, whole, pieces in near:
+    held_columns = parts[1] if len(parts) > 1 else None
+
+    def turn_near(at, whole, pieces):
         size = pieces[0].shape[1]
         out_shape = [jax.ShapeDtypeStruct((size, half), jnp.bfloat16)]
         args = list(pieces)
@@ -426,21 +403,49 @@
             pltpu.VMEM((half, size), jnp.bfloat16),
             pltpu.SemaphoreType.DMA((len(pieces),)),
         ]
-        if cols is not None:
-            out_shape.append(jax.ShapeDtypeStruct((cols[1], size), jnp.bfloat16))
+        cost = 4 * half * size
+        if held_columns is not None:
+            out_shape.append(jax.ShapeDtypeStruct((held_columns[1], size), jnp.bfloat16))
             args += [coupling, edge]
             scratch.append(pltpu.SemaphoreType.DMA((COPIES + 1,)))
-        part, *rest = local_call(
-            functools.partial(near_kernel, at, whole, cols, len(pieces)),
+            cost += 2 * held_columns[1] * size
+        return local_call(
+            functools.partial(near_kernel, at, whole, held_columns, len(pieces)),
             tuple(out_shape),
             "a" * len(args),
             args,
             scratch,
-            cost=(10**8, 4 * half * size + (2 * cols[1] * size if cols else 0)),
+            cost=(10**8, cost),
             room=2 * half * size * (2 if large else 1),
         )
-        turned_near.append(part)
-        held += rest
+
+    longer = grid_size // 2
+    order = [0]
+    for hop in range(1, longer):
+        order += [-hop, hop]
+    order.append(longer)
+    turned_near, held, far, far_edges = [], [], [], []
+    for number, at in enumerate(range(0, depth, K_BLOCK)):
+        own = amplitudes[:, at : at + K_BLOCK]
+        size = own.shape[1]
+        own = jnp.pad(own, ((0, 0), (0, ceil_to(size, LANES) - size)))
+        ahead = behind = own
+        pieces = [own]
+        for hop in range(1, longer + 1):
+            if hop == longer:
+                part, *rest = turn_near(at, size // LANES * LANES, pieces[:longer])
+                ahead, behind, part = lax.optimization_barrier((ahead, behind, part))
+                turned_near.append(part)
+                held += rest
+            if hop < longer or number % 2 == 0:
+                ahead = lax.ppermute(ahead, "grid", onward)
+                pieces.append(ahead)
+            if hop < longer or number % 2 == 1:
+                behind = lax.ppermute(behind, "grid", back)
+                pieces.append(behind)
+        far += pieces[longer:]
+        far_edges += [at] * longer
+
     totals, sends, got = [], [], []
     for part, (cols, span, bp) in enumerate(zip(parts, spans, bps)):
         cost = (2 * cols[1] * deep * slab, 2 * cols[1] * deep)

time: 109 us -> 111 us (1.018)
  starting transfers between devices: 40.6 us -> 29 us
  waiting for transfers between devices: 24.8 us -> 32.3 us
  local copies, waits for them, and re-layouts: 6.83 us -> 13.6 us
    ppermute x10 -> x7, starting transfers between devices: 21.7 us -> 11.1 us  [go_back(): return lax.ppermute(block, 'grid', pairs)]
    ppermute x7, waiting for transfers between devices: 7.82 us -> 16.2 us  [body(): behind = lax.ppermute(behind, 'grid', back)]
    unnamed x22 -> x38, local copies, waits for them, and re-layouts: 3.3 us -> 10.1 us
    ppermute x7, waiting for transfers between devices: 8.68 us -> 4.69 us  [body(): ahead = lax.ppermute(ahead, 'grid', onward)]
    ppermute x10 -> x7, waiting for transfers between devices: 2.91 us -> 4.58 us  [go_back(): return lax.ppermute(block, 'grid', pairs)]
    ppermute x2, waiting for transfers between devices: 1.68 us -> 3.15 us  [body(): got = [lax.ppermute(send, 'rep', high_pairs) for send in sends]]
  transfers between devices with their start and end apart: 28 -> 25, of which waited for: 12 -> 12; matrix products, arithmetic and copies ran while one was open for 2% -> 2% of each run, Pallas kernels for 12% -> 11%
where the time goes in v8:
time: 111 us
  Pallas kernels  35.8 us (32%)
  waiting for transfers between devices  32.3 us (29%)
  starting transfers between devices  29 us (26%)
  local copies, waits for them, and re-layouts  13.6 us (12%)
    pallas_call x11, Pallas kernels, local_call(): pl.pallas_call(kernel, out_shape=out_shape, in_specs=[pl.BlockSpec(memory...  35.8 us
    ppermute x7, waiting for transfers between devices, body(): behind = lax.ppermute(behind, 'grid', back)  16.2 us
    ppermute x7, starting transfers between devices, body(): ahead = lax.ppermute(ahead, 'grid', onward)  13.1 us
    ppermute x7, starting transfers between devices, go_back(): return lax.ppermute(block, 'grid', pairs)  11.1 us
    unnamed x38, local copies, waits for them, and re-layouts  10.1 us
    ppermute x7, waiting for transfers between devices, body(): ahead = lax.ppermute(ahead, 'grid', onward)  4.69 us
    ppermute x7, waiting for transfers between devices, go_back(): return lax.ppermute(block, 'grid', pairs)  4.58 us
    ppermute x2, waiting for transfers between devices, body(): arrived = lax.ppermute(send, 'rep', low_pairs)  3.7 us
  transfers between devices with their start and end apart: 25, of which 12 were waited for; matrix products, arithmetic and copies ran while one was open for 2% of the time, Pallas kernels for 11%

profile of v8, /device:TPU:0, one launch (start us, length us, event | category | flops | bytes accessed | tf_op | source)
XLA Modules:
  0.0 111.0 jit_solution(14559025768067948041)
XLA Ops:
  1.0 3.1 %collective-permute-start = (bf16[32,3840]{1,0:T(8,128)(2,1)S(1)}, bf16[32,3840]{1,0:T(8,128)(2,1)S(1)}, u32[]{:S(2)}, u32[]{:S(2)}) collective-permute-start(bf16[32,3840]{1,0:T(8,128)(2,1)S(1)} %slice.9.refs_0_), channel_id=1, source_target_pairs={{0,8},{8,16},{16,24},{24,28},{28,20},{20,12},{12,4},{4,0},{1,9},{9... | collective-permute-start | bytes 737288 | tf_op jit(solution)/shard_map/ppermute | solution.py:441
  5.0 2.0 %collective-permute-start.9 = (bf16[32,3712]{1,0:T(8,128)(2,1)S(1)}, bf16[32,3712]{1,0:T(8,128)(2,1)S(1)}, u32[]{:S(2)}, u32[]{:S(2)}) collective-permute-start(bf16[32,3712]{1,0:T(8,128)(2,1)S(1)} %pad.9.refs_0_), channel_id=1, source_target_pairs={{8,0},{16,8},{24,16},{28,24},{20,28},{12,20},{4,12},{0,4},{9,1},{1... | collective-permute-start | bytes 712712 | tf_op jit(solution)/shard_map/ppermute | solution.py:444
  7.2 3.6 %collective-permute-done.refs_1_ = bf16[32,3840]{1,0:T(8,128)(2,1)S(1)} collective-permute-done((bf16[32,3840]{1,0:T(8,128)(2,1)S(1)}, bf16[32,3840]{1,0:T(8,128)(2,1)S(1)}, u32[]{:S(2)}, u32[]{:S(2)}) %collective-permute-start) | collective-permute-done | bytes 245792 | tf_op jit(solution)/shard_map/ppermute | solution.py:441
  10.8 2.1 %collective-permute-start.1 = (bf16[32,3840]{1,0:T(8,128)(2,1)S(1)}, bf16[32,3840]{1,0:T(8,128)(2,1)S(1)}, u32[]{:S(2)}, u32[]{:S(2)}) collective-permute-start(bf16[32,3840]{1,0:T(8,128)(2,1)S(1)} %collective-permute-done.refs_1_), channel_id=1, source_target_pairs={{0,8},{8,16},{16,24},{24,28},{28,20},{20,12},{12,4},{4,0},{1,9},{9... | collective-permute-start | bytes 737288 | tf_op jit(solution)/shard_map/ppermute | solution.py:441
  12.9 5.1 %collective-permute-done.9.refs_2_ = bf16[32,3712]{1,0:T(8,128)(2,1)S(1)} collective-permute-done((bf16[32,3712]{1,0:T(8,128)(2,1)S(1)}, bf16[32,3712]{1,0:T(8,128)(2,1)S(1)}, u32[]{:S(2)}, u32[]{:S(2)}) %collective-permute-start.9) | collective-permute-done | bytes 237600 | tf_op jit(solution)/shard_map/ppermute | solution.py:444
  18.0 2.0 %collective-permute-start.7 = (bf16[32,3712]{1,0:T(8,128)(2,1)S(1)}, bf16[32,3712]{1,0:T(8,128)(2,1)S(1)}, u32[]{:S(2)}, u32[]{:S(2)}) collective-permute-start(bf16[32,3712]{1,0:T(8,128)(2,1)S(1)} %collective-permute-done.6.refs_1_), channel_id=1, source_target_pairs={{0,8},{8,16},{16,24},{24,28},{28,20},{20,12},{12,4},{4,0},{1,9},{9... | collective-permute-start | bytes 712712 | tf_op jit(solution)/shard_map/ppermute | solution.py:441
  21.1 2.1 %collective-permute-start.2 = (bf16[32,3840]{1,0:T(8,128)(2,1)S(1)}, bf16[32,3840]{1,0:T(8,128)(2,1)S(1)}, u32[]{:S(2)}, u32[]{:S(2)}) collective-permute-start(bf16[32,3840]{1,0:T(8,128)(2,1)S(1)} %collective-permute-done.1.refs_3_), channel_id=1, source_target_pairs={{0,8},{8,16},{16,24},{24,28},{28,20},{20,12},{12,4},{4,0},{1,9},{9... | collective-permute-start | bytes 737288 | tf_op jit(solution)/shard_map/ppermute | solution.py:441
  23.3 5.1 %collective-permute-done.10.refs_6_ = bf16[32,3712]{1,0:T(8,128)(2,1)S(1)} collective-permute-done((bf16[32,3712]{1,0:T(8,128)(2,1)S(1)}, bf16[32,3712]{1,0:T(8,128)(2,1)S(1)}, u32[]{:S(2)}, u32[]{:S(2)}) %collective-permute-start.10) | collective-permute-done | bytes 237600 | tf_op jit(solution)/shard_map/ppermute | solution.py:444
  28.4 2.0 %collective-permute-start.8 = (bf16[32,3712]{1,0:T(8,128)(2,1)S(1)}, bf16[32,3712]{1,0:T(8,128)(2,1)S(1)}, u32[]{:S(2)}, u32[]{:S(2)}) collective-permute-start(bf16[32,3712]{1,0:T(8,128)(2,1)S(1)} %collective-permute-done.7.refs_3_), channel_id=1, source_target_pairs={{0,8},{8,16},{16,24},{24,28},{28,20},{20,12},{12,4},{4,0},{1,9},{9... | collective-permute-start | bytes 712712 | tf_op jit(solution)/shard_map/ppermute | solution.py:441
  31.8 2.8 %near_kernel.2 = (bf16[3840,128]{1,0:T(8,128)(2,1)S(1)}, bf16[784,3840]{1,0:T(8,128)(2,1)S(1)}) custom-call(bf16[32,3840]{1,0:T(8,128)(2,1)S(1)} %slice.9.refs_0_, bf16[32,3840]{1,0:T(8,128)(2,1)S(1)} %collective-permute-done.refs_1_, bf16[32,3840]{1,0:T(8,128)(2,1)S(1)} %collective-permute-done.3.refs_2_, ...), custom_call_target="tpu_custom_call" | custom-call | flops 100000000 | bytes 7987200 | tf_op jit(solution)/shard_map/near_kernel/pallas_call | solution.py:328
  34.7 2.5 %copy-done = bf16[784,3840]{1,0:T(8,128)(2,1)} copy-done((bf16[784,3840]{1,0:T(8,128)(2,1)}, bf16[784,3840]{1,0:T(8,128)(2,1)S(1)}, u32[]{:S(2)}) %copy-start) | copy-done | bytes 6021144
  37.9 1.6 %collective-permute-start.12 = (bf16[32,3840]{1,0:T(8,128)(2,1)S(1)}, bf16[32,3840]{1,0:T(8,128)(2,1)}, u32[]{:S(2)}, u32[]{:S(2)}) collective-permute-start(bf16[32,3840]{1,0:T(8,128)(2,1)S(1)} %collective-permute-done.2.refs_3_), channel_id=1, source_target_pairs={{0,8},{8,16},{16,24},{24,28},{28,20},{20,12},{12,4},{4,0},{1,9},{9... | collective-permute-start | bytes 737288 | tf_op jit(solution)/shard_map/ppermute | solution.py:441
  39.5 2.7 %near_kernel.3 = (bf16[3712,128]{1,0:T(8,128)(2,1)S(1)}, bf16[784,3712]{1,0:T(8,128)(2,1)S(1)}) custom-call(bf16[32,3712]{1,0:T(8,128)(2,1)S(1)} %pad.9.refs_0_, bf16[32,3712]{1,0:T(8,128)(2,1)S(1)} %collective-permute-done.6.refs_1_, bf16[32,3712]{1,0:T(8,128)(2,1)S(1)} %collective-permute-done.9.refs_2_, ...), custom_call_target="tpu_custom_call" | custom-call | flops 100000000 | bytes 7720960 | tf_op jit(solution)/shard_map/near_kernel/pallas_call | solution.py:328
  42.3 2.4 %copy-done.1 = bf16[784,3712]{1,0:T(8,128)(2,1)} copy-done((bf16[784,3712]{1,0:T(8,128)(2,1)}, bf16[784,3712]{1,0:T(8,128)(2,1)S(1)}, u32[]{:S(2)}) %copy-start.1) | copy-done | bytes 5820440
  45.9 6.0 %collective-permute-done.13.refs_9_ = bf16[32,3712]{1,0:T(8,128)(2,1)} collective-permute-done((bf16[32,3712]{1,0:T(8,128)(2,1)}, bf16[32,3712]{1,0:T(8,128)(2,1)}, u32[]{:S(2)}, u32[]{:S(2)}) %collective-permute-start.13) | collective-permute-done | bytes 237600 | tf_op jit(solution)/shard_map/ppermute | solution.py:444
  55.5 20.0 %lead_kernel.1 = (f32[2,2880,128]{2,1,0:T(8,128)S(1)}, bf16[7552,256]{1,0:T(8,128)(2,1)S(1)}, s16[2,15,48,256]{3,2,1,0:T(8,128)(2,1)S(1)}) custom-call(s32[1]{0:T(128)} %bitcast.1.rep_ref, bf16[3840,128]{1,0:T(8,128)(2,1)S(1)} %get-tuple-element.29.refs_0_, bf16[3712,128]{1,0:T(8,128)(2,1)S(1)} %get-tuple-element.31.refs_1_, ...), custom_call_target="tpu_custom_call" | custom-call | flops 10950279168 | bytes 42774528 | tf_op jit(solution)/shard_map/lead_kernel/pallas_call | solution.py:328
  75.5 2.2 %collective-permute-done.14.got_ref = s16[2,15,48,256]{3,2,1,0:T(8,128)(2,1)S(1)} collective-permute-done((s16[2,15,48,256]{3,2,1,0:T(8,128)(2,1)S(1)}, s16[2,15,48,256]{3,2,1,0:T(8,128)(2,1)S(1)}, u32[]{:S(2)}, u32[]{:S(2)}) %collective-permute-start.14) | collective-permute-done | bytes 737312 | tf_op jit(solution)/shard_map/ppermute | solution.py:484
  80.1 4.2 %rest_kernel.1 = (f32[2,964,128]{2,1,0:T(8,128)S(1)}, s16[2,15,16,256]{3,2,1,0:T(8,128)(2,1)S(1)}) custom-call(s32[1]{0:T(128)} %bitcast.1.rep_ref, bf16[7552,256]{1,0:T(8,128)(2,1)S(1)} %get-tuple-element.37.turned, bf16[784,3840]{1,0:T(8,128)(2,1)S(1)} %bitcast.10, bf16[784,3712]{1,0:T(8,128)(2,1)S(1)} %bitcast.12), custom_call_target="tpu_custom_call" | custom-call | flops 3031433216 | bytes 11841536 | tf_op jit(solution)/shard_map/rest_kernel/pallas_call | solution.py:328
  90.3 1.9 %collective-permute-done.16.got_ref = s16[15,16,256]{2,1,0:T(8,128)(2,1)S(1)} collective-permute-done((s16[15,16,256]{2,1,0:T(8,128)(2,1)S(1)}, s16[15,16,256]{2,1,0:T(8,128)(2,1)S(1)}, u32[]{:S(2)}, u32[]{:S(2)}) %collective-permute-start.16) | collective-permute-done | bytes 122912 | tf_op jit(solution)/shard_map/ppermute | solution.py:504
  95.3 2.6 %collective-permute-start.21 = (s16[4,64,128]{2,1,0:T(8,128)(2,1)S(1)}, s16[4,64,128]{2,1,0:T(8,128)(2,1)S(1)}, u32[]{:S(2)}, u32[]{:S(2)}) collective-permute-start(s16[4,64,128]{2,1,0:T(8,128)(2,1)S(1)} %get-tuple-element.47), channel_id=1, source_target_pairs={{0,16},{8,24},{16,28},{24,20},{28,12},{20,4},{12,0},{4,8},{1,17},{... | collective-permute-start | bytes 196616 | tf_op jit(solution)/shard_map/ppermute | solution.py:531
  99.2 2.5 %collective-permute-start.23 = (s16[4,64,128]{2,1,0:T(8,128)(2,1)S(1)}, s16[4,64,128]{2,1,0:T(8,128)(2,1)S(1)}, u32[]{:S(2)}, u32[]{:S(2)}) collective-permute-start(s16[4,64,128]{2,1,0:T(8,128)(2,1)S(1)} %get-tuple-element.49), channel_id=1, source_target_pairs={{0,24},{8,28},{16,20},{24,12},{28,4},{20,0},{12,8},{4,16},{1,25},{... | collective-permute-start | bytes 196616 | tf_op jit(solution)/shard_map/ppermute | solution.py:531
  101.7 2.3 %collective-permute-start.24 = (s16[4,64,128]{2,1,0:T(8,128)(2,1)S(1)}, s16[4,64,128]{2,1,0:T(8,128)(2,1)S(1)}, u32[]{:S(2)}, u32[]{:S(2)}) collective-permute-start(s16[4,64,128]{2,1,0:T(8,128)(2,1)S(1)} %get-tuple-element.50), channel_id=1, source_target_pairs={{0,28},{8,20},{16,12},{24,4},{28,0},{20,8},{12,16},{4,24},{1,29},{... | collective-permute-start | bytes 196616 | tf_op jit(solution)/shard_map/ppermute | solution.py:531
  104.6 3.3 %collective-permute-done.23.refs_6_ = s16[4,64,128]{2,1,0:T(8,128)(2,1)S(1)} collective-permute-done((s16[4,64,128]{2,1,0:T(8,128)(2,1)S(1)}, s16[4,64,128]{2,1,0:T(8,128)(2,1)S(1)}, u32[]{:S(2)}, u32[]{:S(2)}) %collective-permute-start.23) | collective-permute-done | bytes 65568 | tf_op jit(solution)/shard_map/ppermute | solution.py:531
  108.8 2.2 %update_kernel.1 = f32[15,32,480]{2,1,0:T(8,128)} custom-call(s32[1]{0:T(128)} %bitcast.me_ref, f32[15]{0:T(128)S(1)} %copy-done.11, s32[15]{0:T(128)S(1)} %copy-done.12, s16[4,64,128]{2,1,0:T(8,128)(2,1)S(1)} %get-tuple-element.43.refs_0_, s16[4,64,128]{2,1,0:T(8,128)(2,1)S(1)} %collective-permute-done.18.refs_1_, ...), custom_call_target="tpu_custom_call" | custom-call | flops 10000000 | bytes 4000000 | tf_op jit(solution)/shard_map/update_kernel/pallas_call | solution.py:328
  (84 shorter events, 24.4 us)
Async XLA Ops:
  1.0 9.8 %collective-permute-start = (bf16[32,3840]{1,0:T(8,128)(2,1)S(1)}, bf16[32,3840]{1,0:T(8,128)(2,1)S(1)}, u32[]{:S(2)}, u32[]{:S(2)}) collective-permute-start(bf16[32,3840]{1,0:T(8,128)(2,1)S(1)} %slice.9.refs_0_), channel_id=1, source_target_pairs={{0,8},{8,16},{16,24},{24,28},{28,20},{20,12},{12,4},{4,0},{1,9},{9... | collective-permute-start | bytes 737288 | tf_op jit(solution)/shard_map/ppermute | solution.py:441
  4.0 8.9 %collective-permute-start.3 = (bf16[32,3840]{1,0:T(8,128)(2,1)S(1)}, bf16[32,3840]{1,0:T(8,128)(2,1)S(1)}, u32[]{:S(2)}, u32[]{:S(2)}) collective-permute-start(bf16[32,3840]{1,0:T(8,128)(2,1)S(1)} %slice.9.refs_0_), channel_id=1, source_target_pairs={{8,0},{16,8},{24,16},{28,24},{20,28},{12,20},{4,12},{0,4},{9,1},{1... | collective-permute-start | bytes 737288 | tf_op jit(solution)/shard_map/ppermute | solution.py:444
  5.0 13.0 %collective-permute-start.9 = (bf16[32,3712]{1,0:T(8,128)(2,1)S(1)}, bf16[32,3712]{1,0:T(8,128)(2,1)S(1)}, u32[]{:S(2)}, u32[]{:S(2)}) collective-permute-start(bf16[32,3712]{1,0:T(8,128)(2,1)S(1)} %pad.9.refs_0_), channel_id=1, source_target_pairs={{8,0},{16,8},{24,16},{28,24},{20,28},{12,20},{4,12},{0,4},{9,1},{1... | collective-permute-start | bytes 712712 | tf_op jit(solution)/shard_map/ppermute | solution.py:444
  7.1 11.0 %collective-permute-start.6 = (bf16[32,3712]{1,0:T(8,128)(2,1)S(1)}, bf16[32,3712]{1,0:T(8,128)(2,1)S(1)}, u32[]{:S(2)}, u32[]{:S(2)}) collective-permute-start(bf16[32,3712]{1,0:T(8,128)(2,1)S(1)} %pad.9.refs_0_), channel_id=1, source_target_pairs={{0,8},{8,16},{16,24},{24,28},{28,20},{20,12},{12,4},{4,0},{1,9},{9... | collective-permute-start | bytes 712712 | tf_op jit(solution)/shard_map/ppermute | solution.py:441
  10.8 10.4 %collective-permute-start.1 = (bf16[32,3840]{1,0:T(8,128)(2,1)S(1)}, bf16[32,3840]{1,0:T(8,128)(2,1)S(1)}, u32[]{:S(2)}, u32[]{:S(2)}) collective-permute-start(bf16[32,3840]{1,0:T(8,128)(2,1)S(1)} %collective-permute-done.refs_1_), channel_id=1, source_target_pairs={{0,8},{8,16},{16,24},{24,28},{28,20},{20,12},{12,4},{4,0},{1,9},{9... | collective-permute-start | bytes 737288 | tf_op jit(solution)/shard_map/ppermute | solution.py:441
  12.9 10.4 %collective-permute-start.4 = (bf16[32,3840]{1,0:T(8,128)(2,1)S(1)}, bf16[32,3840]{1,0:T(8,128)(2,1)S(1)}, u32[]{:S(2)}, u32[]{:S(2)}) collective-permute-start(bf16[32,3840]{1,0:T(8,128)(2,1)S(1)} %collective-permute-done.3.refs_2_), channel_id=1, source_target_pairs={{8,0},{16,8},{24,16},{28,24},{20,28},{12,20},{4,12},{0,4},{9,1},{1... | collective-permute-start | bytes 737288 | tf_op jit(solution)/shard_map/ppermute | solution.py:444
  18.0 10.4 %collective-permute-start.10 = (bf16[32,3712]{1,0:T(8,128)(2,1)S(1)}, bf16[32,3712]{1,0:T(8,128)(2,1)S(1)}, u32[]{:S(2)}, u32[]{:S(2)}) collective-permute-start(bf16[32,3712]{1,0:T(8,128)(2,1)S(1)} %collective-permute-done.9.refs_2_), channel_id=1, source_target_pairs={{8,0},{16,8},{24,16},{28,24},{20,28},{12,20},{4,12},{0,4},{9,1},{1... | collective-permute-start | bytes 712712 | tf_op jit(solution)/shard_map/ppermute | solution.py:444
  18.0 10.4 %collective-permute-start.7 = (bf16[32,3712]{1,0:T(8,128)(2,1)S(1)}, bf16[32,3712]{1,0:T(8,128)(2,1)S(1)}, u32[]{:S(2)}, u32[]{:S(2)}) collective-permute-start(bf16[32,3712]{1,0:T(8,128)(2,1)S(1)} %collective-permute-done.6.refs_1_), channel_id=1, source_target_pairs={{0,8},{8,16},{16,24},{24,28},{28,20},{20,12},{12,4},{4,0},{1,9},{9... | collective-permute-start | bytes 712712 | tf_op jit(solution)/shard_map/ppermute | solution.py:441
  21.1 16.1 %collective-permute-start.2 = (bf16[32,3840]{1,0:T(8,128)(2,1)S(1)}, bf16[32,3840]{1,0:T(8,128)(2,1)S(1)}, u32[]{:S(2)}, u32[]{:S(2)}) collective-permute-start(bf16[32,3840]{1,0:T(8,128)(2,1)S(1)} %collective-permute-done.1.refs_3_), channel_id=1, source_target_pairs={{0,8},{8,16},{16,24},{24,28},{28,20},{20,12},{12,4},{4,0},{1,9},{9... | collective-permute-start | bytes 737288 | tf_op jit(solution)/shard_map/ppermute | solution.py:441
  23.3 14.0 %collective-permute-start.5 = (bf16[32,3840]{1,0:T(8,128)(2,1)S(1)}, bf16[32,3840]{1,0:T(8,128)(2,1)S(1)}, u32[]{:S(2)}, u32[]{:S(2)}) collective-permute-start(bf16[32,3840]{1,0:T(8,128)(2,1)S(1)} %collective-permute-done.4.refs_2_), channel_id=1, source_target_pairs={{8,0},{16,8},{24,16},{28,24},{20,28},{12,20},{4,12},{0,4},{9,1},{1... | collective-permute-start | bytes 737288 | tf_op jit(solution)/shard_map/ppermute | solution.py:444
  28.4 16.3 %collective-permute-start.11 = (bf16[32,3712]{1,0:T(8,128)(2,1)S(1)}, bf16[32,3712]{1,0:T(8,128)(2,1)}, u32[]{:S(2)}, u32[]{:S(2)}) collective-permute-start(bf16[32,3712]{1,0:T(8,128)(2,1)S(1)} %collective-permute-done.10.refs_6_), channel_id=1, source_target_pairs={{8,0},{16,8},{24,16},{28,24},{20,28},{12,20},{4,12},{0,4},{9,1},{1... | collective-permute-start | bytes 712712 | tf_op jit(solution)/shard_map/ppermute | solution.py:444
  28.4 16.3 %collective-permute-start.8 = (bf16[32,3712]{1,0:T(8,128)(2,1)S(1)}, bf16[32,3712]{1,0:T(8,128)(2,1)S(1)}, u32[]{:S(2)}, u32[]{:S(2)}) collective-permute-start(bf16[32,3712]{1,0:T(8,128)(2,1)S(1)} %collective-permute-done.7.refs_3_), channel_id=1, source_target_pairs={{0,8},{8,16},{16,24},{24,28},{28,20},{20,12},{12,4},{4,0},{1,9},{9... | collective-permute-start | bytes 712712 | tf_op jit(solution)/shard_map/ppermute | solution.py:441
  37.9 13.9 %collective-permute-start.12 = (bf16[32,3840]{1,0:T(8,128)(2,1)S(1)}, bf16[32,3840]{1,0:T(8,128)(2,1)}, u32[]{:S(2)}, u32[]{:S(2)}) collective-permute-start(bf16[32,3840]{1,0:T(8,128)(2,1)S(1)} %collective-permute-done.2.refs_3_), channel_id=1, source_target_pairs={{0,8},{8,16},{16,24},{24,28},{28,20},{20,12},{12,4},{4,0},{1,9},{9... | collective-permute-start | bytes 737288 | tf_op jit(solution)/shard_map/ppermute | solution.py:441
  45.4 6.4 %collective-permute-start.13 = (bf16[32,3712]{1,0:T(8,128)(2,1)}, bf16[32,3712]{1,0:T(8,128)(2,1)}, u32[]{:S(2)}, u32[]{:S(2)}) collective-permute-start(bf16[32,3712]{1,0:T(8,128)(2,1)} %collective-permute-done.11.refs_8_), channel_id=1, source_target_pairs={{8,0},{16,8},{24,16},{28,24},{20,28},{12,20},{4,12},{0,4},{9,1},{1... | collective-permute-start | bytes 712712 | tf_op jit(solution)/shard_map/ppermute | solution.py:444
  75.4 2.3 %collective-permute-start.14 = (s16[2,15,48,256]{3,2,1,0:T(8,128)(2,1)S(1)}, s16[2,15,48,256]{3,2,1,0:T(8,128)(2,1)S(1)}, u32[]{:S(2)}, u32[]{:S(2)}) collective-permute-start(s16[2,15,48,256]{3,2,1,0:T(8,128)(2,1)S(1)} %get-tuple-element.36), channel_id=1, source_target_pairs={{0,1},{1,0},{2,3},{3,2},{4,5},{5,4},{6,7},{7,6},{8,9},{9,8},{10,11... | collective-permute-start | bytes 2211848 | tf_op jit(solution)/shard_map/ppermute | solution.py:484
  78.6 10.7 %collective-permute-start.17 = (s16[15,48,256]{2,1,0:T(8,128)(2,1)S(1)}, s16[15,48,256]{2,1,0:T(8,128)(2,1)S(1)}, u32[]{:S(2)}, u32[]{:S(2)}) collective-permute-start(s16[15,48,256]{2,1,0:T(8,128)(2,1)S(1)} %second_send_kernel.2), channel_id=1, source_target_pairs={{0,2},{1,3},{2,0},{3,1},{4,6},{5,7},{6,4},{7,5},{8,10},{9,11},{10,... | collective-permute-start | bytes 1105928 | tf_op jit(solution)/shard_map/ppermute | solution.py:504
  86.8 5.4 %collective-permute-start.16 = (s16[15,16,256]{2,1,0:T(8,128)(2,1)S(1)}, s16[15,16,256]{2,1,0:T(8,128)(2,1)S(1)}, u32[]{:S(2)}, u32[]{:S(2)}) collective-permute-start(s16[15,16,256]{2,1,0:T(8,128)(2,1)S(1)} %second_send_kernel.3), channel_id=1, source_target_pairs={{0,2},{1,3},{2,0},{3,1},{4,6},{5,7},{6,4},{7,5},{8,10},{9,11},{10,... | collective-permute-start | bytes 368648 | tf_op jit(solution)/shard_map/ppermute | solution.py:504
  92.9 6.3 %collective-permute-start.18 = (s16[4,64,128]{2,1,0:T(8,128)(2,1)S(1)}, s16[4,64,128]{2,1,0:T(8,128)(2,1)S(1)}, u32[]{:S(2)}, u32[]{:S(2)}) collective-permute-start(s16[4,64,128]{2,1,0:T(8,128)(2,1)S(1)} %get-tuple-element.44), channel_id=1, source_target_pairs={{0,4},{8,0},{16,8},{24,16},{28,24},{20,28},{12,20},{4,12},{1,5},{9... | collective-permute-start | bytes 196616 | tf_op jit(solution)/shard_map/ppermute | solution.py:531
  93.4 8.3 %collective-permute-start.19 = (s16[4,64,128]{2,1,0:T(8,128)(2,1)S(1)}, s16[4,64,128]{2,1,0:T(8,128)(2,1)S(1)}, u32[]{:S(2)}, u32[]{:S(2)}) collective-permute-start(s16[4,64,128]{2,1,0:T(8,128)(2,1)S(1)} %get-tuple-element.45), channel_id=1, source_target_pairs={{0,8},{8,16},{16,24},{24,28},{28,20},{20,12},{12,4},{4,0},{1,9},{9... | collective-permute-start | bytes 196616 | tf_op jit(solution)/shard_map/ppermute | solution.py:531
  95.0 9.2 %collective-permute-start.20 = (s16[4,64,128]{2,1,0:T(8,128)(2,1)S(1)}, s16[4,64,128]{2,1,0:T(8,128)(2,1)S(1)}, u32[]{:S(2)}, u32[]{:S(2)}) collective-permute-start(s16[4,64,128]{2,1,0:T(8,128)(2,1)S(1)} %get-tuple-element.46), channel_id=1, source_target_pairs={{0,12},{8,4},{16,0},{24,8},{28,16},{20,24},{12,28},{4,20},{1,13},{... | collective-permute-start | bytes 196616 | tf_op jit(solution)/shard_map/ppermute | solution.py:531
  95.3 8.9 %collective-permute-start.21 = (s16[4,64,128]{2,1,0:T(8,128)(2,1)S(1)}, s16[4,64,128]{2,1,0:T(8,128)(2,1)S(1)}, u32[]{:S(2)}, u32[]{:S(2)}) collective-permute-start(s16[4,64,128]{2,1,0:T(8,128)(2,1)S(1)} %get-tuple-element.47), channel_id=1, source_target_pairs={{0,16},{8,24},{16,28},{24,20},{28,12},{20,4},{12,0},{4,8},{1,17},{... | collective-permute-start | bytes 196616 | tf_op jit(solution)/shard_map/ppermute | solution.py:531
  97.9 6.7 %collective-permute-start.22 = (s16[4,64,128]{2,1,0:T(8,128)(2,1)S(1)}, s16[4,64,128]{2,1,0:T(8,128)(2,1)S(1)}, u32[]{:S(2)}, u32[]{:S(2)}) collective-permute-start(s16[4,64,128]{2,1,0:T(8,128)(2,1)S(1)} %get-tuple-element.48), channel_id=1, source_target_pairs={{0,20},{8,12},{16,4},{24,0},{28,8},{20,16},{12,24},{4,28},{1,21},{... | collective-permute-start | bytes 196616 | tf_op jit(solution)/shard_map/ppermute | solution.py:531
  99.2 8.7 %collective-permute-start.23 = (s16[4,64,128]{2,1,0:T(8,128)(2,1)S(1)}, s16[4,64,128]{2,1,0:T(8,128)(2,1)S(1)}, u32[]{:S(2)}, u32[]{:S(2)}) collective-permute-start(s16[4,64,128]{2,1,0:T(8,128)(2,1)S(1)} %get-tuple-element.49), channel_id=1, source_target_pairs={{0,24},{8,28},{16,20},{24,12},{28,4},{20,0},{12,8},{4,16},{1,25},{... | collective-permute-start | bytes 196616 | tf_op jit(solution)/shard_map/ppermute | solution.py:531
  101.7 7.1 %collective-permute-start.24 = (s16[4,64,128]{2,1,0:T(8,128)(2,1)S(1)}, s16[4,64,128]{2,1,0:T(8,128)(2,1)S(1)}, u32[]{:S(2)}, u32[]{:S(2)}) collective-permute-start(s16[4,64,128]{2,1,0:T(8,128)(2,1)S(1)} %get-tuple-element.50), channel_id=1, source_target_pairs={{0,28},{8,20},{16,12},{24,4},{28,0},{20,8},{12,16},{4,24},{1,29},{... | collective-permute-start | bytes 196616 | tf_op jit(solution)/shard_map/ppermute | solution.py:531
  (20 other events, 285.4 us)

commit v9 on v6

--- a/solution.py
+++ b/solution.py
@@ -13,7 +13,7 @@
 C_BLOCK = 480
 SLOTS = 3
 COPIES = 4
-FIRST_PART = 47
+FIRST_PART = 45
 STEPS = 8.0
 TOP = 32767.0
 MIB = 1024 * 1024
@@ -192,40 +192,28 @@
     lax.fori_loop(0, width, step, 0)
 
 
-def pack_rows(count, rows_dev, kept_ref, got_ref, stage):
+def third_send_kernel(count, rows_dev, order, me_ref, kept_ref, got_ref, out_ref):
     pack = LANES // rows_dev
-    groups = stage.shape[1]
-    size, _, slab = kept_ref.shape
+    groups = out_ref.shape[1]
+    size = kept_ref.shape[0]
+    grid_size = len(order)
+    place = walk_place(me_ref[0], grid_size)
 
     def step(jj, carry):
         coded = []
         for jq in range(pack):
             j = jnp.minimum(jq * groups + jj, size - 1)
             coded.append(encode(kept_ref[j] + decode(from_code(got_ref[j]), count), count))
-        for g in range(slab // rows_dev):
-            own = [block[:, g * rows_dev : (g + 1) * rows_dev] for block in coded]
-            stage[g, jj] = to_code(jnp.concatenate(own, axis=1))
+        for number, offset in enumerate(order):
+            own = [block[:, number * rows_dev : (number + 1) * rows_dev] for block in coded]
+            target = walk_index(lax.rem(place + offset + grid_size, grid_size), grid_size)
+            out_ref[target, jj] = to_code(jnp.concatenate(own, axis=1))
         return carry
 
     lax.fori_loop(0, groups, step, 0)
 
 
-def third_send_kernel(count, rows_dev, kept_ref, got_ref, stage):
-    pack_rows(count, rows_dev, kept_ref, got_ref, stage)
-
-
-def last_send_kernel(count, rows_dev, parts, kept_ref, got_ref, *refs):
-    earlier, targets, stage = refs[: parts - 1], refs[parts - 1 : -1], refs[-1]
-    pack_rows(count, rows_dev, kept_ref, got_ref, stage)
-    for number, target in enumerate(targets):
-        at = 0
-        for source in (*earlier, stage):
-            bp = source.shape[2]
-            target[:, at : at + bp, :] = source[number]
-            at += bp
-
-
-def update_kernel(counts, bps, width, rows_dev, order, me_ref, occ_energy_ref, occ_irrep_ref, *refs):
+def update_kernel(counts, width, rows_dev, occ_energy_ref, occ_irrep_ref, *refs):
     (
         integrals_ref,
         row_energy_ref,
@@ -233,28 +221,21 @@
         row_irrep_ref,
         vir_irrep_ref,
         out_ref,
-        blocks,
         stage,
-    ) = refs[-8:]
-    arrived = refs[:-8]
-    grid_size = len(arrived)
-    place = walk_place(me_ref[0], grid_size)
-    for offset, got_ref in zip(order, arrived):
-        source = walk_index(lax.rem(place - offset + grid_size, grid_size), grid_size)
-        blocks[source] = got_ref[...]
+    ) = refs[-7:]
+    arrived = refs[:-7]
     pack = LANES // rows_dev
-    for jj in range(blocks.shape[1]):
+    grid_size, groups = arrived[0].shape[:2]
+    for jj in range(groups):
         at = 0
-        for g in range(len(arrived)):
-            row = 0
-            for count, bp in zip(counts, bps):
-                block = decode(from_code(blocks[g, jj, row : row + bp, :]), count)
+        for g in range(grid_size):
+            for count, got_ref in zip(counts, arrived):
+                block = decode(from_code(got_ref[g, jj]), count)
                 stage[at : at + count, :] = block[:count]
                 at += count
-                row += bp
         turned = stage[...].T
         for jq in range(pack):
-            j = jq * blocks.shape[1] + jj
+            j = jq * groups + jj
             if j >= width:
                 continue
             cycle = turned[jq * rows_dev : (jq + 1) * rows_dev]
@@ -371,7 +352,8 @@
         cost=(10**8, 4 * half * deep),
         room=2 * half * deep + (2 * half * deep if slab > 2 * LANES else 0),
     )
-    totals, sends, got = [], [], []
+    groups = -(-width // (LANES // rows_dev))
+    sends, arrived = [], []
     for part, (cols, span, bp) in enumerate(zip(parts, spans, bps)):
         block = min(C_BLOCK, ceil_to(cols[1] // 2, 16))
         scratch = [
@@ -407,61 +389,38 @@
                 cost=cost,
                 room=room,
             )
-        arrived = lax.ppermute(send, "rep", low_pairs)
-        totals.append(total)
-        got.append(arrived)
-        sends.append(
-            local_call(
-                functools.partial(second_send_kernel, span),
-                jax.ShapeDtypeStruct((width, bp, slab), jnp.int16),
-                "svv",
-                (rep, total, arrived),
-            )
-        )
-    kept = [
-        local_call(
+        got = lax.ppermute(send, "rep", low_pairs)
+        if arrived:
+            got, _ = lax.optimization_barrier((got, back_send))
+        send = local_call(
+            functools.partial(second_send_kernel, span),
+            jax.ShapeDtypeStruct((width, bp, slab), jnp.int16),
+            "svv",
+            (rep, total, got),
+        )
+        sends.append(send)
+        kept = local_call(
             functools.partial(keep_kernel, span),
             jax.ShapeDtypeStruct((width, bp, slab), jnp.float32),
             "svv",
-            (rep, total, arrived),
-        )
-        for span, bp, total, arrived in zip(spans, bps, totals, got)
-    ]
-    got = [lax.ppermute(send, "rep", high_pairs) for send in sends]
-
-    groups = -(-width // (LANES // rows_dev))
-    staged = []
-    for part, span in enumerate(spans[:-1]):
-        mine, _ = lax.optimization_barrier((kept[part], sends[-1]))
-        staged.append(
-            local_call(
-                functools.partial(third_send_kernel, span[1], rows_dev),
-                jax.ShapeDtypeStruct((grid_size, groups, bps[part], LANES), jnp.int16),
-                "vv",
-                (mine, got[part]),
-            )
-        )
-    targets = local_call(
-        functools.partial(last_send_kernel, counts[-1], rows_dev, len(counts)),
-        (jax.ShapeDtypeStruct((groups, sum(bps), LANES), jnp.int16),) * grid_size,
-        "vv" + "v" * len(staged),
-        (kept[-1], got[-1], *staged),
-        [pltpu.VMEM((grid_size, groups, bps[-1], LANES), jnp.int16)],
-    )
-    arrived = list(targets)
-    for number in range(1, grid_size)[::-1]:
-        arrived[number] = lax.ppermute(
-            targets[number],
-            "grid",
-            [(walk[i], walk[(i + order[number]) % grid_size]) for i in range(grid_size)],
+            (rep, total, got),
+        )
+        got = lax.ppermute(send, "rep", high_pairs)
+        back_send = local_call(
+            functools.partial(third_send_kernel, span[1], rows_dev, order),
+            jax.ShapeDtypeStruct((grid_size, groups, bp, LANES), jnp.int16),
+            "svv",
+            (me, kept, got),
+        )
+        arrived.append(
+            lax.all_to_all(back_send, "grid", split_axis=0, concat_axis=0, tiled=True)
         )
 
     updated = local_call(
-        functools.partial(update_kernel, counts, bps, width, rows_dev, order),
+        functools.partial(update_kernel, counts, width, rows_dev),
         jax.ShapeDtypeStruct((width, rows_dev, count * grid_size), jnp.float32),
-        "sss" + "v" * (len(arrived) + 5),
+        "ss" + "v" * (len(arrived) + 5),
         (
-            me,
             occ_energy,
             occ_irrep,
             *arrived,
@@ -471,10 +430,7 @@
             row_irrep[:, None],
             vir_irrep[None, :],
         ),
-        [
-            pltpu.VMEM((grid_size, groups, sum(bps), LANES), jnp.int16),
-            pltpu.VMEM((count * grid_size, LANES), jnp.float32),
-        ],
+        [pltpu.VMEM((count * grid_size, LANES), jnp.float32)],
     )
     return jnp.transpose(updated, (1, 0, 2))
 

time: 99.8 us -> 124 us (1.24)
  blocking collectives: 0 us -> 13 us
  local copies, waits for them, and re-layouts: 5.21 us -> 15.7 us
  starting transfers between devices: 31.7 us -> 22.2 us
  waiting for transfers between devices: 30.3 us -> 36.4 us
  Pallas kernels: 32.1 us -> 35.4 us
    all_to_all x0 -> x1, blocking collectives: none -> 13 us  [body(): lax.all_to_all(back_send, 'grid', split_axis=0, concat_axis=0, tiled=True)]
    ppermute x11 -> x4, starting transfers between devices: 15.1 us -> 2.19 us  [the longest x2 2.11 us: body(): got = lax.ppermute(send, 'rep', high_pairs)]
    unnamed x18 -> x50, local copies, waits for them, and re-layouts: 1.67 us -> 12.2 us
    all_to_all x0 -> x1, waiting for transfers between devices: none -> 10.3 us  [body(): lax.all_to_all(back_send, 'grid', split_axis=0, concat_axis=0, tiled=True)]
    ppermute x11 -> x4, waiting for transfers between devices: 10.6 us -> 7.02 us  [the longest x2 4.82 us: body(): got = lax.ppermute(send, 'rep', high_pairs)]
    all_to_all x0 -> x1, starting transfers between devices: none -> 3.45 us  [body(): lax.all_to_all(back_send, 'grid', split_axis=0, concat_axis=0, tiled=True)]
    pallas_call x10, Pallas kernels: 32.1 us -> 35.4 us  [local_call(): pl.pallas_call(kernel, out_shape=out_shape, in_specs=[pl.BlockSpec(memory...]
  transfers between devices with their start and end apart: 25 -> 19, of which waited for: 12 -> 10; matrix products, arithmetic and copies ran while one was open for 3% -> 2% of each run, Pallas kernels for 12% -> 11%
where the time goes in v9:
time: 124 us; the launch traced here: 123 us
  waiting for transfers between devices  36.4 us (29%)
  Pallas kernels  35.4 us (29%)
  starting transfers between devices  22.2 us (18%)
  local copies, waits for them, and re-layouts  15.7 us (13%)
  blocking collectives  13 us (10%)
    pallas_call x10, Pallas kernels, local_call(): pl.pallas_call(kernel, out_shape=out_shape, in_specs=[pl.BlockSpec(memory...  35.4 us
    ppermute x7, starting transfers between devices, body(): ahead = lax.ppermute(ahead, 'grid', onward)  14.1 us
    all_to_all x1, blocking collectives, body(): lax.all_to_all(back_send, 'grid', split_axis=0, concat_axis=0, tiled=True)  13 us
    unnamed x50, local copies, waits for them, and re-layouts  12.2 us
    ppermute x7, waiting for transfers between devices, body(): ahead = lax.ppermute(ahead, 'grid', onward)  10.7 us
    all_to_all x1, waiting for transfers between devices, body(): lax.all_to_all(back_send, 'grid', split_axis=0, concat_axis=0, tiled=True)  10.3 us
    ppermute x7, waiting for transfers between devices, body(): behind = lax.ppermute(behind, 'grid', back)  8.51 us
    ppermute x2, waiting for transfers between devices, body(): got = lax.ppermute(send, 'rep', high_pairs)  4.82 us
  transfers between devices with their start and end apart: 19, of which 10 were waited for; matrix products, arithmetic and copies ran while one was open for 2% of the time, Pallas kernels for 11%

profile of v9, /device:TPU:0, one launch (start us, length us, event | category | flops | bytes accessed | tf_op | source)
XLA Modules:
  0.0 123.0 jit_solution(5069637034765118958)
XLA Ops:
  1.0 3.1 %collective-permute-start = (bf16[32,3840]{1,0:T(8,128)(2,1)S(1)}, bf16[32,3840]{1,0:T(8,128)(2,1)S(1)}, u32[]{:S(2)}, u32[]{:S(2)}) collective-permute-start(bf16[32,3840]{1,0:T(8,128)(2,1)S(1)} %slice.9.refs_0_), channel_id=1, source_target_pairs={{0,8},{8,16},{16,24},{24,28},{28,20},{20,12},{12,4},{4,0},{1,9},{9... | collective-permute-start | bytes 737288 | tf_op jit(solution)/shard_map/ppermute | solution.py:311
  5.1 2.0 %collective-permute-start.1 = (bf16[32,3840]{1,0:T(8,128)(2,1)S(1)}, bf16[32,3840]{1,0:T(8,128)(2,1)S(1)}, u32[]{:S(2)}, u32[]{:S(2)}) collective-permute-start(bf16[32,3840]{1,0:T(8,128)(2,1)S(1)} %slice.9.refs_0_), channel_id=1, source_target_pairs={{8,0},{16,8},{24,16},{28,24},{20,28},{12,20},{4,12},{0,4},{9,1},{1... | collective-permute-start | bytes 737288 | tf_op jit(solution)/shard_map/ppermute | solution.py:314
  7.1 2.9 %collective-permute-done.refs_1_ = bf16[32,3840]{1,0:T(8,128)(2,1)S(1)} collective-permute-done((bf16[32,3840]{1,0:T(8,128)(2,1)S(1)}, bf16[32,3840]{1,0:T(8,128)(2,1)S(1)}, u32[]{:S(2)}, u32[]{:S(2)}) %collective-permute-start) | collective-permute-done | bytes 245792 | tf_op jit(solution)/shard_map/ppermute | solution.py:311
  9.9 1.8 %collective-permute-start.2 = (bf16[32,3840]{1,0:T(8,128)(2,1)S(1)}, bf16[32,3840]{1,0:T(8,128)(2,1)S(1)}, u32[]{:S(2)}, u32[]{:S(2)}) collective-permute-start(bf16[32,3840]{1,0:T(8,128)(2,1)S(1)} %collective-permute-done.refs_1_), channel_id=1, source_target_pairs={{0,8},{8,16},{16,24},{24,28},{28,20},{20,12},{12,4},{4,0},{1,9},{9... | collective-permute-start | bytes 737288 | tf_op jit(solution)/shard_map/ppermute | solution.py:311
  13.8 5.3 %collective-permute-done.1.refs_2_ = bf16[32,3840]{1,0:T(8,128)(2,1)S(1)} collective-permute-done((bf16[32,3840]{1,0:T(8,128)(2,1)S(1)}, bf16[32,3840]{1,0:T(8,128)(2,1)S(1)}, u32[]{:S(2)}, u32[]{:S(2)}) %collective-permute-start.1) | collective-permute-done | bytes 245792 | tf_op jit(solution)/shard_map/ppermute | solution.py:314
  19.1 2.0 %collective-permute-start.7 = (bf16[32,3840]{1,0:T(8,128)(2,1)S(1)}, bf16[32,3840]{1,0:T(8,128)(2,1)S(1)}, u32[]{:S(2)}, u32[]{:S(2)}) collective-permute-start(bf16[32,3840]{1,0:T(8,128)(2,1)S(1)} %collective-permute-done.2.refs_3_), channel_id=1, source_target_pairs={{0,8},{8,16},{16,24},{24,28},{28,20},{20,12},{12,4},{4,0},{1,9},{9... | collective-permute-start | bytes 737288 | tf_op jit(solution)/shard_map/ppermute | solution.py:311
  21.1 2.8 %collective-permute-done.3.refs_5_ = bf16[32,3712]{1,0:T(8,128)(2,1)S(1)} collective-permute-done((bf16[32,3712]{1,0:T(8,128)(2,1)S(1)}, bf16[32,3712]{1,0:T(8,128)(2,1)S(1)}, u32[]{:S(2)}, u32[]{:S(2)}) %collective-permute-start.3) | collective-permute-done | bytes 237600 | tf_op jit(solution)/shard_map/ppermute | solution.py:311
  23.9 1.8 %collective-permute-start.5 = (bf16[32,3712]{1,0:T(8,128)(2,1)S(1)}, bf16[32,3712]{1,0:T(8,128)(2,1)}, u32[]{:S(2)}, u32[]{:S(2)}) collective-permute-start(bf16[32,3712]{1,0:T(8,128)(2,1)S(1)} %collective-permute-done.3.refs_5_), channel_id=1, source_target_pairs={{0,8},{8,16},{16,24},{24,28},{28,20},{20,12},{12,4},{4,0},{1,9},{9... | collective-permute-start | bytes 712712 | tf_op jit(solution)/shard_map/ppermute | solution.py:311
  26.6 2.8 %collective-permute-done.6.refs_0_ = bf16[32,3840]{1,0:T(8,128)(2,1)S(1)} collective-permute-done((bf16[32,3840]{1,0:T(8,128)(2,1)S(1)}, bf16[32,3840]{1,0:T(8,128)(2,1)S(1)}, u32[]{:S(2)}, u32[]{:S(2)}) %collective-permute-start.6) | collective-permute-done | bytes 245792 | tf_op jit(solution)/shard_map/ppermute | solution.py:314
  29.4 2.0 %collective-permute-start.9 = (bf16[32,3840]{1,0:T(8,128)(2,1)S(1)}, bf16[32,3840]{1,0:T(8,128)(2,1)S(1)}, u32[]{:S(2)}, u32[]{:S(2)}) collective-permute-start(bf16[32,3840]{1,0:T(8,128)(2,1)S(1)} %collective-permute-done.7.refs_1_), channel_id=1, source_target_pairs={{0,8},{8,16},{16,24},{24,28},{28,20},{20,12},{12,4},{4,0},{1,9},{9... | collective-permute-start | bytes 737288 | tf_op jit(solution)/shard_map/ppermute | solution.py:311
  31.4 2.9 %collective-permute-done.5.refs_7_ = bf16[32,3712]{1,0:T(8,128)(2,1)} collective-permute-done((bf16[32,3712]{1,0:T(8,128)(2,1)S(1)}, bf16[32,3712]{1,0:T(8,128)(2,1)}, u32[]{:S(2)}, u32[]{:S(2)}) %collective-permute-start.5) | collective-permute-done | bytes 237600 | tf_op jit(solution)/shard_map/ppermute | solution.py:311
  34.4 1.8 %collective-permute-start.11 = (bf16[32,3712]{1,0:T(8,128)(2,1)}, bf16[32,3712]{1,0:T(8,128)(2,1)S(1)}, u32[]{:S(2)}, u32[]{:S(2)}) collective-permute-start(bf16[32,3712]{1,0:T(8,128)(2,1)} %collective-permute-done.5.refs_7_), channel_id=1, source_target_pairs={{0,8},{8,16},{16,24},{24,28},{28,20},{20,12},{12,4},{4,0},{1,9},{9... | collective-permute-start | bytes 712712 | tf_op jit(solution)/shard_map/ppermute | solution.py:311
  38.8 2.1 %near_kernel.1.near = bf16[7552,128]{1,0:T(8,128)(2,1)S(1)} custom-call(bf16[32,3840]{1,0:T(8,128)(2,1)S(1)} %slice.9.refs_0_, bf16[32,3840]{1,0:T(8,128)(2,1)S(1)} %collective-permute-done.refs_1_, bf16[32,3840]{1,0:T(8,128)(2,1)S(1)} %collective-permute-done.1.refs_2_, bf16[32,3840]{1,0:T(8,128)(2,1)S(1)} %collective-permute-done.2.refs_3_, ...), custom_call_target="tpu_custom_call" | custom-call | flops 100000000 | bytes 3866624 | tf_op jit(solution)/shard_map/near_kernel/pallas_call | solution.py:251
  40.9 2.0 %collective-permute-done.11.refs_5_ = bf16[32,3712]{1,0:T(8,128)(2,1)S(1)} collective-permute-done((bf16[32,3712]{1,0:T(8,128)(2,1)}, bf16[32,3712]{1,0:T(8,128)(2,1)S(1)}, u32[]{:S(2)}, u32[]{:S(2)}) %collective-permute-start.11) | collective-permute-done | bytes 237600 | tf_op jit(solution)/shard_map/ppermute | solution.py:311
  51.3 16.9 %lead_kernel.1 = (f32[2,2880,128]{2,1,0:T(8,128)S(1)}, bf16[7552,256]{1,0:T(8,128)(2,1)S(1)}, s16[2,15,48,256]{3,2,1,0:T(8,128)(2,1)S(1)}) custom-call(s32[1]{0:T(128)} %bitcast.1.rep_ref, bf16[7552,128]{1,0:T(8,128)(2,1)S(1)} %near_kernel.1.near, bf16[32,3840]{1,0:T(8,128)(2,1)S(1)} %collective-permute-done.6.refs_0_, ...), custom_call_target="tpu_custom_call" | custom-call | flops 10455351296 | bytes 40841216 | tf_op jit(solution)/shard_map/lead_kernel/pallas_call | solution.py:251
  68.3 2.2 %collective-permute-done.14.got_ref = s16[2,15,48,256]{3,2,1,0:T(8,128)(2,1)S(1)} collective-permute-done((s16[2,15,48,256]{3,2,1,0:T(8,128)(2,1)S(1)}, s16[2,15,48,256]{3,2,1,0:T(8,128)(2,1)S(1)}, u32[]{:S(2)}, u32[]{:S(2)}) %collective-permute-start.14) | collective-permute-done | bytes 737312 | tf_op jit(solution)/shard_map/ppermute | solution.py:392
  70.5 1.6 %second_send_kernel.2 = s16[15,48,256]{2,1,0:T(8,128)(2,1)} custom-call(s32[1]{0:T(128)} %bitcast.1.rep_ref, f32[2,2880,128]{2,1,0:T(8,128)S(1)} %get-tuple-element.12.total_ref, s16[2,15,48,256]{3,2,1,0:T(8,128)(2,1)S(1)} %collective-permute-done.14.got_ref), custom_call_target="tpu_custom_call" | custom-call | flops 10000000 | bytes 4000000 | tf_op jit(solution)/shard_map/second_send_kernel/pallas_call | solution.py:251
  73.4 7.8 %rest_kernel.1 = (f32[2,972,128]{2,1,0:T(8,128)S(1)}, s16[2,15,16,256]{3,2,1,0:T(8,128)(2,1)S(1)}) custom-call(s32[1]{0:T(128)} %bitcast.1.rep_ref, bf16[7552,256]{1,0:T(8,128)(2,1)S(1)} %get-tuple-element.15.turned, bf16[3600,7500]{1,0:T(8,128)(2,1)} %bitcast.14, bf16[3600,128]{1,0:T(8,128)(2,1)S(1)} %pad.9.refs_9_.edge_ref), custom_call_target="tpu_custom_call" | custom-call | flops 3526361088 | bytes 13774848 | tf_op jit(solution)/shard_map/rest_kernel/pallas_call | solution.py:251
  83.7 3.0 %third_send_kernel.2 = s16[8,4,48,128]{3,2,1,0:T(8,128)(2,1)} custom-call(s32[1]{0:T(128)} %bitcast.me_ref, f32[15,48,256]{2,1,0:T(8,128)S(1)} %keep_kernel.2.kept_ref, s16[15,48,256]{2,1,0:T(8,128)(2,1)} %collective-permute-done.15.got_ref), custom_call_target="tpu_custom_call" | custom-call | flops 10000000 | bytes 4000000 | tf_op jit(solution)/shard_map/third_send_kernel/pallas_call | solution.py:251
  88.5 4.8 %collective-permute-done.17.got_ref = s16[15,16,256]{2,1,0:T(8,128)(2,1)S(1)} collective-permute-done((s16[15,16,256]{2,1,0:T(8,128)(2,1)S(1)}, s16[15,16,256]{2,1,0:T(8,128)(2,1)S(1)}, u32[]{:S(2)}, u32[]{:S(2)}) %collective-permute-start.17) | collective-permute-done | bytes 122912 | tf_op jit(solution)/shard_map/ppermute | solution.py:408
  94.0 13.0 %all_to_all.10.refs_1_ = s16[8,4,16,128]{3,2,1,0:T(8,128)(2,1)S(1)} all-to-all(s16[8,4,16,128]{3,2,1,0:T(8,128)(2,1)S(1)} %third_send_kernel.3), channel_id=1, replica_groups=mesh['grid'=8,'rep'=4] {'grid'}, dimensions={0} | all-to-all | bytes 262144 | tf_op jit(solution)/shard_map/all_to_all | solution.py:416
  106.9 3.5 %all-to-all-start = ((s16[8,4,48,128]{3,2,1,0:T(8,128)(2,1)}), s16[8,4,48,128]{3,2,1,0:T(8,128)(2,1)S(1)}, u32[]{:S(2)}, u32[]{:S(2)}) async-start(s16[8,4,48,128]{3,2,1,0:T(8,128)(2,1)} %third_send_kernel.2), calls=%async_computation | async-start | bytes 786432 | tf_op jit(solution)/shard_map/all_to_all | solution.py:416
  110.6 10.3 %all-to-all-done.refs_0_ = s16[8,4,48,128]{3,2,1,0:T(8,128)(2,1)S(1)} async-done(((s16[8,4,48,128]{3,2,1,0:T(8,128)(2,1)}), s16[8,4,48,128]{3,2,1,0:T(8,128)(2,1)S(1)}, u32[]{:S(2)}, u32[]{:S(2)}) %all-to-all-start) | async-done | bytes 393248 | tf_op jit(solution)/shard_map/all_to_all | solution.py:416
  120.9 2.1 %update_kernel.1 = f32[15,32,480]{2,1,0:T(8,128)} custom-call(f32[15]{0:T(128)S(1)} %copy-done.21, s32[15]{0:T(128)S(1)} %copy-done.22, s16[8,4,48,128]{3,2,1,0:T(8,128)(2,1)S(1)} %all-to-all-done.refs_0_, s16[8,4,16,128]{3,2,1,0:T(8,128)(2,1)S(1)} %all_to_all.10.refs_1_, f32[15,32,480]{2,1,0:T(8,128)S(1)} %bitcast.9, f32[32,1]{1,0:T(8,128)S(1)} %copy.10.refs_3_, ...), custom_call_target="tpu_custom_call" | custom-call | flops 10000000 | bytes 4000000 | tf_op jit(solution)/shard_map/update_kernel/pallas_call | solution.py:251
  (82 shorter events, 22.5 us)
Async XLA Ops:
  1.0 9.0 %collective-permute-start = (bf16[32,3840]{1,0:T(8,128)(2,1)S(1)}, bf16[32,3840]{1,0:T(8,128)(2,1)S(1)}, u32[]{:S(2)}, u32[]{:S(2)}) collective-permute-start(bf16[32,3840]{1,0:T(8,128)(2,1)S(1)} %slice.9.refs_0_), channel_id=1, source_target_pairs={{0,8},{8,16},{16,24},{24,28},{28,20},{20,12},{12,4},{4,0},{1,9},{9... | collective-permute-start | bytes 737288 | tf_op jit(solution)/shard_map/ppermute | solution.py:311
  5.0 8.8 %collective-permute-start.4 = (bf16[32,3712]{1,0:T(8,128)(2,1)S(1)}, bf16[32,3712]{1,0:T(8,128)(2,1)S(1)}, u32[]{:S(2)}, u32[]{:S(2)}) collective-permute-start(bf16[32,3712]{1,0:T(8,128)(2,1)S(1)} %pad.8.refs_4_), channel_id=1, source_target_pairs={{8,0},{16,8},{24,16},{28,24},{20,28},{12,20},{4,12},{0,4},{9,1},{1... | collective-permute-start | bytes 712712 | tf_op jit(solution)/shard_map/ppermute | solution.py:314
  5.1 14.0 %collective-permute-start.1 = (bf16[32,3840]{1,0:T(8,128)(2,1)S(1)}, bf16[32,3840]{1,0:T(8,128)(2,1)S(1)}, u32[]{:S(2)}, u32[]{:S(2)}) collective-permute-start(bf16[32,3840]{1,0:T(8,128)(2,1)S(1)} %slice.9.refs_0_), channel_id=1, source_target_pairs={{8,0},{16,8},{24,16},{28,24},{20,28},{12,20},{4,12},{0,4},{9,1},{1... | collective-permute-start | bytes 737288 | tf_op jit(solution)/shard_map/ppermute | solution.py:314
  9.9 9.1 %collective-permute-start.2 = (bf16[32,3840]{1,0:T(8,128)(2,1)S(1)}, bf16[32,3840]{1,0:T(8,128)(2,1)S(1)}, u32[]{:S(2)}, u32[]{:S(2)}) collective-permute-start(bf16[32,3840]{1,0:T(8,128)(2,1)S(1)} %collective-permute-done.refs_1_), channel_id=1, source_target_pairs={{0,8},{8,16},{16,24},{24,28},{28,20},{20,12},{12,4},{4,0},{1,9},{9... | collective-permute-start | bytes 737288 | tf_op jit(solution)/shard_map/ppermute | solution.py:311
  11.7 12.2 %collective-permute-start.3 = (bf16[32,3712]{1,0:T(8,128)(2,1)S(1)}, bf16[32,3712]{1,0:T(8,128)(2,1)S(1)}, u32[]{:S(2)}, u32[]{:S(2)}) collective-permute-start(bf16[32,3712]{1,0:T(8,128)(2,1)S(1)} %pad.8.refs_4_), channel_id=1, source_target_pairs={{0,8},{8,16},{16,24},{24,28},{28,20},{20,12},{12,4},{4,0},{1,9},{9... | collective-permute-start | bytes 712712 | tf_op jit(solution)/shard_map/ppermute | solution.py:311
  13.8 12.6 %collective-permute-start.10 = (bf16[32,3712]{1,0:T(8,128)(2,1)S(1)}, bf16[32,3712]{1,0:T(8,128)(2,1)S(1)}, u32[]{:S(2)}, u32[]{:S(2)}) collective-permute-start(bf16[32,3712]{1,0:T(8,128)(2,1)S(1)} %collective-permute-done.4.refs_6_), channel_id=1, source_target_pairs={{8,0},{16,8},{24,16},{28,24},{20,28},{12,20},{4,12},{0,4},{9,1},{1... | collective-permute-start | bytes 712712 | tf_op jit(solution)/shard_map/ppermute | solution.py:314
  19.1 10.4 %collective-permute-start.6 = (bf16[32,3840]{1,0:T(8,128)(2,1)S(1)}, bf16[32,3840]{1,0:T(8,128)(2,1)S(1)}, u32[]{:S(2)}, u32[]{:S(2)}) collective-permute-start(bf16[32,3840]{1,0:T(8,128)(2,1)S(1)} %collective-permute-done.1.refs_2_), channel_id=1, source_target_pairs={{8,0},{16,8},{24,16},{28,24},{20,28},{12,20},{4,12},{0,4},{9,1},{1... | collective-permute-start | bytes 737288 | tf_op jit(solution)/shard_map/ppermute | solution.py:314
  19.1 10.4 %collective-permute-start.7 = (bf16[32,3840]{1,0:T(8,128)(2,1)S(1)}, bf16[32,3840]{1,0:T(8,128)(2,1)S(1)}, u32[]{:S(2)}, u32[]{:S(2)}) collective-permute-start(bf16[32,3840]{1,0:T(8,128)(2,1)S(1)} %collective-permute-done.2.refs_3_), channel_id=1, source_target_pairs={{0,8},{8,16},{16,24},{24,28},{28,20},{20,12},{12,4},{4,0},{1,9},{9... | collective-permute-start | bytes 737288 | tf_op jit(solution)/shard_map/ppermute | solution.py:311
  23.9 10.5 %collective-permute-start.5 = (bf16[32,3712]{1,0:T(8,128)(2,1)S(1)}, bf16[32,3712]{1,0:T(8,128)(2,1)}, u32[]{:S(2)}, u32[]{:S(2)}) collective-permute-start(bf16[32,3712]{1,0:T(8,128)(2,1)S(1)} %collective-permute-done.3.refs_5_), channel_id=1, source_target_pairs={{0,8},{8,16},{16,24},{24,28},{28,20},{20,12},{12,4},{4,0},{1,9},{9... | collective-permute-start | bytes 712712 | tf_op jit(solution)/shard_map/ppermute | solution.py:311
  26.4 9.8 %collective-permute-start.12 = (bf16[32,3712]{1,0:T(8,128)(2,1)S(1)}, bf16[32,3712]{1,0:T(8,128)(2,1)S(1)}, u32[]{:S(2)}, u32[]{:S(2)}) collective-permute-start(bf16[32,3712]{1,0:T(8,128)(2,1)S(1)} %collective-permute-done.10.refs_4_), channel_id=1, source_target_pairs={{8,0},{16,8},{24,16},{28,24},{20,28},{12,20},{4,12},{0,4},{9,1},{1... | collective-permute-start | bytes 712712 | tf_op jit(solution)/shard_map/ppermute | solution.py:314
  29.4 14.2 %collective-permute-start.8 = (bf16[32,3840]{1,0:T(8,128)(2,1)S(1)}, bf16[32,3840]{1,0:T(8,128)(2,1)S(1)}, u32[]{:S(2)}, u32[]{:S(2)}) collective-permute-start(bf16[32,3840]{1,0:T(8,128)(2,1)S(1)} %collective-permute-done.6.refs_0_), channel_id=1, source_target_pairs={{8,0},{16,8},{24,16},{28,24},{20,28},{12,20},{4,12},{0,4},{9,1},{1... | collective-permute-start | bytes 737288 | tf_op jit(solution)/shard_map/ppermute | solution.py:314
  29.4 15.5 %collective-permute-start.9 = (bf16[32,3840]{1,0:T(8,128)(2,1)S(1)}, bf16[32,3840]{1,0:T(8,128)(2,1)S(1)}, u32[]{:S(2)}, u32[]{:S(2)}) collective-permute-start(bf16[32,3840]{1,0:T(8,128)(2,1)S(1)} %collective-permute-done.7.refs_1_), channel_id=1, source_target_pairs={{0,8},{8,16},{16,24},{24,28},{28,20},{20,12},{12,4},{4,0},{1,9},{9... | collective-permute-start | bytes 737288 | tf_op jit(solution)/shard_map/ppermute | solution.py:311
  34.4 8.5 %collective-permute-start.11 = (bf16[32,3712]{1,0:T(8,128)(2,1)}, bf16[32,3712]{1,0:T(8,128)(2,1)S(1)}, u32[]{:S(2)}, u32[]{:S(2)}) collective-permute-start(bf16[32,3712]{1,0:T(8,128)(2,1)} %collective-permute-done.5.refs_7_), channel_id=1, source_target_pairs={{0,8},{8,16},{16,24},{24,28},{28,20},{20,12},{12,4},{4,0},{1,9},{9... | collective-permute-start | bytes 712712 | tf_op jit(solution)/shard_map/ppermute | solution.py:311
  36.2 8.1 %collective-permute-start.13 = (bf16[32,3712]{1,0:T(8,128)(2,1)S(1)}, bf16[32,3712]{1,0:T(8,128)(2,1)S(1)}, u32[]{:S(2)}, u32[]{:S(2)}) collective-permute-start(bf16[32,3712]{1,0:T(8,128)(2,1)S(1)} %collective-permute-done.12.refs_6_), channel_id=1, source_target_pairs={{8,0},{16,8},{24,16},{28,24},{20,28},{12,20},{4,12},{0,4},{9,1},{1... | collective-permute-start | bytes 712712 | tf_op jit(solution)/shard_map/ppermute | solution.py:314
  68.2 2.3 %collective-permute-start.14 = (s16[2,15,48,256]{3,2,1,0:T(8,128)(2,1)S(1)}, s16[2,15,48,256]{3,2,1,0:T(8,128)(2,1)S(1)}, u32[]{:S(2)}, u32[]{:S(2)}) collective-permute-start(s16[2,15,48,256]{3,2,1,0:T(8,128)(2,1)S(1)} %get-tuple-element.13), channel_id=1, source_target_pairs={{0,1},{1,0},{2,3},{3,2},{4,5},{5,4},{6,7},{7,6},{8,9},{9,8},{10,11... | collective-permute-start | bytes 2211848 | tf_op jit(solution)/shard_map/ppermute | solution.py:392
  72.0 11.7 %collective-permute-start.15 = (s16[15,48,256]{2,1,0:T(8,128)(2,1)}, s16[15,48,256]{2,1,0:T(8,128)(2,1)}, u32[]{:S(2)}, u32[]{:S(2)}) collective-permute-start(s16[15,48,256]{2,1,0:T(8,128)(2,1)} %second_send_kernel.2), channel_id=1, source_target_pairs={{0,2},{1,3},{2,0},{3,1},{4,6},{5,7},{6,4},{7,5},{8,10},{9,11},{10,... | collective-permute-start | bytes 1105928 | tf_op jit(solution)/shard_map/ppermute | solution.py:408
  82.2 4.5 %collective-permute-start.16 = (s16[2,15,16,256]{3,2,1,0:T(8,128)(2,1)S(1)}, s16[2,15,16,256]{3,2,1,0:T(8,128)(2,1)S(1)}, u32[]{:S(2)}, u32[]{:S(2)}) collective-permute-start(s16[2,15,16,256]{3,2,1,0:T(8,128)(2,1)S(1)} %get-tuple-element.17), channel_id=1, source_target_pairs={{0,1},{1,0},{2,3},{3,2},{4,5},{5,4},{6,7},{7,6},{8,9},{9,8},{10,11... | collective-permute-start | bytes 737288 | tf_op jit(solution)/shard_map/ppermute | solution.py:392
  83.7 37.2 %copy-start.4 = (f32[32,15,480]{2,0,1:T(8,128)S(1)}, f32[32,15,480]{2,0,1:T(8,128)}, u32[]{:S(2)}) copy-start(f32[32,15,480]{2,0,1:T(8,128)} %param.11) | copy-start | bytes 2764804
  83.7 37.2 %copy-start.19 = (f32[480]{0:T(512)S(1)}, f32[480]{0:T(512)}, u32[]{:S(2)}) copy-start(f32[480]{0:T(512)} %param.14) | copy-start | bytes 5764
  83.7 37.1 %copy-start.20 = (s32[480]{0:T(512)S(1)}, s32[480]{0:T(512)}, u32[]{:S(2)}) copy-start(s32[480]{0:T(512)} %param.17) | copy-start | bytes 5764
  83.7 37.1 %copy-start.21 = (f32[15]{0:T(128)S(1)}, f32[15]{0:T(128)}, u32[]{:S(2)}) copy-start(f32[15]{0:T(128)} %occ_energy_ref.1) | copy-start | bytes 184
  83.7 37.1 %copy-start.22 = (s32[15]{0:T(128)S(1)}, s32[15]{0:T(128)}, u32[]{:S(2)}) copy-start(s32[15]{0:T(128)} %occ_irrep_ref.1) | copy-start | bytes 184
  87.5 5.8 %collective-permute-start.17 = (s16[15,16,256]{2,1,0:T(8,128)(2,1)S(1)}, s16[15,16,256]{2,1,0:T(8,128)(2,1)S(1)}, u32[]{:S(2)}, u32[]{:S(2)}) collective-permute-start(s16[15,16,256]{2,1,0:T(8,128)(2,1)S(1)} %second_send_kernel.3), channel_id=1, source_target_pairs={{0,2},{1,3},{2,0},{3,1},{4,6},{5,7},{6,4},{7,5},{8,10},{9,11},{10,... | collective-permute-start | bytes 368648 | tf_op jit(solution)/shard_map/ppermute | solution.py:408
  106.9 13.9 %all-to-all-start = ((s16[8,4,48,128]{3,2,1,0:T(8,128)(2,1)}), s16[8,4,48,128]{3,2,1,0:T(8,128)(2,1)S(1)}, u32[]{:S(2)}, u32[]{:S(2)}) async-start(s16[8,4,48,128]{3,2,1,0:T(8,128)(2,1)} %third_send_kernel.2), calls=%async_computation | async-start | bytes 786432 | tf_op jit(solution)/shard_map/all_to_all | solution.py:416
  (20 other events, 99.4 us)

commit v10 on v8

--- a/solution.py
+++ b/solution.py
@@ -127,37 +127,9 @@
         turned[at : at + LANES, lanes : lanes + slots * rows] = gathered[:, at : at + LANES].T
 
 
-def near_kernel(at, whole, columns, count, *refs):
-    pieces, refs = refs[:count], refs[count:]
-    if columns is None:
-        turned, gathered, sems = refs
-        turn_pieces((0,) * count, pieces, gathered, sems, turned, 0)
-        return
-    coupling_ref, edge_ref, turned, held, gathered, sems, held_sems = refs
-    low, many = columns
-    rows = pl.ds(low, many)
-    quarter = ceil_to(-(-whole // COPIES), LANES)
-    copies = []
-    for number, k in enumerate(range(0, whole, quarter)):
-        size = min(quarter, whole - k)
-        copies.append(
-            pltpu.make_async_copy(
-                coupling_ref.at[rows, pl.ds(at + k, size)],
-                held.at[:, pl.ds(k, size)],
-                held_sems.at[number],
-            )
-        )
-    if whole < held.shape[1]:
-        copies.append(
-            pltpu.make_async_copy(
-                edge_ref.at[rows, :], held.at[:, pl.ds(whole, LANES)], held_sems.at[COPIES]
-            )
-        )
-    for copy in copies:
-        copy.start()
-    turn_pieces((0,) * count, pieces, gathered, sems, turned, 0)
-    for copy in copies:
-        copy.wait()
+def near_kernel(edges, *refs):
+    *pieces, turned, gathered, sems = refs
+    turn_pieces(edges, pieces, gathered, sems, turned, 0)
 
 
 def lead_kernel(edges, columns, span, nears, rep_ref, *refs):
@@ -175,26 +147,8 @@
     first_send(span, rep_ref, total, send)
 
 
-def rest_kernel(span, rep_ref, turned, *refs):
-    *held, total, send = refs
-    many = held[0].shape[0]
-    block = min(C_BLOCK, ceil_to(many // 2, 16))
-
-    def step(number, carry):
-        start = pl.multiple_of(jnp.minimum(number * block, many - block), 16)
-        rows = pl.ds(start, block)
-        at, products = 0, 0.0
-        for part in held:
-            size = part.shape[1]
-            products += jnp.dot(
-                part[rows, :], turned[at : at + size, :], preferred_element_type=jnp.float32
-            )
-            at += size
-        for part in range(total.shape[0]):
-            total[part, rows, :] = products[:, part * LANES : (part + 1) * LANES]
-        return carry
-
-    lax.fori_loop(0, -(-many // block), step, 0)
+def rest_kernel(columns, span, rep_ref, turned, coupling_ref, edge_ref, total, send, buffer, sems):
+    multiply(coupling_ref, edge_ref, buffer, sems, turned, total, columns)
     first_send(span, rep_ref, total, send)
 
 
@@ -393,29 +347,16 @@
 
     half = slab // 2
     large = slab > 2 * LANES
-    held_columns = parts[1] if len(parts) > 1 else None
-
-    def turn_near(at, whole, pieces):
+
+    def turn_near(pieces):
         size = pieces[0].shape[1]
-        out_shape = [jax.ShapeDtypeStruct((size, half), jnp.bfloat16)]
-        args = list(pieces)
-        scratch = [
-            pltpu.VMEM((half, size), jnp.bfloat16),
-            pltpu.SemaphoreType.DMA((len(pieces),)),
-        ]
-        cost = 4 * half * size
-        if held_columns is not None:
-            out_shape.append(jax.ShapeDtypeStruct((held_columns[1], size), jnp.bfloat16))
-            args += [coupling, edge]
-            scratch.append(pltpu.SemaphoreType.DMA((COPIES + 1,)))
-            cost += 2 * held_columns[1] * size
         return local_call(
-            functools.partial(near_kernel, at, whole, held_columns, len(pieces)),
-            tuple(out_shape),
-            "a" * len(args),
-            args,
-            scratch,
-            cost=(10**8, cost),
+            functools.partial(near_kernel, (0,) * len(pieces)),
+            jax.ShapeDtypeStruct((size, half), jnp.bfloat16),
+            "a" * len(pieces),
+            pieces,
+            [pltpu.VMEM((half, size), jnp.bfloat16), pltpu.SemaphoreType.DMA((len(pieces),))],
+            cost=(10**8, 4 * half * size),
             room=2 * half * size * (2 if large else 1),
         )
 
@@ -424,7 +365,7 @@
     for hop in range(1, longer):
         order += [-hop, hop]
     order.append(longer)
-    turned_near, held, far, far_edges = [], [], [], []
+    turned_near, far, far_edges = [], [], []
     for number, at in enumerate(range(0, depth, K_BLOCK)):
         own = amplitudes[:, at : at + K_BLOCK]
         size = own.shape[1]
@@ -433,10 +374,9 @@
         pieces = [own]
         for hop in range(1, longer + 1):
             if hop == longer:
-                part, *rest = turn_near(at, size // LANES * LANES, pieces[:longer])
+                part = turn_near(pieces[:longer])
                 ahead, behind, part = lax.optimization_barrier((ahead, behind, part))
                 turned_near.append(part)
-                held += rest
             if hop < longer or number % 2 == 0:
                 ahead = lax.ppermute(ahead, "grid", onward)
                 pieces.append(ahead)
@@ -474,12 +414,18 @@
             )
         else:
             turned, _ = lax.optimization_barrier((turned, sends[0]))
+            block = min(C_BLOCK, ceil_to(cols[1] // 2, 16))
             total, send = local_call(
-                functools.partial(rest_kernel, span),
+                functools.partial(rest_kernel, cols, span),
                 (total_shapes[part], send_shapes[part]),
-                "sv" + "v" * len(held),
-                (rep, turned, *held),
+                "svaa",
+                (rep, turned, coupling, edge),
+                [
+                    pltpu.VMEM((SLOTS, block, deep), jnp.bfloat16),
+                    pltpu.SemaphoreType.DMA((SLOTS, COPIES + 1)),
+                ],
                 cost=cost,
+                room=2 * SLOTS * block * deep,
             )
         arrived = lax.ppermute(send, "rep", low_pairs)
         totals.append(total)

time: 111 us -> 105 us (0.946)
  local copies, waits for them, and re-layouts: 13.6 us -> 5.21 us
  starting transfers between devices: 29 us -> 32.6 us
  waiting for transfers between devices: 32.3 us -> 31 us
    unnamed x38 -> x18, local copies, waits for them, and re-layouts: 10.1 us -> 1.68 us
    ppermute x7, starting transfers between devices: 11.1 us -> 13.4 us  [go_back(): return lax.ppermute(block, 'grid', pairs)]
    ppermute x7, starting transfers between devices: 2.48 us -> 3.82 us  [body(): behind = lax.ppermute(behind, 'grid', back)]
  transfers between devices with their start and end apart: 25 -> 25, of which waited for: 12 -> 11; matrix products, arithmetic and copies ran while one was open for 2% -> 2% of each run, Pallas kernels for 11% -> 12%
where the time goes in v10:
time: 105 us
  Pallas kernels  36 us (34%)
  starting transfers between devices  32.6 us (31%)
  waiting for transfers between devices  31 us (30%)
  local copies, waits for them, and re-layouts  5.21 us (5%)
    pallas_call x11, Pallas kernels, local_call(): pl.pallas_call(kernel, out_shape=out_shape, in_specs=[pl.BlockSpec(memory...  36 us
    ppermute x7, waiting for transfers between devices, body(): behind = lax.ppermute(behind, 'grid', back)  15.6 us
    ppermute x7, starting transfers between devices, go_back(): return lax.ppermute(block, 'grid', pairs)  13.4 us
    ppermute x7, starting transfers between devices, body(): ahead = lax.ppermute(ahead, 'grid', onward)  13.1 us
    ppermute x7, waiting for transfers between devices, body(): ahead = lax.ppermute(ahead, 'grid', onward)  4.7 us
    ppermute x7, starting transfers between devices, body(): behind = lax.ppermute(behind, 'grid', back)  3.82 us
    ppermute x7, waiting for transfers between devices, go_back(): return lax.ppermute(block, 'grid', pairs)  3.8 us
    ppermute x2, waiting for transfers between devices, body(): arrived = lax.ppermute(send, 'rep', low_pairs)  3.7 us
  transfers between devices with their start and end apart: 25, of which 11 were waited for; matrix products, arithmetic and copies ran while one was open for 2% of the time, Pallas kernels for 12%

profile of v10, /device:TPU:0, one launch (start us, length us, event | category | flops | bytes accessed | tf_op | source)
XLA Modules:
  0.0 105.0 jit_solution(11079642351804077193)
XLA Ops:
  1.0 3.1 %collective-permute-start = (bf16[32,3840]{1,0:T(8,128)(2,1)S(1)}, bf16[32,3840]{1,0:T(8,128)(2,1)S(1)}, u32[]{:S(2)}, u32[]{:S(2)}) collective-permute-start(bf16[32,3840]{1,0:T(8,128)(2,1)S(1)} %slice.9.refs_0_), channel_id=1, source_target_pairs={{0,8},{8,16},{16,24},{24,28},{28,20},{20,12},{12,4},{4,0},{1,9},{9... | collective-permute-start | bytes 737288 | tf_op jit(solution)/shard_map/ppermute | solution.py:381
  5.0 2.0 %collective-permute-start.9 = (bf16[32,3712]{1,0:T(8,128)(2,1)S(1)}, bf16[32,3712]{1,0:T(8,128)(2,1)S(1)}, u32[]{:S(2)}, u32[]{:S(2)}) collective-permute-start(bf16[32,3712]{1,0:T(8,128)(2,1)S(1)} %pad.8.refs_0_), channel_id=1, source_target_pairs={{8,0},{16,8},{24,16},{28,24},{20,28},{12,20},{4,12},{0,4},{9,1},{1... | collective-permute-start | bytes 712712 | tf_op jit(solution)/shard_map/ppermute | solution.py:384
  7.2 3.6 %collective-permute-done.refs_1_ = bf16[32,3840]{1,0:T(8,128)(2,1)S(1)} collective-permute-done((bf16[32,3840]{1,0:T(8,128)(2,1)S(1)}, bf16[32,3840]{1,0:T(8,128)(2,1)S(1)}, u32[]{:S(2)}, u32[]{:S(2)}) %collective-permute-start) | collective-permute-done | bytes 245792 | tf_op jit(solution)/shard_map/ppermute | solution.py:381
  10.8 2.1 %collective-permute-start.1 = (bf16[32,3840]{1,0:T(8,128)(2,1)S(1)}, bf16[32,3840]{1,0:T(8,128)(2,1)S(1)}, u32[]{:S(2)}, u32[]{:S(2)}) collective-permute-start(bf16[32,3840]{1,0:T(8,128)(2,1)S(1)} %collective-permute-done.refs_1_), channel_id=1, source_target_pairs={{0,8},{8,16},{16,24},{24,28},{28,20},{20,12},{12,4},{4,0},{1,9},{9... | collective-permute-start | bytes 737288 | tf_op jit(solution)/shard_map/ppermute | solution.py:381
  12.9 5.1 %collective-permute-done.9.refs_2_ = bf16[32,3712]{1,0:T(8,128)(2,1)S(1)} collective-permute-done((bf16[32,3712]{1,0:T(8,128)(2,1)S(1)}, bf16[32,3712]{1,0:T(8,128)(2,1)S(1)}, u32[]{:S(2)}, u32[]{:S(2)}) %collective-permute-start.9) | collective-permute-done | bytes 237600 | tf_op jit(solution)/shard_map/ppermute | solution.py:384
  18.0 2.0 %collective-permute-start.7 = (bf16[32,3712]{1,0:T(8,128)(2,1)S(1)}, bf16[32,3712]{1,0:T(8,128)(2,1)S(1)}, u32[]{:S(2)}, u32[]{:S(2)}) collective-permute-start(bf16[32,3712]{1,0:T(8,128)(2,1)S(1)} %collective-permute-done.6.refs_1_), channel_id=1, source_target_pairs={{0,8},{8,16},{16,24},{24,28},{28,20},{20,12},{12,4},{4,0},{1,9},{9... | collective-permute-start | bytes 712712 | tf_op jit(solution)/shard_map/ppermute | solution.py:381
  21.1 2.1 %collective-permute-start.2 = (bf16[32,3840]{1,0:T(8,128)(2,1)S(1)}, bf16[32,3840]{1,0:T(8,128)(2,1)S(1)}, u32[]{:S(2)}, u32[]{:S(2)}) collective-permute-start(bf16[32,3840]{1,0:T(8,128)(2,1)S(1)} %collective-permute-done.1.refs_3_), channel_id=1, source_target_pairs={{0,8},{8,16},{16,24},{24,28},{28,20},{20,12},{12,4},{4,0},{1,9},{9... | collective-permute-start | bytes 737288 | tf_op jit(solution)/shard_map/ppermute | solution.py:381
  23.3 5.1 %collective-permute-done.10.refs_6_ = bf16[32,3712]{1,0:T(8,128)(2,1)S(1)} collective-permute-done((bf16[32,3712]{1,0:T(8,128)(2,1)S(1)}, bf16[32,3712]{1,0:T(8,128)(2,1)S(1)}, u32[]{:S(2)}, u32[]{:S(2)}) %collective-permute-start.10) | collective-permute-done | bytes 237600 | tf_op jit(solution)/shard_map/ppermute | solution.py:384
  28.4 2.0 %collective-permute-start.8 = (bf16[32,3712]{1,0:T(8,128)(2,1)S(1)}, bf16[32,3712]{1,0:T(8,128)(2,1)S(1)}, u32[]{:S(2)}, u32[]{:S(2)}) collective-permute-start(bf16[32,3712]{1,0:T(8,128)(2,1)S(1)} %collective-permute-done.7.refs_3_), channel_id=1, source_target_pairs={{0,8},{8,16},{16,24},{24,28},{28,20},{20,12},{12,4},{4,0},{1,9},{9... | collective-permute-start | bytes 712712 | tf_op jit(solution)/shard_map/ppermute | solution.py:381
  30.4 1.6 %near_kernel.2.refs_0_ = bf16[3840,128]{1,0:T(8,128)(2,1)S(1)} custom-call(bf16[32,3840]{1,0:T(8,128)(2,1)S(1)} %slice.9.refs_0_, bf16[32,3840]{1,0:T(8,128)(2,1)S(1)} %collective-permute-done.refs_1_, bf16[32,3840]{1,0:T(8,128)(2,1)S(1)} %collective-permute-done.3.refs_2_, bf16[32,3840]{1,0:T(8,128)(2,1)S(1)} %collective-permute-done.1.refs_3_), custom_call_target="tpu_custom_call" | custom-call | flops 100000000 | bytes 1966080 | tf_op jit(solution)/shard_map/near_kernel/pallas_call | solution.py:282
  32.0 1.6 %collective-permute-done.5.refs_4_ = bf16[32,3840]{1,0:T(8,128)(2,1)S(1)} collective-permute-done((bf16[32,3840]{1,0:T(8,128)(2,1)S(1)}, bf16[32,3840]{1,0:T(8,128)(2,1)S(1)}, u32[]{:S(2)}, u32[]{:S(2)}) %collective-permute-start.5) | collective-permute-done | bytes 245792 | tf_op jit(solution)/shard_map/ppermute | solution.py:384
  33.6 1.6 %collective-permute-start.12 = (bf16[32,3840]{1,0:T(8,128)(2,1)S(1)}, bf16[32,3840]{1,0:T(8,128)(2,1)S(1)}, u32[]{:S(2)}, u32[]{:S(2)}) collective-permute-start(bf16[32,3840]{1,0:T(8,128)(2,1)S(1)} %collective-permute-done.2.refs_3_), channel_id=1, source_target_pairs={{0,8},{8,16},{16,24},{24,28},{28,20},{20,12},{12,4},{4,0},{1,9},{9... | collective-permute-start | bytes 737288 | tf_op jit(solution)/shard_map/ppermute | solution.py:381
  38.0 1.8 %collective-permute-start.13 = (bf16[32,3712]{1,0:T(8,128)(2,1)S(1)}, bf16[32,3712]{1,0:T(8,128)(2,1)}, u32[]{:S(2)}, u32[]{:S(2)}) collective-permute-start(bf16[32,3712]{1,0:T(8,128)(2,1)S(1)} %collective-permute-done.11.refs_8_), channel_id=1, source_target_pairs={{8,0},{16,8},{24,16},{28,24},{20,28},{12,20},{4,12},{0,4},{9,1},{1... | collective-permute-start | bytes 712712 | tf_op jit(solution)/shard_map/ppermute | solution.py:384
  41.2 3.2 %collective-permute-done.13.refs_9_ = bf16[32,3712]{1,0:T(8,128)(2,1)} collective-permute-done((bf16[32,3712]{1,0:T(8,128)(2,1)S(1)}, bf16[32,3712]{1,0:T(8,128)(2,1)}, u32[]{:S(2)}, u32[]{:S(2)}) %collective-permute-start.13) | collective-permute-done | bytes 237600 | tf_op jit(solution)/shard_map/ppermute | solution.py:384
  45.3 19.7 %lead_kernel.1 = (f32[2,2880,128]{2,1,0:T(8,128)S(1)}, bf16[7552,256]{1,0:T(8,128)(2,1)S(1)}, s16[2,15,48,256]{3,2,1,0:T(8,128)(2,1)S(1)}) custom-call(s32[1]{0:T(128)} %bitcast.1.rep_ref, bf16[3840,128]{1,0:T(8,128)(2,1)S(1)} %near_kernel.2.refs_0_, bf16[3712,128]{1,0:T(8,128)(2,1)S(1)} %near_kernel.3.refs_1_, ...), custom_call_target="tpu_custom_call" | custom-call | flops 10950279168 | bytes 42774528 | tf_op jit(solution)/shard_map/lead_kernel/pallas_call | solution.py:282
  65.2 2.2 %collective-permute-done.14.got_ref = s16[2,15,48,256]{3,2,1,0:T(8,128)(2,1)S(1)} collective-permute-done((s16[2,15,48,256]{3,2,1,0:T(8,128)(2,1)S(1)}, s16[2,15,48,256]{3,2,1,0:T(8,128)(2,1)S(1)}, u32[]{:S(2)}, u32[]{:S(2)}) %collective-permute-start.14) | collective-permute-done | bytes 737312 | tf_op jit(solution)/shard_map/ppermute | solution.py:430
  68.2 1.6 %collective-permute-start.17 = (s16[15,48,256]{2,1,0:T(8,128)(2,1)S(1)}, s16[15,48,256]{2,1,0:T(8,128)(2,1)S(1)}, u32[]{:S(2)}, u32[]{:S(2)}) collective-permute-start(s16[15,48,256]{2,1,0:T(8,128)(2,1)S(1)} %second_send_kernel.2), channel_id=1, source_target_pairs={{0,2},{1,3},{2,0},{3,1},{4,6},{5,7},{6,4},{7,5},{8,10},{9,11},{10,... | collective-permute-start | bytes 1105928 | tf_op jit(solution)/shard_map/ppermute | solution.py:450
  69.8 7.0 %rest_kernel.1 = (f32[2,964,128]{2,1,0:T(8,128)S(1)}, s16[2,15,16,256]{3,2,1,0:T(8,128)(2,1)S(1)}) custom-call(s32[1]{0:T(128)} %bitcast.1.rep_ref, bf16[7552,256]{1,0:T(8,128)(2,1)S(1)} %get-tuple-element.31.turned, bf16[3600,7500]{1,0:T(8,128)(2,1)} %bitcast.14, bf16[3600,128]{1,0:T(8,128)(2,1)S(1)} %pad.9.refs_11_.edge_ref), custom_call_target="tpu_custom_call" | custom-call | flops 3031433216 | bytes 11841536 | tf_op jit(solution)/shard_map/rest_kernel/pallas_call | solution.py:282
  81.5 3.2 %collective-permute-done.16.got_ref = s16[15,16,256]{2,1,0:T(8,128)(2,1)S(1)} collective-permute-done((s16[15,16,256]{2,1,0:T(8,128)(2,1)S(1)}, s16[15,16,256]{2,1,0:T(8,128)(2,1)S(1)}, u32[]{:S(2)}, u32[]{:S(2)}) %collective-permute-start.16) | collective-permute-done | bytes 122912 | tf_op jit(solution)/shard_map/ppermute | solution.py:450
  87.4 2.5 %collective-permute-start.20 = (s16[4,64,128]{2,1,0:T(8,128)(2,1)S(1)}, s16[4,64,128]{2,1,0:T(8,128)(2,1)S(1)}, u32[]{:S(2)}, u32[]{:S(2)}) collective-permute-start(s16[4,64,128]{2,1,0:T(8,128)(2,1)S(1)} %get-tuple-element.38), channel_id=1, source_target_pairs={{0,12},{8,4},{16,0},{24,8},{28,16},{20,24},{12,28},{4,20},{1,13},{... | collective-permute-start | bytes 196616 | tf_op jit(solution)/shard_map/ppermute | solution.py:477
  90.4 3.6 %collective-permute-start.22 = (s16[4,64,128]{2,1,0:T(8,128)(2,1)S(1)}, s16[4,64,128]{2,1,0:T(8,128)(2,1)S(1)}, u32[]{:S(2)}, u32[]{:S(2)}) collective-permute-start(s16[4,64,128]{2,1,0:T(8,128)(2,1)S(1)} %get-tuple-element.40), channel_id=1, source_target_pairs={{0,20},{8,12},{16,4},{24,0},{28,8},{20,16},{12,24},{4,28},{1,21},{... | collective-permute-start | bytes 196616 | tf_op jit(solution)/shard_map/ppermute | solution.py:477
  94.2 4.6 %collective-permute-start.24 = (s16[4,64,128]{2,1,0:T(8,128)(2,1)S(1)}, s16[4,64,128]{2,1,0:T(8,128)(2,1)S(1)}, u32[]{:S(2)}, u32[]{:S(2)}) collective-permute-start(s16[4,64,128]{2,1,0:T(8,128)(2,1)S(1)} %get-tuple-element.42), channel_id=1, source_target_pairs={{0,28},{8,20},{16,12},{24,4},{28,0},{20,8},{12,16},{4,24},{1,29},{... | collective-permute-start | bytes 196616 | tf_op jit(solution)/shard_map/ppermute | solution.py:477
  99.0 3.8 %collective-permute-done.23.refs_6_ = s16[4,64,128]{2,1,0:T(8,128)(2,1)S(1)} collective-permute-done((s16[4,64,128]{2,1,0:T(8,128)(2,1)S(1)}, s16[4,64,128]{2,1,0:T(8,128)(2,1)S(1)}, u32[]{:S(2)}, u32[]{:S(2)}) %collective-permute-start.23) | collective-permute-done | bytes 65568 | tf_op jit(solution)/shard_map/ppermute | solution.py:477
  102.8 2.2 %update_kernel.1 = f32[15,32,480]{2,1,0:T(8,128)} custom-call(s32[1]{0:T(128)} %bitcast.me_ref, f32[15]{0:T(128)S(1)} %copy-done.5, s32[15]{0:T(128)S(1)} %copy-done.6, s16[4,64,128]{2,1,0:T(8,128)(2,1)S(1)} %get-tuple-element.35.refs_0_, s16[4,64,128]{2,1,0:T(8,128)(2,1)S(1)} %collective-permute-done.18.refs_1_, ...), custom_call_target="tpu_custom_call" | custom-call | flops 10000000 | bytes 4000000 | tf_op jit(solution)/shard_map/update_kernel/pallas_call | solution.py:282
  (62 shorter events, 17.5 us)
Async XLA Ops:
  1.0 9.8 %collective-permute-start = (bf16[32,3840]{1,0:T(8,128)(2,1)S(1)}, bf16[32,3840]{1,0:T(8,128)(2,1)S(1)}, u32[]{:S(2)}, u32[]{:S(2)}) collective-permute-start(bf16[32,3840]{1,0:T(8,128)(2,1)S(1)} %slice.9.refs_0_), channel_id=1, source_target_pairs={{0,8},{8,16},{16,24},{24,28},{28,20},{20,12},{12,4},{4,0},{1,9},{9... | collective-permute-start | bytes 737288 | tf_op jit(solution)/shard_map/ppermute | solution.py:381
  4.0 8.9 %collective-permute-start.3 = (bf16[32,3840]{1,0:T(8,128)(2,1)S(1)}, bf16[32,3840]{1,0:T(8,128)(2,1)S(1)}, u32[]{:S(2)}, u32[]{:S(2)}) collective-permute-start(bf16[32,3840]{1,0:T(8,128)(2,1)S(1)} %slice.9.refs_0_), channel_id=1, source_target_pairs={{8,0},{16,8},{24,16},{28,24},{20,28},{12,20},{4,12},{0,4},{9,1},{1... | collective-permute-start | bytes 737288 | tf_op jit(solution)/shard_map/ppermute | solution.py:384
  5.0 13.0 %collective-permute-start.9 = (bf16[32,3712]{1,0:T(8,128)(2,1)S(1)}, bf16[32,3712]{1,0:T(8,128)(2,1)S(1)}, u32[]{:S(2)}, u32[]{:S(2)}) collective-permute-start(bf16[32,3712]{1,0:T(8,128)(2,1)S(1)} %pad.8.refs_0_), channel_id=1, source_target_pairs={{8,0},{16,8},{24,16},{28,24},{20,28},{12,20},{4,12},{0,4},{9,1},{1... | collective-permute-start | bytes 712712 | tf_op jit(solution)/shard_map/ppermute | solution.py:384
  7.1 11.0 %collective-permute-start.6 = (bf16[32,3712]{1,0:T(8,128)(2,1)S(1)}, bf16[32,3712]{1,0:T(8,128)(2,1)S(1)}, u32[]{:S(2)}, u32[]{:S(2)}) collective-permute-start(bf16[32,3712]{1,0:T(8,128)(2,1)S(1)} %pad.8.refs_0_), channel_id=1, source_target_pairs={{0,8},{8,16},{16,24},{24,28},{28,20},{20,12},{12,4},{4,0},{1,9},{9... | collective-permute-start | bytes 712712 | tf_op jit(solution)/shard_map/ppermute | solution.py:381
  10.8 10.4 %collective-permute-start.1 = (bf16[32,3840]{1,0:T(8,128)(2,1)S(1)}, bf16[32,3840]{1,0:T(8,128)(2,1)S(1)}, u32[]{:S(2)}, u32[]{:S(2)}) collective-permute-start(bf16[32,3840]{1,0:T(8,128)(2,1)S(1)} %collective-permute-done.refs_1_), channel_id=1, source_target_pairs={{0,8},{8,16},{16,24},{24,28},{28,20},{20,12},{12,4},{4,0},{1,9},{9... | collective-permute-start | bytes 737288 | tf_op jit(solution)/shard_map/ppermute | solution.py:381
  12.9 10.4 %collective-permute-start.4 = (bf16[32,3840]{1,0:T(8,128)(2,1)S(1)}, bf16[32,3840]{1,0:T(8,128)(2,1)S(1)}, u32[]{:S(2)}, u32[]{:S(2)}) collective-permute-start(bf16[32,3840]{1,0:T(8,128)(2,1)S(1)} %collective-permute-done.3.refs_2_), channel_id=1, source_target_pairs={{8,0},{16,8},{24,16},{28,24},{20,28},{12,20},{4,12},{0,4},{9,1},{1... | collective-permute-start | bytes 737288 | tf_op jit(solution)/shard_map/ppermute | solution.py:384
  18.0 10.4 %collective-permute-start.10 = (bf16[32,3712]{1,0:T(8,128)(2,1)S(1)}, bf16[32,3712]{1,0:T(8,128)(2,1)S(1)}, u32[]{:S(2)}, u32[]{:S(2)}) collective-permute-start(bf16[32,3712]{1,0:T(8,128)(2,1)S(1)} %collective-permute-done.9.refs_2_), channel_id=1, source_target_pairs={{8,0},{16,8},{24,16},{28,24},{20,28},{12,20},{4,12},{0,4},{9,1},{1... | collective-permute-start | bytes 712712 | tf_op jit(solution)/shard_map/ppermute | solution.py:384
  18.0 10.4 %collective-permute-start.7 = (bf16[32,3712]{1,0:T(8,128)(2,1)S(1)}, bf16[32,3712]{1,0:T(8,128)(2,1)S(1)}, u32[]{:S(2)}, u32[]{:S(2)}) collective-permute-start(bf16[32,3712]{1,0:T(8,128)(2,1)S(1)} %collective-permute-done.6.refs_1_), channel_id=1, source_target_pairs={{0,8},{8,16},{16,24},{24,28},{28,20},{20,12},{12,4},{4,0},{1,9},{9... | collective-permute-start | bytes 712712 | tf_op jit(solution)/shard_map/ppermute | solution.py:381
  21.1 10.9 %collective-permute-start.2 = (bf16[32,3840]{1,0:T(8,128)(2,1)S(1)}, bf16[32,3840]{1,0:T(8,128)(2,1)S(1)}, u32[]{:S(2)}, u32[]{:S(2)}) collective-permute-start(bf16[32,3840]{1,0:T(8,128)(2,1)S(1)} %collective-permute-done.1.refs_3_), channel_id=1, source_target_pairs={{0,8},{8,16},{16,24},{24,28},{28,20},{20,12},{12,4},{4,0},{1,9},{9... | collective-permute-start | bytes 737288 | tf_op jit(solution)/shard_map/ppermute | solution.py:381
  23.3 10.4 %collective-permute-start.5 = (bf16[32,3840]{1,0:T(8,128)(2,1)S(1)}, bf16[32,3840]{1,0:T(8,128)(2,1)S(1)}, u32[]{:S(2)}, u32[]{:S(2)}) collective-permute-start(bf16[32,3840]{1,0:T(8,128)(2,1)S(1)} %collective-permute-done.4.refs_2_), channel_id=1, source_target_pairs={{8,0},{16,8},{24,16},{28,24},{20,28},{12,20},{4,12},{0,4},{9,1},{1... | collective-permute-start | bytes 737288 | tf_op jit(solution)/shard_map/ppermute | solution.py:384
  28.4 8.9 %collective-permute-start.11 = (bf16[32,3712]{1,0:T(8,128)(2,1)S(1)}, bf16[32,3712]{1,0:T(8,128)(2,1)S(1)}, u32[]{:S(2)}, u32[]{:S(2)}) collective-permute-start(bf16[32,3712]{1,0:T(8,128)(2,1)S(1)} %collective-permute-done.10.refs_6_), channel_id=1, source_target_pairs={{8,0},{16,8},{24,16},{28,24},{20,28},{12,20},{4,12},{0,4},{9,1},{1... | collective-permute-start | bytes 712712 | tf_op jit(solution)/shard_map/ppermute | solution.py:384
  28.4 8.9 %collective-permute-start.8 = (bf16[32,3712]{1,0:T(8,128)(2,1)S(1)}, bf16[32,3712]{1,0:T(8,128)(2,1)S(1)}, u32[]{:S(2)}, u32[]{:S(2)}) collective-permute-start(bf16[32,3712]{1,0:T(8,128)(2,1)S(1)} %collective-permute-done.7.refs_3_), channel_id=1, source_target_pairs={{0,8},{8,16},{16,24},{24,28},{28,20},{20,12},{12,4},{4,0},{1,9},{9... | collective-permute-start | bytes 712712 | tf_op jit(solution)/shard_map/ppermute | solution.py:381
  33.6 10.8 %collective-permute-start.12 = (bf16[32,3840]{1,0:T(8,128)(2,1)S(1)}, bf16[32,3840]{1,0:T(8,128)(2,1)S(1)}, u32[]{:S(2)}, u32[]{:S(2)}) collective-permute-start(bf16[32,3840]{1,0:T(8,128)(2,1)S(1)} %collective-permute-done.2.refs_3_), channel_id=1, source_target_pairs={{0,8},{8,16},{16,24},{24,28},{28,20},{20,12},{12,4},{4,0},{1,9},{9... | collective-permute-start | bytes 737288 | tf_op jit(solution)/shard_map/ppermute | solution.py:381
  38.0 6.4 %collective-permute-start.13 = (bf16[32,3712]{1,0:T(8,128)(2,1)S(1)}, bf16[32,3712]{1,0:T(8,128)(2,1)}, u32[]{:S(2)}, u32[]{:S(2)}) collective-permute-start(bf16[32,3712]{1,0:T(8,128)(2,1)S(1)} %collective-permute-done.11.refs_8_), channel_id=1, source_target_pairs={{8,0},{16,8},{24,16},{28,24},{20,28},{12,20},{4,12},{0,4},{9,1},{1... | collective-permute-start | bytes 712712 | tf_op jit(solution)/shard_map/ppermute | solution.py:384
  65.1 2.3 %collective-permute-start.14 = (s16[2,15,48,256]{3,2,1,0:T(8,128)(2,1)S(1)}, s16[2,15,48,256]{3,2,1,0:T(8,128)(2,1)S(1)}, u32[]{:S(2)}, u32[]{:S(2)}) collective-permute-start(s16[2,15,48,256]{3,2,1,0:T(8,128)(2,1)S(1)} %get-tuple-element.30), channel_id=1, source_target_pairs={{0,1},{1,0},{2,3},{3,2},{4,5},{5,4},{6,7},{7,6},{8,9},{9,8},{10,11... | collective-permute-start | bytes 2211848 | tf_op jit(solution)/shard_map/ppermute | solution.py:430
  68.2 12.2 %collective-permute-start.17 = (s16[15,48,256]{2,1,0:T(8,128)(2,1)S(1)}, s16[15,48,256]{2,1,0:T(8,128)(2,1)S(1)}, u32[]{:S(2)}, u32[]{:S(2)}) collective-permute-start(s16[15,48,256]{2,1,0:T(8,128)(2,1)S(1)} %second_send_kernel.2), channel_id=1, source_target_pairs={{0,2},{1,3},{2,0},{3,1},{4,6},{5,7},{6,4},{7,5},{8,10},{9,11},{10,... | collective-permute-start | bytes 1105928 | tf_op jit(solution)/shard_map/ppermute | solution.py:450
  79.2 5.4 %collective-permute-start.16 = (s16[15,16,256]{2,1,0:T(8,128)(2,1)S(1)}, s16[15,16,256]{2,1,0:T(8,128)(2,1)S(1)}, u32[]{:S(2)}, u32[]{:S(2)}) collective-permute-start(s16[15,16,256]{2,1,0:T(8,128)(2,1)S(1)} %second_send_kernel.3), channel_id=1, source_target_pairs={{0,2},{1,3},{2,0},{3,1},{4,6},{5,7},{6,4},{7,5},{8,10},{9,11},{10,... | collective-permute-start | bytes 368648 | tf_op jit(solution)/shard_map/ppermute | solution.py:450
  85.4 8.6 %collective-permute-start.18 = (s16[4,64,128]{2,1,0:T(8,128)(2,1)S(1)}, s16[4,64,128]{2,1,0:T(8,128)(2,1)S(1)}, u32[]{:S(2)}, u32[]{:S(2)}) collective-permute-start(s16[4,64,128]{2,1,0:T(8,128)(2,1)S(1)} %get-tuple-element.36), channel_id=1, source_target_pairs={{0,4},{8,0},{16,8},{24,16},{28,24},{20,28},{12,20},{4,12},{1,5},{9... | collective-permute-start | bytes 196616 | tf_op jit(solution)/shard_map/ppermute | solution.py:477
  86.9 7.3 %collective-permute-start.19 = (s16[4,64,128]{2,1,0:T(8,128)(2,1)S(1)}, s16[4,64,128]{2,1,0:T(8,128)(2,1)S(1)}, u32[]{:S(2)}, u32[]{:S(2)}) collective-permute-start(s16[4,64,128]{2,1,0:T(8,128)(2,1)S(1)} %get-tuple-element.37), channel_id=1, source_target_pairs={{0,8},{8,16},{16,24},{24,28},{28,20},{20,12},{12,4},{4,0},{1,9},{9... | collective-permute-start | bytes 196616 | tf_op jit(solution)/shard_map/ppermute | solution.py:477
  87.4 11.5 %collective-permute-start.20 = (s16[4,64,128]{2,1,0:T(8,128)(2,1)S(1)}, s16[4,64,128]{2,1,0:T(8,128)(2,1)S(1)}, u32[]{:S(2)}, u32[]{:S(2)}) collective-permute-start(s16[4,64,128]{2,1,0:T(8,128)(2,1)S(1)} %get-tuple-element.38), channel_id=1, source_target_pairs={{0,12},{8,4},{16,0},{24,8},{28,16},{20,24},{12,28},{4,20},{1,13},{... | collective-permute-start | bytes 196616 | tf_op jit(solution)/shard_map/ppermute | solution.py:477
  90.0 9.0 %collective-permute-start.21 = (s16[4,64,128]{2,1,0:T(8,128)(2,1)S(1)}, s16[4,64,128]{2,1,0:T(8,128)(2,1)S(1)}, u32[]{:S(2)}, u32[]{:S(2)}) collective-permute-start(s16[4,64,128]{2,1,0:T(8,128)(2,1)S(1)} %get-tuple-element.39), channel_id=1, source_target_pairs={{0,16},{8,24},{16,28},{24,20},{28,12},{20,4},{12,0},{4,8},{1,17},{... | collective-permute-start | bytes 196616 | tf_op jit(solution)/shard_map/ppermute | solution.py:477
  90.4 8.6 %collective-permute-start.22 = (s16[4,64,128]{2,1,0:T(8,128)(2,1)S(1)}, s16[4,64,128]{2,1,0:T(8,128)(2,1)S(1)}, u32[]{:S(2)}, u32[]{:S(2)}) collective-permute-start(s16[4,64,128]{2,1,0:T(8,128)(2,1)S(1)} %get-tuple-element.40), channel_id=1, source_target_pairs={{0,20},{8,12},{16,4},{24,0},{28,8},{20,16},{12,24},{4,28},{1,21},{... | collective-permute-start | bytes 196616 | tf_op jit(solution)/shard_map/ppermute | solution.py:477
  93.9 8.8 %collective-permute-start.23 = (s16[4,64,128]{2,1,0:T(8,128)(2,1)S(1)}, s16[4,64,128]{2,1,0:T(8,128)(2,1)S(1)}, u32[]{:S(2)}, u32[]{:S(2)}) collective-permute-start(s16[4,64,128]{2,1,0:T(8,128)(2,1)S(1)} %get-tuple-element.41), channel_id=1, source_target_pairs={{0,24},{8,28},{16,20},{24,12},{28,4},{20,0},{12,8},{4,16},{1,25},{... | collective-permute-start | bytes 196616 | tf_op jit(solution)/shard_map/ppermute | solution.py:477
  94.2 8.6 %collective-permute-start.24 = (s16[4,64,128]{2,1,0:T(8,128)(2,1)S(1)}, s16[4,64,128]{2,1,0:T(8,128)(2,1)S(1)}, u32[]{:S(2)}, u32[]{:S(2)}) collective-permute-start(s16[4,64,128]{2,1,0:T(8,128)(2,1)S(1)} %get-tuple-element.42), channel_id=1, source_target_pairs={{0,28},{8,20},{16,12},{24,4},{28,0},{20,8},{12,16},{4,24},{1,29},{... | collective-permute-start | bytes 196616 | tf_op jit(solution)/shard_map/ppermute | solution.py:477
  (10 other events, 160.4 us)

commit v11 on v6

--- a/solution.py
+++ b/solution.py
@@ -326,6 +326,8 @@
         ahead = behind = own
         pieces = [own]
         for hop in range(1, longer + 1):
+            if hop == longer:
+                ahead, behind = lax.optimization_barrier((ahead, behind))
             if hop < longer or number % 2 == 0:
                 ahead = lax.ppermute(ahead, "grid", onward)
                 pieces.append(ahead)

time: 99.8 us -> 100 us (level)
  local copies, waits for them, and re-layouts: 5.21 us -> 6.83 us
    ppermute x7, waiting for transfers between devices: 9.02 us -> 3.35 us  [body(): behind = lax.ppermute(behind, 'grid', back)]
    ppermute x7, waiting for transfers between devices: 10.7 us -> 15.8 us  [body(): ahead = lax.ppermute(ahead, 'grid', onward)]
    unnamed x18 -> x22, local copies, waits for them, and re-layouts: 1.67 us -> 3.3 us
    ppermute x7, starting transfers between devices: 14.1 us -> 15.2 us  [body(): ahead = lax.ppermute(ahead, 'grid', onward)]
    ppermute x7, starting transfers between devices: 2.48 us -> 1.4 us  [body(): behind = lax.ppermute(behind, 'grid', back)]
  transfers between devices with their start and end apart: 25 -> 25, of which waited for: 12 -> 13; matrix products, arithmetic and copies ran while one was open for 3% -> 3% of each run, Pallas kernels for 12% -> 11%
where the time goes in v11:
time: 100 us
  starting transfers between devices  31.9 us (32%)
  Pallas kernels  31.2 us (31%)
  waiting for transfers between devices  29.9 us (30%)
  local copies, waits for them, and re-layouts  6.83 us (7%)
    pallas_call x10, Pallas kernels, local_call(): pl.pallas_call(kernel, out_shape=out_shape, in_specs=[pl.BlockSpec(memory...  31.2 us
    ppermute x7, waiting for transfers between devices, body(): ahead = lax.ppermute(ahead, 'grid', onward)  15.8 us
    ppermute x7, starting transfers between devices, body(): ahead = lax.ppermute(ahead, 'grid', onward)  15.2 us
    ppermute x7, starting transfers between devices, body(): lax.ppermute(targets[number], 'grid', [(walk[i], walk[(i + order[number])...  13 us
    ppermute x7, waiting for transfers between devices, body(): lax.ppermute(targets[number], 'grid', [(walk[i], walk[(i + order[number])...  3.93 us
    ppermute x2, waiting for transfers between devices, body(): arrived = lax.ppermute(send, 'rep', low_pairs)  3.7 us
    ppermute x7, waiting for transfers between devices, body(): behind = lax.ppermute(behind, 'grid', back)  3.35 us
    unnamed x22, local copies, waits for them, and re-layouts  3.3 us
  transfers between devices with their start and end apart: 25, of which 13 were waited for; matrix products, arithmetic and copies ran while one was open for 3% of the time, Pallas kernels for 11%

profile of v11, /device:TPU:0, one launch (start us, length us, event | category | flops | bytes accessed | tf_op | source)
XLA Modules:
  0.0 100.1 jit_solution(18189490010665882612)
XLA Ops:
  1.0 3.1 %collective-permute-start = (bf16[32,3840]{1,0:T(8,128)(2,1)S(1)}, bf16[32,3840]{1,0:T(8,128)(2,1)S(1)}, u32[]{:S(2)}, u32[]{:S(2)}) collective-permute-start(bf16[32,3840]{1,0:T(8,128)(2,1)S(1)} %slice.9.refs_0_), channel_id=1, source_target_pairs={{0,8},{8,16},{16,24},{24,28},{28,20},{20,12},{12,4},{4,0},{1,9},{9... | collective-permute-start | bytes 737288 | tf_op jit(solution)/shard_map/ppermute | solution.py:332
  5.0 2.1 %collective-permute-start.3 = (bf16[32,3712]{1,0:T(8,128)(2,1)S(1)}, bf16[32,3712]{1,0:T(8,128)(2,1)S(1)}, u32[]{:S(2)}, u32[]{:S(2)}) collective-permute-start(bf16[32,3712]{1,0:T(8,128)(2,1)S(1)} %pad.8.refs_4_), channel_id=1, source_target_pairs={{0,8},{8,16},{16,24},{24,28},{28,20},{20,12},{12,4},{4,0},{1,9},{9... | collective-permute-start | bytes 712712 | tf_op jit(solution)/shard_map/ppermute | solution.py:332
  7.1 3.6 %collective-permute-done.refs_1_ = bf16[32,3840]{1,0:T(8,128)(2,1)S(1)} collective-permute-done((bf16[32,3840]{1,0:T(8,128)(2,1)S(1)}, bf16[32,3840]{1,0:T(8,128)(2,1)S(1)}, u32[]{:S(2)}, u32[]{:S(2)}) %collective-permute-start) | collective-permute-done | bytes 245792 | tf_op jit(solution)/shard_map/ppermute | solution.py:332
  10.8 2.1 %collective-permute-start.2 = (bf16[32,3840]{1,0:T(8,128)(2,1)S(1)}, bf16[32,3840]{1,0:T(8,128)(2,1)S(1)}, u32[]{:S(2)}, u32[]{:S(2)}) collective-permute-start(bf16[32,3840]{1,0:T(8,128)(2,1)S(1)} %collective-permute-done.refs_1_), channel_id=1, source_target_pairs={{0,8},{8,16},{16,24},{24,28},{28,20},{20,12},{12,4},{4,0},{1,9},{9... | collective-permute-start | bytes 737288 | tf_op jit(solution)/shard_map/ppermute | solution.py:332
  12.9 2.9 %collective-permute-done.3.refs_5_ = bf16[32,3712]{1,0:T(8,128)(2,1)S(1)} collective-permute-done((bf16[32,3712]{1,0:T(8,128)(2,1)S(1)}, bf16[32,3712]{1,0:T(8,128)(2,1)S(1)}, u32[]{:S(2)}, u32[]{:S(2)}) %collective-permute-start.3) | collective-permute-done | bytes 237600 | tf_op jit(solution)/shard_map/ppermute | solution.py:332
  15.9 2.1 %collective-permute-start.5 = (bf16[32,3712]{1,0:T(8,128)(2,1)S(1)}, bf16[32,3712]{1,0:T(8,128)(2,1)S(1)}, u32[]{:S(2)}, u32[]{:S(2)}) collective-permute-start(bf16[32,3712]{1,0:T(8,128)(2,1)S(1)} %collective-permute-done.3.refs_5_), channel_id=1, source_target_pairs={{0,8},{8,16},{16,24},{24,28},{28,20},{20,12},{12,4},{4,0},{1,9},{9... | collective-permute-start | bytes 712712 | tf_op jit(solution)/shard_map/ppermute | solution.py:332
  18.7 2.4 %collective-permute-done.2.refs_3_ = bf16[32,3840]{1,0:T(8,128)(2,1)S(1)} collective-permute-done((bf16[32,3840]{1,0:T(8,128)(2,1)S(1)}, bf16[32,3840]{1,0:T(8,128)(2,1)S(1)}, u32[]{:S(2)}, u32[]{:S(2)}) %collective-permute-start.2) | collective-permute-done | bytes 245792 | tf_op jit(solution)/shard_map/ppermute | solution.py:332
  21.1 2.1 %collective-permute-start.7 = (bf16[32,3840]{1,0:T(8,128)(2,1)S(1)}, bf16[32,3840]{1,0:T(8,128)(2,1)S(1)}, u32[]{:S(2)}, u32[]{:S(2)}) collective-permute-start(bf16[32,3840]{1,0:T(8,128)(2,1)S(1)} %collective-permute-done.2.refs_3_), channel_id=1, source_target_pairs={{0,8},{8,16},{16,24},{24,28},{28,20},{20,12},{12,4},{4,0},{1,9},{9... | collective-permute-start | bytes 737288 | tf_op jit(solution)/shard_map/ppermute | solution.py:332
  23.3 2.9 %collective-permute-done.5.refs_7_ = bf16[32,3712]{1,0:T(8,128)(2,1)S(1)} collective-permute-done((bf16[32,3712]{1,0:T(8,128)(2,1)S(1)}, bf16[32,3712]{1,0:T(8,128)(2,1)S(1)}, u32[]{:S(2)}, u32[]{:S(2)}) %collective-permute-start.5) | collective-permute-done | bytes 237600 | tf_op jit(solution)/shard_map/ppermute | solution.py:332
  26.2 2.1 %collective-permute-start.11 = (bf16[32,3712]{1,0:T(8,128)(2,1)S(1)}, bf16[32,3712]{1,0:T(8,128)(2,1)S(1)}, u32[]{:S(2)}, u32[]{:S(2)}) collective-permute-start(bf16[32,3712]{1,0:T(8,128)(2,1)S(1)} %collective-permute-done.5.refs_7_), channel_id=1, source_target_pairs={{0,8},{8,16},{16,24},{24,28},{28,20},{20,12},{12,4},{4,0},{1,9},{9... | collective-permute-start | bytes 712712 | tf_op jit(solution)/shard_map/ppermute | solution.py:332
  29.0 2.5 %collective-permute-done.7.refs_1_ = bf16[32,3840]{1,0:T(8,128)(2,1)S(1)} collective-permute-done((bf16[32,3840]{1,0:T(8,128)(2,1)S(1)}, bf16[32,3840]{1,0:T(8,128)(2,1)S(1)}, u32[]{:S(2)}, u32[]{:S(2)}) %collective-permute-start.7) | collective-permute-done | bytes 245792 | tf_op jit(solution)/shard_map/ppermute | solution.py:332
  31.5 2.2 %collective-permute-done.8.refs_2_ = bf16[32,3840]{1,0:T(8,128)(2,1)S(1)} collective-permute-done((bf16[32,3840]{1,0:T(8,128)(2,1)S(1)}, bf16[32,3840]{1,0:T(8,128)(2,1)S(1)}, u32[]{:S(2)}, u32[]{:S(2)}) %collective-permute-start.8) | collective-permute-done | bytes 245792 | tf_op jit(solution)/shard_map/ppermute | solution.py:335
  33.6 1.6 %collective-permute-start.9 = (bf16[32,3840]{1,0:T(8,128)(2,1)S(1)}, bf16[32,3840]{1,0:T(8,128)(2,1)S(1)}, u32[]{:S(2)}, u32[]{:S(2)}) collective-permute-start(bf16[32,3840]{1,0:T(8,128)(2,1)S(1)} %collective-permute-done.7.refs_1_), channel_id=1, source_target_pairs={{0,8},{8,16},{16,24},{24,28},{28,20},{20,12},{12,4},{4,0},{1,9},{9... | collective-permute-start | bytes 737288 | tf_op jit(solution)/shard_map/ppermute | solution.py:332
  43.6 16.9 %lead_kernel.1 = (f32[2,2880,128]{2,1,0:T(8,128)S(1)}, bf16[7552,256]{1,0:T(8,128)(2,1)S(1)}, s16[2,15,48,256]{3,2,1,0:T(8,128)(2,1)S(1)}) custom-call(s32[1]{0:T(128)} %bitcast.1.rep_ref, bf16[7552,128]{1,0:T(8,128)(2,1)S(1)} %near_kernel.1.near, bf16[32,3840]{1,0:T(8,128)(2,1)S(1)} %collective-permute-done.6.refs_0_, ...), custom_call_target="tpu_custom_call" | custom-call | flops 10950279168 | bytes 42774528 | tf_op jit(solution)/shard_map/lead_kernel/pallas_call | solution.py:270
  60.6 2.2 %collective-permute-done.14.got_ref = s16[2,15,48,256]{3,2,1,0:T(8,128)(2,1)S(1)} collective-permute-done((s16[2,15,48,256]{3,2,1,0:T(8,128)(2,1)S(1)}, s16[2,15,48,256]{3,2,1,0:T(8,128)(2,1)S(1)}, u32[]{:S(2)}, u32[]{:S(2)}) %collective-permute-start.14) | collective-permute-done | bytes 737312 | tf_op jit(solution)/shard_map/ppermute | solution.py:412
  63.6 1.5 %collective-permute-start.17 = (s16[15,48,256]{2,1,0:T(8,128)(2,1)S(1)}, s16[15,48,256]{2,1,0:T(8,128)(2,1)S(1)}, u32[]{:S(2)}, u32[]{:S(2)}) collective-permute-start(s16[15,48,256]{2,1,0:T(8,128)(2,1)S(1)} %second_send_kernel.2), channel_id=1, source_target_pairs={{0,2},{1,3},{2,0},{3,1},{4,6},{5,7},{6,4},{7,5},{8,10},{9,11},{10,... | collective-permute-start | bytes 1105928 | tf_op jit(solution)/shard_map/ppermute | solution.py:432
  65.2 7.0 %rest_kernel.1 = (f32[2,964,128]{2,1,0:T(8,128)S(1)}, s16[2,15,16,256]{3,2,1,0:T(8,128)(2,1)S(1)}) custom-call(s32[1]{0:T(128)} %bitcast.1.rep_ref, bf16[7552,256]{1,0:T(8,128)(2,1)S(1)} %get-tuple-element.27.turned, bf16[3600,7500]{1,0:T(8,128)(2,1)} %bitcast.14, bf16[3600,128]{1,0:T(8,128)(2,1)S(1)} %pad.9.refs_9_.edge_ref), custom_call_target="tpu_custom_call" | custom-call | flops 3031433216 | bytes 11841536 | tf_op jit(solution)/shard_map/rest_kernel/pallas_call | solution.py:270
  72.3 1.5 %collective-permute-done.15.got_ref = s16[2,15,16,256]{3,2,1,0:T(8,128)(2,1)S(1)} collective-permute-done((s16[2,15,16,256]{3,2,1,0:T(8,128)(2,1)S(1)}, s16[2,15,16,256]{3,2,1,0:T(8,128)(2,1)S(1)}, u32[]{:S(2)}, u32[]{:S(2)}) %collective-permute-start.15) | collective-permute-done | bytes 245792 | tf_op jit(solution)/shard_map/ppermute | solution.py:412
  76.9 3.1 %collective-permute-done.16.got_ref = s16[15,16,256]{2,1,0:T(8,128)(2,1)S(1)} collective-permute-done((s16[15,16,256]{2,1,0:T(8,128)(2,1)S(1)}, s16[15,16,256]{2,1,0:T(8,128)(2,1)S(1)}, u32[]{:S(2)}, u32[]{:S(2)}) %collective-permute-start.16) | collective-permute-done | bytes 122912 | tf_op jit(solution)/shard_map/ppermute | solution.py:432
  82.8 2.2 %collective-permute-start.20 = (s16[4,64,128]{2,1,0:T(8,128)(2,1)S(1)}, s16[4,64,128]{2,1,0:T(8,128)(2,1)S(1)}, u32[]{:S(2)}, u32[]{:S(2)}) collective-permute-start(s16[4,64,128]{2,1,0:T(8,128)(2,1)S(1)} %get-tuple-element.34), channel_id=1, source_target_pairs={{0,12},{8,4},{16,0},{24,8},{28,16},{20,24},{12,28},{4,20},{1,13},{... | collective-permute-start | bytes 196616 | tf_op jit(solution)/shard_map/ppermute | solution.py:455
  85.7 3.2 %collective-permute-start.22 = (s16[4,64,128]{2,1,0:T(8,128)(2,1)S(1)}, s16[4,64,128]{2,1,0:T(8,128)(2,1)S(1)}, u32[]{:S(2)}, u32[]{:S(2)}) collective-permute-start(s16[4,64,128]{2,1,0:T(8,128)(2,1)S(1)} %get-tuple-element.36), channel_id=1, source_target_pairs={{0,20},{8,12},{16,4},{24,0},{28,8},{20,16},{12,24},{4,28},{1,21},{... | collective-permute-start | bytes 196616 | tf_op jit(solution)/shard_map/ppermute | solution.py:455
  89.6 4.2 %collective-permute-start.24 = (s16[4,64,128]{2,1,0:T(8,128)(2,1)S(1)}, s16[4,64,128]{2,1,0:T(8,128)(2,1)S(1)}, u32[]{:S(2)}, u32[]{:S(2)}) collective-permute-start(s16[4,64,128]{2,1,0:T(8,128)(2,1)S(1)} %get-tuple-element.38), channel_id=1, source_target_pairs={{0,28},{8,20},{16,12},{24,4},{28,0},{20,8},{12,16},{4,24},{1,29},{... | collective-permute-start | bytes 196616 | tf_op jit(solution)/shard_map/ppermute | solution.py:455
  94.0 3.9 %collective-permute-done.23.refs_6_ = s16[4,64,128]{2,1,0:T(8,128)(2,1)S(1)} collective-permute-done((s16[4,64,128]{2,1,0:T(8,128)(2,1)S(1)}, s16[4,64,128]{2,1,0:T(8,128)(2,1)S(1)}, u32[]{:S(2)}, u32[]{:S(2)}) %collective-permute-start.23) | collective-permute-done | bytes 65568 | tf_op jit(solution)/shard_map/ppermute | solution.py:455
  97.9 2.2 %update_kernel.1 = f32[15,32,480]{2,1,0:T(8,128)} custom-call(s32[1]{0:T(128)} %bitcast.me_ref, f32[15]{0:T(128)S(1)} %copy-done.7, s32[15]{0:T(128)S(1)} %copy-done.8, s16[4,64,128]{2,1,0:T(8,128)(2,1)S(1)} %get-tuple-element.31.refs_0_, s16[4,64,128]{2,1,0:T(8,128)(2,1)S(1)} %collective-permute-done.18.refs_1_, ...), custom_call_target="tpu_custom_call" | custom-call | flops 10000000 | bytes 4000000 | tf_op jit(solution)/shard_map/update_kernel/pallas_call | solution.py:270
  (65 shorter events, 20.1 us)
Async XLA Ops:
  1.0 9.8 %collective-permute-start = (bf16[32,3840]{1,0:T(8,128)(2,1)S(1)}, bf16[32,3840]{1,0:T(8,128)(2,1)S(1)}, u32[]{:S(2)}, u32[]{:S(2)}) collective-permute-start(bf16[32,3840]{1,0:T(8,128)(2,1)S(1)} %slice.9.refs_0_), channel_id=1, source_target_pairs={{0,8},{8,16},{16,24},{24,28},{28,20},{20,12},{12,4},{4,0},{1,9},{9... | collective-permute-start | bytes 737288 | tf_op jit(solution)/shard_map/ppermute | solution.py:332
  4.0 8.9 %collective-permute-start.1 = (bf16[32,3840]{1,0:T(8,128)(2,1)S(1)}, bf16[32,3840]{1,0:T(8,128)(2,1)S(1)}, u32[]{:S(2)}, u32[]{:S(2)}) collective-permute-start(bf16[32,3840]{1,0:T(8,128)(2,1)S(1)} %slice.9.refs_0_), channel_id=1, source_target_pairs={{8,0},{16,8},{24,16},{28,24},{20,28},{12,20},{4,12},{0,4},{9,1},{1... | collective-permute-start | bytes 737288 | tf_op jit(solution)/shard_map/ppermute | solution.py:335
  5.0 10.8 %collective-permute-start.3 = (bf16[32,3712]{1,0:T(8,128)(2,1)S(1)}, bf16[32,3712]{1,0:T(8,128)(2,1)S(1)}, u32[]{:S(2)}, u32[]{:S(2)}) collective-permute-start(bf16[32,3712]{1,0:T(8,128)(2,1)S(1)} %pad.8.refs_4_), channel_id=1, source_target_pairs={{0,8},{8,16},{16,24},{24,28},{28,20},{20,12},{12,4},{4,0},{1,9},{9... | collective-permute-start | bytes 712712 | tf_op jit(solution)/shard_map/ppermute | solution.py:332
  7.1 10.9 %collective-permute-start.4 = (bf16[32,3712]{1,0:T(8,128)(2,1)S(1)}, bf16[32,3712]{1,0:T(8,128)(2,1)S(1)}, u32[]{:S(2)}, u32[]{:S(2)}) collective-permute-start(bf16[32,3712]{1,0:T(8,128)(2,1)S(1)} %pad.8.refs_4_), channel_id=1, source_target_pairs={{8,0},{16,8},{24,16},{28,24},{20,28},{12,20},{4,12},{0,4},{9,1},{1... | collective-permute-start | bytes 712712 | tf_op jit(solution)/shard_map/ppermute | solution.py:335
  10.8 10.4 %collective-permute-start.2 = (bf16[32,3840]{1,0:T(8,128)(2,1)S(1)}, bf16[32,3840]{1,0:T(8,128)(2,1)S(1)}, u32[]{:S(2)}, u32[]{:S(2)}) collective-permute-start(bf16[32,3840]{1,0:T(8,128)(2,1)S(1)} %collective-permute-done.refs_1_), channel_id=1, source_target_pairs={{0,8},{8,16},{16,24},{24,28},{28,20},{20,12},{12,4},{4,0},{1,9},{9... | collective-permute-start | bytes 737288 | tf_op jit(solution)/shard_map/ppermute | solution.py:332
  12.9 10.4 %collective-permute-start.6 = (bf16[32,3840]{1,0:T(8,128)(2,1)S(1)}, bf16[32,3840]{1,0:T(8,128)(2,1)S(1)}, u32[]{:S(2)}, u32[]{:S(2)}) collective-permute-start(bf16[32,3840]{1,0:T(8,128)(2,1)S(1)} %collective-permute-done.1.refs_2_), channel_id=1, source_target_pairs={{8,0},{16,8},{24,16},{28,24},{20,28},{12,20},{4,12},{0,4},{9,1},{1... | collective-permute-start | bytes 737288 | tf_op jit(solution)/shard_map/ppermute | solution.py:335
  15.9 10.4 %collective-permute-start.5 = (bf16[32,3712]{1,0:T(8,128)(2,1)S(1)}, bf16[32,3712]{1,0:T(8,128)(2,1)S(1)}, u32[]{:S(2)}, u32[]{:S(2)}) collective-permute-start(bf16[32,3712]{1,0:T(8,128)(2,1)S(1)} %collective-permute-done.3.refs_5_), channel_id=1, source_target_pairs={{0,8},{8,16},{16,24},{24,28},{28,20},{20,12},{12,4},{4,0},{1,9},{9... | collective-permute-start | bytes 712712 | tf_op jit(solution)/shard_map/ppermute | solution.py:332
  18.0 11.0 %collective-permute-start.10 = (bf16[32,3712]{1,0:T(8,128)(2,1)S(1)}, bf16[32,3712]{1,0:T(8,128)(2,1)S(1)}, u32[]{:S(2)}, u32[]{:S(2)}) collective-permute-start(bf16[32,3712]{1,0:T(8,128)(2,1)S(1)} %collective-permute-done.4.refs_6_), channel_id=1, source_target_pairs={{8,0},{16,8},{24,16},{28,24},{20,28},{12,20},{4,12},{0,4},{9,1},{1... | collective-permute-start | bytes 712712 | tf_op jit(solution)/shard_map/ppermute | solution.py:335
  21.1 10.4 %collective-permute-start.7 = (bf16[32,3840]{1,0:T(8,128)(2,1)S(1)}, bf16[32,3840]{1,0:T(8,128)(2,1)S(1)}, u32[]{:S(2)}, u32[]{:S(2)}) collective-permute-start(bf16[32,3840]{1,0:T(8,128)(2,1)S(1)} %collective-permute-done.2.refs_3_), channel_id=1, source_target_pairs={{0,8},{8,16},{16,24},{24,28},{28,20},{20,12},{12,4},{4,0},{1,9},{9... | collective-permute-start | bytes 737288 | tf_op jit(solution)/shard_map/ppermute | solution.py:332
  23.3 10.4 %collective-permute-start.8 = (bf16[32,3840]{1,0:T(8,128)(2,1)S(1)}, bf16[32,3840]{1,0:T(8,128)(2,1)S(1)}, u32[]{:S(2)}, u32[]{:S(2)}) collective-permute-start(bf16[32,3840]{1,0:T(8,128)(2,1)S(1)} %collective-permute-done.6.refs_0_), channel_id=1, source_target_pairs={{8,0},{16,8},{24,16},{28,24},{20,28},{12,20},{4,12},{0,4},{9,1},{1... | collective-permute-start | bytes 737288 | tf_op jit(solution)/shard_map/ppermute | solution.py:335
  26.2 10.4 %collective-permute-start.11 = (bf16[32,3712]{1,0:T(8,128)(2,1)S(1)}, bf16[32,3712]{1,0:T(8,128)(2,1)S(1)}, u32[]{:S(2)}, u32[]{:S(2)}) collective-permute-start(bf16[32,3712]{1,0:T(8,128)(2,1)S(1)} %collective-permute-done.5.refs_7_), channel_id=1, source_target_pairs={{0,8},{8,16},{16,24},{24,28},{28,20},{20,12},{12,4},{4,0},{1,9},{9... | collective-permute-start | bytes 712712 | tf_op jit(solution)/shard_map/ppermute | solution.py:332
  29.0 8.2 %collective-permute-start.12 = (bf16[32,3712]{1,0:T(8,128)(2,1)S(1)}, bf16[32,3712]{1,0:T(8,128)(2,1)S(1)}, u32[]{:S(2)}, u32[]{:S(2)}) collective-permute-start(bf16[32,3712]{1,0:T(8,128)(2,1)S(1)} %collective-permute-done.10.refs_4_), channel_id=1, source_target_pairs={{8,0},{16,8},{24,16},{28,24},{20,28},{12,20},{4,12},{0,4},{9,1},{1... | collective-permute-start | bytes 712712 | tf_op jit(solution)/shard_map/ppermute | solution.py:335
  33.6 10.0 %collective-permute-start.9 = (bf16[32,3840]{1,0:T(8,128)(2,1)S(1)}, bf16[32,3840]{1,0:T(8,128)(2,1)S(1)}, u32[]{:S(2)}, u32[]{:S(2)}) collective-permute-start(bf16[32,3840]{1,0:T(8,128)(2,1)S(1)} %collective-permute-done.7.refs_1_), channel_id=1, source_target_pairs={{0,8},{8,16},{16,24},{24,28},{28,20},{20,12},{12,4},{4,0},{1,9},{9... | collective-permute-start | bytes 737288 | tf_op jit(solution)/shard_map/ppermute | solution.py:332
  37.3 6.3 %collective-permute-start.13 = (bf16[32,3712]{1,0:T(8,128)(2,1)S(1)}, bf16[32,3712]{1,0:T(8,128)(2,1)S(1)}, u32[]{:S(2)}, u32[]{:S(2)}) collective-permute-start(bf16[32,3712]{1,0:T(8,128)(2,1)S(1)} %collective-permute-done.12.refs_6_), channel_id=1, source_target_pairs={{8,0},{16,8},{24,16},{28,24},{20,28},{12,20},{4,12},{0,4},{9,1},{1... | collective-permute-start | bytes 712712 | tf_op jit(solution)/shard_map/ppermute | solution.py:335
  60.5 2.3 %collective-permute-start.14 = (s16[2,15,48,256]{3,2,1,0:T(8,128)(2,1)S(1)}, s16[2,15,48,256]{3,2,1,0:T(8,128)(2,1)S(1)}, u32[]{:S(2)}, u32[]{:S(2)}) collective-permute-start(s16[2,15,48,256]{3,2,1,0:T(8,128)(2,1)S(1)} %get-tuple-element.26), channel_id=1, source_target_pairs={{0,1},{1,0},{2,3},{3,2},{4,5},{5,4},{6,7},{7,6},{8,9},{9,8},{10,11... | collective-permute-start | bytes 2211848 | tf_op jit(solution)/shard_map/ppermute | solution.py:412
  63.6 12.2 %collective-permute-start.17 = (s16[15,48,256]{2,1,0:T(8,128)(2,1)S(1)}, s16[15,48,256]{2,1,0:T(8,128)(2,1)S(1)}, u32[]{:S(2)}, u32[]{:S(2)}) collective-permute-start(s16[15,48,256]{2,1,0:T(8,128)(2,1)S(1)} %second_send_kernel.2), channel_id=1, source_target_pairs={{0,2},{1,3},{2,0},{3,1},{4,6},{5,7},{6,4},{7,5},{8,10},{9,11},{10,... | collective-permute-start | bytes 1105928 | tf_op jit(solution)/shard_map/ppermute | solution.py:432
  74.6 5.4 %collective-permute-start.16 = (s16[15,16,256]{2,1,0:T(8,128)(2,1)S(1)}, s16[15,16,256]{2,1,0:T(8,128)(2,1)S(1)}, u32[]{:S(2)}, u32[]{:S(2)}) collective-permute-start(s16[15,16,256]{2,1,0:T(8,128)(2,1)S(1)} %second_send_kernel.3), channel_id=1, source_target_pairs={{0,2},{1,3},{2,0},{3,1},{4,6},{5,7},{6,4},{7,5},{8,10},{9,11},{10,... | collective-permute-start | bytes 368648 | tf_op jit(solution)/shard_map/ppermute | solution.py:432
  80.7 8.2 %collective-permute-start.18 = (s16[4,64,128]{2,1,0:T(8,128)(2,1)S(1)}, s16[4,64,128]{2,1,0:T(8,128)(2,1)S(1)}, u32[]{:S(2)}, u32[]{:S(2)}) collective-permute-start(s16[4,64,128]{2,1,0:T(8,128)(2,1)S(1)} %get-tuple-element.32), channel_id=1, source_target_pairs={{0,4},{8,0},{16,8},{24,16},{28,24},{20,28},{12,20},{4,12},{1,5},{9... | collective-permute-start | bytes 196616 | tf_op jit(solution)/shard_map/ppermute | solution.py:455
  82.0 7.6 %collective-permute-start.19 = (s16[4,64,128]{2,1,0:T(8,128)(2,1)S(1)}, s16[4,64,128]{2,1,0:T(8,128)(2,1)S(1)}, u32[]{:S(2)}, u32[]{:S(2)}) collective-permute-start(s16[4,64,128]{2,1,0:T(8,128)(2,1)S(1)} %get-tuple-element.33), channel_id=1, source_target_pairs={{0,8},{8,16},{16,24},{24,28},{28,20},{20,12},{12,4},{4,0},{1,9},{9... | collective-permute-start | bytes 196616 | tf_op jit(solution)/shard_map/ppermute | solution.py:455
  82.8 11.1 %collective-permute-start.20 = (s16[4,64,128]{2,1,0:T(8,128)(2,1)S(1)}, s16[4,64,128]{2,1,0:T(8,128)(2,1)S(1)}, u32[]{:S(2)}, u32[]{:S(2)}) collective-permute-start(s16[4,64,128]{2,1,0:T(8,128)(2,1)S(1)} %get-tuple-element.34), channel_id=1, source_target_pairs={{0,12},{8,4},{16,0},{24,8},{28,16},{20,24},{12,28},{4,20},{1,13},{... | collective-permute-start | bytes 196616 | tf_op jit(solution)/shard_map/ppermute | solution.py:455
  85.0 8.9 %collective-permute-start.21 = (s16[4,64,128]{2,1,0:T(8,128)(2,1)S(1)}, s16[4,64,128]{2,1,0:T(8,128)(2,1)S(1)}, u32[]{:S(2)}, u32[]{:S(2)}) collective-permute-start(s16[4,64,128]{2,1,0:T(8,128)(2,1)S(1)} %get-tuple-element.35), channel_id=1, source_target_pairs={{0,16},{8,24},{16,28},{24,20},{28,12},{20,4},{12,0},{4,8},{1,17},{... | collective-permute-start | bytes 196616 | tf_op jit(solution)/shard_map/ppermute | solution.py:455
  85.7 8.2 %collective-permute-start.22 = (s16[4,64,128]{2,1,0:T(8,128)(2,1)S(1)}, s16[4,64,128]{2,1,0:T(8,128)(2,1)S(1)}, u32[]{:S(2)}, u32[]{:S(2)}) collective-permute-start(s16[4,64,128]{2,1,0:T(8,128)(2,1)S(1)} %get-tuple-element.36), channel_id=1, source_target_pairs={{0,20},{8,12},{16,4},{24,0},{28,8},{20,16},{12,24},{4,28},{1,21},{... | collective-permute-start | bytes 196616 | tf_op jit(solution)/shard_map/ppermute | solution.py:455
  89.0 8.9 %collective-permute-start.23 = (s16[4,64,128]{2,1,0:T(8,128)(2,1)S(1)}, s16[4,64,128]{2,1,0:T(8,128)(2,1)S(1)}, u32[]{:S(2)}, u32[]{:S(2)}) collective-permute-start(s16[4,64,128]{2,1,0:T(8,128)(2,1)S(1)} %get-tuple-element.37), channel_id=1, source_target_pairs={{0,24},{8,28},{16,20},{24,12},{28,4},{20,0},{12,8},{4,16},{1,25},{... | collective-permute-start | bytes 196616 | tf_op jit(solution)/shard_map/ppermute | solution.py:455
  89.6 8.3 %collective-permute-start.24 = (s16[4,64,128]{2,1,0:T(8,128)(2,1)S(1)}, s16[4,64,128]{2,1,0:T(8,128)(2,1)S(1)}, u32[]{:S(2)}, u32[]{:S(2)}) collective-permute-start(s16[4,64,128]{2,1,0:T(8,128)(2,1)S(1)} %get-tuple-element.38), channel_id=1, source_target_pairs={{0,28},{8,20},{16,12},{24,4},{28,0},{20,8},{12,16},{4,24},{1,29},{... | collective-permute-start | bytes 196616 | tf_op jit(solution)/shard_map/ppermute | solution.py:455
  (12 other events, 160.0 us)

commit v12 on v11

--- a/solution.py
+++ b/solution.py
@@ -10,8 +10,8 @@
 NOCC = 60
 LANES = 128
 K_BLOCK = 3840
-C_BLOCK = 480
-SLOTS = 3
+C_BLOCK = 320
+SLOTS = 4
 COPIES = 4
 FIRST_PART = 47
 STEPS = 8.0
@@ -375,7 +375,7 @@
     )
     totals, sends, got = [], [], []
     for part, (cols, span, bp) in enumerate(zip(parts, spans, bps)):
-        block = min(C_BLOCK, ceil_to(cols[1] // 2, 16))
+        block = min(C_BLOCK, ceil_to(-(-cols[1] // 3), 16))
         scratch = [
             pltpu.VMEM((SLOTS, block, deep), jnp.bfloat16),
             pltpu.SemaphoreType.DMA((SLOTS, COPIES + 1)),

time: 100 us -> 99.9 us (level)
  transfers between devices with their start and end apart: 25 -> 25, of which waited for: 13 -> 13; matrix products, arithmetic and copies ran while one was open for 3% -> 3% of each run, Pallas kernels for 11% -> 10%
where the time goes in v12:
time: 99.9 us; the launch traced here: 99.6 us
  starting transfers between devices  31.9 us (32%)
  Pallas kernels  30.8 us (31%)
  waiting for transfers between devices  29.9 us (30%)
  local copies, waits for them, and re-layouts  6.83 us (7%)
    pallas_call x10, Pallas kernels, local_call(): pl.pallas_call(kernel, out_shape=out_shape, in_specs=[pl.BlockSpec(memory...  30.8 us
    ppermute x7, waiting for transfers between devices, body(): ahead = lax.ppermute(ahead, 'grid', onward)  15.8 us
    ppermute x7, starting transfers between devices, body(): ahead = lax.ppermute(ahead, 'grid', onward)  15.2 us
    ppermute x7, starting transfers between devices, body(): lax.ppermute(targets[number], 'grid', [(walk[i], walk[(i + order[number])...  13 us
    ppermute x7, waiting for transfers between devices, body(): lax.ppermute(targets[number], 'grid', [(walk[i], walk[(i + order[number])...  3.92 us
    ppermute x2, waiting for transfers between devices, body(): arrived = lax.ppermute(send, 'rep', low_pairs)  3.7 us
    ppermute x7, waiting for transfers between devices, body(): behind = lax.ppermute(behind, 'grid', back)  3.35 us
    unnamed x22, local copies, waits for them, and re-layouts  3.3 us
  transfers between devices with their start and end apart: 25, of which 13 were waited for; matrix products, arithmetic and copies ran while one was open for 3% of the time, Pallas kernels for 10%

profile of v12, /device:TPU:0, one launch (start us, length us, event | category | flops | bytes accessed | tf_op | source)
XLA Modules:
  0.0 99.6 jit_solution(3823898133123183848)
XLA Ops:
  1.0 3.1 %collective-permute-start = (bf16[32,3840]{1,0:T(8,128)(2,1)S(1)}, bf16[32,3840]{1,0:T(8,128)(2,1)S(1)}, u32[]{:S(2)}, u32[]{:S(2)}) collective-permute-start(bf16[32,3840]{1,0:T(8,128)(2,1)S(1)} %slice.9.refs_0_), channel_id=1, source_target_pairs={{0,8},{8,16},{16,24},{24,28},{28,20},{20,12},{12,4},{4,0},{1,9},{9... | collective-permute-start | bytes 737288 | tf_op jit(solution)/shard_map/ppermute | solution.py:332
  5.0 2.1 %collective-permute-start.3 = (bf16[32,3712]{1,0:T(8,128)(2,1)S(1)}, bf16[32,3712]{1,0:T(8,128)(2,1)S(1)}, u32[]{:S(2)}, u32[]{:S(2)}) collective-permute-start(bf16[32,3712]{1,0:T(8,128)(2,1)S(1)} %pad.8.refs_4_), channel_id=1, source_target_pairs={{0,8},{8,16},{16,24},{24,28},{28,20},{20,12},{12,4},{4,0},{1,9},{9... | collective-permute-start | bytes 712712 | tf_op jit(solution)/shard_map/ppermute | solution.py:332
  7.1 3.6 %collective-permute-done.refs_1_ = bf16[32,3840]{1,0:T(8,128)(2,1)S(1)} collective-permute-done((bf16[32,3840]{1,0:T(8,128)(2,1)S(1)}, bf16[32,3840]{1,0:T(8,128)(2,1)S(1)}, u32[]{:S(2)}, u32[]{:S(2)}) %collective-permute-start) | collective-permute-done | bytes 245792 | tf_op jit(solution)/shard_map/ppermute | solution.py:332
  10.8 2.1 %collective-permute-start.2 = (bf16[32,3840]{1,0:T(8,128)(2,1)S(1)}, bf16[32,3840]{1,0:T(8,128)(2,1)S(1)}, u32[]{:S(2)}, u32[]{:S(2)}) collective-permute-start(bf16[32,3840]{1,0:T(8,128)(2,1)S(1)} %collective-permute-done.refs_1_), channel_id=1, source_target_pairs={{0,8},{8,16},{16,24},{24,28},{28,20},{20,12},{12,4},{4,0},{1,9},{9... | collective-permute-start | bytes 737288 | tf_op jit(solution)/shard_map/ppermute | solution.py:332
  12.9 2.9 %collective-permute-done.3.refs_5_ = bf16[32,3712]{1,0:T(8,128)(2,1)S(1)} collective-permute-done((bf16[32,3712]{1,0:T(8,128)(2,1)S(1)}, bf16[32,3712]{1,0:T(8,128)(2,1)S(1)}, u32[]{:S(2)}, u32[]{:S(2)}) %collective-permute-start.3) | collective-permute-done | bytes 237600 | tf_op jit(solution)/shard_map/ppermute | solution.py:332
  15.9 2.1 %collective-permute-start.5 = (bf16[32,3712]{1,0:T(8,128)(2,1)S(1)}, bf16[32,3712]{1,0:T(8,128)(2,1)S(1)}, u32[]{:S(2)}, u32[]{:S(2)}) collective-permute-start(bf16[32,3712]{1,0:T(8,128)(2,1)S(1)} %collective-permute-done.3.refs_5_), channel_id=1, source_target_pairs={{0,8},{8,16},{16,24},{24,28},{28,20},{20,12},{12,4},{4,0},{1,9},{9... | collective-permute-start | bytes 712712 | tf_op jit(solution)/shard_map/ppermute | solution.py:332
  18.7 2.4 %collective-permute-done.2.refs_3_ = bf16[32,3840]{1,0:T(8,128)(2,1)S(1)} collective-permute-done((bf16[32,3840]{1,0:T(8,128)(2,1)S(1)}, bf16[32,3840]{1,0:T(8,128)(2,1)S(1)}, u32[]{:S(2)}, u32[]{:S(2)}) %collective-permute-start.2) | collective-permute-done | bytes 245792 | tf_op jit(solution)/shard_map/ppermute | solution.py:332
  21.1 2.1 %collective-permute-start.7 = (bf16[32,3840]{1,0:T(8,128)(2,1)S(1)}, bf16[32,3840]{1,0:T(8,128)(2,1)S(1)}, u32[]{:S(2)}, u32[]{:S(2)}) collective-permute-start(bf16[32,3840]{1,0:T(8,128)(2,1)S(1)} %collective-permute-done.2.refs_3_), channel_id=1, source_target_pairs={{0,8},{8,16},{16,24},{24,28},{28,20},{20,12},{12,4},{4,0},{1,9},{9... | collective-permute-start | bytes 737288 | tf_op jit(solution)/shard_map/ppermute | solution.py:332
  23.3 2.9 %collective-permute-done.5.refs_7_ = bf16[32,3712]{1,0:T(8,128)(2,1)S(1)} collective-permute-done((bf16[32,3712]{1,0:T(8,128)(2,1)S(1)}, bf16[32,3712]{1,0:T(8,128)(2,1)S(1)}, u32[]{:S(2)}, u32[]{:S(2)}) %collective-permute-start.5) | collective-permute-done | bytes 237600 | tf_op jit(solution)/shard_map/ppermute | solution.py:332
  26.2 2.1 %collective-permute-start.11 = (bf16[32,3712]{1,0:T(8,128)(2,1)S(1)}, bf16[32,3712]{1,0:T(8,128)(2,1)S(1)}, u32[]{:S(2)}, u32[]{:S(2)}) collective-permute-start(bf16[32,3712]{1,0:T(8,128)(2,1)S(1)} %collective-permute-done.5.refs_7_), channel_id=1, source_target_pairs={{0,8},{8,16},{16,24},{24,28},{28,20},{20,12},{12,4},{4,0},{1,9},{9... | collective-permute-start | bytes 712712 | tf_op jit(solution)/shard_map/ppermute | solution.py:332
  29.0 2.5 %collective-permute-done.7.refs_1_ = bf16[32,3840]{1,0:T(8,128)(2,1)S(1)} collective-permute-done((bf16[32,3840]{1,0:T(8,128)(2,1)S(1)}, bf16[32,3840]{1,0:T(8,128)(2,1)S(1)}, u32[]{:S(2)}, u32[]{:S(2)}) %collective-permute-start.7) | collective-permute-done | bytes 245792 | tf_op jit(solution)/shard_map/ppermute | solution.py:332
  31.5 2.2 %collective-permute-done.8.refs_2_ = bf16[32,3840]{1,0:T(8,128)(2,1)S(1)} collective-permute-done((bf16[32,3840]{1,0:T(8,128)(2,1)S(1)}, bf16[32,3840]{1,0:T(8,128)(2,1)S(1)}, u32[]{:S(2)}, u32[]{:S(2)}) %collective-permute-start.8) | collective-permute-done | bytes 245792 | tf_op jit(solution)/shard_map/ppermute | solution.py:335
  33.6 1.6 %collective-permute-start.9 = (bf16[32,3840]{1,0:T(8,128)(2,1)S(1)}, bf16[32,3840]{1,0:T(8,128)(2,1)S(1)}, u32[]{:S(2)}, u32[]{:S(2)}) collective-permute-start(bf16[32,3840]{1,0:T(8,128)(2,1)S(1)} %collective-permute-done.7.refs_1_), channel_id=1, source_target_pairs={{0,8},{8,16},{16,24},{24,28},{28,20},{20,12},{12,4},{4,0},{1,9},{9... | collective-permute-start | bytes 737288 | tf_op jit(solution)/shard_map/ppermute | solution.py:332
  43.6 16.7 %lead_kernel.1 = (f32[2,2880,128]{2,1,0:T(8,128)S(1)}, bf16[7552,256]{1,0:T(8,128)(2,1)S(1)}, s16[2,15,48,256]{3,2,1,0:T(8,128)(2,1)S(1)}) custom-call(s32[1]{0:T(128)} %bitcast.1.rep_ref, bf16[7552,128]{1,0:T(8,128)(2,1)S(1)} %near_kernel.1.near, bf16[32,3840]{1,0:T(8,128)(2,1)S(1)} %collective-permute-done.6.refs_0_, ...), custom_call_target="tpu_custom_call" | custom-call | flops 10950279168 | bytes 42774528 | tf_op jit(solution)/shard_map/lead_kernel/pallas_call | solution.py:270
  60.4 2.2 %collective-permute-done.14.got_ref = s16[2,15,48,256]{3,2,1,0:T(8,128)(2,1)S(1)} collective-permute-done((s16[2,15,48,256]{3,2,1,0:T(8,128)(2,1)S(1)}, s16[2,15,48,256]{3,2,1,0:T(8,128)(2,1)S(1)}, u32[]{:S(2)}, u32[]{:S(2)}) %collective-permute-start.14) | collective-permute-done | bytes 737312 | tf_op jit(solution)/shard_map/ppermute | solution.py:412
  63.4 1.6 %collective-permute-start.17 = (s16[15,48,256]{2,1,0:T(8,128)(2,1)S(1)}, s16[15,48,256]{2,1,0:T(8,128)(2,1)S(1)}, u32[]{:S(2)}, u32[]{:S(2)}) collective-permute-start(s16[15,48,256]{2,1,0:T(8,128)(2,1)S(1)} %second_send_kernel.2), channel_id=1, source_target_pairs={{0,2},{1,3},{2,0},{3,1},{4,6},{5,7},{6,4},{7,5},{8,10},{9,11},{10,... | collective-permute-start | bytes 1105928 | tf_op jit(solution)/shard_map/ppermute | solution.py:432
  65.0 6.7 %rest_kernel.1 = (f32[2,964,128]{2,1,0:T(8,128)S(1)}, s16[2,15,16,256]{3,2,1,0:T(8,128)(2,1)S(1)}) custom-call(s32[1]{0:T(128)} %bitcast.1.rep_ref, bf16[7552,256]{1,0:T(8,128)(2,1)S(1)} %get-tuple-element.27.turned, bf16[3600,7500]{1,0:T(8,128)(2,1)} %bitcast.14, bf16[3600,128]{1,0:T(8,128)(2,1)S(1)} %pad.9.refs_9_.edge_ref), custom_call_target="tpu_custom_call" | custom-call | flops 3031433216 | bytes 11841536 | tf_op jit(solution)/shard_map/rest_kernel/pallas_call | solution.py:270
  71.8 1.5 %collective-permute-done.15.got_ref = s16[2,15,16,256]{3,2,1,0:T(8,128)(2,1)S(1)} collective-permute-done((s16[2,15,16,256]{3,2,1,0:T(8,128)(2,1)S(1)}, s16[2,15,16,256]{3,2,1,0:T(8,128)(2,1)S(1)}, u32[]{:S(2)}, u32[]{:S(2)}) %collective-permute-start.15) | collective-permute-done | bytes 245792 | tf_op jit(solution)/shard_map/ppermute | solution.py:412
  76.4 3.2 %collective-permute-done.16.got_ref = s16[15,16,256]{2,1,0:T(8,128)(2,1)S(1)} collective-permute-done((s16[15,16,256]{2,1,0:T(8,128)(2,1)S(1)}, s16[15,16,256]{2,1,0:T(8,128)(2,1)S(1)}, u32[]{:S(2)}, u32[]{:S(2)}) %collective-permute-start.16) | collective-permute-done | bytes 122912 | tf_op jit(solution)/shard_map/ppermute | solution.py:432
  82.4 2.2 %collective-permute-start.20 = (s16[4,64,128]{2,1,0:T(8,128)(2,1)S(1)}, s16[4,64,128]{2,1,0:T(8,128)(2,1)S(1)}, u32[]{:S(2)}, u32[]{:S(2)}) collective-permute-start(s16[4,64,128]{2,1,0:T(8,128)(2,1)S(1)} %get-tuple-element.34), channel_id=1, source_target_pairs={{0,12},{8,4},{16,0},{24,8},{28,16},{20,24},{12,28},{4,20},{1,13},{... | collective-permute-start | bytes 196616 | tf_op jit(solution)/shard_map/ppermute | solution.py:455
  85.3 3.2 %collective-permute-start.22 = (s16[4,64,128]{2,1,0:T(8,128)(2,1)S(1)}, s16[4,64,128]{2,1,0:T(8,128)(2,1)S(1)}, u32[]{:S(2)}, u32[]{:S(2)}) collective-permute-start(s16[4,64,128]{2,1,0:T(8,128)(2,1)S(1)} %get-tuple-element.36), channel_id=1, source_target_pairs={{0,20},{8,12},{16,4},{24,0},{28,8},{20,16},{12,24},{4,28},{1,21},{... | collective-permute-start | bytes 196616 | tf_op jit(solution)/shard_map/ppermute | solution.py:455
  89.1 4.2 %collective-permute-start.24 = (s16[4,64,128]{2,1,0:T(8,128)(2,1)S(1)}, s16[4,64,128]{2,1,0:T(8,128)(2,1)S(1)}, u32[]{:S(2)}, u32[]{:S(2)}) collective-permute-start(s16[4,64,128]{2,1,0:T(8,128)(2,1)S(1)} %get-tuple-element.38), channel_id=1, source_target_pairs={{0,28},{8,20},{16,12},{24,4},{28,0},{20,8},{12,16},{4,24},{1,29},{... | collective-permute-start | bytes 196616 | tf_op jit(solution)/shard_map/ppermute | solution.py:455
  93.5 3.9 %collective-permute-done.23.refs_6_ = s16[4,64,128]{2,1,0:T(8,128)(2,1)S(1)} collective-permute-done((s16[4,64,128]{2,1,0:T(8,128)(2,1)S(1)}, s16[4,64,128]{2,1,0:T(8,128)(2,1)S(1)}, u32[]{:S(2)}, u32[]{:S(2)}) %collective-permute-start.23) | collective-permute-done | bytes 65568 | tf_op jit(solution)/shard_map/ppermute | solution.py:455
  97.5 2.2 %update_kernel.1 = f32[15,32,480]{2,1,0:T(8,128)} custom-call(s32[1]{0:T(128)} %bitcast.me_ref, f32[15]{0:T(128)S(1)} %copy-done.7, s32[15]{0:T(128)S(1)} %copy-done.8, s16[4,64,128]{2,1,0:T(8,128)(2,1)S(1)} %get-tuple-element.31.refs_0_, s16[4,64,128]{2,1,0:T(8,128)(2,1)S(1)} %collective-permute-done.18.refs_1_, ...), custom_call_target="tpu_custom_call" | custom-call | flops 10000000 | bytes 4000000 | tf_op jit(solution)/shard_map/update_kernel/pallas_call | solution.py:270
  (65 shorter events, 20.1 us)
Async XLA Ops:
  1.0 9.8 %collective-permute-start = (bf16[32,3840]{1,0:T(8,128)(2,1)S(1)}, bf16[32,3840]{1,0:T(8,128)(2,1)S(1)}, u32[]{:S(2)}, u32[]{:S(2)}) collective-permute-start(bf16[32,3840]{1,0:T(8,128)(2,1)S(1)} %slice.9.refs_0_), channel_id=1, source_target_pairs={{0,8},{8,16},{16,24},{24,28},{28,20},{20,12},{12,4},{4,0},{1,9},{9... | collective-permute-start | bytes 737288 | tf_op jit(solution)/shard_map/ppermute | solution.py:332
  4.0 8.9 %collective-permute-start.1 = (bf16[32,3840]{1,0:T(8,128)(2,1)S(1)}, bf16[32,3840]{1,0:T(8,128)(2,1)S(1)}, u32[]{:S(2)}, u32[]{:S(2)}) collective-permute-start(bf16[32,3840]{1,0:T(8,128)(2,1)S(1)} %slice.9.refs_0_), channel_id=1, source_target_pairs={{8,0},{16,8},{24,16},{28,24},{20,28},{12,20},{4,12},{0,4},{9,1},{1... | collective-permute-start | bytes 737288 | tf_op jit(solution)/shard_map/ppermute | solution.py:335
  5.0 10.8 %collective-permute-start.3 = (bf16[32,3712]{1,0:T(8,128)(2,1)S(1)}, bf16[32,3712]{1,0:T(8,128)(2,1)S(1)}, u32[]{:S(2)}, u32[]{:S(2)}) collective-permute-start(bf16[32,3712]{1,0:T(8,128)(2,1)S(1)} %pad.8.refs_4_), channel_id=1, source_target_pairs={{0,8},{8,16},{16,24},{24,28},{28,20},{20,12},{12,4},{4,0},{1,9},{9... | collective-permute-start | bytes 712712 | tf_op jit(solution)/shard_map/ppermute | solution.py:332
  7.1 10.9 %collective-permute-start.4 = (bf16[32,3712]{1,0:T(8,128)(2,1)S(1)}, bf16[32,3712]{1,0:T(8,128)(2,1)S(1)}, u32[]{:S(2)}, u32[]{:S(2)}) collective-permute-start(bf16[32,3712]{1,0:T(8,128)(2,1)S(1)} %pad.8.refs_4_), channel_id=1, source_target_pairs={{8,0},{16,8},{24,16},{28,24},{20,28},{12,20},{4,12},{0,4},{9,1},{1... | collective-permute-start | bytes 712712 | tf_op jit(solution)/shard_map/ppermute | solution.py:335
  10.8 10.4 %collective-permute-start.2 = (bf16[32,3840]{1,0:T(8,128)(2,1)S(1)}, bf16[32,3840]{1,0:T(8,128)(2,1)S(1)}, u32[]{:S(2)}, u32[]{:S(2)}) collective-permute-start(bf16[32,3840]{1,0:T(8,128)(2,1)S(1)} %collective-permute-done.refs_1_), channel_id=1, source_target_pairs={{0,8},{8,16},{16,24},{24,28},{28,20},{20,12},{12,4},{4,0},{1,9},{9... | collective-permute-start | bytes 737288 | tf_op jit(solution)/shard_map/ppermute | solution.py:332
  12.9 10.4 %collective-permute-start.6 = (bf16[32,3840]{1,0:T(8,128)(2,1)S(1)}, bf16[32,3840]{1,0:T(8,128)(2,1)S(1)}, u32[]{:S(2)}, u32[]{:S(2)}) collective-permute-start(bf16[32,3840]{1,0:T(8,128)(2,1)S(1)} %collective-permute-done.1.refs_2_), channel_id=1, source_target_pairs={{8,0},{16,8},{24,16},{28,24},{20,28},{12,20},{4,12},{0,4},{9,1},{1... | collective-permute-start | bytes 737288 | tf_op jit(solution)/shard_map/ppermute | solution.py:335
  15.9 10.4 %collective-permute-start.5 = (bf16[32,3712]{1,0:T(8,128)(2,1)S(1)}, bf16[32,3712]{1,0:T(8,128)(2,1)S(1)}, u32[]{:S(2)}, u32[]{:S(2)}) collective-permute-start(bf16[32,3712]{1,0:T(8,128)(2,1)S(1)} %collective-permute-done.3.refs_5_), channel_id=1, source_target_pairs={{0,8},{8,16},{16,24},{24,28},{28,20},{20,12},{12,4},{4,0},{1,9},{9... | collective-permute-start | bytes 712712 | tf_op jit(solution)/shard_map/ppermute | solution.py:332
  18.0 11.0 %collective-permute-start.10 = (bf16[32,3712]{1,0:T(8,128)(2,1)S(1)}, bf16[32,3712]{1,0:T(8,128)(2,1)S(1)}, u32[]{:S(2)}, u32[]{:S(2)}) collective-permute-start(bf16[32,3712]{1,0:T(8,128)(2,1)S(1)} %collective-permute-done.4.refs_6_), channel_id=1, source_target_pairs={{8,0},{16,8},{24,16},{28,24},{20,28},{12,20},{4,12},{0,4},{9,1},{1... | collective-permute-start | bytes 712712 | tf_op jit(solution)/shard_map/ppermute | solution.py:335
  21.1 10.4 %collective-permute-start.7 = (bf16[32,3840]{1,0:T(8,128)(2,1)S(1)}, bf16[32,3840]{1,0:T(8,128)(2,1)S(1)}, u32[]{:S(2)}, u32[]{:S(2)}) collective-permute-start(bf16[32,3840]{1,0:T(8,128)(2,1)S(1)} %collective-permute-done.2.refs_3_), channel_id=1, source_target_pairs={{0,8},{8,16},{16,24},{24,28},{28,20},{20,12},{12,4},{4,0},{1,9},{9... | collective-permute-start | bytes 737288 | tf_op jit(solution)/shard_map/ppermute | solution.py:332
  23.3 10.4 %collective-permute-start.8 = (bf16[32,3840]{1,0:T(8,128)(2,1)S(1)}, bf16[32,3840]{1,0:T(8,128)(2,1)S(1)}, u32[]{:S(2)}, u32[]{:S(2)}) collective-permute-start(bf16[32,3840]{1,0:T(8,128)(2,1)S(1)} %collective-permute-done.6.refs_0_), channel_id=1, source_target_pairs={{8,0},{16,8},{24,16},{28,24},{20,28},{12,20},{4,12},{0,4},{9,1},{1... | collective-permute-start | bytes 737288 | tf_op jit(solution)/shard_map/ppermute | solution.py:335
  26.2 10.4 %collective-permute-start.11 = (bf16[32,3712]{1,0:T(8,128)(2,1)S(1)}, bf16[32,3712]{1,0:T(8,128)(2,1)S(1)}, u32[]{:S(2)}, u32[]{:S(2)}) collective-permute-start(bf16[32,3712]{1,0:T(8,128)(2,1)S(1)} %collective-permute-done.5.refs_7_), channel_id=1, source_target_pairs={{0,8},{8,16},{16,24},{24,28},{28,20},{20,12},{12,4},{4,0},{1,9},{9... | collective-permute-start | bytes 712712 | tf_op jit(solution)/shard_map/ppermute | solution.py:332
  29.0 8.2 %collective-permute-start.12 = (bf16[32,3712]{1,0:T(8,128)(2,1)S(1)}, bf16[32,3712]{1,0:T(8,128)(2,1)S(1)}, u32[]{:S(2)}, u32[]{:S(2)}) collective-permute-start(bf16[32,3712]{1,0:T(8,128)(2,1)S(1)} %collective-permute-done.10.refs_4_), channel_id=1, source_target_pairs={{8,0},{16,8},{24,16},{28,24},{20,28},{12,20},{4,12},{0,4},{9,1},{1... | collective-permute-start | bytes 712712 | tf_op jit(solution)/shard_map/ppermute | solution.py:335
  33.6 10.0 %collective-permute-start.9 = (bf16[32,3840]{1,0:T(8,128)(2,1)S(1)}, bf16[32,3840]{1,0:T(8,128)(2,1)S(1)}, u32[]{:S(2)}, u32[]{:S(2)}) collective-permute-start(bf16[32,3840]{1,0:T(8,128)(2,1)S(1)} %collective-permute-done.7.refs_1_), channel_id=1, source_target_pairs={{0,8},{8,16},{16,24},{24,28},{28,20},{20,12},{12,4},{4,0},{1,9},{9... | collective-permute-start | bytes 737288 | tf_op jit(solution)/shard_map/ppermute | solution.py:332
  37.3 6.3 %collective-permute-start.13 = (bf16[32,3712]{1,0:T(8,128)(2,1)S(1)}, bf16[32,3712]{1,0:T(8,128)(2,1)S(1)}, u32[]{:S(2)}, u32[]{:S(2)}) collective-permute-start(bf16[32,3712]{1,0:T(8,128)(2,1)S(1)} %collective-permute-done.12.refs_6_), channel_id=1, source_target_pairs={{8,0},{16,8},{24,16},{28,24},{20,28},{12,20},{4,12},{0,4},{9,1},{1... | collective-permute-start | bytes 712712 | tf_op jit(solution)/shard_map/ppermute | solution.py:335
  60.3 2.3 %collective-permute-start.14 = (s16[2,15,48,256]{3,2,1,0:T(8,128)(2,1)S(1)}, s16[2,15,48,256]{3,2,1,0:T(8,128)(2,1)S(1)}, u32[]{:S(2)}, u32[]{:S(2)}) collective-permute-start(s16[2,15,48,256]{3,2,1,0:T(8,128)(2,1)S(1)} %get-tuple-element.26), channel_id=1, source_target_pairs={{0,1},{1,0},{2,3},{3,2},{4,5},{5,4},{6,7},{7,6},{8,9},{9,8},{10,11... | collective-permute-start | bytes 2211848 | tf_op jit(solution)/shard_map/ppermute | solution.py:412
  63.4 11.9 %collective-permute-start.17 = (s16[15,48,256]{2,1,0:T(8,128)(2,1)S(1)}, s16[15,48,256]{2,1,0:T(8,128)(2,1)S(1)}, u32[]{:S(2)}, u32[]{:S(2)}) collective-permute-start(s16[15,48,256]{2,1,0:T(8,128)(2,1)S(1)} %second_send_kernel.2), channel_id=1, source_target_pairs={{0,2},{1,3},{2,0},{3,1},{4,6},{5,7},{6,4},{7,5},{8,10},{9,11},{10,... | collective-permute-start | bytes 1105928 | tf_op jit(solution)/shard_map/ppermute | solution.py:432
  74.2 5.4 %collective-permute-start.16 = (s16[15,16,256]{2,1,0:T(8,128)(2,1)S(1)}, s16[15,16,256]{2,1,0:T(8,128)(2,1)S(1)}, u32[]{:S(2)}, u32[]{:S(2)}) collective-permute-start(s16[15,16,256]{2,1,0:T(8,128)(2,1)S(1)} %second_send_kernel.3), channel_id=1, source_target_pairs={{0,2},{1,3},{2,0},{3,1},{4,6},{5,7},{6,4},{7,5},{8,10},{9,11},{10,... | collective-permute-start | bytes 368648 | tf_op jit(solution)/shard_map/ppermute | solution.py:432
  80.3 8.2 %collective-permute-start.18 = (s16[4,64,128]{2,1,0:T(8,128)(2,1)S(1)}, s16[4,64,128]{2,1,0:T(8,128)(2,1)S(1)}, u32[]{:S(2)}, u32[]{:S(2)}) collective-permute-start(s16[4,64,128]{2,1,0:T(8,128)(2,1)S(1)} %get-tuple-element.32), channel_id=1, source_target_pairs={{0,4},{8,0},{16,8},{24,16},{28,24},{20,28},{12,20},{4,12},{1,5},{9... | collective-permute-start | bytes 196616 | tf_op jit(solution)/shard_map/ppermute | solution.py:455
  81.5 7.6 %collective-permute-start.19 = (s16[4,64,128]{2,1,0:T(8,128)(2,1)S(1)}, s16[4,64,128]{2,1,0:T(8,128)(2,1)S(1)}, u32[]{:S(2)}, u32[]{:S(2)}) collective-permute-start(s16[4,64,128]{2,1,0:T(8,128)(2,1)S(1)} %get-tuple-element.33), channel_id=1, source_target_pairs={{0,8},{8,16},{16,24},{24,28},{28,20},{20,12},{12,4},{4,0},{1,9},{9... | collective-permute-start | bytes 196616 | tf_op jit(solution)/shard_map/ppermute | solution.py:455
  82.4 11.1 %collective-permute-start.20 = (s16[4,64,128]{2,1,0:T(8,128)(2,1)S(1)}, s16[4,64,128]{2,1,0:T(8,128)(2,1)S(1)}, u32[]{:S(2)}, u32[]{:S(2)}) collective-permute-start(s16[4,64,128]{2,1,0:T(8,128)(2,1)S(1)} %get-tuple-element.34), channel_id=1, source_target_pairs={{0,12},{8,4},{16,0},{24,8},{28,16},{20,24},{12,28},{4,20},{1,13},{... | collective-permute-start | bytes 196616 | tf_op jit(solution)/shard_map/ppermute | solution.py:455
  84.6 8.9 %collective-permute-start.21 = (s16[4,64,128]{2,1,0:T(8,128)(2,1)S(1)}, s16[4,64,128]{2,1,0:T(8,128)(2,1)S(1)}, u32[]{:S(2)}, u32[]{:S(2)}) collective-permute-start(s16[4,64,128]{2,1,0:T(8,128)(2,1)S(1)} %get-tuple-element.35), channel_id=1, source_target_pairs={{0,16},{8,24},{16,28},{24,20},{28,12},{20,4},{12,0},{4,8},{1,17},{... | collective-permute-start | bytes 196616 | tf_op jit(solution)/shard_map/ppermute | solution.py:455
  85.3 8.2 %collective-permute-start.22 = (s16[4,64,128]{2,1,0:T(8,128)(2,1)S(1)}, s16[4,64,128]{2,1,0:T(8,128)(2,1)S(1)}, u32[]{:S(2)}, u32[]{:S(2)}) collective-permute-start(s16[4,64,128]{2,1,0:T(8,128)(2,1)S(1)} %get-tuple-element.36), channel_id=1, source_target_pairs={{0,20},{8,12},{16,4},{24,0},{28,8},{20,16},{12,24},{4,28},{1,21},{... | collective-permute-start | bytes 196616 | tf_op jit(solution)/shard_map/ppermute | solution.py:455
  88.5 8.9 %collective-permute-start.23 = (s16[4,64,128]{2,1,0:T(8,128)(2,1)S(1)}, s16[4,64,128]{2,1,0:T(8,128)(2,1)S(1)}, u32[]{:S(2)}, u32[]{:S(2)}) collective-permute-start(s16[4,64,128]{2,1,0:T(8,128)(2,1)S(1)} %get-tuple-element.37), channel_id=1, source_target_pairs={{0,24},{8,28},{16,20},{24,12},{28,4},{20,0},{12,8},{4,16},{1,25},{... | collective-permute-start | bytes 196616 | tf_op jit(solution)/shard_map/ppermute | solution.py:455
  89.1 8.3 %collective-permute-start.24 = (s16[4,64,128]{2,1,0:T(8,128)(2,1)S(1)}, s16[4,64,128]{2,1,0:T(8,128)(2,1)S(1)}, u32[]{:S(2)}, u32[]{:S(2)}) collective-permute-start(s16[4,64,128]{2,1,0:T(8,128)(2,1)S(1)} %get-tuple-element.38), channel_id=1, source_target_pairs={{0,28},{8,20},{16,12},{24,4},{28,0},{20,8},{12,16},{4,24},{1,29},{... | collective-permute-start | bytes 196616 | tf_op jit(solution)/shard_map/ppermute | solution.py:455
  (12 other events, 159.9 us)

commit v13 on v12

--- a/solution.py
+++ b/solution.py
@@ -144,8 +144,28 @@
     first_send(span, rep_ref, total, send)
 
 
-def rest_kernel(columns, span, rep_ref, turned, coupling_ref, edge_ref, total, send, buffer, sems):
+def some_kernel(columns, turned, coupling_ref, edge_ref, total, buffer, sems):
     multiply(coupling_ref, edge_ref, buffer, sems, turned, total, columns)
+
+
+def rest_kernel(columns, span, rep_ref, turned, begun, coupling_ref, edge_ref, *refs):
+    total, send, buffer, sems = refs
+    done = begun.shape[1]
+
+    def before():
+        total[:, :done, :] = begun[...]
+
+    low, many = columns
+    multiply(
+        coupling_ref,
+        edge_ref,
+        buffer,
+        sems,
+        turned,
+        total.at[:, done : done + many, :],
+        columns,
+        before,
+    )
     first_send(span, rep_ref, total, send)
 
 
@@ -374,17 +394,24 @@
         room=2 * half * deep + (2 * half * deep if slab > 2 * LANES else 0),
     )
     totals, sends, got = [], [], []
-    for part, (cols, span, bp) in enumerate(zip(parts, spans, bps)):
-        block = min(C_BLOCK, ceil_to(-(-cols[1] // 3), 16))
+    def buffers(many, steps):
+        block = min(C_BLOCK, ceil_to(-(-many // steps), 16))
         scratch = [
             pltpu.VMEM((SLOTS, block, deep), jnp.bfloat16),
             pltpu.SemaphoreType.DMA((SLOTS, COPIES + 1)),
         ]
-        cost = (2 * cols[1] * deep * slab, 2 * cols[1] * deep)
-        room = 2 * SLOTS * block * deep + (slab * deep if part == 0 else 0)
-        if slab > 2 * LANES:
-            room += 3 * slab * deep + 4 * slab * total_shapes[part].shape[1]
+        return scratch, 2 * SLOTS * block * deep
+
+    def work(many):
+        return 2 * many * deep * slab, 2 * many * deep
+
+    for part, (cols, span, bp) in enumerate(zip(parts, spans, bps)):
+        low, many = cols
         if part == 0:
+            scratch, room = buffers(many, 3)
+            room += slab * deep
+            if slab > 2 * LANES:
+                room += 3 * slab * deep + 4 * slab * total_shapes[part].shape[1]
             total, turned, send = local_call(
                 functools.partial(lead_kernel, tuple(far_edges), cols, span),
                 (
@@ -395,21 +422,39 @@
                 "sv" + "a" * (len(far) + 2),
                 (rep, near, *far, coupling, edge),
                 [*turn_scratch, *scratch],
-                cost=cost,
+                cost=work(many),
                 room=room,
             )
+            if len(parts) > 1:
+                first, other = parts[1]
+                begun_columns = other // 3 // 16 * 16
+                scratch, room = buffers(begun_columns, 2)
+                begun = local_call(
+                    functools.partial(some_kernel, (first, begun_columns)),
+                    jax.ShapeDtypeStruct((slab // LANES, begun_columns, LANES), jnp.float32),
+                    "vaa",
+                    (turned, coupling, edge),
+                    scratch,
+                    cost=work(begun_columns),
+                    room=room,
+                )
         else:
             turned, _ = lax.optimization_barrier((turned, sends[0]))
+            rest_columns = (low + begun_columns, many - begun_columns)
+            scratch, room = buffers(rest_columns[1], 3)
             total, send = local_call(
-                functools.partial(rest_kernel, cols, span),
+                functools.partial(rest_kernel, rest_columns, span),
                 (total_shapes[part], send_shapes[part]),
-                "svaa",
-                (rep, turned, coupling, edge),
+                "svvaa",
+                (rep, turned, begun, coupling, edge),
                 scratch,
-                cost=cost,
+                cost=work(rest_columns[1]),
                 room=room,
             )
+
         arrived = lax.ppermute(send, "rep", low_pairs)
+        if part == 0 and len(parts) > 1:
+            arrived, begun = lax.optimization_barrier((arrived, begun))
         totals.append(total)
         got.append(arrived)
         sends.append(

time: 99.9 us -> 99.3 us (level)
  waiting for transfers between devices: 29.9 us -> 27.6 us
  Pallas kernels: 30.8 us -> 32.3 us
    ppermute x2, waiting for transfers between devices: 3.7 us -> 1.31 us  [body(): arrived = lax.ppermute(send, 'rep', low_pairs)]
    pallas_call x10 -> x11, Pallas kernels: 30.8 us -> 32.3 us  [local_call(): pl.pallas_call(kernel, out_shape=out_shape, in_specs=[pl.BlockSpec(memory...]
  transfers between devices with their start and end apart: 25 -> 25, of which waited for: 13 -> 13; matrix products, arithmetic and copies ran while one was open for 3% -> 3% of each run, Pallas kernels for 10% -> 12%
where the time goes in v13:
time: 99.3 us; the launch traced here: 99 us
  Pallas kernels  32.3 us (33%)
  starting transfers between devices  32.1 us (32%)
  waiting for transfers between devices  27.6 us (28%)
  local copies, waits for them, and re-layouts  6.83 us (7%)
    pallas_call x11, Pallas kernels, local_call(): pl.pallas_call(kernel, out_shape=out_shape, in_specs=[pl.BlockSpec(memory...  32.3 us
    ppermute x7, waiting for transfers between devices, body(): ahead = lax.ppermute(ahead, 'grid', onward)  15.8 us
    ppermute x7, starting transfers between devices, body(): ahead = lax.ppermute(ahead, 'grid', onward)  15.2 us
    ppermute x7, starting transfers between devices, body(): lax.ppermute(targets[number], 'grid', [(walk[i], walk[(i + order[number])...  13 us
    ppermute x7, waiting for transfers between devices, body(): lax.ppermute(targets[number], 'grid', [(walk[i], walk[(i + order[number])...  3.91 us
    ppermute x7, waiting for transfers between devices, body(): behind = lax.ppermute(behind, 'grid', back)  3.35 us
    unnamed x22, local copies, waits for them, and re-layouts  3.3 us
    ppermute x2, waiting for transfers between devices, body(): got = [lax.ppermute(send, 'rep', high_pairs) for send in sends]  3.25 us
  transfers between devices with their start and end apart: 25, of which 13 were waited for; matrix products, arithmetic and copies ran while one was open for 3% of the time, Pallas kernels for 12%

profile of v13, /device:TPU:0, one launch (start us, length us, event | category | flops | bytes accessed | tf_op | source)
XLA Modules:
  0.0 99.0 jit_solution(13096684214422811490)
XLA Ops:
  1.0 3.1 %collective-permute-start = (bf16[32,3840]{1,0:T(8,128)(2,1)S(1)}, bf16[32,3840]{1,0:T(8,128)(2,1)S(1)}, u32[]{:S(2)}, u32[]{:S(2)}) collective-permute-start(bf16[32,3840]{1,0:T(8,128)(2,1)S(1)} %slice.9.refs_0_), channel_id=1, source_target_pairs={{0,8},{8,16},{16,24},{24,28},{28,20},{20,12},{12,4},{4,0},{1,9},{9... | collective-permute-start | bytes 737288 | tf_op jit(solution)/shard_map/ppermute | solution.py:352
  5.0 2.1 %collective-permute-start.3 = (bf16[32,3712]{1,0:T(8,128)(2,1)S(1)}, bf16[32,3712]{1,0:T(8,128)(2,1)S(1)}, u32[]{:S(2)}, u32[]{:S(2)}) collective-permute-start(bf16[32,3712]{1,0:T(8,128)(2,1)S(1)} %pad.8.refs_4_), channel_id=1, source_target_pairs={{0,8},{8,16},{16,24},{24,28},{28,20},{20,12},{12,4},{4,0},{1,9},{9... | collective-permute-start | bytes 712712 | tf_op jit(solution)/shard_map/ppermute | solution.py:352
  7.1 3.6 %collective-permute-done.refs_1_ = bf16[32,3840]{1,0:T(8,128)(2,1)S(1)} collective-permute-done((bf16[32,3840]{1,0:T(8,128)(2,1)S(1)}, bf16[32,3840]{1,0:T(8,128)(2,1)S(1)}, u32[]{:S(2)}, u32[]{:S(2)}) %collective-permute-start) | collective-permute-done | bytes 245792 | tf_op jit(solution)/shard_map/ppermute | solution.py:352
  10.8 2.1 %collective-permute-start.2 = (bf16[32,3840]{1,0:T(8,128)(2,1)S(1)}, bf16[32,3840]{1,0:T(8,128)(2,1)S(1)}, u32[]{:S(2)}, u32[]{:S(2)}) collective-permute-start(bf16[32,3840]{1,0:T(8,128)(2,1)S(1)} %collective-permute-done.refs_1_), channel_id=1, source_target_pairs={{0,8},{8,16},{16,24},{24,28},{28,20},{20,12},{12,4},{4,0},{1,9},{9... | collective-permute-start | bytes 737288 | tf_op jit(solution)/shard_map/ppermute | solution.py:352
  12.9 2.9 %collective-permute-done.3.refs_5_ = bf16[32,3712]{1,0:T(8,128)(2,1)S(1)} collective-permute-done((bf16[32,3712]{1,0:T(8,128)(2,1)S(1)}, bf16[32,3712]{1,0:T(8,128)(2,1)S(1)}, u32[]{:S(2)}, u32[]{:S(2)}) %collective-permute-start.3) | collective-permute-done | bytes 237600 | tf_op jit(solution)/shard_map/ppermute | solution.py:352
  15.9 2.1 %collective-permute-start.5 = (bf16[32,3712]{1,0:T(8,128)(2,1)S(1)}, bf16[32,3712]{1,0:T(8,128)(2,1)S(1)}, u32[]{:S(2)}, u32[]{:S(2)}) collective-permute-start(bf16[32,3712]{1,0:T(8,128)(2,1)S(1)} %collective-permute-done.3.refs_5_), channel_id=1, source_target_pairs={{0,8},{8,16},{16,24},{24,28},{28,20},{20,12},{12,4},{4,0},{1,9},{9... | collective-permute-start | bytes 712712 | tf_op jit(solution)/shard_map/ppermute | solution.py:352
  18.7 2.4 %collective-permute-done.2.refs_3_ = bf16[32,3840]{1,0:T(8,128)(2,1)S(1)} collective-permute-done((bf16[32,3840]{1,0:T(8,128)(2,1)S(1)}, bf16[32,3840]{1,0:T(8,128)(2,1)S(1)}, u32[]{:S(2)}, u32[]{:S(2)}) %collective-permute-start.2) | collective-permute-done | bytes 245792 | tf_op jit(solution)/shard_map/ppermute | solution.py:352
  21.1 2.1 %collective-permute-start.7 = (bf16[32,3840]{1,0:T(8,128)(2,1)S(1)}, bf16[32,3840]{1,0:T(8,128)(2,1)S(1)}, u32[]{:S(2)}, u32[]{:S(2)}) collective-permute-start(bf16[32,3840]{1,0:T(8,128)(2,1)S(1)} %collective-permute-done.2.refs_3_), channel_id=1, source_target_pairs={{0,8},{8,16},{16,24},{24,28},{28,20},{20,12},{12,4},{4,0},{1,9},{9... | collective-permute-start | bytes 737288 | tf_op jit(solution)/shard_map/ppermute | solution.py:352
  23.3 2.9 %collective-permute-done.5.refs_7_ = bf16[32,3712]{1,0:T(8,128)(2,1)S(1)} collective-permute-done((bf16[32,3712]{1,0:T(8,128)(2,1)S(1)}, bf16[32,3712]{1,0:T(8,128)(2,1)S(1)}, u32[]{:S(2)}, u32[]{:S(2)}) %collective-permute-start.5) | collective-permute-done | bytes 237600 | tf_op jit(solution)/shard_map/ppermute | solution.py:352
  26.2 2.1 %collective-permute-start.11 = (bf16[32,3712]{1,0:T(8,128)(2,1)S(1)}, bf16[32,3712]{1,0:T(8,128)(2,1)S(1)}, u32[]{:S(2)}, u32[]{:S(2)}) collective-permute-start(bf16[32,3712]{1,0:T(8,128)(2,1)S(1)} %collective-permute-done.5.refs_7_), channel_id=1, source_target_pairs={{0,8},{8,16},{16,24},{24,28},{28,20},{20,12},{12,4},{4,0},{1,9},{9... | collective-permute-start | bytes 712712 | tf_op jit(solution)/shard_map/ppermute | solution.py:352
  29.0 2.5 %collective-permute-done.7.refs_1_ = bf16[32,3840]{1,0:T(8,128)(2,1)S(1)} collective-permute-done((bf16[32,3840]{1,0:T(8,128)(2,1)S(1)}, bf16[32,3840]{1,0:T(8,128)(2,1)S(1)}, u32[]{:S(2)}, u32[]{:S(2)}) %collective-permute-start.7) | collective-permute-done | bytes 245792 | tf_op jit(solution)/shard_map/ppermute | solution.py:352
  31.5 2.2 %collective-permute-done.8.refs_2_ = bf16[32,3840]{1,0:T(8,128)(2,1)S(1)} collective-permute-done((bf16[32,3840]{1,0:T(8,128)(2,1)S(1)}, bf16[32,3840]{1,0:T(8,128)(2,1)S(1)}, u32[]{:S(2)}, u32[]{:S(2)}) %collective-permute-start.8) | collective-permute-done | bytes 245792 | tf_op jit(solution)/shard_map/ppermute | solution.py:355
  33.6 1.6 %collective-permute-start.9 = (bf16[32,3840]{1,0:T(8,128)(2,1)S(1)}, bf16[32,3840]{1,0:T(8,128)(2,1)S(1)}, u32[]{:S(2)}, u32[]{:S(2)}) collective-permute-start(bf16[32,3840]{1,0:T(8,128)(2,1)S(1)} %collective-permute-done.7.refs_1_), channel_id=1, source_target_pairs={{0,8},{8,16},{16,24},{24,28},{28,20},{20,12},{12,4},{4,0},{1,9},{9... | collective-permute-start | bytes 737288 | tf_op jit(solution)/shard_map/ppermute | solution.py:352
  37.3 1.4 %collective-permute-start.13 = (bf16[32,3712]{1,0:T(8,128)(2,1)S(1)}, bf16[32,3712]{1,0:T(8,128)(2,1)S(1)}, u32[]{:S(2)}, u32[]{:S(2)}) collective-permute-start(bf16[32,3712]{1,0:T(8,128)(2,1)S(1)} %collective-permute-done.12.refs_6_), channel_id=1, source_target_pairs={{8,0},{16,8},{24,16},{28,24},{20,28},{12,20},{4,12},{0,4},{9,1},{1... | collective-permute-start | bytes 712712 | tf_op jit(solution)/shard_map/ppermute | solution.py:355
  43.6 16.7 %lead_kernel.1 = (f32[2,2880,128]{2,1,0:T(8,128)S(1)}, bf16[7552,256]{1,0:T(8,128)(2,1)S(1)}, s16[2,15,48,256]{3,2,1,0:T(8,128)(2,1)S(1)}) custom-call(s32[1]{0:T(128)} %bitcast.1.rep_ref, bf16[7552,128]{1,0:T(8,128)(2,1)S(1)} %near_kernel.1.near, bf16[32,3840]{1,0:T(8,128)(2,1)S(1)} %collective-permute-done.6.refs_0_, ...), custom_call_target="tpu_custom_call" | custom-call | flops 10950279168 | bytes 42774528 | tf_op jit(solution)/shard_map/lead_kernel/pallas_call | solution.py:290
  60.4 3.1 %some_kernel.1.begun = f32[2,256,128]{2,1,0:T(8,128)S(1)} custom-call(bf16[7552,256]{1,0:T(8,128)(2,1)S(1)} %get-tuple-element.30.turned, bf16[3600,7500]{1,0:T(8,128)(2,1)} %bitcast.14, bf16[3600,128]{1,0:T(8,128)(2,1)S(1)} %pad.9.refs_9_.edge_ref), custom_call_target="tpu_custom_call" | custom-call | flops 989855744 | bytes 3866624 | tf_op jit(solution)/shard_map/some_kernel/pallas_call | solution.py:290
  64.3 1.6 %collective-permute-start.17 = (s16[15,48,256]{2,1,0:T(8,128)(2,1)S(1)}, s16[15,48,256]{2,1,0:T(8,128)(2,1)S(1)}, u32[]{:S(2)}, u32[]{:S(2)}) collective-permute-start(s16[15,48,256]{2,1,0:T(8,128)(2,1)S(1)} %second_send_kernel.2), channel_id=1, source_target_pairs={{0,2},{1,3},{2,0},{3,1},{4,6},{5,7},{6,4},{7,5},{8,10},{9,11},{10,... | collective-permute-start | bytes 1105928 | tf_op jit(solution)/shard_map/ppermute | solution.py:477
  65.9 5.1 %rest_kernel.1 = (f32[2,964,128]{2,1,0:T(8,128)S(1)}, s16[2,15,16,256]{3,2,1,0:T(8,128)(2,1)S(1)}) custom-call(s32[1]{0:T(128)} %bitcast.1.rep_ref, bf16[7552,256]{1,0:T(8,128)(2,1)S(1)} %get-tuple-element.30.turned, f32[2,256,128]{2,1,0:T(8,128)S(1)} %some_kernel.1.begun, bf16[3600,7500]{1,0:T(8,128)(2,1)} %bitcast.15, ...), custom_call_target="tpu_custom_call" | custom-call | flops 2041577472 | bytes 7974912 | tf_op jit(solution)/shard_map/rest_kernel/pallas_call | solution.py:290
  76.5 2.5 %collective-permute-done.16.got_ref = s16[15,16,256]{2,1,0:T(8,128)(2,1)S(1)} collective-permute-done((s16[15,16,256]{2,1,0:T(8,128)(2,1)S(1)}, s16[15,16,256]{2,1,0:T(8,128)(2,1)S(1)}, u32[]{:S(2)}, u32[]{:S(2)}) %collective-permute-start.16) | collective-permute-done | bytes 122912 | tf_op jit(solution)/shard_map/ppermute | solution.py:477
  81.8 2.2 %collective-permute-start.20 = (s16[4,64,128]{2,1,0:T(8,128)(2,1)S(1)}, s16[4,64,128]{2,1,0:T(8,128)(2,1)S(1)}, u32[]{:S(2)}, u32[]{:S(2)}) collective-permute-start(s16[4,64,128]{2,1,0:T(8,128)(2,1)S(1)} %get-tuple-element.38), channel_id=1, source_target_pairs={{0,12},{8,4},{16,0},{24,8},{28,16},{20,24},{12,28},{4,20},{1,13},{... | collective-permute-start | bytes 196616 | tf_op jit(solution)/shard_map/ppermute | solution.py:500
  84.7 3.2 %collective-permute-start.22 = (s16[4,64,128]{2,1,0:T(8,128)(2,1)S(1)}, s16[4,64,128]{2,1,0:T(8,128)(2,1)S(1)}, u32[]{:S(2)}, u32[]{:S(2)}) collective-permute-start(s16[4,64,128]{2,1,0:T(8,128)(2,1)S(1)} %get-tuple-element.40), channel_id=1, source_target_pairs={{0,20},{8,12},{16,4},{24,0},{28,8},{20,16},{12,24},{4,28},{1,21},{... | collective-permute-start | bytes 196616 | tf_op jit(solution)/shard_map/ppermute | solution.py:500
  88.5 4.2 %collective-permute-start.24 = (s16[4,64,128]{2,1,0:T(8,128)(2,1)S(1)}, s16[4,64,128]{2,1,0:T(8,128)(2,1)S(1)}, u32[]{:S(2)}, u32[]{:S(2)}) collective-permute-start(s16[4,64,128]{2,1,0:T(8,128)(2,1)S(1)} %get-tuple-element.42), channel_id=1, source_target_pairs={{0,28},{8,20},{16,12},{24,4},{28,0},{20,8},{12,16},{4,24},{1,29},{... | collective-permute-start | bytes 196616 | tf_op jit(solution)/shard_map/ppermute | solution.py:500
  92.9 3.9 %collective-permute-done.23.refs_6_ = s16[4,64,128]{2,1,0:T(8,128)(2,1)S(1)} collective-permute-done((s16[4,64,128]{2,1,0:T(8,128)(2,1)S(1)}, s16[4,64,128]{2,1,0:T(8,128)(2,1)S(1)}, u32[]{:S(2)}, u32[]{:S(2)}) %collective-permute-start.23) | collective-permute-done | bytes 65568 | tf_op jit(solution)/shard_map/ppermute | solution.py:500
  96.8 2.2 %update_kernel.1 = f32[15,32,480]{2,1,0:T(8,128)} custom-call(s32[1]{0:T(128)} %bitcast.me_ref, f32[15]{0:T(128)S(1)} %copy-done.7, s32[15]{0:T(128)S(1)} %copy-done.8, s16[4,64,128]{2,1,0:T(8,128)(2,1)S(1)} %get-tuple-element.35.refs_0_, s16[4,64,128]{2,1,0:T(8,128)(2,1)S(1)} %collective-permute-done.18.refs_1_, ...), custom_call_target="tpu_custom_call" | custom-call | flops 10000000 | bytes 4000000 | tf_op jit(solution)/shard_map/update_kernel/pallas_call | solution.py:290
  (66 shorter events, 21.0 us)
Async XLA Ops:
  1.0 9.8 %collective-permute-start = (bf16[32,3840]{1,0:T(8,128)(2,1)S(1)}, bf16[32,3840]{1,0:T(8,128)(2,1)S(1)}, u32[]{:S(2)}, u32[]{:S(2)}) collective-permute-start(bf16[32,3840]{1,0:T(8,128)(2,1)S(1)} %slice.9.refs_0_), channel_id=1, source_target_pairs={{0,8},{8,16},{16,24},{24,28},{28,20},{20,12},{12,4},{4,0},{1,9},{9... | collective-permute-start | bytes 737288 | tf_op jit(solution)/shard_map/ppermute | solution.py:352
  4.0 8.9 %collective-permute-start.1 = (bf16[32,3840]{1,0:T(8,128)(2,1)S(1)}, bf16[32,3840]{1,0:T(8,128)(2,1)S(1)}, u32[]{:S(2)}, u32[]{:S(2)}) collective-permute-start(bf16[32,3840]{1,0:T(8,128)(2,1)S(1)} %slice.9.refs_0_), channel_id=1, source_target_pairs={{8,0},{16,8},{24,16},{28,24},{20,28},{12,20},{4,12},{0,4},{9,1},{1... | collective-permute-start | bytes 737288 | tf_op jit(solution)/shard_map/ppermute | solution.py:355
  5.0 10.8 %collective-permute-start.3 = (bf16[32,3712]{1,0:T(8,128)(2,1)S(1)}, bf16[32,3712]{1,0:T(8,128)(2,1)S(1)}, u32[]{:S(2)}, u32[]{:S(2)}) collective-permute-start(bf16[32,3712]{1,0:T(8,128)(2,1)S(1)} %pad.8.refs_4_), channel_id=1, source_target_pairs={{0,8},{8,16},{16,24},{24,28},{28,20},{20,12},{12,4},{4,0},{1,9},{9... | collective-permute-start | bytes 712712 | tf_op jit(solution)/shard_map/ppermute | solution.py:352
  7.1 10.9 %collective-permute-start.4 = (bf16[32,3712]{1,0:T(8,128)(2,1)S(1)}, bf16[32,3712]{1,0:T(8,128)(2,1)S(1)}, u32[]{:S(2)}, u32[]{:S(2)}) collective-permute-start(bf16[32,3712]{1,0:T(8,128)(2,1)S(1)} %pad.8.refs_4_), channel_id=1, source_target_pairs={{8,0},{16,8},{24,16},{28,24},{20,28},{12,20},{4,12},{0,4},{9,1},{1... | collective-permute-start | bytes 712712 | tf_op jit(solution)/shard_map/ppermute | solution.py:355
  10.8 10.4 %collective-permute-start.2 = (bf16[32,3840]{1,0:T(8,128)(2,1)S(1)}, bf16[32,3840]{1,0:T(8,128)(2,1)S(1)}, u32[]{:S(2)}, u32[]{:S(2)}) collective-permute-start(bf16[32,3840]{1,0:T(8,128)(2,1)S(1)} %collective-permute-done.refs_1_), channel_id=1, source_target_pairs={{0,8},{8,16},{16,24},{24,28},{28,20},{20,12},{12,4},{4,0},{1,9},{9... | collective-permute-start | bytes 737288 | tf_op jit(solution)/shard_map/ppermute | solution.py:352
  12.9 10.4 %collective-permute-start.6 = (bf16[32,3840]{1,0:T(8,128)(2,1)S(1)}, bf16[32,3840]{1,0:T(8,128)(2,1)S(1)}, u32[]{:S(2)}, u32[]{:S(2)}) collective-permute-start(bf16[32,3840]{1,0:T(8,128)(2,1)S(1)} %collective-permute-done.1.refs_2_), channel_id=1, source_target_pairs={{8,0},{16,8},{24,16},{28,24},{20,28},{12,20},{4,12},{0,4},{9,1},{1... | collective-permute-start | bytes 737288 | tf_op jit(solution)/shard_map/ppermute | solution.py:355
  15.9 10.4 %collective-permute-start.5 = (bf16[32,3712]{1,0:T(8,128)(2,1)S(1)}, bf16[32,3712]{1,0:T(8,128)(2,1)S(1)}, u32[]{:S(2)}, u32[]{:S(2)}) collective-permute-start(bf16[32,3712]{1,0:T(8,128)(2,1)S(1)} %collective-permute-done.3.refs_5_), channel_id=1, source_target_pairs={{0,8},{8,16},{16,24},{24,28},{28,20},{20,12},{12,4},{4,0},{1,9},{9... | collective-permute-start | bytes 712712 | tf_op jit(solution)/shard_map/ppermute | solution.py:352
  18.0 11.0 %collective-permute-start.10 = (bf16[32,3712]{1,0:T(8,128)(2,1)S(1)}, bf16[32,3712]{1,0:T(8,128)(2,1)S(1)}, u32[]{:S(2)}, u32[]{:S(2)}) collective-permute-start(bf16[32,3712]{1,0:T(8,128)(2,1)S(1)} %collective-permute-done.4.refs_6_), channel_id=1, source_target_pairs={{8,0},{16,8},{24,16},{28,24},{20,28},{12,20},{4,12},{0,4},{9,1},{1... | collective-permute-start | bytes 712712 | tf_op jit(solution)/shard_map/ppermute | solution.py:355
  21.1 10.4 %collective-permute-start.7 = (bf16[32,3840]{1,0:T(8,128)(2,1)S(1)}, bf16[32,3840]{1,0:T(8,128)(2,1)S(1)}, u32[]{:S(2)}, u32[]{:S(2)}) collective-permute-start(bf16[32,3840]{1,0:T(8,128)(2,1)S(1)} %collective-permute-done.2.refs_3_), channel_id=1, source_target_pairs={{0,8},{8,16},{16,24},{24,28},{28,20},{20,12},{12,4},{4,0},{1,9},{9... | collective-permute-start | bytes 737288 | tf_op jit(solution)/shard_map/ppermute | solution.py:352
  23.3 10.4 %collective-permute-start.8 = (bf16[32,3840]{1,0:T(8,128)(2,1)S(1)}, bf16[32,3840]{1,0:T(8,128)(2,1)S(1)}, u32[]{:S(2)}, u32[]{:S(2)}) collective-permute-start(bf16[32,3840]{1,0:T(8,128)(2,1)S(1)} %collective-permute-done.6.refs_0_), channel_id=1, source_target_pairs={{8,0},{16,8},{24,16},{28,24},{20,28},{12,20},{4,12},{0,4},{9,1},{1... | collective-permute-start | bytes 737288 | tf_op jit(solution)/shard_map/ppermute | solution.py:355
  26.2 10.4 %collective-permute-start.11 = (bf16[32,3712]{1,0:T(8,128)(2,1)S(1)}, bf16[32,3712]{1,0:T(8,128)(2,1)S(1)}, u32[]{:S(2)}, u32[]{:S(2)}) collective-permute-start(bf16[32,3712]{1,0:T(8,128)(2,1)S(1)} %collective-permute-done.5.refs_7_), channel_id=1, source_target_pairs={{0,8},{8,16},{16,24},{24,28},{28,20},{20,12},{12,4},{4,0},{1,9},{9... | collective-permute-start | bytes 712712 | tf_op jit(solution)/shard_map/ppermute | solution.py:352
  29.0 8.2 %collective-permute-start.12 = (bf16[32,3712]{1,0:T(8,128)(2,1)S(1)}, bf16[32,3712]{1,0:T(8,128)(2,1)S(1)}, u32[]{:S(2)}, u32[]{:S(2)}) collective-permute-start(bf16[32,3712]{1,0:T(8,128)(2,1)S(1)} %collective-permute-done.10.refs_4_), channel_id=1, source_target_pairs={{8,0},{16,8},{24,16},{28,24},{20,28},{12,20},{4,12},{0,4},{9,1},{1... | collective-permute-start | bytes 712712 | tf_op jit(solution)/shard_map/ppermute | solution.py:355
  33.6 10.0 %collective-permute-start.9 = (bf16[32,3840]{1,0:T(8,128)(2,1)S(1)}, bf16[32,3840]{1,0:T(8,128)(2,1)S(1)}, u32[]{:S(2)}, u32[]{:S(2)}) collective-permute-start(bf16[32,3840]{1,0:T(8,128)(2,1)S(1)} %collective-permute-done.7.refs_1_), channel_id=1, source_target_pairs={{0,8},{8,16},{16,24},{24,28},{28,20},{20,12},{12,4},{4,0},{1,9},{9... | collective-permute-start | bytes 737288 | tf_op jit(solution)/shard_map/ppermute | solution.py:352
  37.3 6.3 %collective-permute-start.13 = (bf16[32,3712]{1,0:T(8,128)(2,1)S(1)}, bf16[32,3712]{1,0:T(8,128)(2,1)S(1)}, u32[]{:S(2)}, u32[]{:S(2)}) collective-permute-start(bf16[32,3712]{1,0:T(8,128)(2,1)S(1)} %collective-permute-done.12.refs_6_), channel_id=1, source_target_pairs={{8,0},{16,8},{24,16},{28,24},{20,28},{12,20},{4,12},{0,4},{9,1},{1... | collective-permute-start | bytes 712712 | tf_op jit(solution)/shard_map/ppermute | solution.py:355
  60.3 3.2 %collective-permute-start.14 = (s16[2,15,48,256]{3,2,1,0:T(8,128)(2,1)S(1)}, s16[2,15,48,256]{3,2,1,0:T(8,128)(2,1)S(1)}, u32[]{:S(2)}, u32[]{:S(2)}) collective-permute-start(s16[2,15,48,256]{3,2,1,0:T(8,128)(2,1)S(1)} %get-tuple-element.28), channel_id=1, source_target_pairs={{0,1},{1,0},{2,3},{3,2},{4,5},{5,4},{6,7},{7,6},{8,9},{9,8},{10,11... | collective-permute-start | bytes 2211848 | tf_op jit(solution)/shard_map/ppermute | solution.py:455
  64.3 11.1 %collective-permute-start.17 = (s16[15,48,256]{2,1,0:T(8,128)(2,1)S(1)}, s16[15,48,256]{2,1,0:T(8,128)(2,1)S(1)}, u32[]{:S(2)}, u32[]{:S(2)}) collective-permute-start(s16[15,48,256]{2,1,0:T(8,128)(2,1)S(1)} %second_send_kernel.2), channel_id=1, source_target_pairs={{0,2},{1,3},{2,0},{3,1},{4,6},{5,7},{6,4},{7,5},{8,10},{9,11},{10,... | collective-permute-start | bytes 1105928 | tf_op jit(solution)/shard_map/ppermute | solution.py:477
  73.5 5.5 %collective-permute-start.16 = (s16[15,16,256]{2,1,0:T(8,128)(2,1)S(1)}, s16[15,16,256]{2,1,0:T(8,128)(2,1)S(1)}, u32[]{:S(2)}, u32[]{:S(2)}) collective-permute-start(s16[15,16,256]{2,1,0:T(8,128)(2,1)S(1)} %second_send_kernel.3), channel_id=1, source_target_pairs={{0,2},{1,3},{2,0},{3,1},{4,6},{5,7},{6,4},{7,5},{8,10},{9,11},{10,... | collective-permute-start | bytes 368648 | tf_op jit(solution)/shard_map/ppermute | solution.py:477
  79.7 8.2 %collective-permute-start.18 = (s16[4,64,128]{2,1,0:T(8,128)(2,1)S(1)}, s16[4,64,128]{2,1,0:T(8,128)(2,1)S(1)}, u32[]{:S(2)}, u32[]{:S(2)}) collective-permute-start(s16[4,64,128]{2,1,0:T(8,128)(2,1)S(1)} %get-tuple-element.36), channel_id=1, source_target_pairs={{0,4},{8,0},{16,8},{24,16},{28,24},{20,28},{12,20},{4,12},{1,5},{9... | collective-permute-start | bytes 196616 | tf_op jit(solution)/shard_map/ppermute | solution.py:500
  81.0 7.6 %collective-permute-start.19 = (s16[4,64,128]{2,1,0:T(8,128)(2,1)S(1)}, s16[4,64,128]{2,1,0:T(8,128)(2,1)S(1)}, u32[]{:S(2)}, u32[]{:S(2)}) collective-permute-start(s16[4,64,128]{2,1,0:T(8,128)(2,1)S(1)} %get-tuple-element.37), channel_id=1, source_target_pairs={{0,8},{8,16},{16,24},{24,28},{28,20},{20,12},{12,4},{4,0},{1,9},{9... | collective-permute-start | bytes 196616 | tf_op jit(solution)/shard_map/ppermute | solution.py:500
  81.8 11.1 %collective-permute-start.20 = (s16[4,64,128]{2,1,0:T(8,128)(2,1)S(1)}, s16[4,64,128]{2,1,0:T(8,128)(2,1)S(1)}, u32[]{:S(2)}, u32[]{:S(2)}) collective-permute-start(s16[4,64,128]{2,1,0:T(8,128)(2,1)S(1)} %get-tuple-element.38), channel_id=1, source_target_pairs={{0,12},{8,4},{16,0},{24,8},{28,16},{20,24},{12,28},{4,20},{1,13},{... | collective-permute-start | bytes 196616 | tf_op jit(solution)/shard_map/ppermute | solution.py:500
  84.0 8.9 %collective-permute-start.21 = (s16[4,64,128]{2,1,0:T(8,128)(2,1)S(1)}, s16[4,64,128]{2,1,0:T(8,128)(2,1)S(1)}, u32[]{:S(2)}, u32[]{:S(2)}) collective-permute-start(s16[4,64,128]{2,1,0:T(8,128)(2,1)S(1)} %get-tuple-element.39), channel_id=1, source_target_pairs={{0,16},{8,24},{16,28},{24,20},{28,12},{20,4},{12,0},{4,8},{1,17},{... | collective-permute-start | bytes 196616 | tf_op jit(solution)/shard_map/ppermute | solution.py:500
  84.7 8.2 %collective-permute-start.22 = (s16[4,64,128]{2,1,0:T(8,128)(2,1)S(1)}, s16[4,64,128]{2,1,0:T(8,128)(2,1)S(1)}, u32[]{:S(2)}, u32[]{:S(2)}) collective-permute-start(s16[4,64,128]{2,1,0:T(8,128)(2,1)S(1)} %get-tuple-element.40), channel_id=1, source_target_pairs={{0,20},{8,12},{16,4},{24,0},{28,8},{20,16},{12,24},{4,28},{1,21},{... | collective-permute-start | bytes 196616 | tf_op jit(solution)/shard_map/ppermute | solution.py:500
  87.9 8.9 %collective-permute-start.23 = (s16[4,64,128]{2,1,0:T(8,128)(2,1)S(1)}, s16[4,64,128]{2,1,0:T(8,128)(2,1)S(1)}, u32[]{:S(2)}, u32[]{:S(2)}) collective-permute-start(s16[4,64,128]{2,1,0:T(8,128)(2,1)S(1)} %get-tuple-element.41), channel_id=1, source_target_pairs={{0,24},{8,28},{16,20},{24,12},{28,4},{20,0},{12,8},{4,16},{1,25},{... | collective-permute-start | bytes 196616 | tf_op jit(solution)/shard_map/ppermute | solution.py:500
  88.5 8.3 %collective-permute-start.24 = (s16[4,64,128]{2,1,0:T(8,128)(2,1)S(1)}, s16[4,64,128]{2,1,0:T(8,128)(2,1)S(1)}, u32[]{:S(2)}, u32[]{:S(2)}) collective-permute-start(s16[4,64,128]{2,1,0:T(8,128)(2,1)S(1)} %get-tuple-element.42), channel_id=1, source_target_pairs={{0,28},{8,20},{16,12},{24,4},{28,0},{20,8},{12,16},{4,24},{1,29},{... | collective-permute-start | bytes 196616 | tf_op jit(solution)/shard_map/ppermute | solution.py:500
  (12 other events, 160.4 us)

commit v14 on v13

--- a/solution.py
+++ b/solution.py
@@ -427,8 +427,8 @@
             )
             if len(parts) > 1:
                 first, other = parts[1]
-                begun_columns = other // 3 // 16 * 16
-                scratch, room = buffers(begun_columns, 2)
+                begun_columns = other * 9 // 40 // 16 * 16
+                scratch, room = buffers(begun_columns, 1)
                 begun = local_call(
                     functools.partial(some_kernel, (first, begun_columns)),
                     jax.ShapeDtypeStruct((slab // LANES, begun_columns, LANES), jnp.float32),

time: 99.3 us -> 99.5 us (level)
  no operation moved by 1% of the time
where the time goes in v14:
time: 99.5 us; the launch traced here: 99.3 us
  Pallas kernels  32.5 us (33%)
  starting transfers between devices  32.1 us (32%)
  waiting for transfers between devices  27.6 us (28%)
  local copies, waits for them, and re-layouts  6.83 us (7%)
    pallas_call x11, Pallas kernels, local_call(): pl.pallas_call(kernel, out_shape=out_shape, in_specs=[pl.BlockSpec(memory...  32.5 us
    ppermute x7, waiting for transfers between devices, body(): ahead = lax.ppermute(ahead, 'grid', onward)  15.8 us
    ppermute x7, starting transfers between devices, body(): ahead = lax.ppermute(ahead, 'grid', onward)  15.2 us
    ppermute x7, starting transfers between devices, body(): lax.ppermute(targets[number], 'grid', [(walk[i], walk[(i + order[number])...  13 us
    ppermute x7, waiting for transfers between devices, body(): lax.ppermute(targets[number], 'grid', [(walk[i], walk[(i + order[number])...  3.92 us
    ppermute x7, waiting for transfers between devices, body(): behind = lax.ppermute(behind, 'grid', back)  3.35 us
    unnamed x22, local copies, waits for them, and re-layouts  3.3 us
    ppermute x2, waiting for transfers between devices, body(): got = [lax.ppermute(send, 'rep', high_pairs) for send in sends]  3.25 us
  transfers between devices with their start and end apart: 25, of which 13 were waited for; matrix products, arithmetic and copies ran while one was open for 3% of the time, Pallas kernels for 12%

profile of v14, /device:TPU:0, one launch (start us, length us, event | category | flops | bytes accessed | tf_op | source)
XLA Modules:
  0.0 99.3 jit_solution(5004183920372752214)
XLA Ops:
  1.0 3.1 %collective-permute-start = (bf16[32,3840]{1,0:T(8,128)(2,1)S(1)}, bf16[32,3840]{1,0:T(8,128)(2,1)S(1)}, u32[]{:S(2)}, u32[]{:S(2)}) collective-permute-start(bf16[32,3840]{1,0:T(8,128)(2,1)S(1)} %slice.9.refs_0_), channel_id=1, source_target_pairs={{0,8},{8,16},{16,24},{24,28},{28,20},{20,12},{12,4},{4,0},{1,9},{9... | collective-permute-start | bytes 737288 | tf_op jit(solution)/shard_map/ppermute | solution.py:352
  5.0 2.1 %collective-permute-start.3 = (bf16[32,3712]{1,0:T(8,128)(2,1)S(1)}, bf16[32,3712]{1,0:T(8,128)(2,1)S(1)}, u32[]{:S(2)}, u32[]{:S(2)}) collective-permute-start(bf16[32,3712]{1,0:T(8,128)(2,1)S(1)} %pad.8.refs_4_), channel_id=1, source_target_pairs={{0,8},{8,16},{16,24},{24,28},{28,20},{20,12},{12,4},{4,0},{1,9},{9... | collective-permute-start | bytes 712712 | tf_op jit(solution)/shard_map/ppermute | solution.py:352
  7.1 3.6 %collective-permute-done.refs_1_ = bf16[32,3840]{1,0:T(8,128)(2,1)S(1)} collective-permute-done((bf16[32,3840]{1,0:T(8,128)(2,1)S(1)}, bf16[32,3840]{1,0:T(8,128)(2,1)S(1)}, u32[]{:S(2)}, u32[]{:S(2)}) %collective-permute-start) | collective-permute-done | bytes 245792 | tf_op jit(solution)/shard_map/ppermute | solution.py:352
  10.8 2.1 %collective-permute-start.2 = (bf16[32,3840]{1,0:T(8,128)(2,1)S(1)}, bf16[32,3840]{1,0:T(8,128)(2,1)S(1)}, u32[]{:S(2)}, u32[]{:S(2)}) collective-permute-start(bf16[32,3840]{1,0:T(8,128)(2,1)S(1)} %collective-permute-done.refs_1_), channel_id=1, source_target_pairs={{0,8},{8,16},{16,24},{24,28},{28,20},{20,12},{12,4},{4,0},{1,9},{9... | collective-permute-start | bytes 737288 | tf_op jit(solution)/shard_map/ppermute | solution.py:352
  12.9 2.9 %collective-permute-done.3.refs_5_ = bf16[32,3712]{1,0:T(8,128)(2,1)S(1)} collective-permute-done((bf16[32,3712]{1,0:T(8,128)(2,1)S(1)}, bf16[32,3712]{1,0:T(8,128)(2,1)S(1)}, u32[]{:S(2)}, u32[]{:S(2)}) %collective-permute-start.3) | collective-permute-done | bytes 237600 | tf_op jit(solution)/shard_map/ppermute | solution.py:352
  15.9 2.1 %collective-permute-start.5 = (bf16[32,3712]{1,0:T(8,128)(2,1)S(1)}, bf16[32,3712]{1,0:T(8,128)(2,1)S(1)}, u32[]{:S(2)}, u32[]{:S(2)}) collective-permute-start(bf16[32,3712]{1,0:T(8,128)(2,1)S(1)} %collective-permute-done.3.refs_5_), channel_id=1, source_target_pairs={{0,8},{8,16},{16,24},{24,28},{28,20},{20,12},{12,4},{4,0},{1,9},{9... | collective-permute-start | bytes 712712 | tf_op jit(solution)/shard_map/ppermute | solution.py:352
  18.7 2.4 %collective-permute-done.2.refs_3_ = bf16[32,3840]{1,0:T(8,128)(2,1)S(1)} collective-permute-done((bf16[32,3840]{1,0:T(8,128)(2,1)S(1)}, bf16[32,3840]{1,0:T(8,128)(2,1)S(1)}, u32[]{:S(2)}, u32[]{:S(2)}) %collective-permute-start.2) | collective-permute-done | bytes 245792 | tf_op jit(solution)/shard_map/ppermute | solution.py:352
  21.1 2.1 %collective-permute-start.7 = (bf16[32,3840]{1,0:T(8,128)(2,1)S(1)}, bf16[32,3840]{1,0:T(8,128)(2,1)S(1)}, u32[]{:S(2)}, u32[]{:S(2)}) collective-permute-start(bf16[32,3840]{1,0:T(8,128)(2,1)S(1)} %collective-permute-done.2.refs_3_), channel_id=1, source_target_pairs={{0,8},{8,16},{16,24},{24,28},{28,20},{20,12},{12,4},{4,0},{1,9},{9... | collective-permute-start | bytes 737288 | tf_op jit(solution)/shard_map/ppermute | solution.py:352
  23.3 2.9 %collective-permute-done.5.refs_7_ = bf16[32,3712]{1,0:T(8,128)(2,1)S(1)} collective-permute-done((bf16[32,3712]{1,0:T(8,128)(2,1)S(1)}, bf16[32,3712]{1,0:T(8,128)(2,1)S(1)}, u32[]{:S(2)}, u32[]{:S(2)}) %collective-permute-start.5) | collective-permute-done | bytes 237600 | tf_op jit(solution)/shard_map/ppermute | solution.py:352
  26.2 2.1 %collective-permute-start.11 = (bf16[32,3712]{1,0:T(8,128)(2,1)S(1)}, bf16[32,3712]{1,0:T(8,128)(2,1)S(1)}, u32[]{:S(2)}, u32[]{:S(2)}) collective-permute-start(bf16[32,3712]{1,0:T(8,128)(2,1)S(1)} %collective-permute-done.5.refs_7_), channel_id=1, source_target_pairs={{0,8},{8,16},{16,24},{24,28},{28,20},{20,12},{12,4},{4,0},{1,9},{9... | collective-permute-start | bytes 712712 | tf_op jit(solution)/shard_map/ppermute | solution.py:352
  29.0 2.5 %collective-permute-done.7.refs_1_ = bf16[32,3840]{1,0:T(8,128)(2,1)S(1)} collective-permute-done((bf16[32,3840]{1,0:T(8,128)(2,1)S(1)}, bf16[32,3840]{1,0:T(8,128)(2,1)S(1)}, u32[]{:S(2)}, u32[]{:S(2)}) %collective-permute-start.7) | collective-permute-done | bytes 245792 | tf_op jit(solution)/shard_map/ppermute | solution.py:352
  31.5 2.2 %collective-permute-done.8.refs_2_ = bf16[32,3840]{1,0:T(8,128)(2,1)S(1)} collective-permute-done((bf16[32,3840]{1,0:T(8,128)(2,1)S(1)}, bf16[32,3840]{1,0:T(8,128)(2,1)S(1)}, u32[]{:S(2)}, u32[]{:S(2)}) %collective-permute-start.8) | collective-permute-done | bytes 245792 | tf_op jit(solution)/shard_map/ppermute | solution.py:355
  33.6 1.6 %collective-permute-start.9 = (bf16[32,3840]{1,0:T(8,128)(2,1)S(1)}, bf16[32,3840]{1,0:T(8,128)(2,1)S(1)}, u32[]{:S(2)}, u32[]{:S(2)}) collective-permute-start(bf16[32,3840]{1,0:T(8,128)(2,1)S(1)} %collective-permute-done.7.refs_1_), channel_id=1, source_target_pairs={{0,8},{8,16},{16,24},{24,28},{28,20},{20,12},{12,4},{4,0},{1,9},{9... | collective-permute-start | bytes 737288 | tf_op jit(solution)/shard_map/ppermute | solution.py:352
  37.3 1.4 %collective-permute-start.13 = (bf16[32,3712]{1,0:T(8,128)(2,1)S(1)}, bf16[32,3712]{1,0:T(8,128)(2,1)S(1)}, u32[]{:S(2)}, u32[]{:S(2)}) collective-permute-start(bf16[32,3712]{1,0:T(8,128)(2,1)S(1)} %collective-permute-done.12.refs_6_), channel_id=1, source_target_pairs={{8,0},{16,8},{24,16},{28,24},{20,28},{12,20},{4,12},{0,4},{9,1},{1... | collective-permute-start | bytes 712712 | tf_op jit(solution)/shard_map/ppermute | solution.py:355
  43.6 16.7 %lead_kernel.1 = (f32[2,2880,128]{2,1,0:T(8,128)S(1)}, bf16[7552,256]{1,0:T(8,128)(2,1)S(1)}, s16[2,15,48,256]{3,2,1,0:T(8,128)(2,1)S(1)}) custom-call(s32[1]{0:T(128)} %bitcast.1.rep_ref, bf16[7552,128]{1,0:T(8,128)(2,1)S(1)} %near_kernel.1.near, bf16[32,3840]{1,0:T(8,128)(2,1)S(1)} %collective-permute-done.6.refs_0_, ...), custom_call_target="tpu_custom_call" | custom-call | flops 10950279168 | bytes 42774528 | tf_op jit(solution)/shard_map/lead_kernel/pallas_call | solution.py:290
  60.4 2.7 %some_kernel.1.begun = f32[2,176,128]{2,1,0:T(8,128)S(1)} custom-call(bf16[7552,256]{1,0:T(8,128)(2,1)S(1)} %get-tuple-element.30.turned, bf16[3600,7500]{1,0:T(8,128)(2,1)} %bitcast.14, bf16[3600,128]{1,0:T(8,128)(2,1)S(1)} %pad.9.refs_9_.edge_ref), custom_call_target="tpu_custom_call" | custom-call | flops 680525824 | bytes 2658304 | tf_op jit(solution)/shard_map/some_kernel/pallas_call | solution.py:290
  64.0 1.6 %collective-permute-start.17 = (s16[15,48,256]{2,1,0:T(8,128)(2,1)S(1)}, s16[15,48,256]{2,1,0:T(8,128)(2,1)S(1)}, u32[]{:S(2)}, u32[]{:S(2)}) collective-permute-start(s16[15,48,256]{2,1,0:T(8,128)(2,1)S(1)} %second_send_kernel.2), channel_id=1, source_target_pairs={{0,2},{1,3},{2,0},{3,1},{4,6},{5,7},{6,4},{7,5},{8,10},{9,11},{10,... | collective-permute-start | bytes 1105928 | tf_op jit(solution)/shard_map/ppermute | solution.py:477
  65.6 5.7 %rest_kernel.1 = (f32[2,964,128]{2,1,0:T(8,128)S(1)}, s16[2,15,16,256]{3,2,1,0:T(8,128)(2,1)S(1)}) custom-call(s32[1]{0:T(128)} %bitcast.1.rep_ref, bf16[7552,256]{1,0:T(8,128)(2,1)S(1)} %get-tuple-element.30.turned, f32[2,176,128]{2,1,0:T(8,128)S(1)} %some_kernel.1.begun, bf16[3600,7500]{1,0:T(8,128)(2,1)} %bitcast.15, ...), custom_call_target="tpu_custom_call" | custom-call | flops 2350907392 | bytes 9183232 | tf_op jit(solution)/shard_map/rest_kernel/pallas_call | solution.py:290
  76.1 3.1 %collective-permute-done.16.got_ref = s16[15,16,256]{2,1,0:T(8,128)(2,1)S(1)} collective-permute-done((s16[15,16,256]{2,1,0:T(8,128)(2,1)S(1)}, s16[15,16,256]{2,1,0:T(8,128)(2,1)S(1)}, u32[]{:S(2)}, u32[]{:S(2)}) %collective-permute-start.16) | collective-permute-done | bytes 122912 | tf_op jit(solution)/shard_map/ppermute | solution.py:477
  82.0 2.2 %collective-permute-start.20 = (s16[4,64,128]{2,1,0:T(8,128)(2,1)S(1)}, s16[4,64,128]{2,1,0:T(8,128)(2,1)S(1)}, u32[]{:S(2)}, u32[]{:S(2)}) collective-permute-start(s16[4,64,128]{2,1,0:T(8,128)(2,1)S(1)} %get-tuple-element.38), channel_id=1, source_target_pairs={{0,12},{8,4},{16,0},{24,8},{28,16},{20,24},{12,28},{4,20},{1,13},{... | collective-permute-start | bytes 196616 | tf_op jit(solution)/shard_map/ppermute | solution.py:500
  84.9 3.2 %collective-permute-start.22 = (s16[4,64,128]{2,1,0:T(8,128)(2,1)S(1)}, s16[4,64,128]{2,1,0:T(8,128)(2,1)S(1)}, u32[]{:S(2)}, u32[]{:S(2)}) collective-permute-start(s16[4,64,128]{2,1,0:T(8,128)(2,1)S(1)} %get-tuple-element.40), channel_id=1, source_target_pairs={{0,20},{8,12},{16,4},{24,0},{28,8},{20,16},{12,24},{4,28},{1,21},{... | collective-permute-start | bytes 196616 | tf_op jit(solution)/shard_map/ppermute | solution.py:500
  88.7 4.2 %collective-permute-start.24 = (s16[4,64,128]{2,1,0:T(8,128)(2,1)S(1)}, s16[4,64,128]{2,1,0:T(8,128)(2,1)S(1)}, u32[]{:S(2)}, u32[]{:S(2)}) collective-permute-start(s16[4,64,128]{2,1,0:T(8,128)(2,1)S(1)} %get-tuple-element.42), channel_id=1, source_target_pairs={{0,28},{8,20},{16,12},{24,4},{28,0},{20,8},{12,16},{4,24},{1,29},{... | collective-permute-start | bytes 196616 | tf_op jit(solution)/shard_map/ppermute | solution.py:500
  93.1 3.9 %collective-permute-done.23.refs_6_ = s16[4,64,128]{2,1,0:T(8,128)(2,1)S(1)} collective-permute-done((s16[4,64,128]{2,1,0:T(8,128)(2,1)S(1)}, s16[4,64,128]{2,1,0:T(8,128)(2,1)S(1)}, u32[]{:S(2)}, u32[]{:S(2)}) %collective-permute-start.23) | collective-permute-done | bytes 65568 | tf_op jit(solution)/shard_map/ppermute | solution.py:500
  97.1 2.2 %update_kernel.1 = f32[15,32,480]{2,1,0:T(8,128)} custom-call(s32[1]{0:T(128)} %bitcast.me_ref, f32[15]{0:T(128)S(1)} %copy-done.7, s32[15]{0:T(128)S(1)} %copy-done.8, s16[4,64,128]{2,1,0:T(8,128)(2,1)S(1)} %get-tuple-element.35.refs_0_, s16[4,64,128]{2,1,0:T(8,128)(2,1)S(1)} %collective-permute-done.18.refs_1_, ...), custom_call_target="tpu_custom_call" | custom-call | flops 10000000 | bytes 4000000 | tf_op jit(solution)/shard_map/update_kernel/pallas_call | solution.py:290
  (66 shorter events, 20.4 us)
Async XLA Ops:
  1.0 9.8 %collective-permute-start = (bf16[32,3840]{1,0:T(8,128)(2,1)S(1)}, bf16[32,3840]{1,0:T(8,128)(2,1)S(1)}, u32[]{:S(2)}, u32[]{:S(2)}) collective-permute-start(bf16[32,3840]{1,0:T(8,128)(2,1)S(1)} %slice.9.refs_0_), channel_id=1, source_target_pairs={{0,8},{8,16},{16,24},{24,28},{28,20},{20,12},{12,4},{4,0},{1,9},{9... | collective-permute-start | bytes 737288 | tf_op jit(solution)/shard_map/ppermute | solution.py:352
  4.0 8.9 %collective-permute-start.1 = (bf16[32,3840]{1,0:T(8,128)(2,1)S(1)}, bf16[32,3840]{1,0:T(8,128)(2,1)S(1)}, u32[]{:S(2)}, u32[]{:S(2)}) collective-permute-start(bf16[32,3840]{1,0:T(8,128)(2,1)S(1)} %slice.9.refs_0_), channel_id=1, source_target_pairs={{8,0},{16,8},{24,16},{28,24},{20,28},{12,20},{4,12},{0,4},{9,1},{1... | collective-permute-start | bytes 737288 | tf_op jit(solution)/shard_map/ppermute | solution.py:355
  5.0 10.8 %collective-permute-start.3 = (bf16[32,3712]{1,0:T(8,128)(2,1)S(1)}, bf16[32,3712]{1,0:T(8,128)(2,1)S(1)}, u32[]{:S(2)}, u32[]{:S(2)}) collective-permute-start(bf16[32,3712]{1,0:T(8,128)(2,1)S(1)} %pad.8.refs_4_), channel_id=1, source_target_pairs={{0,8},{8,16},{16,24},{24,28},{28,20},{20,12},{12,4},{4,0},{1,9},{9... | collective-permute-start | bytes 712712 | tf_op jit(solution)/shard_map/ppermute | solution.py:352
  7.1 10.9 %collective-permute-start.4 = (bf16[32,3712]{1,0:T(8,128)(2,1)S(1)}, bf16[32,3712]{1,0:T(8,128)(2,1)S(1)}, u32[]{:S(2)}, u32[]{:S(2)}) collective-permute-start(bf16[32,3712]{1,0:T(8,128)(2,1)S(1)} %pad.8.refs_4_), channel_id=1, source_target_pairs={{8,0},{16,8},{24,16},{28,24},{20,28},{12,20},{4,12},{0,4},{9,1},{1... | collective-permute-start | bytes 712712 | tf_op jit(solution)/shard_map/ppermute | solution.py:355
  10.8 10.4 %collective-permute-start.2 = (bf16[32,3840]{1,0:T(8,128)(2,1)S(1)}, bf16[32,3840]{1,0:T(8,128)(2,1)S(1)}, u32[]{:S(2)}, u32[]{:S(2)}) collective-permute-start(bf16[32,3840]{1,0:T(8,128)(2,1)S(1)} %collective-permute-done.refs_1_), channel_id=1, source_target_pairs={{0,8},{8,16},{16,24},{24,28},{28,20},{20,12},{12,4},{4,0},{1,9},{9... | collective-permute-start | bytes 737288 | tf_op jit(solution)/shard_map/ppermute | solution.py:352
  12.9 10.4 %collective-permute-start.6 = (bf16[32,3840]{1,0:T(8,128)(2,1)S(1)}, bf16[32,3840]{1,0:T(8,128)(2,1)S(1)}, u32[]{:S(2)}, u32[]{:S(2)}) collective-permute-start(bf16[32,3840]{1,0:T(8,128)(2,1)S(1)} %collective-permute-done.1.refs_2_), channel_id=1, source_target_pairs={{8,0},{16,8},{24,16},{28,24},{20,28},{12,20},{4,12},{0,4},{9,1},{1... | collective-permute-start | bytes 737288 | tf_op jit(solution)/shard_map/ppermute | solution.py:355
  15.9 10.4 %collective-permute-start.5 = (bf16[32,3712]{1,0:T(8,128)(2,1)S(1)}, bf16[32,3712]{1,0:T(8,128)(2,1)S(1)}, u32[]{:S(2)}, u32[]{:S(2)}) collective-permute-start(bf16[32,3712]{1,0:T(8,128)(2,1)S(1)} %collective-permute-done.3.refs_5_), channel_id=1, source_target_pairs={{0,8},{8,16},{16,24},{24,28},{28,20},{20,12},{12,4},{4,0},{1,9},{9... | collective-permute-start | bytes 712712 | tf_op jit(solution)/shard_map/ppermute | solution.py:352
  18.0 11.0 %collective-permute-start.10 = (bf16[32,3712]{1,0:T(8,128)(2,1)S(1)}, bf16[32,3712]{1,0:T(8,128)(2,1)S(1)}, u32[]{:S(2)}, u32[]{:S(2)}) collective-permute-start(bf16[32,3712]{1,0:T(8,128)(2,1)S(1)} %collective-permute-done.4.refs_6_), channel_id=1, source_target_pairs={{8,0},{16,8},{24,16},{28,24},{20,28},{12,20},{4,12},{0,4},{9,1},{1... | collective-permute-start | bytes 712712 | tf_op jit(solution)/shard_map/ppermute | solution.py:355
  21.1 10.4 %collective-permute-start.7 = (bf16[32,3840]{1,0:T(8,128)(2,1)S(1)}, bf16[32,3840]{1,0:T(8,128)(2,1)S(1)}, u32[]{:S(2)}, u32[]{:S(2)}) collective-permute-start(bf16[32,3840]{1,0:T(8,128)(2,1)S(1)} %collective-permute-done.2.refs_3_), channel_id=1, source_target_pairs={{0,8},{8,16},{16,24},{24,28},{28,20},{20,12},{12,4},{4,0},{1,9},{9... | collective-permute-start | bytes 737288 | tf_op jit(solution)/shard_map/ppermute | solution.py:352
  23.3 10.4 %collective-permute-start.8 = (bf16[32,3840]{1,0:T(8,128)(2,1)S(1)}, bf16[32,3840]{1,0:T(8,128)(2,1)S(1)}, u32[]{:S(2)}, u32[]{:S(2)}) collective-permute-start(bf16[32,3840]{1,0:T(8,128)(2,1)S(1)} %collective-permute-done.6.refs_0_), channel_id=1, source_target_pairs={{8,0},{16,8},{24,16},{28,24},{20,28},{12,20},{4,12},{0,4},{9,1},{1... | collective-permute-start | bytes 737288 | tf_op jit(solution)/shard_map/ppermute | solution.py:355
  26.2 10.4 %collective-permute-start.11 = (bf16[32,3712]{1,0:T(8,128)(2,1)S(1)}, bf16[32,3712]{1,0:T(8,128)(2,1)S(1)}, u32[]{:S(2)}, u32[]{:S(2)}) collective-permute-start(bf16[32,3712]{1,0:T(8,128)(2,1)S(1)} %collective-permute-done.5.refs_7_), channel_id=1, source_target_pairs={{0,8},{8,16},{16,24},{24,28},{28,20},{20,12},{12,4},{4,0},{1,9},{9... | collective-permute-start | bytes 712712 | tf_op jit(solution)/shard_map/ppermute | solution.py:352
  29.0 8.2 %collective-permute-start.12 = (bf16[32,3712]{1,0:T(8,128)(2,1)S(1)}, bf16[32,3712]{1,0:T(8,128)(2,1)S(1)}, u32[]{:S(2)}, u32[]{:S(2)}) collective-permute-start(bf16[32,3712]{1,0:T(8,128)(2,1)S(1)} %collective-permute-done.10.refs_4_), channel_id=1, source_target_pairs={{8,0},{16,8},{24,16},{28,24},{20,28},{12,20},{4,12},{0,4},{9,1},{1... | collective-permute-start | bytes 712712 | tf_op jit(solution)/shard_map/ppermute | solution.py:355
  33.6 10.0 %collective-permute-start.9 = (bf16[32,3840]{1,0:T(8,128)(2,1)S(1)}, bf16[32,3840]{1,0:T(8,128)(2,1)S(1)}, u32[]{:S(2)}, u32[]{:S(2)}) collective-permute-start(bf16[32,3840]{1,0:T(8,128)(2,1)S(1)} %collective-permute-done.7.refs_1_), channel_id=1, source_target_pairs={{0,8},{8,16},{16,24},{24,28},{28,20},{20,12},{12,4},{4,0},{1,9},{9... | collective-permute-start | bytes 737288 | tf_op jit(solution)/shard_map/ppermute | solution.py:352
  37.3 6.3 %collective-permute-start.13 = (bf16[32,3712]{1,0:T(8,128)(2,1)S(1)}, bf16[32,3712]{1,0:T(8,128)(2,1)S(1)}, u32[]{:S(2)}, u32[]{:S(2)}) collective-permute-start(bf16[32,3712]{1,0:T(8,128)(2,1)S(1)} %collective-permute-done.12.refs_6_), channel_id=1, source_target_pairs={{8,0},{16,8},{24,16},{28,24},{20,28},{12,20},{4,12},{0,4},{9,1},{1... | collective-permute-start | bytes 712712 | tf_op jit(solution)/shard_map/ppermute | solution.py:355
  60.3 2.8 %collective-permute-start.14 = (s16[2,15,48,256]{3,2,1,0:T(8,128)(2,1)S(1)}, s16[2,15,48,256]{3,2,1,0:T(8,128)(2,1)S(1)}, u32[]{:S(2)}, u32[]{:S(2)}) collective-permute-start(s16[2,15,48,256]{3,2,1,0:T(8,128)(2,1)S(1)} %get-tuple-element.28), channel_id=1, source_target_pairs={{0,1},{1,0},{2,3},{3,2},{4,5},{5,4},{6,7},{7,6},{8,9},{9,8},{10,11... | collective-permute-start | bytes 2211848 | tf_op jit(solution)/shard_map/ppermute | solution.py:455
  64.0 11.0 %collective-permute-start.17 = (s16[15,48,256]{2,1,0:T(8,128)(2,1)S(1)}, s16[15,48,256]{2,1,0:T(8,128)(2,1)S(1)}, u32[]{:S(2)}, u32[]{:S(2)}) collective-permute-start(s16[15,48,256]{2,1,0:T(8,128)(2,1)S(1)} %second_send_kernel.2), channel_id=1, source_target_pairs={{0,2},{1,3},{2,0},{3,1},{4,6},{5,7},{6,4},{7,5},{8,10},{9,11},{10,... | collective-permute-start | bytes 1105928 | tf_op jit(solution)/shard_map/ppermute | solution.py:477
  73.7 5.5 %collective-permute-start.16 = (s16[15,16,256]{2,1,0:T(8,128)(2,1)S(1)}, s16[15,16,256]{2,1,0:T(8,128)(2,1)S(1)}, u32[]{:S(2)}, u32[]{:S(2)}) collective-permute-start(s16[15,16,256]{2,1,0:T(8,128)(2,1)S(1)} %second_send_kernel.3), channel_id=1, source_target_pairs={{0,2},{1,3},{2,0},{3,1},{4,6},{5,7},{6,4},{7,5},{8,10},{9,11},{10,... | collective-permute-start | bytes 368648 | tf_op jit(solution)/shard_map/ppermute | solution.py:477
  79.9 8.2 %collective-permute-start.18 = (s16[4,64,128]{2,1,0:T(8,128)(2,1)S(1)}, s16[4,64,128]{2,1,0:T(8,128)(2,1)S(1)}, u32[]{:S(2)}, u32[]{:S(2)}) collective-permute-start(s16[4,64,128]{2,1,0:T(8,128)(2,1)S(1)} %get-tuple-element.36), channel_id=1, source_target_pairs={{0,4},{8,0},{16,8},{24,16},{28,24},{20,28},{12,20},{4,12},{1,5},{9... | collective-permute-start | bytes 196616 | tf_op jit(solution)/shard_map/ppermute | solution.py:500
  81.2 7.6 %collective-permute-start.19 = (s16[4,64,128]{2,1,0:T(8,128)(2,1)S(1)}, s16[4,64,128]{2,1,0:T(8,128)(2,1)S(1)}, u32[]{:S(2)}, u32[]{:S(2)}) collective-permute-start(s16[4,64,128]{2,1,0:T(8,128)(2,1)S(1)} %get-tuple-element.37), channel_id=1, source_target_pairs={{0,8},{8,16},{16,24},{24,28},{28,20},{20,12},{12,4},{4,0},{1,9},{9... | collective-permute-start | bytes 196616 | tf_op jit(solution)/shard_map/ppermute | solution.py:500
  82.0 11.1 %collective-permute-start.20 = (s16[4,64,128]{2,1,0:T(8,128)(2,1)S(1)}, s16[4,64,128]{2,1,0:T(8,128)(2,1)S(1)}, u32[]{:S(2)}, u32[]{:S(2)}) collective-permute-start(s16[4,64,128]{2,1,0:T(8,128)(2,1)S(1)} %get-tuple-element.38), channel_id=1, source_target_pairs={{0,12},{8,4},{16,0},{24,8},{28,16},{20,24},{12,28},{4,20},{1,13},{... | collective-permute-start | bytes 196616 | tf_op jit(solution)/shard_map/ppermute | solution.py:500
  84.2 8.9 %collective-permute-start.21 = (s16[4,64,128]{2,1,0:T(8,128)(2,1)S(1)}, s16[4,64,128]{2,1,0:T(8,128)(2,1)S(1)}, u32[]{:S(2)}, u32[]{:S(2)}) collective-permute-start(s16[4,64,128]{2,1,0:T(8,128)(2,1)S(1)} %get-tuple-element.39), channel_id=1, source_target_pairs={{0,16},{8,24},{16,28},{24,20},{28,12},{20,4},{12,0},{4,8},{1,17},{... | collective-permute-start | bytes 196616 | tf_op jit(solution)/shard_map/ppermute | solution.py:500
  84.9 8.2 %collective-permute-start.22 = (s16[4,64,128]{2,1,0:T(8,128)(2,1)S(1)}, s16[4,64,128]{2,1,0:T(8,128)(2,1)S(1)}, u32[]{:S(2)}, u32[]{:S(2)}) collective-permute-start(s16[4,64,128]{2,1,0:T(8,128)(2,1)S(1)} %get-tuple-element.40), channel_id=1, source_target_pairs={{0,20},{8,12},{16,4},{24,0},{28,8},{20,16},{12,24},{4,28},{1,21},{... | collective-permute-start | bytes 196616 | tf_op jit(solution)/shard_map/ppermute | solution.py:500
  88.1 8.9 %collective-permute-start.23 = (s16[4,64,128]{2,1,0:T(8,128)(2,1)S(1)}, s16[4,64,128]{2,1,0:T(8,128)(2,1)S(1)}, u32[]{:S(2)}, u32[]{:S(2)}) collective-permute-start(s16[4,64,128]{2,1,0:T(8,128)(2,1)S(1)} %get-tuple-element.41), channel_id=1, source_target_pairs={{0,24},{8,28},{16,20},{24,12},{28,4},{20,0},{12,8},{4,16},{1,25},{... | collective-permute-start | bytes 196616 | tf_op jit(solution)/shard_map/ppermute | solution.py:500
  88.7 8.3 %collective-permute-start.24 = (s16[4,64,128]{2,1,0:T(8,128)(2,1)S(1)}, s16[4,64,128]{2,1,0:T(8,128)(2,1)S(1)}, u32[]{:S(2)}, u32[]{:S(2)}) collective-permute-start(s16[4,64,128]{2,1,0:T(8,128)(2,1)S(1)} %get-tuple-element.42), channel_id=1, source_target_pairs={{0,28},{8,20},{16,12},{24,4},{28,0},{20,8},{12,16},{4,24},{1,29},{... | collective-permute-start | bytes 196616 | tf_op jit(solution)/shard_map/ppermute | solution.py:500
  (12 other events, 160.5 us)
